TPU v7x, 32 devices: a whole 2x2x4 slice. The times are simulated.
32 devices in a mesh: dp: 16 (over z, y, x), tensor: 2 (over core).
Axes of the slice: x: 2, y: 2, z: 4, core: 2. Of those that a mesh axis runs over, the one named last changes fastest.
Arguments:
- tokens: bfloat16 [16384, 1536], P(('dp', 'tensor')), may hold values from -6 to 6
- w_query: float32 [1536, 1536], P('dp', 'tensor'), may hold values from -0.15625 to 0.15625
- w_key: float32 [1536, 1536], P('dp', 'tensor'), may hold values from -0.15625 to 0.15625
- w_value: float32 [1536, 1536], P('dp', 'tensor'), may hold values from -0.15625 to 0.15625
- w_gate_attn: float32 [1536, 1536], P('dp', 'tensor'), may hold values from -0.15625 to 0.15625
- w_forget: float32 [1536, 24], P('dp', 'tensor'), may hold values from -0.15625 to 0.15625
- forget_bias: float32 [24], P('tensor'), may hold values from 1 to 7
- w_out: float32 [1536, 1536], P('tensor', 'dp'), may hold values from -2.5 to 2.5
- norm_attn: float32 [1536], P(('dp', 'tensor')), may hold values from 0.25 to 1.75
- norm_mlp: float32 [1536], P(('dp', 'tensor')), may hold values from 0.25 to 1.75
- w_gate: float32 [1536, 4096], P('dp', 'tensor'), may hold values from -0.15625 to 0.15625
- w_up: float32 [1536, 4096], P('dp', 'tensor'), may hold values from -0.15625 to 0.15625
- w_down: float32 [4096, 1536], P('tensor', 'dp'), may hold values from -0.09375 to 0.09375
- cotangent: bfloat16 [16384, 1536], P(('dp', 'tensor')), may hold values from -6 to 6
Outputs:
- mixed: bfloat16 [16384, 1536], P(('dp', 'tensor'))
- tokens_grad: bfloat16 [16384, 1536], P(('dp', 'tensor'))
- query_grad: float32 [1536, 1536], P('dp', 'tensor')
- key_grad: float32 [1536, 1536], P('dp', 'tensor')
- value_grad: float32 [1536, 1536], P('dp', 'tensor')
- gate_attn_grad: float32 [1536, 1536], P('dp', 'tensor')
- forget_grad: float32 [1536, 24], P('dp', 'tensor')
- forget_bias_grad: float32 [24], P('tensor')
- out_grad: float32 [1536, 1536], P('tensor', 'dp')
- norm_attn_grad: float32 [1536], P(('dp', 'tensor'))
- norm_mlp_grad: float32 [1536], P(('dp', 'tensor'))
- gate_grad: float32 [1536, 4096], P('dp', 'tensor')
- up_grad: float32 [1536, 4096], P('dp', 'tensor')
- down_grad: float32 [4096, 1536], P('tensor', 'dp')
All inputs are finite; a program needn't handle non-finite values.
Results may differ from a plain program's by a relative error of at most 0.014.
The roundings to bfloat16 on the way count: a program that leaves them out, or rounds other values in their place, can miss the bound.
Values may be sent and summed in bfloat16 or wider, within the bound.
No kernel may reach another device: no remote copies, remote signals or barrier semaphores. Data moves between devices by JAX's collectives and lax.ppermute only.
A program may use at most 256 MiB of HBM per device.

v0:
```python
import jax
import jax.numpy as jnp
from jax import lax
from jax.sharding import PartitionSpec as P

EPSILON = 1e-06


def lower(values):
    return values.astype(jnp.bfloat16)


def matmul(left, right):
    return jnp.dot(left, right, preferred_element_type=jnp.float32)


def first_contract(left, right):
    return lax.dot_general(
        left, right, (((0,), (0,)), ((), ())), preferred_element_type=jnp.float32
    )


def second_contract(left, right):
    return lax.dot_general(
        left, right, (((1,), (1,)), ((), ())), preferred_element_type=jnp.float32
    )


def statistics(values):
    inverse = lax.rsqrt(jnp.mean(values * values, axis=-1, keepdims=True) + EPSILON)
    return (values * inverse, inverse)


def norm_backward(unit, inverse, gain, grad):
    scaled = gain * grad
    return inverse * (scaled - unit * jnp.mean(scaled * unit, axis=-1, keepdims=True))


def gather_rows(values):
    return lax.all_gather(values, "tensor", axis=0, tiled=True)


def reduce_rows(values):
    return lax.psum_scatter(values, "tensor", scatter_dimension=0, tiled=True)


def gather_grads(values):
    return lax.all_gather(values, "tensor", axis=0, tiled=True)


def reduce_grads(values):
    return lax.psum_scatter(values, "tensor", scatter_dimension=0, tiled=True)


def per_device(
    tokens,
    w_query,
    w_key,
    w_value,
    w_gate_attn,
    w_forget,
    forget_bias,
    w_out,
    norm_attn,
    norm_mlp,
    w_gate,
    w_up,
    w_down,
    cotangent,
):
    heads_here = forget_bias.shape[0]
    head_size = w_query.shape[1] // heads_here
    scale = head_size ** (-0.5)
    dp_count = lax.axis_size("dp")
    gain_attn, gain_mlp = (
        lax.all_gather(norm_attn, ("dp", "tensor"), axis=0, tiled=True),
        lax.all_gather(norm_mlp, ("dp", "tensor"), axis=0, tiled=True),
    )
    attn_weights = (
        lax.all_gather(lower(w_query), "dp", axis=0, tiled=True),
        lax.all_gather(lower(w_key), "dp", axis=0, tiled=True),
        lax.all_gather(lower(w_value), "dp", axis=0, tiled=True),
        lax.all_gather(lower(w_gate_attn), "dp", axis=0, tiled=True),
        lax.all_gather(lower(w_forget), "dp", axis=0, tiled=True),
        lax.all_gather(lower(w_out), "dp", axis=1, tiled=True),
    )
    query_full, key_full, value_full, gate_full, forget_full, out_full = attn_weights
    residual = tokens.astype(jnp.float32)
    unit_attn, inverse_attn = statistics(residual)
    normed_attn = gather_rows(lower(unit_attn * gain_attn))
    length = normed_attn.shape[0]
    span = min(512, length)
    blocks = length // span
    queries = lower(matmul(normed_attn, query_full)).reshape(length, heads_here, head_size)
    keys = lower(matmul(normed_attn, key_full)).reshape(length, heads_here, head_size)
    values_all = lower(matmul(normed_attn, value_full)).reshape(length, heads_here, head_size)
    forget_logit = matmul(normed_attn, forget_full) + forget_bias
    decay_heads = jnp.cumsum(-jnp.log1p(jnp.exp(-forget_logit)), axis=0).T
    gate_logit = matmul(normed_attn, gate_full)
    key_place = lax.broadcasted_iota(jnp.int32, (span, length), 1)
    query_place = lax.broadcasted_iota(jnp.int32, (span, length), 0)

    def block_scores(offset, query_block):
        raw_scores = jnp.einsum(
            "qhd,khd->hqk", query_block, keys, preferred_element_type=jnp.float32
        )
        nearby = lax.dynamic_slice_in_dim(decay_heads, offset, span, 1)
        scores = raw_scores * scale + nearby[:, :, None] - decay_heads[:, None, :]
        return jnp.where((key_place <= query_place + offset)[None], scores, -1e30)

    def forward_block(number):
        offset = number * span
        query_block = lax.dynamic_slice_in_dim(queries, offset, span, 0)
        scores = block_scores(offset, query_block)
        highest = jnp.max(scores, axis=-1, keepdims=True)
        exp_scores = jnp.exp(scores - highest)
        totals = jnp.sum(exp_scores, axis=-1, keepdims=True)
        probs = lower(exp_scores / totals)
        output = jnp.einsum("hqk,khd->qhd", probs, values_all, preferred_element_type=jnp.float32)
        return (output, (highest + jnp.log(totals))[:, :, 0])

    outputs, logsums = lax.map(forward_block, jnp.arange(blocks))
    attended = outputs.reshape(length, heads_here * head_size)
    gate_sig = jax.nn.sigmoid(gate_logit)
    gated = lower(attended * gate_sig)
    middle = residual + reduce_rows(matmul(gated, out_full))
    unit_mlp, inverse_mlp = statistics(middle)
    normed_mlp = gather_rows(lower(unit_mlp * gain_mlp))
    mlp_weights = (
        lax.all_gather(lower(w_gate), "dp", axis=0, tiled=True),
        lax.all_gather(lower(w_up), "dp", axis=0, tiled=True),
        lax.all_gather(lower(w_down), "dp", axis=1, tiled=True),
    )
    gate_w, up_w, down_w = mlp_weights
    gate_act = matmul(normed_mlp, gate_w)
    up_act = matmul(normed_mlp, up_w)
    gate_sigmoid = jax.nn.sigmoid(gate_act)
    hidden = lower(gate_act * gate_sigmoid * up_act)
    mixed = (middle + reduce_rows(matmul(hidden, down_w))).astype(jnp.bfloat16)
    gate_back, up_back, down_back = (
        lax.all_gather(lower(w_gate), "dp", axis=0, tiled=True),
        lax.all_gather(lower(w_up), "dp", axis=0, tiled=True),
        lax.all_gather(lower(w_down), "dp", axis=1, tiled=True),
    )
    grad_output = gather_grads(cotangent)
    down_part = first_contract(hidden, grad_output)
    grad_hidden = second_contract(grad_output, down_back)
    grad_up = lower(grad_hidden * (gate_act * gate_sigmoid))
    grad_gate = lower(grad_hidden * up_act * gate_sigmoid * (1.0 + gate_act * (1.0 - gate_sigmoid)))
    gate_grad, up_grad, down_grad = (
        lax.psum_scatter(
            first_contract(normed_mlp, grad_gate), "dp", scatter_dimension=0, tiled=True
        ),
        lax.psum_scatter(
            first_contract(normed_mlp, grad_up), "dp", scatter_dimension=0, tiled=True
        ),
        lax.psum_scatter(down_part, "dp", scatter_dimension=1, tiled=True),
    )
    grad_normed_mlp = reduce_grads(
        second_contract(grad_gate, gate_back) + second_contract(grad_up, up_back)
    )
    gain_mlp_part = jnp.sum(grad_normed_mlp * unit_mlp, axis=0)
    grad_middle = cotangent.astype(jnp.float32) + norm_backward(
        unit_mlp, inverse_mlp, gain_mlp, grad_normed_mlp
    )
    query_back, key_back, value_back, gate_attn_back, forget_back, out_back = (
        lax.all_gather(lower(w_query), "dp", axis=0, tiled=True),
        lax.all_gather(lower(w_key), "dp", axis=0, tiled=True),
        lax.all_gather(lower(w_value), "dp", axis=0, tiled=True),
        lax.all_gather(lower(w_gate_attn), "dp", axis=0, tiled=True),
        lax.all_gather(lower(w_forget), "dp", axis=0, tiled=True),
        lax.all_gather(lower(w_out), "dp", axis=1, tiled=True),
    )
    grad_branch = gather_grads(lower(grad_middle))
    out_part = first_contract(gated, grad_branch)
    grad_gated = second_contract(grad_branch, out_back)
    grad_attended = lower(grad_gated * gate_sig).reshape(length, heads_here, head_size)
    grad_gate_logit = lower(grad_gated * attended * gate_sig * (1.0 - gate_sig))

    def backward_block(carry, number):
        key_total, value_total, column_total = carry
        offset = number * span
        query_block = lax.dynamic_slice_in_dim(queries, offset, span, 0)
        grad_block = lax.dynamic_slice_in_dim(grad_attended, offset, span, 0)
        scores = block_scores(offset, query_block)
        probs = jnp.exp(scores - logsums[number][:, :, None])
        value_total = value_total + jnp.einsum(
            "hqk,qhd->khd", lower(probs), grad_block, preferred_element_type=jnp.float32
        )
        grad_probs = jnp.einsum(
            "qhd,khd->hqk", grad_block, values_all, preferred_element_type=jnp.float32
        )
        centre = jnp.sum(probs * grad_probs, axis=-1, keepdims=True)
        grad_scores = lower(probs * (grad_probs - centre))
        query_part = (
            jnp.einsum("hqk,khd->qhd", grad_scores, keys, preferred_element_type=jnp.float32)
            * scale
        )
        key_total = (
            key_total
            + jnp.einsum(
                "hqk,qhd->khd", grad_scores, query_block, preferred_element_type=jnp.float32
            )
            * scale
        )
        wide_scores = grad_scores.astype(jnp.float32)
        column_total = column_total + jnp.sum(wide_scores, axis=1)
        return ((key_total, value_total, column_total), (query_part, jnp.sum(wide_scores, axis=2)))

    start_carry = (
        jnp.zeros((length, heads_here, head_size), jnp.float32),
        jnp.zeros((length, heads_here, head_size), jnp.float32),
        jnp.zeros((heads_here, length), jnp.float32),
    )
    (key_total, value_total, column_total), (query_parts, row_parts) = lax.scan(
        backward_block, start_carry, jnp.arange(blocks)
    )
    grad_queries = lower(query_parts.reshape(length, heads_here * head_size))
    grad_keys = lower(key_total.reshape(length, heads_here * head_size))
    grad_values = lower(value_total.reshape(length, heads_here * head_size))
    row_total = row_parts.transpose(1, 0, 2).reshape(heads_here, length)
    grad_decay = (row_total - column_total).T
    grad_log = lax.cumsum(grad_decay, axis=0, reverse=True)
    grad_forget = lower(grad_log * jax.nn.sigmoid(-forget_logit))
    bias_part = jnp.sum(grad_forget.astype(jnp.float32), axis=0)
    bias_rows = jnp.broadcast_to(bias_part[None, :], (dp_count, heads_here))
    attention_sums = (
        lax.psum_scatter(
            first_contract(normed_attn, grad_queries), "dp", scatter_dimension=0, tiled=True
        ),
        lax.psum_scatter(
            first_contract(normed_attn, grad_keys), "dp", scatter_dimension=0, tiled=True
        ),
        lax.psum_scatter(
            first_contract(normed_attn, grad_values), "dp", scatter_dimension=0, tiled=True
        ),
        lax.psum_scatter(
            first_contract(normed_attn, grad_gate_logit), "dp", scatter_dimension=0, tiled=True
        ),
        lax.psum_scatter(
            first_contract(normed_attn, grad_forget), "dp", scatter_dimension=0, tiled=True
        ),
        lax.psum_scatter(out_part, "dp", scatter_dimension=1, tiled=True),
        lax.psum_scatter(bias_rows, "dp", scatter_dimension=0, tiled=True),
    )
    query_grad, key_grad, value_grad, gate_attn_grad, forget_grad, out_grad, bias_sum = (
        attention_sums
    )
    grad_normed_attn = reduce_grads(
        second_contract(grad_queries, query_back)
        + second_contract(grad_keys, key_back)
        + second_contract(grad_values, value_back)
        + second_contract(grad_gate_logit, gate_attn_back)
        + second_contract(grad_forget, forget_back)
    )
    gain_attn_part = jnp.sum(grad_normed_attn * unit_attn, axis=0)
    tokens_grad = (
        grad_middle + norm_backward(unit_attn, inverse_attn, gain_attn, grad_normed_attn)
    ).astype(jnp.bfloat16)
    norm_attn_grad, norm_mlp_grad = (
        lax.psum_scatter(gain_attn_part, ("dp", "tensor"), scatter_dimension=0, tiled=True),
        lax.psum_scatter(gain_mlp_part, ("dp", "tensor"), scatter_dimension=0, tiled=True),
    )
    return (
        mixed,
        tokens_grad,
        query_grad,
        key_grad,
        value_grad,
        gate_attn_grad,
        forget_grad,
        bias_sum.reshape(heads_here),
        out_grad,
        norm_attn_grad,
        norm_mlp_grad,
        gate_grad,
        up_grad,
        down_grad,
    )


def solution(mesh):
    return jax.shard_map(
        per_device,
        mesh=mesh,
        in_specs=(
            P(("dp", "tensor"), None),
            P("dp", "tensor"),
            P("dp", "tensor"),
            P("dp", "tensor"),
            P("dp", "tensor"),
            P("dp", "tensor"),
            P("tensor"),
            P("tensor", "dp"),
            P(("dp", "tensor")),
            P(("dp", "tensor")),
            P("dp", "tensor"),
            P("dp", "tensor"),
            P("tensor", "dp"),
            P(("dp", "tensor"), None),
        ),
        out_specs=(
            P(("dp", "tensor"), None),
            P(("dp", "tensor"), None),
            P("dp", "tensor"),
            P("dp", "tensor"),
            P("dp", "tensor"),
            P("dp", "tensor"),
            P("dp", "tensor"),
            P("tensor"),
            P("tensor", "dp"),
            P(("dp", "tensor")),
            P(("dp", "tensor")),
            P("dp", "tensor"),
            P("dp", "tensor"),
            P("tensor", "dp"),
        ),
        check_vma=False,
    )
```

profile of v0, /device:TPU:0, one launch (start us, length us, event | category | flops | bytes accessed | tf_op | source)
XLA Modules:
  0.0 2557.8 jit_solution(13196720891665984049)
XLA Ops:
  10.9 42.1 %all-reduce.6 = (f32[1536]{0:T(1024)S(1)}, f32[1536]{0:T(1024)}) all-reduce(f32[1536]{0:T(1024)S(1)} %dynamic-update-slice, f32[1536]{0:T(1024)S(1)} %dynamic-update-slice.1), channel_id=1, replica_groups=mesh['dp'=16,'tensor'=2] {'dp','tensor'}, use_global_device_ids=true, to_apply=%add | all-reduce | flops 3072 | bytes 24576
  60.0 40.4 %all-gather = bf16[16,96,12]{1,2,0:T(8,128)(2,1)S(1)} all-gather(bf16[1,96,12]{1,2,0:T(8,128)(2,1)S(1)} %convert_bitcast_fusion), channel_id=1, replica_groups=mesh['dp'=16,'tensor'=2] {'dp'}, dimensions={0}, use_global_device_ids=true | all-gather | bytes 39168 | tf_op jit(solution)/shard_map/all_gather | solution.py:84
  107.9 27.7 %all-gather.20.cloned.1.call-done = bf16[1536,768]{1,0:T(8,128)(2,1)} async-done(((bf16[96,768]{1,0:T(8,128)(2,1)}), bf16[1536,768]{1,0:T(8,128)(2,1)}) %all-gather.20.cloned.1.call-update) | async-done | bytes 2359312 | tf_op jit(solution)/shard_map/all_gather | solution.py:82
  140.9 59.2 %all-gather.18.cloned.1.call-done = bf16[1536,768]{1,0:T(8,128)(2,1)} async-done(((bf16[96,768]{1,0:T(8,128)(2,1)}), bf16[1536,768]{1,0:T(8,128)(2,1)}) %all-gather.18.cloned.1.call-update) | async-done | bytes 2359312 | tf_op jit(solution)/shard_map/all_gather | solution.py:81
  206.6 57.9 %all-gather.16.cloned.1.call-done = bf16[1536,768]{1,0:T(8,128)(2,1)} async-done(((bf16[96,768]{1,0:T(8,128)(2,1)}), bf16[1536,768]{1,0:T(8,128)(2,1)}) %all-gather.16.cloned.1.call-update) | async-done | bytes 2359312 | tf_op jit(solution)/shard_map/all_gather | solution.py:80
  270.9 145.4 %while.32 = (s32[]{:T(128)}, f32[2,512,12,64]{1,0,3,2:T(2,128)}, f32[2,12,512]{2,1,0:T(8,128)S(1)}, s32[2]{0:T(128)S(1)}, bf16[1024,12,64]{0,2,1:T(8,128)(2,1)},...) while((s32[]{:T(128)}, f32[2,512,12,64]{1,0,3,2:T(2,128)}, ...), condition=%wide.region_6.7_spmd.clone, body=%wide.region_3.6_spmd.clone.sunk | while | flops 1724901376 | bytes 190546144 | solution.py:122
  272.8 13.4 fusion.142
  286.2 13.8 fusion.143
  315.0 28.7 %dynamic_update_slice.26 = f32[2,512,12,64]{1,0,3,2:T(2,128)} dynamic-update-slice(f32[2,512,12,64]{1,0,3,2:T(2,128)} %get-tuple-element.447, f32[1,512,12,64]{1,0,3,2:T(1,128)S(1)} %copy.72, s32[]{:T(128)S(6)} %copy.82, s32[]{:T(128)} %constant.42.clone.1..sunk, s32[]{:T(128)} %constant.42.clone.1..sunk, s32[]{:T(128)} %constant.42.clone.1..sunk) | dynamic-update-slice | bytes 3145732 | tf_op jit(solution)/shard_map/while/body/jit(dynamic_update_index_in_dim)/dynamic_update_slice | solution.py:122
  345.4 13.5 fusion.142
  358.9 13.7 fusion.143
  374.5 10.0 fusion.144
  387.5 28.7 %dynamic_update_slice.26 = f32[2,512,12,64]{1,0,3,2:T(2,128)} dynamic-update-slice(f32[2,512,12,64]{1,0,3,2:T(2,128)} %get-tuple-element.447, f32[1,512,12,64]{1,0,3,2:T(1,128)S(1)} %copy.72, s32[]{:T(128)S(6)} %copy.82, s32[]{:T(128)} %constant.42.clone.1..sunk, s32[]{:T(128)} %constant.42.clone.1..sunk, s32[]{:T(128)} %constant.42.clone.1..sunk) | dynamic-update-slice | bytes 3145732 | tf_op jit(solution)/shard_map/while/body/jit(dynamic_update_index_in_dim)/dynamic_update_slice | solution.py:122
  438.4 11.6 reduce-scatter.16.cloned.1.call-done
  459.4 89.6 %all-gather.30.cloned.1.call-done = bf16[1536,2048]{1,0:T(8,128)(2,1)} async-done(((bf16[96,2048]{1,0:T(8,128)(2,1)}), bf16[1536,2048]{1,0:T(8,128)(2,1)}) %all-gather.30.cloned.1.call-update) | async-done | bytes 6291472 | tf_op jit(solution)/shard_map/all_gather | solution.py:131
  549.0 12.1 all-gather.26.cloned.1.call-done
  561.1 12.0 fusion.48
  573.1 86.9 %all-gather.28.cloned.1.call-done = bf16[1536,2048]{1,0:T(8,128)(2,1)} async-done(((bf16[96,2048]{1,0:T(8,128)(2,1)}), bf16[1536,2048]{1,0:T(8,128)(2,1)}) %all-gather.28.cloned.1.call-update) | async-done | bytes 6291472 | tf_op jit(solution)/shard_map/all_gather | solution.py:130
  660.0 11.7 fusion.47
  672.0 98.9 %all-gather.32.cloned.1.call-done = bf16[2048,1536]{0,1:T(8,128)(2,1)} async-done(((bf16[2048,96]{0,1:T(8,128)(2,1)}), bf16[2048,1536]{0,1:T(8,128)(2,1)}) %all-gather.32.cloned.1.call-update) | async-done | bytes 6291472 | tf_op jit(solution)/shard_map/all_gather | solution.py:132
  771.0 19.0 multiply_convert_fusion.1
  798.9 10.8 convolution_add_fusion
  809.7 12.9 reduce-scatter.20.cloned.1.call-done
  828.2 13.3 all-gather.36.cloned.1.call-done
  851.3 178.6 %while.33 = (s32[]{:T(128)}, f32[1024,12,64]{0,2,1:T(8,128)S(1)}, f32[1024,12,64]{0,2,1:T(8,128)}, f32[12,1024]{1,0:T(8,128)S(1)}, bf16[2,512,12,64]{1,3,2,0:T(8...) while((s32[]{:T(128)}, f32[1024,12,64]{0,2,1:T(8,128)S(1)}, ...), condition=%wide.region_16.17_spmd.clone, body=%wide.region_12.16_spmd.clone.sunk | while | flops 4119986176 | bytes 219029888 | solution.py:215
  856.2 13.4 fusion.154
  869.6 19.7 multiply_reduce_fusion.5
  889.2 21.6 convert_reduce_fusion.4
  910.8 12.1 bitcast_add_fusion.5
  944.7 13.4 fusion.154
  958.1 19.7 multiply_reduce_fusion.5
  977.8 21.6 convert_reduce_fusion.4
  999.3 13.0 bitcast_add_fusion.5
  1030.9 14.9 reduce-window.16
  1070.8 11.9 fusion.49
  1084.6 11.4 fusion.63
  1097.9 11.4 fusion.62
  1109.4 11.4 fusion.61
  1154.9 42.4 %all-reduce.2 = f32[16,12]{1,0:T(8,128)S(1)} all-reduce(f32[16,12]{1,0:T(8,128)S(1)} %broadcast_in_dim.60), channel_id=11, replica_groups=mesh['dp'=16,'tensor'=2] {'dp'}, use_global_device_ids=true, to_apply=%region_27.28.clone | all-reduce | flops 192 | bytes 1536
  1203.7 38.3 %all-reduce.5 = (f32[1536]{0:T(1024)S(1)}, f32[1536]{0:T(1024)S(1)}) all-reduce(f32[1536]{0:T(1024)S(1)} %get-tuple-element.224, f32[1536]{0:T(1024)S(1)} %copy-done.29), channel_id=13, replica_groups=mesh['dp'=16,'tensor'=2] {'dp','tensor'}, use_global_device_ids=true, to_apply=%region_30.31.clone | all-reduce | flops 3072 | bytes 24576
  1250.1 169.3 %reduce-scatter.38.cloned.1.call-done = f32[2048,96]{0,1:T(8,128)} async-done(((f32[2048,1536]{0,1:T(8,128)}), f32[2048,96]{0,1:T(8,128)}) %reduce-scatter.38.cloned.1.call-update) | async-done | bytes 786448 | tf_op jit(solution)/shard_map/reduce_scatter | solution.py:157
  1419.4 210.8 %reduce-scatter.36.cloned.1.call-done = f32[96,2048]{1,0:T(8,128)} async-done(((f32[1536,2048]{1,0:T(8,128)}), f32[96,2048]{1,0:T(8,128)}) %reduce-scatter.36.cloned.1.call-update) | async-done | bytes 786448 | tf_op jit(solution)/shard_map/reduce_scatter | solution.py:154
  1630.2 209.8 %reduce-scatter.34.cloned.1.call-done = f32[96,2048]{1,0:T(8,128)} async-done(((f32[1536,2048]{1,0:T(8,128)}), f32[96,2048]{1,0:T(8,128)}) %reduce-scatter.34.cloned.1.call-update) | async-done | bytes 786448 | tf_op jit(solution)/shard_map/reduce_scatter | solution.py:151
  1840.0 142.8 %reduce-scatter.32.cloned.1.call-done = f32[768,96]{0,1:T(8,128)} async-done(((f32[768,1536]{0,1:T(8,128)}), f32[768,96]{0,1:T(8,128)}) %reduce-scatter.32.cloned.1.call-update) | async-done | bytes 294928 | tf_op jit(solution)/shard_map/reduce_scatter | solution.py:243
  1982.8 141.4 %reduce-scatter.24.cloned.1.call-done = f32[96,768]{1,0:T(8,128)} async-done(((f32[1536,768]{1,0:T(8,128)}), f32[96,768]{1,0:T(8,128)}) %reduce-scatter.24.cloned.1.call-update) | async-done | bytes 294928 | tf_op jit(solution)/shard_map/reduce_scatter | solution.py:228
  2124.2 143.1 %reduce-scatter.28.cloned.1.call-done = f32[96,768]{1,0:T(8,128)} async-done(((f32[1536,768]{1,0:T(8,128)}), f32[96,768]{1,0:T(8,128)}) %reduce-scatter.28.cloned.1.call-update) | async-done | bytes 294928 | tf_op jit(solution)/shard_map/reduce_scatter | solution.py:234
  2267.3 141.2 %reduce-scatter.26.cloned.1.call-done = f32[96,768]{1,0:T(8,128)} async-done(((f32[1536,768]{1,0:T(8,128)}), f32[96,768]{1,0:T(8,128)}) %reduce-scatter.26.cloned.1.call-update) | async-done | bytes 294928 | tf_op jit(solution)/shard_map/reduce_scatter | solution.py:231
  2408.5 142.6 %reduce-scatter.30.cloned.1.call-done = f32[96,768]{1,0:T(8,128)} async-done(((f32[1536,768]{1,0:T(8,128)}), f32[96,768]{1,0:T(8,128)}) %reduce-scatter.30.cloned.1.call-update) | async-done | bytes 294928 | tf_op jit(solution)/shard_map/reduce_scatter | solution.py:237
  (279 shorter events, 230.0 us)
Async XLA Ops:
  7.2 93.4 %all-gather.14.cloned.1.call-start = ((), (), s32[]{:S(2)}) async-start(), calls=%async_computation.13 | async-start | bytes 4718592 | tf_op jit(solution)/shard_map/all_gather | solution.py:40
  7.2 48.9 %copy-start.16 = (f32[96,768]{1,0:T(8,128)S(1)}, f32[96,768]{1,0:T(8,128)}, u32[]{:S(2)}) copy-start(f32[96,768]{1,0:T(8,128)} %param.21) | copy-start | bytes 884740
  7.2 49.7 %copy-start.17 = (f32[96,768]{1,0:T(8,128)S(1)}, f32[96,768]{1,0:T(8,128)}, u32[]{:S(2)}) copy-start(f32[96,768]{1,0:T(8,128)} %param.20) | copy-start | bytes 884740
  9.1 48.6 %copy-start.18 = (f32[96,768]{1,0:T(8,128)S(1)}, f32[96,768]{1,0:T(8,128)}, u32[]{:S(2)}) copy-start(f32[96,768]{1,0:T(8,128)} %param.19) | copy-start | bytes 884740
  9.1 49.2 %copy-start.30 = (f32[512]{0:T(512)}, f32[512]{0:T(512)S(1)}, u32[]{:S(2)}) copy-start(f32[512]{0:T(512)S(1)} %add_rsqrt_fusion.1) | copy-start | bytes 6148
  56.1 44.5 %copy-start.35 = (f32[12]{0:T(128)S(1)}, f32[12]{0:T(128)}, u32[]{:S(2)}) copy-start(f32[12]{0:T(128)} %param.24) | copy-start | bytes 148
  56.1 79.6 %all-gather.20.cloned.1.call-start = ((), (), s32[]{:S(2)}) async-start(), calls=%async_computation.16 | async-start | bytes 2506752 | tf_op jit(solution)/shard_map/all_gather | solution.py:82
  56.8 143.3 %all-gather.18.cloned.1.call-start = ((), (), s32[]{:S(2)}) async-start(), calls=%async_computation.15 | async-start | bytes 2506752 | tf_op jit(solution)/shard_map/all_gather | solution.py:81
  57.6 206.9 %all-gather.16.cloned.1.call-start = ((), (), s32[]{:S(2)}) async-start(), calls=%async_computation.14 | async-start | bytes 2506752 | tf_op jit(solution)/shard_map/all_gather | solution.py:80
  58.4 362.8 %all-gather.22.cloned.1.call-start = ((), (), s32[]{:S(2)}) async-start(), calls=%async_computation.17 | async-start | bytes 2506752 | tf_op jit(solution)/shard_map/all_gather | solution.py:83
  59.1 370.4 %all-gather.24.cloned.1.call-start = ((), (), s32[]{:S(2)}) async-start(), calls=%async_computation.18 | async-start | bytes 2506752 | tf_op jit(solution)/shard_map/all_gather | solution.py:85
  59.9 390.0 %reduce-scatter.16.cloned.1.call-start = ((), (), s32[]{:S(2)}) async-start(), calls=%async_computation.19 | async-start | bytes 9437184 | tf_op jit(solution)/shard_map/reduce_scatter | solution.py:44
  100.6 40.4 %copy-start.13 = (bf16[1536,12]{0,1:T(8,128)(2,1)}, bf16[1536,12]{0,1:T(8,128)(2,1)S(1)}, u32[]{:S(2)}) copy-start(bf16[1536,12]{0,1:T(8,128)(2,1)S(1)} %reshape.162) | copy-start | bytes 110596
  286.2 15.7 copy-start
  358.9 15.6 copy-start
  436.4 112.6 %all-gather.30.cloned.1.call-start = ((), (), s32[]{:S(2)}) async-start(), calls=%async_computation.22 | async-start | bytes 6684672 | tf_op jit(solution)/shard_map/all_gather | solution.py:131
  438.3 14.5 copy-start.23
  438.3 122.8 %all-gather.26.cloned.1.call-start = ((), (), s32[]{:S(2)}) async-start(), calls=%async_computation.20 | async-start | bytes 4718592 | tf_op jit(solution)/shard_map/all_gather | solution.py:40
  452.8 373.2 %copy-start.2 = (f32[512,1536]{1,0:T(8,128)}, f32[512,1536]{1,0:T(8,128)S(1)}, u32[]{:S(2)}) copy-start(f32[512,1536]{1,0:T(8,128)S(1)} %get-tuple-element.276) | copy-start | bytes 9437188
  452.8 373.2 %copy-start.27 = (f32[512]{0:T(512)}, f32[512]{0:T(512)S(1)}, u32[]{:S(2)}) copy-start(f32[512]{0:T(512)S(1)} %add_rsqrt_fusion) | copy-start | bytes 6148
  454.6 205.4 %all-gather.28.cloned.1.call-start = ((), (), s32[]{:S(2)}) async-start(), calls=%async_computation.21 | async-start | bytes 6684672 | tf_op jit(solution)/shard_map/all_gather | solution.py:130
  456.6 215.4 %all-gather.34.cloned.1.call-start = ((), (), s32[]{:S(2)}) async-start(), calls=%async_computation.25 | async-start | bytes 4718592 | tf_op jit(solution)/shard_map/all_gather | solution.py:48
  457.3 313.6 %all-gather.32.cloned.1.call-start = ((), (), s32[]{:S(2)}) async-start(), calls=%async_computation.23 | async-start | bytes 6684672 | tf_op jit(solution)/shard_map/all_gather | solution.py:132
  459.3 363.3 %reduce-scatter.20.cloned.1.call-start = ((), (), s32[]{:S(2)}) async-start(), calls=%async_computation.26 | async-start | bytes 9437184 | tf_op jit(solution)/shard_map/reduce_scatter | solution.py:52
  771.0 19.0 copy-start.36
  809.7 31.9 %all-gather.36.cloned.1.call-start = ((), (), s32[]{:S(2)}) async-start(), calls=%async_computation.27 | async-start | bytes 4718592 | tf_op jit(solution)/shard_map/all_gather | solution.py:48
  828.2 370.3 %reduce-scatter.40.cloned.1.call-start = ((), (), s32[]{:S(2)}) async-start(), calls=%async_computation.37 | async-start | bytes 835584
  851.3 194.8 %copy-start.15 = (f32[1024,12]{0,1:T(8,128)S(1)}, f32[1024,12]{0,1:T(8,128)}, u32[]{:S(2)}) copy-start(f32[1024,12]{0,1:T(8,128)} %get-tuple-element.289) | copy-start | bytes 147460
  889.2 21.6 copy-start.4
  977.8 21.6 copy-start.4
  999.3 13.1 copy-start.21
  1050.1 149.8 %reduce-scatter.22.cloned.1.call-start = ((), (), s32[]{:S(2)}) async-start(), calls=%async_computation.28 | async-start | bytes 9437184 | tf_op jit(solution)/shard_map/reduce_scatter | solution.py:52
  1070.7 172.4 %reduce-scatter.18.cloned.1.call-start = ((), (), s32[]{:S(2)}) async-start(), calls=%async_computation.24 | async-start | bytes 9437184 | tf_op jit(solution)/shard_map/reduce_scatter | solution.py:44
  1082.7 336.7 %reduce-scatter.38.cloned.1.call-start = ((), (), s32[]{:S(2)}) async-start(), calls=%async_computation.36 | async-start | bytes 13369344 | tf_op jit(solution)/shard_map/reduce_scatter | solution.py:157
  1096.0 534.2 %reduce-scatter.36.cloned.1.call-start = ((), (), s32[]{:S(2)}) async-start(), calls=%async_computation.35 | async-start | bytes 13369344 | tf_op jit(solution)/shard_map/reduce_scatter | solution.py:154
  1109.3 730.7 %reduce-scatter.34.cloned.1.call-start = ((), (), s32[]{:S(2)}) async-start(), calls=%async_computation.34 | async-start | bytes 13369344 | tf_op jit(solution)/shard_map/reduce_scatter | solution.py:151
  1120.8 862.0 %reduce-scatter.32.cloned.1.call-start = ((), (), s32[]{:S(2)}) async-start(), calls=%async_computation.33 | async-start | bytes 5013504 | tf_op jit(solution)/shard_map/reduce_scatter | solution.py:243
  1128.5 995.7 %reduce-scatter.24.cloned.1.call-start = ((), (), s32[]{:S(2)}) async-start(), calls=%async_computation.29 | async-start | bytes 5013504 | tf_op jit(solution)/shard_map/reduce_scatter | solution.py:228
  1136.2 1131.2 %reduce-scatter.28.cloned.1.call-start = ((), (), s32[]{:S(2)}) async-start(), calls=%async_computation.31 | async-start | bytes 5013504 | tf_op jit(solution)/shard_map/reduce_scatter | solution.py:234
  1142.0 1266.5 %reduce-scatter.26.cloned.1.call-start = ((), (), s32[]{:S(2)}) async-start(), calls=%async_computation.30 | async-start | bytes 5013504 | tf_op jit(solution)/shard_map/reduce_scatter | solution.py:231
  1147.9 1403.2 %reduce-scatter.30.cloned.1.call-start = ((), (), s32[]{:S(2)}) async-start(), calls=%async_computation.32 | async-start | bytes 5013504 | tf_op jit(solution)/shard_map/reduce_scatter | solution.py:237
  1153.7 46.3 %copy-start.26 = (f32[1536]{0:T(1024)S(1)}, f32[1536]{0:T(1024)}, u32[]{:S(2)}) copy-start(f32[1536]{0:T(1024)} %copy-done.25) | copy-start | bytes 18436
  1153.7 46.3 %copy-start.31 = (f32[512]{0:T(512)S(1)}, f32[512]{0:T(512)}, u32[]{:S(2)}) copy-start(f32[512]{0:T(512)} %copy-done.30) | copy-start | bytes 6148
  1153.7 50.0 %copy-start.29 = (f32[1536]{0:T(1024)S(1)}, f32[1536]{0:T(1024)}, u32[]{:S(2)}) copy-start(f32[1536]{0:T(1024)} %get-tuple-element.222) | copy-start | bytes 18436
  1153.7 89.4 %copy-start.3 = (f32[512,1536]{1,0:T(8,128)S(1)}, f32[512,1536]{1,0:T(8,128)}, u32[]{:S(2)}) copy-start(f32[512,1536]{1,0:T(8,128)} %copy-done.2) | copy-start | bytes 9437188
  1153.7 89.4 %copy-start.24 = (f32[1536]{0:T(1024)S(1)}, f32[1536]{0:T(1024)}, u32[]{:S(2)}) copy-start(f32[1536]{0:T(1024)} %get-tuple-element.271) | copy-start | bytes 18436
  1153.7 89.4 %copy-start.28 = (f32[512]{0:T(512)S(1)}, f32[512]{0:T(512)}, u32[]{:S(2)}) copy-start(f32[512]{0:T(512)} %copy-done.27) | copy-start | bytes 6148
  1153.8 89.4 %copy-start.33 = (f32[512]{0:T(512)S(1)}, f32[512]{0:T(512)}, u32[]{:S(2)}) copy-start(f32[512]{0:T(512)} %copy-done.32) | copy-start | bytes 6148
  (29 other events, 131.6 us)
Sparse Core Ops, SparseCore 0:
  56.2 12.5 all-gather.13
  72.1 63.4 all-gather.19
  139.0 61.0 all-gather.17
  203.4 61.0 all-gather.15
  267.7 61.1 all-gather.21
  332.1 61.1 all-gather.23
  436.5 13.3 reduce-scatter.15
  453.7 95.2 all-gather.29
  550.6 10.3 all-gather.25
  564.6 95.2 all-gather.27
  661.6 10.3 all-gather.33
  675.6 95.2 all-gather.31
  809.8 12.7 reduce-scatter.19
  828.3 13.2 all-gather.35
  1050.2 123.6 reduce-scatter.39
  1176.1 13.5 reduce-scatter.21
  1191.9 15.6 reduce-scatter.17
  1213.7 205.5 reduce-scatter.37
  1426.5 203.6 reduce-scatter.35
  1636.3 203.6 reduce-scatter.33
  1846.6 136.2 reduce-scatter.31
  1988.6 135.5 reduce-scatter.23
  2130.8 136.5 reduce-scatter.27
  2272.9 135.5 reduce-scatter.25
  2415.1 135.9 reduce-scatter.29
where the time goes:
time: 2570 us; the launch traced here: 2560 us
  waiting for transfers between devices  1770 us (69%)
  matrix products  375 us (15%)
  blocking collectives  163 us (6%)
  other arithmetic  129 us (5%)
  local copies, waits for them, and re-layouts  94.1 us (4%)
    reduce_scatter x1, waiting for transfers between devices, per_device(): lax.psum_scatter(first_contract(normed_mlp, grad_up), 'dp', scatter_dimen...  211 us
    reduce_scatter x1, waiting for transfers between devices, per_device(): lax.psum_scatter(first_contract(normed_mlp, grad_gate), 'dp', scatter_dim...  210 us
    reduce_scatter x1, waiting for transfers between devices, per_device(): lax.psum_scatter(down_part, 'dp', scatter_dimension=1, tiled=True)  169 us
    reduce_scatter x1, waiting for transfers between devices, per_device(): lax.psum_scatter(first_contract(normed_attn, grad_values), 'dp', scatter_...  143 us
    reduce_scatter x1, waiting for transfers between devices, per_device(): lax.psum_scatter(out_part, 'dp', scatter_dimension=1, tiled=True)  143 us
    reduce_scatter x1, waiting for transfers between devices, per_device(): lax.psum_scatter(first_contract(normed_attn, grad_gate_logit), 'dp', scat...  143 us
    reduce_scatter x1, waiting for transfers between devices, per_device(): lax.psum_scatter(first_contract(normed_attn, grad_queries), 'dp', scatter...  141 us
    reduce_scatter x1, waiting for transfers between devices, per_device(): lax.psum_scatter(first_contract(normed_attn, grad_keys), 'dp', scatter_di...  141 us
  transfers between devices with their start and end apart: 25, of which 19 were waited for; matrix products, arithmetic and copies ran while one was open for 13% of the time, Pallas kernels for 0%

commit v1 on v0

v1 whole, which is shorter than its diff:
```python
import functools

import jax
import jax.numpy as jnp
from jax import lax
from jax.experimental import pallas as pl
from jax.experimental.pallas import tpu as pltpu
from jax.sharding import PartitionSpec as P

EPSILON = 1e-06
LANES = 128
VMEM_LIMIT = 48 * 2**20


def lower(values):
    return values.astype(jnp.bfloat16)


def wide(values):
    return values.astype(jnp.float32)


def matmul(left, right):
    return jnp.dot(left, right, preferred_element_type=jnp.float32)


def first_contract(left, right):
    return lax.dot_general(
        left, right, (((0,), (0,)), ((), ())), preferred_element_type=jnp.float32
    )


def second_contract(left, right):
    return lax.dot_general(
        left, right, (((1,), (1,)), ((), ())), preferred_element_type=jnp.float32
    )


def statistics(values):
    inverse = lax.rsqrt(jnp.mean(values * values, axis=-1, keepdims=True) + EPSILON)
    return (values * inverse, inverse)


def norm_backward(unit, inverse, gain, grad):
    scaled = gain * grad
    return inverse * (scaled - unit * jnp.mean(scaled * unit, axis=-1, keepdims=True))


def partner(values):
    return lax.ppermute(values, "tensor", [(0, 1), (1, 0)])


class Grid:
    def __init__(self):
        self.count = lax.axis_size("dp")
        self.index = lax.axis_index("dp")
        bits = self.count.bit_length() - 1
        self.line_bits = list(range(2, bits))

    def bit(self, number):
        return (self.index >> number) & 1

    def swap(self, values, number):
        pairs = [(i, i ^ (1 << number)) for i in range(self.count)]
        return lax.ppermute(values, "dp", pairs)

    def place(self, pieces):
        rows, columns = pieces[0][1].shape[1:]
        arrays = [piece for _, piece in pieces]
        codes = [code for found, _ in pieces for code in found]
        kind = arrays[0].dtype

        def body(*refs):
            inputs, (result, sem) = refs[: len(arrays)], refs[len(arrays) :]
            here = lax.axis_index("dp")
            copies = []
            for (found, _), ref in zip(pieces, inputs):
                for number, code in enumerate(found):
                    copies.append(
                        pltpu.make_async_copy(
                            ref.at[number], result.at[here ^ code], sem.at[len(copies)]
                        )
                    )
            for copy in copies:
                copy.start()
            for copy in copies:
                copy.wait()

        size = self.count * rows * columns * kind.itemsize
        return pl.pallas_call(
            body,
            out_shape=jax.ShapeDtypeStruct((self.count, rows, columns), kind),
            in_specs=[pl.BlockSpec(memory_space=pl.ANY)] * len(arrays),
            out_specs=pl.BlockSpec(memory_space=pltpu.VMEM),
            scratch_shapes=[pltpu.SemaphoreType.DMA((len(codes),))],
            compiler_params=pltpu.CompilerParams(vmem_limit_bytes=VMEM_LIMIT),
            cost_estimate=pl.CostEstimate(flops=0, bytes_accessed=2 * size, transcendentals=0),
        )(*arrays).reshape(self.count * rows, columns)

    def spread(self, block, codes, number):
        found = self.swap(block, number)
        return found, [code ^ (1 << number) for code in codes]

    def plane_pieces(self, block, codes):
        half = block.shape[0] // 2
        side_x, codes_x = self.spread(block, codes, 0)
        side_y, codes_y = self.spread(block, codes, 1)
        corner_a, codes_a = self.spread(side_x[:half], codes_x[:half], 1)
        corner_b, codes_b = self.spread(side_y[half:], codes_y[half:], 0)
        return [
            (codes, block),
            (codes_x, side_x),
            (codes_y, side_y),
            (codes_a, corner_a),
            (codes_b, corner_b),
        ]

    def gather_line_first(self, shard):
        block, codes = shard[None], [0]
        for number in reversed(self.line_bits):
            found, found_codes = self.spread(block, codes, number)
            block = jnp.concatenate([block, found], axis=0)
            codes = codes + found_codes
        return self.place(self.plane_pieces(block, codes))

    def gather_plane_first(self, shard):
        rows, columns = shard.shape
        halves = shard.reshape(2, rows // 2, columns)
        pieces = self.plane_pieces(halves, [0, 0])
        (_, mine), (_, side_x), (_, side_y), (_, corner_a), (_, corner_b) = pieces
        block = jnp.concatenate([mine, side_x, side_y, corner_a, corner_b], axis=0)
        block = block.reshape(4, rows, columns)
        codes = [0, 1, 2, 3]
        last = self.line_bits[0]
        for number in reversed(self.line_bits[1:]):
            found, found_codes = self.spread(block, codes, number)
            block = jnp.concatenate([block, found], axis=0)
            codes = codes + found_codes
        found, found_codes = self.spread(block, codes, last)
        return self.place([(codes, block), (found_codes, found)])

    def reduce_rows(self, parts, kind=jnp.bfloat16):
        rows = parts.shape[0] // self.count
        line = self.count // 4
        blocks = parts.astype(kind).reshape(line, 2, 2, rows, parts.shape[1])

        def take(terms, axis, place):
            return [lax.dynamic_index_in_dim(t, place, axis, keepdims=False) for t in terms]

        def total(terms):
            return sum(wide(term) for term in terms)

        def step(terms, axis, number):
            side = self.bit(number)
            sent = self.swap(total(take(terms, axis, 1 - side)).astype(kind), number)
            return take(terms, axis, side) + [sent]

        half = line // 2
        first = step(step([blocks[:half]], 1, 1), 1, 0)
        second = step(step([blocks[half:]], 2, 0), 1, 1)
        terms = [jnp.concatenate([total(first), total(second)], axis=0).astype(kind)]
        for number in self.line_bits:
            terms = [t.reshape((t.shape[0] // 2, 2) + t.shape[1:]) for t in terms]
            terms = step(terms, 1, number)
        return total(terms)[0]


def fwd_kernel(scale, head, q_ref, k_ref, v_ref, col_ref, row_ref, o_ref, lse_ref, out_t):
    length, lanes = q_ref.shape
    span = min(256, length)
    lane = lax.broadcasted_iota(jnp.int32, (span, lanes), 1) // head
    below = lax.broadcasted_iota(jnp.int32, (span, span), 0) <= lax.broadcasted_iota(jnp.int32, (span, span), 1)
    v_t = v_ref[...].T
    for h in range(lanes // head):
        for b in range(length // span):
            lo, hi = b * span, (b + 1) * span
            q = jnp.where(lane == h, q_ref[lo:hi, :] * scale, 0).astype(jnp.bfloat16)
            row = row_ref[0, h:h+1, lo:hi]
            diag = second_contract(k_ref[lo:hi, :], q) + row - col_ref[0, lo:hi, h:h+1]
            diag = jnp.where(below, diag, -1e30)
            top = jnp.max(diag, axis=0, keepdims=True)
            if lo:
                off = second_contract(k_ref[:lo, :], q) + row - col_ref[0, :lo, h:h+1]
                top = jnp.maximum(top, jnp.max(off, axis=0, keepdims=True))
            e = jnp.exp(diag - top)
            total = jnp.sum(e, axis=0, keepdims=True)
            v_h = v_t[h*head:(h+1)*head]
            acc = matmul(v_h[:, lo:hi], lower(e))
            if lo:
                e = jnp.exp(off - top)
                total = total + jnp.sum(e, axis=0, keepdims=True)
                acc = acc + matmul(v_h[:, :lo], lower(e))
            out_t[h*head:(h+1)*head, lo:hi] = acc / total
            lse_ref[0, h:h+1, lo:hi] = top + jnp.log(total)
    o_ref[...] = out_t[...].T

def bwd_kernel(scale, head, q_ref, k_ref, v_ref, do_ref, col_ref, row_ref, lse_ref, dq_ref, dk_ref, dv_ref, drow_ref, dcol_ref, dq_t, dk_acc, dv_acc):
    length, lanes = q_ref.shape
    span = min(256, length)
    heads = lanes // head
    lane = lax.broadcasted_iota(jnp.int32, (span, lanes), 1) // head
    sub = lax.broadcasted_iota(jnp.int32, (lanes, length), 0) // head
    below = lax.broadcasted_iota(jnp.int32, (span, span), 0) <= lax.broadcasted_iota(jnp.int32, (span, span), 1)
    k_t = k_ref[...].T
    one = jnp.bfloat16(1)
    for h in range(heads):
        kt_h = jnp.where(sub == h, k_t, one)
        mine = lane == h
        for b in range(length // span):
            lo, hi = b * span, (b + 1) * span
            q = q_ref[lo:hi, :] * jnp.bfloat16(scale)
            qz = jnp.where(mine, q, jnp.bfloat16(0))
            q1 = jnp.where(mine, q, one)
            do = do_ref[lo:hi, :]
            doz = jnp.where(mine, do, jnp.bfloat16(0))
            row = row_ref[0, h:h+1, lo:hi] - lse_ref[0, h:h+1, lo:hi]
            s = second_contract(k_ref[lo:hi, :], qz) + row - col_ref[0, lo:hi, h:h+1]
            p = jnp.exp(jnp.where(below, s, -1e30))
            dp = second_contract(v_ref[lo:hi, :], doz)
            centre = jnp.sum(p * dp, axis=0, keepdims=True)
            if lo:
                s0 = second_contract(k_ref[:lo, :], qz) + row - col_ref[0, :lo, h:h+1]
                p0 = jnp.exp(s0)
                dp0 = second_contract(v_ref[:lo, :], doz)
                centre = centre + jnp.sum(p0 * dp0, axis=0, keepdims=True)
            ds = lower(p * (dp - centre))
            dqt = matmul(kt_h[:, lo:hi], ds)
            dv_acc[h, lo:hi, :] = matmul(lower(p), do)
            dk_acc[h, lo:hi, :] = matmul(ds, q1)
            if lo:
                ds0 = lower(p0 * (dp0 - centre))
                dqt = dqt + matmul(kt_h[:, :lo], ds0)
                dv_acc[h, :lo, :] = dv_acc[h, :lo, :] + matmul(lower(p0), do)
                dk_acc[h, :lo, :] = dk_acc[h, :lo, :] + matmul(ds0, q1)
            dq_t[h*head:(h+1)*head, lo:hi] = dqt[h*head:(h+1)*head] * scale
            other = ((h + 1) % heads) * head
            drow_ref[0, h:h+1, lo:hi] = dqt[other:other+1]
    lane_all = lax.broadcasted_iota(jnp.int32, (length, lanes), 1) // head
    dk, dv = dk_acc[0], dv_acc[0]
    for h in range(1, heads):
        dk = jnp.where(lane_all == h, dk_acc[h], dk)
        dv = jnp.where(lane_all == h, dv_acc[h], dv)
    for h in range(heads):
        other = ((h + 1) % heads) * head
        dcol_ref[0, :, h:h+1] = dk_acc[h][:, other:other+1]
    dq_ref[...] = lower(dq_t[...].T)
    dk_ref[...] = lower(dk)
    dv_ref[...] = lower(dv)


def pair_specs(length, groups, per):
    def block(offset):
        return pl.BlockSpec((length, LANES), lambda group: (0, group + offset))

    column = pl.BlockSpec((1, length, per), lambda group: (group, 0, 0))
    row = pl.BlockSpec((1, per, length), lambda group: (group, 0, 0))
    return block, column, row


def attention_cost(length, width, head, products):
    return pl.CostEstimate(
        flops=products * length * length * width,
        bytes_accessed=8 * length * width * 2,
        transcendentals=length * length * width // head // 2,
    )


def attend(qk, values, column, row, head):
    length, width = values.shape[0], qk.shape[1] // 2
    groups, per, _ = row.shape
    block, column_spec, row_spec = pair_specs(length, groups, per)
    return pl.pallas_call(
        functools.partial(fwd_kernel, head**-0.5, head),
        grid=(groups,),
        in_specs=[block(0), block(groups), block(0), column_spec, row_spec],
        out_specs=[block(0), row_spec],
        out_shape=[
            jax.ShapeDtypeStruct((length, width), jnp.float32),
            jax.ShapeDtypeStruct(row.shape, jnp.float32),
        ],
        scratch_shapes=[pltpu.VMEM((LANES, length), jnp.float32)],
        cost_estimate=attention_cost(length, width, head, 2),
        compiler_params=pltpu.CompilerParams(vmem_limit_bytes=VMEM_LIMIT),
    )(qk, qk, values, column, row)


def attend_backward(qk, values, grad, column, row, logsum, head):
    length, width = values.shape[0], qk.shape[1] // 2
    groups, per, _ = row.shape
    block, column_spec, row_spec = pair_specs(length, groups, per)
    wide_out = jax.ShapeDtypeStruct((length, width), jnp.bfloat16)
    return pl.pallas_call(
        functools.partial(bwd_kernel, head**-0.5, head),
        grid=(groups,),
        in_specs=[block(0), block(groups), block(0), block(0), column_spec, row_spec, row_spec],
        out_specs=[block(0), block(0), block(0), row_spec, column_spec],
        out_shape=[
            wide_out,
            wide_out,
            wide_out,
            jax.ShapeDtypeStruct(row.shape, jnp.float32),
            jax.ShapeDtypeStruct(column.shape, jnp.float32),
        ],
        scratch_shapes=[
            pltpu.VMEM((LANES, length), jnp.float32),
            pltpu.VMEM((per, length, LANES), jnp.float32),
            pltpu.VMEM((per, length, LANES), jnp.float32),
        ],
        cost_estimate=attention_cost(length, width, head, 5),
        compiler_params=pltpu.CompilerParams(vmem_limit_bytes=VMEM_LIMIT),
    )(qk, qk, values, grad, column, row, logsum)


def per_device(
    tokens,
    w_query,
    w_key,
    w_value,
    w_gate_attn,
    w_forget,
    forget_bias,
    w_out,
    norm_attn,
    norm_mlp,
    w_gate,
    w_up,
    w_down,
    cotangent,
):
    grid = Grid()
    side = lax.axis_index("tensor")
    heads_here = forget_bias.shape[0]
    width = w_query.shape[1]
    head_size = width // heads_here
    hidden_here = w_gate.shape[1]
    scale = head_size ** (-0.5)
    rows_here = tokens.shape[0]
    length = 2 * rows_here

    def in_order(own, other):
        result = jnp.zeros((length,) + own.shape[1:], own.dtype)
        result = lax.dynamic_update_slice_in_dim(result, own, side * rows_here, 0)
        return lax.dynamic_update_slice_in_dim(result, other, (1 - side) * rows_here, 0)

    def gather_rows(values):
        return in_order(values, partner(values))

    def reduce_pair(values):
        own = lax.dynamic_slice_in_dim(values, side * rows_here, rows_here, 0)
        other = lax.dynamic_slice_in_dim(values, (1 - side) * rows_here, rows_here, 0)
        return own + partner(other)

    own_gains = jnp.stack([norm_attn, norm_mlp])
    other_gains = partner(own_gains)
    pair_gains = jnp.where(
        side == 0,
        jnp.concatenate([own_gains, other_gains], axis=1),
        jnp.concatenate([other_gains, own_gains], axis=1),
    )
    gains = grid.gather_line_first(pair_gains)
    gains = gains.reshape(grid.count, 2, pair_gains.shape[1])
    gain_attn = gains[:, 0].reshape(-1)
    gain_mlp = gains[:, 1].reshape(-1)

    padding = jnp.zeros((w_forget.shape[0], LANES - heads_here), jnp.bfloat16)
    pack_qk = grid.gather_line_first(
        jnp.concatenate([lower(w_query), lower(w_key)], axis=1)
    )
    pack_vf = grid.gather_plane_first(
        jnp.concatenate([lower(w_value), lower(w_forget), padding], axis=1)
    )
    pack_go = grid.gather_line_first(
        jnp.concatenate([lower(w_gate_attn), lower(w_out).T], axis=1)
    )
    pack_gu = grid.gather_line_first(jnp.concatenate([lower(w_gate), lower(w_up)], axis=1))
    pack_d = grid.gather_plane_first(lower(w_down).T)

    residual = wide(tokens)
    unit_attn, inverse_attn = statistics(residual)
    normed_attn = gather_rows(lower(unit_attn * gain_attn))
    qk = lower(matmul(normed_attn, pack_qk))
    vf = matmul(normed_attn, pack_vf)
    values_all = lower(vf[:, :width])
    forget_logit = vf[:, width : width + heads_here] + forget_bias
    decay = jnp.cumsum(-jnp.log1p(jnp.exp(-forget_logit)), axis=0)
    per = LANES // head_size
    groups = heads_here // per
    decay_column = decay.reshape(length, groups, per).transpose(1, 0, 2)
    decay_row = decay.T.reshape(groups, per, length)
    gate_w = pack_go[:, :width]
    out_w = pack_go[:, width:]
    gate_logit = matmul(normed_attn, gate_w)
    attended, logsum = attend(qk, values_all, decay_column, decay_row, head_size)
    gate_sig = jax.nn.sigmoid(gate_logit)
    gated = lower(attended * gate_sig)
    middle = residual + reduce_pair(second_contract(gated, out_w))
    unit_mlp, inverse_mlp = statistics(middle)
    own_normed = lower(unit_mlp * gain_mlp)
    normed_mlp = jnp.concatenate([own_normed, partner(own_normed)], axis=0)
    act = matmul(normed_mlp, pack_gu)
    gate_act = act[:, :hidden_here]
    up_act = act[:, hidden_here:]
    gate_sigmoid = jax.nn.sigmoid(gate_act)
    hidden = lower(gate_act * gate_sigmoid * up_act)
    down_rows = second_contract(hidden, pack_d)
    mixed = (middle + (down_rows[:rows_here] + partner(down_rows[rows_here:]))).astype(
        jnp.bfloat16
    )
    grad_output = jnp.concatenate([cotangent, partner(cotangent)], axis=0)
    down_part = lower(first_contract(grad_output, hidden))
    grad_hidden = matmul(grad_output, pack_d)
    grad_up = lower(grad_hidden * (gate_act * gate_sigmoid))
    grad_gate = lower(grad_hidden * up_act * gate_sigmoid * (1.0 + gate_act * (1.0 - gate_sigmoid)))
    grad_gu = jnp.concatenate([grad_gate, grad_up], axis=1)
    down_grad = grid.reduce_rows(down_part).T
    gu_grad = grid.reduce_rows(lower(first_contract(normed_mlp, grad_gu)))
    normed_rows = second_contract(grad_gu, pack_gu)
    grad_normed_mlp = normed_rows[:rows_here] + partner(normed_rows[rows_here:])
    gain_mlp_part = jnp.sum(grad_normed_mlp * unit_mlp, axis=0)
    grad_middle = wide(cotangent) + norm_backward(
        unit_mlp, inverse_mlp, gain_mlp, grad_normed_mlp
    )
    grad_branch = gather_rows(lower(grad_middle))
    out_part = lower(first_contract(grad_branch, gated))
    grad_gated = matmul(grad_branch, out_w)
    grad_attended = lower(grad_gated * gate_sig)
    grad_gate_logit = lower(grad_gated * attended * gate_sig * (1.0 - gate_sig))
    out_grad = grid.reduce_rows(out_part).T
    gate_attn_grad = grid.reduce_rows(lower(first_contract(normed_attn, grad_gate_logit)))

    grad_queries, grad_keys, grad_values, row_total, column_total = attend_backward(
        qk, values_all, grad_attended, decay_column, decay_row, logsum, head_size
    )
    grad_decay = row_total.reshape(heads_here, length).T - column_total.transpose(
        1, 0, 2
    ).reshape(length, heads_here)
    grad_log = lax.cumsum(grad_decay, axis=0, reverse=True)
    grad_forget = lower(grad_log * jax.nn.sigmoid(-forget_logit))
    bias_part = jnp.sum(grad_forget.astype(jnp.float32), axis=0)
    grad_qk = jnp.concatenate([grad_queries, grad_keys], axis=1)
    grad_vf = jnp.concatenate(
        [grad_values, grad_forget, jnp.zeros((length, LANES - heads_here), jnp.bfloat16)], axis=1
    )
    qk_grad = grid.reduce_rows(lower(first_contract(normed_attn, grad_qk)))
    vf_grad = grid.reduce_rows(lower(first_contract(normed_attn, grad_vf)))
    grad_normed_attn = reduce_pair(
        second_contract(grad_qk, pack_qk)
        + second_contract(grad_vf, pack_vf)
        + second_contract(grad_gate_logit, gate_w)
    )
    gain_attn_part = jnp.sum(grad_normed_attn * unit_attn, axis=0)
    tokens_grad = (
        grad_middle + norm_backward(unit_attn, inverse_attn, gain_attn, grad_normed_attn)
    ).astype(jnp.bfloat16)
    small = jnp.concatenate(
        [
            gain_attn_part.reshape(grid.count, -1),
            gain_mlp_part.reshape(grid.count, -1),
            jnp.broadcast_to(bias_part[None, :], (grid.count, heads_here)),
        ],
        axis=1,
    )
    small_sum = grid.reduce_rows(small, jnp.float32).reshape(-1)
    share = norm_attn.shape[0]
    gain_sums = small_sum[: 4 * share].reshape(2, 2, share)
    other_sums = lax.dynamic_index_in_dim(gain_sums, 1 - side, 1, keepdims=False)
    own_sums = lax.dynamic_index_in_dim(gain_sums, side, 1, keepdims=False)
    gain_grads = own_sums + partner(other_sums)
    return (
        mixed,
        tokens_grad,
        qk_grad[:, :width],
        qk_grad[:, width:],
        vf_grad[:, :width],
        gate_attn_grad,
        vf_grad[:, width : width + heads_here],
        small_sum[4 * share :],
        out_grad,
        gain_grads[0],
        gain_grads[1],
        gu_grad[:, :hidden_here],
        gu_grad[:, hidden_here:],
        down_grad,
    )


def solution(mesh):
    return jax.shard_map(
        per_device,
        mesh=mesh,
        in_specs=(
            P(("dp", "tensor"), None),
            P("dp", "tensor"),
            P("dp", "tensor"),
            P("dp", "tensor"),
            P("dp", "tensor"),
            P("dp", "tensor"),
            P("tensor"),
            P("tensor", "dp"),
            P(("dp", "tensor")),
            P(("dp", "tensor")),
            P("dp", "tensor"),
            P("dp", "tensor"),
            P("tensor", "dp"),
            P(("dp", "tensor"), None),
        ),
        out_specs=(
            P(("dp", "tensor"), None),
            P(("dp", "tensor"), None),
            P("dp", "tensor"),
            P("dp", "tensor"),
            P("dp", "tensor"),
            P("dp", "tensor"),
            P("dp", "tensor"),
            P("tensor"),
            P("tensor", "dp"),
            P(("dp", "tensor")),
            P(("dp", "tensor")),
            P("dp", "tensor"),
            P("dp", "tensor"),
            P("tensor", "dp"),
        ),
        check_vma=False,
    )
```

time: 2570 us -> 1050 us (0.41)
  waiting for transfers between devices: 1770 us -> 464 us
  matrix products: 375 us -> 157 us
  blocking collectives: 163 us -> 0 us
  starting transfers between devices: 1.21 us -> 110 us
  Pallas kernels: 0 us -> 83 us
    reduce_scatter x12 -> x0, waiting for transfers between devices: 1330 us -> none  [the longest x1 211 us: per_device(): lax.psum_scatter(first_contract(normed_mlp, grad_up), 'dp', scatter_dimen...]
    ppermute x0 -> x88, waiting for transfers between devices: none -> 464 us  [the longest x78 463 us: swap(): return lax.ppermute(values, 'dp', pairs)]
    all_gather x12 -> x0, waiting for transfers between devices: 446 us -> none  [the longest x1 98.9 us: per_device(): lax.all_gather(lower(w_down), 'dp', axis=1, tiled=True)]
    dot_general x14 -> x0, matrix products: 173 us -> none  [the longest x4 66.3 us: block_scores(): jnp.einsum('qhd,khd->hqk', query_block, keys, preferred_element_type=jnp....]
    unnamed x3 -> x0, blocking collectives: 123 us -> none
    ppermute x0 -> x88, starting transfers between devices: none -> 110 us  [the longest x78 110 us: swap(): return lax.ppermute(values, 'dp', pairs)]
    pallas_call x0 -> x8, Pallas kernels: none -> 83 us  [the longest x1 33.2 us: attend_backward(): pl.pallas_call(functools.partial(bwd_kernel, head ** (-0.5), head), grid=...]
    reduce_sum x4 -> x0, other arithmetic: 70.6 us -> none  [the longest x2 43.1 us: backward_block(): jnp.sum(wide_scores, axis=2)]
  transfers between devices with their start and end apart: 25 -> 88, of which waited for: 19 -> 35; matrix products, arithmetic and copies ran while one was open for 13% -> 26% of each run, Pallas kernels for 0% -> 8%
where the time goes in v1:
time: 1050 us; the launch traced here: 1040 us
  waiting for transfers between devices  464 us (44%)
  matrix products  157 us (15%)
  other arithmetic  115 us (11%)
  starting transfers between devices  110 us (10%)
  local copies, waits for them, and re-layouts  109 us (10%)
  Pallas kernels  83 us (8%)
    ppermute x78, waiting for transfers between devices, swap(): return lax.ppermute(values, 'dp', pairs)  463 us
    ppermute x78, starting transfers between devices, swap(): return lax.ppermute(values, 'dp', pairs)  110 us
    dot_general x6, matrix products, matmul(): return jnp.dot(left, right, preferred_element_type=jnp.float32)  63.1 us
    dot_general x6, matrix products, first_contract(): lax.dot_general(left, right, (((0,), (0,)), ((), ())), preferred_element_...  48 us
    dot_general x6, matrix products, second_contract(): lax.dot_general(left, right, (((1,), (1,)), ((), ())), preferred_element_...  46.2 us
    another operation x17, other arithmetic  35.5 us
    pallas_call x1, Pallas kernels, attend_backward(): pl.pallas_call(functools.partial(bwd_kernel, head ** (-0.5), head), grid=...  33.2 us
    unnamed x184, local copies, waits for them, and re-layouts  31.7 us
  transfers between devices with their start and end apart: 88, of which 35 were waited for; matrix products, arithmetic and copies ran while one was open for 26% of the time, Pallas kernels for 8%

profile of v1, /device:TPU:0, one launch (start us, length us, event | category | flops | bytes accessed | tf_op | source)
XLA Modules:
  0.0 1040.3 jit_solution(6186806011492973069)
XLA Ops:
  15.0 11.7 %collective-permute-done.1 = f32[1,2,96]{2,1,0:T(2,128)S(1)} collective-permute-done((f32[1,2,96]{2,1,0:T(2,128)S(1)}, f32[1,2,96]{2,1,0:T(2,128)S(1)}, u32[]{:S(2)}, u32[]{:S(2)}) %collective-permute-start.1) | collective-permute-done | bytes 800 | tf_op jit(solution)/shard_map/ppermute | solution.py:65
  53.2 15.7 %collective-permute-start.21 = (bf16[2,96,1536]{2,1,0:T(8,128)(2,1)S(1)}, bf16[2,96,1536]{2,1,0:T(8,128)(2,1)S(1)}, u32[]{:S(2)}, u32[]{:S(2)}) collective-permute-start(bf16[2,96,1536]{2,1,0:T(8,128)(2,1)S(1)} %pad_maximum_fusion.17), channel_id=1, source_target_pairs={{0,8},{2,10},{4,12},{6,14},{8,0},{10,2},{12,4},{14,6},{16,24},{18,... | collective-permute-start | bytes 1769480 | tf_op jit(solution)/shard_map/ppermute | solution.py:65
  72.6 6.1 collective-permute-done.9
  84.9 20.5 %collective-permute-done.21 = bf16[2,96,1536]{2,1,0:T(8,128)(2,1)S(1)} collective-permute-done((bf16[2,96,1536]{2,1,0:T(8,128)(2,1)S(1)}, bf16[2,96,1536]{2,1,0:T(8,128)(2,1)S(1)}, u32[]{:S(2)}, u32[]{:S(2)}) %collective-permute-start.21) | collective-permute-done | bytes 589856 | tf_op jit(solution)/shard_map/ppermute | solution.py:65
  107.4 8.0 collective-permute-done.28
  128.8 15.8 %collective-permute-done.22.refs_1_ = bf16[4,96,1536]{2,1,0:T(8,128)(2,1)} collective-permute-done((bf16[4,96,1536]{2,1,0:T(8,128)(2,1)}, bf16[4,96,1536]{2,1,0:T(8,128)(2,1)}, u32[]{:S(2)}, u32[]{:S(2)}) %collective-permute-start.22) | collective-permute-done | bytes 1179680 | tf_op jit(solution)/shard_map/ppermute | solution.py:65
  180.8 4.2 shard_map.246
  185.0 8.9 convolution_convert_fusion.3.q_ref.k_ref
  193.9 21.9 %shard_map.248 = (f32[1024,768]{1,0:T(8,128)S(1)}, f32[6,2,1024]{2,1,0:T(2,128)S(1)}) custom-call(bf16[1024,1536]{1,0:T(8,128)(2,1)} %convolution_convert_fusion.3.q_ref.k_ref, bf16[1024,1536]{1,0:T(8,128)(2,1)} %convolution_convert_fusion.3.q_ref.k_ref, bf16[1024,768]{1,0:T(8,128)(2,1)S(1)} %copy-done.5, f32[6,1024,2]{2,1,0:T(8,128)} %bitcast.496, ...), custom_call_target="tpu_custom_call" | custom-call | flops 1610612736 | bytes 12582912 | tf_op jit(solution)/shard_map/pallas_call | solution.py:272
  217.8 4.3 shard_map.249
  222.1 6.4 multiply_convert_fusion.6
  241.9 46.1 %collective-permute-done.36 = bf16[1,48,2048]{2,1,0:T(8,128)(2,1)S(1)} collective-permute-done((bf16[1,48,2048]{2,1,0:T(8,128)(2,1)S(1)}, bf16[1,48,2048]{2,1,0:T(8,128)(2,1)S(1)}, u32[]{:S(2)}, u32[]{:S(2)}) %collective-permute-start.36) | collective-permute-done | bytes 196640 | tf_op jit(solution)/shard_map/ppermute | solution.py:65
  288.1 5.0 collective-permute-start.38
  293.1 66.3 %collective-permute-done.38 = bf16[4,96,2048]{2,1,0:T(8,128)(2,1)S(1)} collective-permute-done((bf16[4,96,2048]{2,1,0:T(8,128)(2,1)S(1)}, bf16[4,96,2048]{2,1,0:T(8,128)(2,1)S(1)}, u32[]{:S(2)}, u32[]{:S(2)}) %collective-permute-start.38) | collective-permute-done | bytes 1572896 | tf_op jit(solution)/shard_map/ppermute | solution.py:65
  380.2 48.6 %collective-permute-done.39.refs_1_ = bf16[8,96,2048]{2,1,0:T(8,128)(2,1)} collective-permute-done((bf16[8,96,2048]{2,1,0:T(8,128)(2,1)S(1)}, bf16[8,96,2048]{2,1,0:T(8,128)(2,1)}, u32[]{:S(2)}, u32[]{:S(2)}) %collective-permute-start.39) | collective-permute-done | bytes 3145760 | tf_op jit(solution)/shard_map/ppermute | solution.py:65
  428.8 6.2 shard_map.251
  435.1 9.4 shard_map.250
  444.5 20.4 %fusion.32 = f32[1024,4096]{1,0:T(8,128)} fusion(bf16[1536,4096]{1,0:T(8,128)(2,1)} %bitcast.436, bf16[512,1536]{1,0:T(8,128)(2,1)} %collective-permute-done.27, bf16[512,1536]{1,0:T(8,128)(2,1)} %multiply_convert_fusion.5), kind=kOutput, calls=%fused_computation.69 | convolution fusion | flops 12891193344 | bytes 32505856 | tf_op jit(solution)/shard_map/dot_general | solution.py:24
  465.0 17.0 %multiply_convert_fusion.1 = (bf16[1024,2048]{1,0:T(8,128)(2,1)}, bf16[1024,2048]{1,0:T(8,128)(2,1)}, bf16[1024,2048]{1,0:T(8,128)(2,1)}) fusion(f32[1024,4096]{1,0:T(8,128)} %fusion.32, bf16[1024,1536]{1,0:T(8,128)(2,1)} %constant_dynamic-update-slice_fusion.10, bf16[1536,2048]{1,0:T(8,128)(2,1)S(1)} %bitcast.461), kind=kOutput, calls=%fused_computation.3 | convolution fusion | flops 6473908224 | bytes 38797312 | tf_op jit(solution)/shard_map/dot_general | solution.py:24
  482.0 10.6 %fusion.127 = f32[1024,1536]{1,0:T(8,128)} fusion(bf16[1024,2048]{1,0:T(8,128)(2,1)} %get-tuple-element.88, bf16[1536,2048]{1,0:T(8,128)(2,1)S(1)} %bitcast.462), kind=kOutput, calls=%fused_computation.297 | convolution fusion | flops 6442450944 | bytes 16777216 | tf_op jit(solution)/shard_map/dot_general | solution.py:34
  492.7 10.8 %convolution_convert_fusion.2 = bf16[1536,2048]{1,0:T(8,128)(2,1)} fusion(bf16[1024,1536]{1,0:T(8,128)(2,1)} %constant_dynamic-update-slice_fusion.10, bf16[1024,2048]{1,0:T(8,128)(2,1)S(1)} %copy-done.74), kind=kOutput, calls=%fused_computation.8 | convolution fusion | flops 6445596672 | bytes 13631488 | tf_op jit(solution)/shard_map/dot_general | solution.py:28
  503.4 17.3 %fusion.1 = f32[1024,1536]{1,0:T(8,128)S(1)} fusion(bf16[1536,4096]{1,0:T(8,128)(2,1)} %bitcast.437, bf16[1024,2048]{1,0:T(8,128)(2,1)} %get-tuple-element.87, bf16[1024,2048]{1,0:T(8,128)(2,1)S(1)} %copy-done.73), kind=kOutput, calls=%fused_computation.10 | convolution fusion | flops 12901679104 | bytes 27262976 | tf_op jit(solution)/shard_map/dot_general | solution.py:34
  535.7 20.1 %convolution_convert_fusion = bf16[1536,4096]{1,0:T(8,128)(2,1)} fusion(bf16[1024,2048]{1,0:T(8,128)(2,1)} %get-tuple-element.87, bf16[1024,2048]{1,0:T(8,128)(2,1)} %get-tuple-element.86, bf16[512,1536]{1,0:T(8,128)(2,1)} %collective-permute-done.27, bf16[512,1536]{1,0:T(8,128)(2,1)} %multiply_convert_fusion.5), kind=kOutput, calls=%fused_computation | convolution fusion | flops 12914262016 | bytes 24117248 | tf_op jit(solution)/shard_map/dot_general | solution.py:28
  555.8 6.3 fusion.117
  562.1 6.1 collective-permute-done.84
  578.9 8.7 collective-permute-done.85
  590.6 67.9 %collective-permute-done.83 = bf16[2,96,2048]{2,1,0:T(8,128)(2,1)S(1)} collective-permute-done((bf16[2,96,2048]{2,1,0:T(8,128)(2,1)S(1)}, bf16[2,96,2048]{2,1,0:T(8,128)(2,1)S(1)}, u32[]{:S(2)}, u32[]{:S(2)}) %collective-permute-start.83) | collective-permute-done | bytes 786464 | tf_op jit(solution)/shard_map/ppermute | solution.py:65
  663.0 4.6 multiply_reduce_fusion
  667.8 5.6 constant_dynamic-update-slice_fusion.15
  683.7 3.8 fusion.19
  689.0 12.6 %collective-permute-done.87 = bf16[1,96,2048]{2,1,0:T(8,128)(2,1)S(1)} collective-permute-done((bf16[1,96,2048]{2,1,0:T(8,128)(2,1)S(1)}, bf16[1,96,2048]{2,1,0:T(8,128)(2,1)S(1)}, u32[]{:S(2)}, u32[]{:S(2)}) %collective-permute-start.87) | collective-permute-done | bytes 393248 | tf_op jit(solution)/shard_map/ppermute | solution.py:65
  703.9 7.0 multiply_convert_fusion.3
  710.8 33.2 %shard_map.252 = (bf16[1024,768]{1,0:T(8,128)(2,1)S(1)}, bf16[1024,768]{1,0:T(8,128)(2,1)S(1)}, bf16[1024,768]{1,0:T(8,128)(2,1)S(1)}, f32[6,2,1024]{2,1,0:T(2,128)S(1)}, f32[6,1024,2]{2,1,0:T(8,128)}) custom-call(bf16[1024,1536]{1,0:T(8,128)(2,1)} %convolution_convert_fusion.3.q_ref.k_ref, bf16[1024,1536]{1,0:T(8,128)(2,1)} %convolution_convert_fusion.3.q_ref.k_ref, ...), custom_call_target="tpu_custom_call" | custom-call | flops 4026531840 | bytes 12582912 | tf_op jit(solution)/shard_map/pallas_call | solution.py:292
  747.9 14.9 %reduce-window.16 = f32[12,8,128]{2,1,0:T(8,128)S(1)} reduce-window(f32[12,8,128]{2,1,0:T(8,128)S(1)} %slice.320, f32[]{:T(128)} %constant.1294.clone.1), window={size=1x1x128 pad=0_0x0_0x0_127}, to_apply=%region_5.6 | reduce-window | flops 1560576 | bytes 98308 | tf_op jit(solution)/shard_map/reduce-window.2
  767.0 7.2 convolution_convert_fusion.1
  774.3 3.7 convolution_convert_fusion.4
  805.0 7.0 fusion.128
  817.6 5.2 add_add_fusion
  832.4 8.3 collective-permute-done.71
  847.3 4.9 collective-permute-done.60
  853.9 19.4 %collective-permute-done.58 = bf16[2,96,768]{2,1,0:T(8,128)(2,1)S(1)} collective-permute-done((bf16[2,96,768]{2,1,0:T(8,128)(2,1)S(1)}, bf16[2,96,768]{2,1,0:T(8,128)(2,1)S(1)}, u32[]{:S(2)}, u32[]{:S(2)}) %collective-permute-start.58) | collective-permute-done | bytes 294944 | tf_op jit(solution)/shard_map/ppermute | solution.py:65
  875.7 5.2 collective-permute-done.72
  898.3 35.3 %collective-permute-done.61 = bf16[2,96,768]{2,1,0:T(8,128)(2,1)S(1)} collective-permute-done((bf16[2,96,768]{2,1,0:T(8,128)(2,1)}, bf16[2,96,768]{2,1,0:T(8,128)(2,1)S(1)}, u32[]{:S(2)}, u32[]{:S(2)}) %collective-permute-start.61) | collective-permute-done | bytes 294944 | tf_op jit(solution)/shard_map/ppermute | solution.py:65
  960.7 7.2 collective-permute-done.74
  968.7 27.3 %collective-permute-done.56 = bf16[1,96,896]{1,2,0:T(8,128)(2,1)S(1)} collective-permute-done((bf16[1,96,896]{1,2,0:T(8,128)(2,1)S(1)}, bf16[1,96,896]{1,2,0:T(8,128)(2,1)S(1)}, u32[]{:S(2)}, u32[]{:S(2)}) %collective-permute-start.56) | collective-permute-done | bytes 172064 | tf_op jit(solution)/shard_map/ppermute | solution.py:65
  1001.7 11.3 %collective-permute-done.50 = bf16[1,96,1536]{2,1,0:T(8,128)(2,1)S(1)} collective-permute-done((bf16[1,96,1536]{2,1,0:T(8,128)(2,1)S(1)}, bf16[1,96,1536]{2,1,0:T(8,128)(2,1)S(1)}, u32[]{:S(2)}, u32[]{:S(2)}) %collective-permute-start.50) | collective-permute-done | bytes 294944 | tf_op jit(solution)/shard_map/ppermute | solution.py:65
  1015.1 5.4 fusion.12
  1033.1 4.8 fusion.11
  (531 shorter events, 313.3 us)
Async XLA Ops:
  2.7 39.5 %collective-permute-start.14 = (bf16[2,48,896]{2,1,0:T(8,128)(2,1)S(1)}, bf16[2,48,896]{2,1,0:T(8,128)(2,1)}, u32[]{:S(2)}, u32[]{:S(2)}) collective-permute-start(bf16[2,48,896]{2,1,0:T(8,128)(2,1)S(1)} %bitcast.510), channel_id=1, source_target_pairs={{0,2},{2,0},{4,6},{6,4},{8,10},{10,8},{12,14},{14,12},{16,18},{18,... | collective-permute-start | bytes 516104 | tf_op jit(solution)/shard_map/ppermute | solution.py:65
  5.7 38.1 %collective-permute-start.15 = (bf16[2,48,896]{2,1,0:T(8,128)(2,1)S(1)}, bf16[2,48,896]{2,1,0:T(8,128)(2,1)}, u32[]{:S(2)}, u32[]{:S(2)}) collective-permute-start(bf16[2,48,896]{2,1,0:T(8,128)(2,1)S(1)} %bitcast.511), channel_id=1, source_target_pairs={{0,4},{2,6},{4,0},{6,2},{8,12},{10,14},{12,8},{14,10},{16,20},{18,... | collective-permute-start | bytes 516104 | tf_op jit(solution)/shard_map/ppermute | solution.py:65
  9.9 40.2 %collective-permute-start.8 = (bf16[1,96,1536]{2,1,0:T(8,128)(2,1)S(1)}, bf16[1,96,1536]{2,1,0:T(8,128)(2,1)S(1)}, u32[]{:S(2)}, u32[]{:S(2)}) collective-permute-start(bf16[1,96,1536]{2,1,0:T(8,128)(2,1)S(1)} %maximum_bitcast_fusion.1), channel_id=1, source_target_pairs={{0,16},{2,18},{4,20},{6,22},{8,24},{10,26},{12,28},{14,30},{16,0},... | collective-permute-start | bytes 884744 | tf_op jit(solution)/shard_map/ppermute | solution.py:65
  42.1 74.9 %collective-permute-start.7 = (bf16[512,1536]{1,0:T(8,128)(2,1)S(1)}, bf16[512,1536]{1,0:T(8,128)(2,1)S(1)}, u32[]{:S(2)}, u32[]{:S(2)}) collective-permute-start(bf16[512,1536]{1,0:T(8,128)(2,1)S(1)} %get-tuple-element.85), channel_id=1, source_target_pairs={{0,1},{1,0},{2,3},{3,2},{4,5},{5,4},{6,7},{7,6},{8,9},{9,8},{10,11... | collective-permute-start | bytes 4718600 | tf_op jit(solution)/shard_map/ppermute | solution.py:50
  49.2 34.0 %collective-permute-start.18 = (bf16[4,96,896]{2,1,0:T(8,128)(2,1)S(1)}, bf16[4,96,896]{2,1,0:T(8,128)(2,1)S(1)}, u32[]{:S(2)}, u32[]{:S(2)}) collective-permute-start(bf16[4,96,896]{2,1,0:T(8,128)(2,1)S(1)} %bitcast.508), channel_id=1, source_target_pairs={{0,16},{2,18},{4,20},{6,22},{8,24},{10,26},{12,28},{14,30},{16,0},... | collective-permute-start | bytes 2064392 | tf_op jit(solution)/shard_map/ppermute | solution.py:65
  53.2 52.1 %collective-permute-start.21 = (bf16[2,96,1536]{2,1,0:T(8,128)(2,1)S(1)}, bf16[2,96,1536]{2,1,0:T(8,128)(2,1)S(1)}, u32[]{:S(2)}, u32[]{:S(2)}) collective-permute-start(bf16[2,96,1536]{2,1,0:T(8,128)(2,1)S(1)} %pad_maximum_fusion.17), channel_id=1, source_target_pairs={{0,8},{2,10},{4,12},{6,14},{8,0},{10,2},{12,4},{14,6},{16,24},{18,... | collective-permute-start | bytes 1769480 | tf_op jit(solution)/shard_map/ppermute | solution.py:65
  68.9 46.5 %collective-permute-start.28 = (bf16[1,96,4096]{2,1,0:T(8,128)(2,1)S(1)}, bf16[1,96,4096]{2,1,0:T(8,128)(2,1)S(1)}, u32[]{:S(2)}, u32[]{:S(2)}) collective-permute-start(bf16[1,96,4096]{2,1,0:T(8,128)(2,1)S(1)} %maximum_bitcast_fusion), channel_id=1, source_target_pairs={{0,16},{2,18},{4,20},{6,22},{8,24},{10,26},{12,28},{14,30},{16,0},... | collective-permute-start | bytes 2359304 | tf_op jit(solution)/shard_map/ppermute | solution.py:65
  78.8 39.9 %collective-permute-start.10 = (bf16[4,96,1536]{2,1,0:T(8,128)(2,1)S(1)}, bf16[4,96,1536]{2,1,0:T(8,128)(2,1)S(1)}, u32[]{:S(2)}, u32[]{:S(2)}) collective-permute-start(bf16[4,96,1536]{2,1,0:T(8,128)(2,1)S(1)} %pad_maximum_fusion.12.refs_0_), channel_id=1, source_target_pairs={{0,2},{2,0},{4,6},{6,4},{8,10},{10,8},{12,14},{14,12},{16,18},{18,... | collective-permute-start | bytes 3538952 | tf_op jit(solution)/shard_map/ppermute | solution.py:65
  83.2 42.8 %collective-permute-start.11 = (bf16[4,96,1536]{2,1,0:T(8,128)(2,1)S(1)}, bf16[4,96,1536]{2,1,0:T(8,128)(2,1)}, u32[]{:S(2)}, u32[]{:S(2)}) collective-permute-start(bf16[4,96,1536]{2,1,0:T(8,128)(2,1)S(1)} %pad_maximum_fusion.12.refs_0_), channel_id=1, source_target_pairs={{0,4},{2,6},{4,0},{6,2},{8,12},{10,14},{12,8},{14,10},{16,20},{18,... | collective-permute-start | bytes 3538952 | tf_op jit(solution)/shard_map/ppermute | solution.py:65
  105.3 45.5 %collective-permute-start.19 = (bf16[8,96,896]{2,1,0:T(8,128)(2,1)S(1)}, bf16[8,96,896]{2,1,0:T(8,128)(2,1)}, u32[]{:S(2)}, u32[]{:S(2)}) collective-permute-start(bf16[8,96,896]{2,1,0:T(8,128)(2,1)S(1)} %pad_maximum_fusion.11.refs_0_), channel_id=1, source_target_pairs={{0,8},{2,10},{4,12},{6,14},{8,0},{10,2},{12,4},{14,6},{16,24},{18,... | collective-permute-start | bytes 4128776 | tf_op jit(solution)/shard_map/ppermute | solution.py:65
  117.0 31.2 %collective-permute-start.23 = (bf16[4,96,1536]{2,1,0:T(8,128)(2,1)}, bf16[4,96,1536]{2,1,0:T(8,128)(2,1)}, u32[]{:S(2)}, u32[]{:S(2)}) collective-permute-start(bf16[4,96,1536]{2,1,0:T(8,128)(2,1)} %pad_maximum_fusion.13.refs_0_), channel_id=1, source_target_pairs={{0,4},{2,6},{4,0},{6,2},{8,12},{10,14},{12,8},{14,10},{16,20},{18,... | collective-permute-start | bytes 3538952 | tf_op jit(solution)/shard_map/ppermute | solution.py:65
  119.8 55.5 %collective-permute-start.29 = (bf16[2,96,4096]{2,1,0:T(8,128)(2,1)}, bf16[2,96,4096]{2,1,0:T(8,128)(2,1)}, u32[]{:S(2)}, u32[]{:S(2)}) collective-permute-start(bf16[2,96,4096]{2,1,0:T(8,128)(2,1)} %pad_maximum_fusion.9), channel_id=1, source_target_pairs={{0,8},{2,10},{4,12},{6,14},{8,0},{10,2},{12,4},{14,6},{16,24},{18,... | collective-permute-start | bytes 4718600 | tf_op jit(solution)/shard_map/ppermute | solution.py:65
  126.0 109.8 %collective-permute-start.34 = (bf16[2,48,2048]{2,1,0:T(8,128)(2,1)}, bf16[2,48,2048]{2,1,0:T(8,128)(2,1)}, u32[]{:S(2)}, u32[]{:S(2)}) collective-permute-start(bf16[2,48,2048]{2,1,0:T(8,128)(2,1)} %bitcast.20), channel_id=1, source_target_pairs={{0,2},{2,0},{4,6},{6,4},{8,10},{10,8},{12,14},{14,12},{16,18},{18,... | collective-permute-start | bytes 1179656 | tf_op jit(solution)/shard_map/ppermute | solution.py:65
  144.7 93.2 %collective-permute-start.35 = (bf16[2,48,2048]{2,1,0:T(8,128)(2,1)}, bf16[2,48,2048]{2,1,0:T(8,128)(2,1)}, u32[]{:S(2)}, u32[]{:S(2)}) collective-permute-start(bf16[2,48,2048]{2,1,0:T(8,128)(2,1)} %bitcast.20), channel_id=1, source_target_pairs={{0,4},{2,6},{4,0},{6,2},{8,12},{10,14},{12,8},{14,10},{16,20},{18,... | collective-permute-start | bytes 1179656 | tf_op jit(solution)/shard_map/ppermute | solution.py:65
  175.2 40.6 %collective-permute-start.24 = (bf16[2,96,1536]{2,1,0:T(8,128)(2,1)}, bf16[2,96,1536]{2,1,0:T(8,128)(2,1)S(1)}, u32[]{:S(2)}, u32[]{:S(2)}) collective-permute-start(bf16[2,96,1536]{2,1,0:T(8,128)(2,1)} %slice.281), channel_id=1, source_target_pairs={{0,4},{2,6},{4,0},{6,2},{8,12},{10,14},{12,8},{14,10},{16,20},{18,... | collective-permute-start | bytes 1769480 | tf_op jit(solution)/shard_map/ppermute | solution.py:65
  178.6 39.2 %collective-permute-start.25 = (bf16[2,96,1536]{2,1,0:T(8,128)(2,1)S(1)}, bf16[2,96,1536]{2,1,0:T(8,128)(2,1)S(1)}, u32[]{:S(2)}, u32[]{:S(2)}) collective-permute-start(bf16[2,96,1536]{2,1,0:T(8,128)(2,1)S(1)} %copy-done.57), channel_id=1, source_target_pairs={{0,2},{2,0},{4,6},{6,4},{8,10},{10,8},{12,14},{14,12},{16,18},{18,... | collective-permute-start | bytes 1769480 | tf_op jit(solution)/shard_map/ppermute | solution.py:65
  180.7 179.8 %collective-permute-start.30 = (bf16[4,96,4096]{2,1,0:T(8,128)(2,1)}, bf16[4,96,4096]{2,1,0:T(8,128)(2,1)}, u32[]{:S(2)}, u32[]{:S(2)}) collective-permute-start(bf16[4,96,4096]{2,1,0:T(8,128)(2,1)} %pad_maximum_fusion.4.refs_0_), channel_id=1, source_target_pairs={{0,2},{2,0},{4,6},{6,4},{8,10},{10,8},{12,14},{14,12},{16,18},{18,... | collective-permute-start | bytes 9437192 | tf_op jit(solution)/shard_map/ppermute | solution.py:65
  215.8 149.1 %collective-permute-start.31 = (bf16[4,96,4096]{2,1,0:T(8,128)(2,1)}, bf16[4,96,4096]{2,1,0:T(8,128)(2,1)}, u32[]{:S(2)}, u32[]{:S(2)}) collective-permute-start(bf16[4,96,4096]{2,1,0:T(8,128)(2,1)} %pad_maximum_fusion.4.refs_0_), channel_id=1, source_target_pairs={{0,4},{2,6},{4,0},{6,2},{8,12},{10,14},{12,8},{14,10},{16,20},{18,... | collective-permute-start | bytes 9437192 | tf_op jit(solution)/shard_map/ppermute | solution.py:65
  234.8 133.3 %collective-permute-start.26 = (f32[512,1536]{1,0:T(8,128)}, f32[512,1536]{1,0:T(8,128)}, u32[]{:S(2)}, u32[]{:S(2)}) collective-permute-start(f32[512,1536]{1,0:T(8,128)} %constant_dynamic-slice_fusion.30), channel_id=1, source_target_pairs={{0,1},{1,0},{2,3},{3,2},{4,5},{5,4},{6,7},{7,6},{8,9},{9,8},{10,11... | collective-permute-start | bytes 9437192 | tf_op jit(solution)/shard_map/ppermute | solution.py:50
  236.7 51.3 %collective-permute-start.36 = (bf16[1,48,2048]{2,1,0:T(8,128)(2,1)S(1)}, bf16[1,48,2048]{2,1,0:T(8,128)(2,1)S(1)}, u32[]{:S(2)}, u32[]{:S(2)}) collective-permute-start(bf16[1,48,2048]{2,1,0:T(8,128)(2,1)S(1)} %slice.290), channel_id=1, source_target_pairs={{0,4},{2,6},{4,0},{6,2},{8,12},{10,14},{12,8},{14,10},{16,20},{18,... | collective-permute-start | bytes 589832 | tf_op jit(solution)/shard_map/ppermute | solution.py:65
  238.8 49.2 %collective-permute-start.37 = (bf16[1,48,2048]{2,1,0:T(8,128)(2,1)S(1)}, bf16[1,48,2048]{2,1,0:T(8,128)(2,1)S(1)}, u32[]{:S(2)}, u32[]{:S(2)}) collective-permute-start(bf16[1,48,2048]{2,1,0:T(8,128)(2,1)S(1)} %slice.291), channel_id=1, source_target_pairs={{0,2},{2,0},{4,6},{6,4},{8,10},{10,8},{12,14},{14,12},{16,18},{18,... | collective-permute-start | bytes 589832 | tf_op jit(solution)/shard_map/ppermute | solution.py:65
  288.1 71.3 %collective-permute-start.38 = (bf16[4,96,2048]{2,1,0:T(8,128)(2,1)S(1)}, bf16[4,96,2048]{2,1,0:T(8,128)(2,1)S(1)}, u32[]{:S(2)}, u32[]{:S(2)}) collective-permute-start(bf16[4,96,2048]{2,1,0:T(8,128)(2,1)S(1)} %bitcast.499), channel_id=1, source_target_pairs={{0,16},{2,18},{4,20},{6,22},{8,24},{10,26},{12,28},{14,30},{16,0},... | collective-permute-start | bytes 4718600 | tf_op jit(solution)/shard_map/ppermute | solution.py:65
  359.7 69.2 %collective-permute-start.39 = (bf16[8,96,2048]{2,1,0:T(8,128)(2,1)S(1)}, bf16[8,96,2048]{2,1,0:T(8,128)(2,1)}, u32[]{:S(2)}, u32[]{:S(2)}) collective-permute-start(bf16[8,96,2048]{2,1,0:T(8,128)(2,1)S(1)} %pad_maximum_fusion.5.refs_0_), channel_id=1, source_target_pairs={{0,8},{2,10},{4,12},{6,14},{8,0},{10,2},{12,4},{14,6},{16,24},{18,... | collective-permute-start | bytes 9437192 | tf_op jit(solution)/shard_map/ppermute | solution.py:65
  363.4 71.7 %collective-permute-start.32 = (bf16[2,96,4096]{2,1,0:T(8,128)(2,1)}, bf16[2,96,4096]{2,1,0:T(8,128)(2,1)}, u32[]{:S(2)}, u32[]{:S(2)}) collective-permute-start(bf16[2,96,4096]{2,1,0:T(8,128)(2,1)} %slice.286), channel_id=1, source_target_pairs={{0,4},{2,6},{4,0},{6,2},{8,12},{10,14},{12,8},{14,10},{16,20},{18,... | collective-permute-start | bytes 4718600 | tf_op jit(solution)/shard_map/ppermute | solution.py:65
  367.6 67.4 %collective-permute-start.33 = (bf16[2,96,4096]{2,1,0:T(8,128)(2,1)}, bf16[2,96,4096]{2,1,0:T(8,128)(2,1)}, u32[]{:S(2)}, u32[]{:S(2)}) collective-permute-start(bf16[2,96,4096]{2,1,0:T(8,128)(2,1)} %slice.287), channel_id=1, source_target_pairs={{0,2},{2,0},{4,6},{6,4},{8,10},{10,8},{12,14},{14,12},{16,18},{18,... | collective-permute-start | bytes 4718600 | tf_op jit(solution)/shard_map/ppermute | solution.py:65
  374.8 69.7 %collective-permute-start.27 = (bf16[512,1536]{1,0:T(8,128)(2,1)}, bf16[512,1536]{1,0:T(8,128)(2,1)}, u32[]{:S(2)}, u32[]{:S(2)}) collective-permute-start(bf16[512,1536]{1,0:T(8,128)(2,1)} %multiply_convert_fusion.5), channel_id=1, source_target_pairs={{0,1},{1,0},{2,3},{3,2},{4,5},{5,4},{6,7},{7,6},{8,9},{9,8},{10,11... | collective-permute-start | bytes 4718600 | tf_op jit(solution)/shard_map/ppermute | solution.py:50
  525.4 137.5 %collective-permute-start.42 = (f32[512,1536]{1,0:T(8,128)}, f32[512,1536]{1,0:T(8,128)}, u32[]{:S(2)}, u32[]{:S(2)}) collective-permute-start(f32[512,1536]{1,0:T(8,128)} %slice.295), channel_id=1, source_target_pairs={{0,1},{1,0},{2,3},{3,2},{4,5},{5,4},{6,7},{7,6},{8,9},{9,8},{10,11... | collective-permute-start | bytes 9437192 | tf_op jit(solution)/shard_map/ppermute | solution.py:50
  528.8 134.1 %collective-permute-start.40 = (f32[512,1536]{1,0:T(8,128)}, f32[512,1536]{1,0:T(8,128)}, u32[]{:S(2)}, u32[]{:S(2)}) collective-permute-start(f32[512,1536]{1,0:T(8,128)} %slice.293), channel_id=1, source_target_pairs={{0,1},{1,0},{2,3},{3,2},{4,5},{5,4},{6,7},{7,6},{8,9},{9,8},{10,11... | collective-permute-start | bytes 9437192 | tf_op jit(solution)/shard_map/ppermute | solution.py:50
  532.3 35.9 %collective-permute-start.84 = (bf16[2,2,96,2048]{3,2,0,1:T(8,128)(2,1)}, bf16[2,2,96,2048]{3,2,0,1:T(8,128)(2,1)}, u32[]{:S(2)}, u32[]{:S(2)}) collective-permute-start(bf16[2,2,96,2048]{3,2,0,1:T(8,128)(2,1)} %copy_bitcast_fusion.2), channel_id=1, source_target_pairs={{0,2},{2,0},{4,6},{6,4},{8,10},{10,8},{12,14},{14,12},{16,18},{18,... | collective-permute-start | bytes 4718600 | tf_op jit(solution)/shard_map/ppermute | solution.py:65
  535.2 38.6 %collective-permute-start.82 = (bf16[2,2,96,2048]{3,2,0,1:T(8,128)(2,1)}, bf16[2,2,96,2048]{3,2,0,1:T(8,128)(2,1)}, u32[]{:S(2)}, u32[]{:S(2)}) collective-permute-start(bf16[2,2,96,2048]{3,2,0,1:T(8,128)(2,1)} %copy_bitcast_fusion.3), channel_id=1, source_target_pairs={{0,4},{2,6},{4,0},{6,2},{8,12},{10,14},{12,8},{14,10},{16,20},{18,... | collective-permute-start | bytes 4718600 | tf_op jit(solution)/shard_map/ppermute | solution.py:65
  573.3 101.8 %collective-permute-start.78 = (bf16[2,2,96,4096]{3,2,0,1:T(8,128)(2,1)}, bf16[2,2,96,4096]{3,2,0,1:T(8,128)(2,1)}, u32[]{:S(2)}, u32[]{:S(2)}) collective-permute-start(bf16[2,2,96,4096]{3,2,0,1:T(8,128)(2,1)} %copy_bitcast_fusion), channel_id=1, source_target_pairs={{0,2},{2,0},{4,6},{6,4},{8,10},{10,8},{12,14},{14,12},{16,18},{18,... | collective-permute-start | bytes 9437192 | tf_op jit(solution)/shard_map/ppermute | solution.py:65
  575.2 83.3 %collective-permute-start.83 = (bf16[2,96,2048]{2,1,0:T(8,128)(2,1)S(1)}, bf16[2,96,2048]{2,1,0:T(8,128)(2,1)S(1)}, u32[]{:S(2)}, u32[]{:S(2)}) collective-permute-start(bf16[2,96,2048]{2,1,0:T(8,128)(2,1)S(1)} %fusion.38), channel_id=1, source_target_pairs={{0,2},{2,0},{4,6},{6,4},{8,10},{10,8},{12,14},{14,12},{16,18},{18,... | collective-permute-start | bytes 2359304 | tf_op jit(solution)/shard_map/ppermute | solution.py:65
  587.6 96.2 %collective-permute-start.76 = (bf16[2,2,96,4096]{3,2,0,1:T(8,128)(2,1)}, bf16[2,2,96,4096]{3,2,0,1:T(8,128)(2,1)}, u32[]{:S(2)}, u32[]{:S(2)}) collective-permute-start(bf16[2,2,96,4096]{3,2,0,1:T(8,128)(2,1)} %copy_bitcast_fusion.1), channel_id=1, source_target_pairs={{0,4},{2,6},{4,0},{6,2},{8,12},{10,14},{12,8},{14,10},{16,20},{18,... | collective-permute-start | bytes 9437192 | tf_op jit(solution)/shard_map/ppermute | solution.py:65
  678.7 116.6 %collective-permute-start.79 = (bf16[2,96,4096]{2,1,0:T(8,128)(2,1)}, bf16[2,96,4096]{2,1,0:T(8,128)(2,1)}, u32[]{:S(2)}, u32[]{:S(2)}) collective-permute-start(bf16[2,96,4096]{2,1,0:T(8,128)(2,1)} %fusion.16), channel_id=1, source_target_pairs={{0,4},{2,6},{4,0},{6,2},{8,12},{10,14},{12,8},{14,10},{16,20},{18,... | collective-permute-start | bytes 4718600 | tf_op jit(solution)/shard_map/ppermute | solution.py:65
  687.5 124.5 %collective-permute-start.77 = (bf16[2,96,4096]{2,1,0:T(8,128)(2,1)}, bf16[2,96,4096]{2,1,0:T(8,128)(2,1)}, u32[]{:S(2)}, u32[]{:S(2)}) collective-permute-start(bf16[2,96,4096]{2,1,0:T(8,128)(2,1)} %fusion.19), channel_id=1, source_target_pairs={{0,2},{2,0},{4,6},{6,4},{8,10},{10,8},{12,14},{14,12},{16,18},{18,... | collective-permute-start | bytes 4718600 | tf_op jit(solution)/shard_map/ppermute | solution.py:65
  779.2 63.8 %collective-permute-start.53 = (bf16[2,2,96,896]{3,2,0,1:T(8,128)(2,1)}, bf16[2,2,96,896]{3,2,0,1:T(8,128)(2,1)}, u32[]{:S(2)}, u32[]{:S(2)}) collective-permute-start(bf16[2,2,96,896]{3,2,0,1:T(8,128)(2,1)} %copy_bitcast_fusion.6), channel_id=1, source_target_pairs={{0,2},{2,0},{4,6},{6,4},{8,10},{10,8},{12,14},{14,12},{16,18},{18,... | collective-permute-start | bytes 2064392 | tf_op jit(solution)/shard_map/ppermute | solution.py:65
  781.6 63.9 %collective-permute-start.51 = (bf16[2,2,96,896]{3,2,0,1:T(8,128)(2,1)}, bf16[2,2,96,896]{3,2,0,1:T(8,128)(2,1)}, u32[]{:S(2)}, u32[]{:S(2)}) collective-permute-start(bf16[2,2,96,896]{3,2,0,1:T(8,128)(2,1)} %copy_bitcast_fusion.7), channel_id=1, source_target_pairs={{0,4},{2,6},{4,0},{6,2},{8,12},{10,14},{12,8},{14,10},{16,20},{18,... | collective-permute-start | bytes 2064392 | tf_op jit(solution)/shard_map/ppermute | solution.py:65
  786.4 41.9 %collective-permute-start.59 = (bf16[2,2,96,768]{3,2,0,1:T(8,128)(2,1)}, bf16[2,2,96,768]{3,2,0,1:T(8,128)(2,1)}, u32[]{:S(2)}, u32[]{:S(2)}) collective-permute-start(bf16[2,2,96,768]{3,2,0,1:T(8,128)(2,1)} %copy_bitcast_fusion.10), channel_id=1, source_target_pairs={{0,2},{2,0},{4,6},{6,4},{8,10},{10,8},{12,14},{14,12},{16,18},{18,... | collective-permute-start | bytes 1769480 | tf_op jit(solution)/shard_map/ppermute | solution.py:65
  795.3 36.0 %collective-permute-start.57 = (bf16[2,2,96,768]{3,2,0,1:T(8,128)(2,1)}, bf16[2,2,96,768]{3,2,0,1:T(8,128)(2,1)}, u32[]{:S(2)}, u32[]{:S(2)}) collective-permute-start(bf16[2,2,96,768]{3,2,0,1:T(8,128)(2,1)} %copy_bitcast_fusion.11), channel_id=1, source_target_pairs={{0,4},{2,6},{4,0},{6,2},{8,12},{10,14},{12,8},{14,10},{16,20},{18,... | collective-permute-start | bytes 1769480 | tf_op jit(solution)/shard_map/ppermute | solution.py:65
  831.3 183.8 %collective-permute-start.44 = (f32[512,1536]{1,0:T(8,128)}, f32[512,1536]{1,0:T(8,128)}, u32[]{:S(2)}, u32[]{:S(2)}) collective-permute-start(f32[512,1536]{1,0:T(8,128)} %constant_dynamic-slice_fusion.29), channel_id=1, source_target_pairs={{0,1},{1,0},{2,3},{3,2},{4,5},{5,4},{6,7},{7,6},{8,9},{9,8},{10,11... | collective-permute-start | bytes 9437192 | tf_op jit(solution)/shard_map/ppermute | solution.py:50
  840.7 56.1 %collective-permute-start.47 = (bf16[2,2,96,1536]{3,2,0,1:T(8,128)(2,1)}, bf16[2,2,96,1536]{3,2,0,1:T(8,128)(2,1)}, u32[]{:S(2)}, u32[]{:S(2)}) collective-permute-start(bf16[2,2,96,1536]{3,2,0,1:T(8,128)(2,1)} %copy_bitcast_fusion.4), channel_id=1, source_target_pairs={{0,2},{2,0},{4,6},{6,4},{8,10},{10,8},{12,14},{14,12},{16,18},{18,... | collective-permute-start | bytes 3538952 | tf_op jit(solution)/shard_map/ppermute | solution.py:65
  843.0 91.6 %collective-permute-start.45 = (bf16[2,2,96,1536]{3,2,0,1:T(8,128)(2,1)}, bf16[2,2,96,1536]{3,2,0,1:T(8,128)(2,1)}, u32[]{:S(2)}, u32[]{:S(2)}) collective-permute-start(bf16[2,2,96,1536]{3,2,0,1:T(8,128)(2,1)} %copy_bitcast_fusion.5), channel_id=1, source_target_pairs={{0,4},{2,6},{4,0},{6,2},{8,12},{10,14},{12,8},{14,10},{16,20},{18,... | collective-permute-start | bytes 3538952 | tf_op jit(solution)/shard_map/ppermute | solution.py:65
  888.2 57.8 %collective-permute-start.80 = (bf16[2,96,4096]{2,1,0:T(8,128)(2,1)}, bf16[2,96,4096]{2,1,0:T(8,128)(2,1)}, u32[]{:S(2)}, u32[]{:S(2)}) collective-permute-start(bf16[2,96,4096]{2,1,0:T(8,128)(2,1)} %dynamic-slice_bitcast_fusion), channel_id=1, source_target_pairs={{0,8},{2,10},{4,12},{6,14},{8,0},{10,2},{12,4},{14,6},{16,24},{18,... | collective-permute-start | bytes 4718600 | tf_op jit(solution)/shard_map/ppermute | solution.py:65
  889.3 44.3 %collective-permute-start.61 = (bf16[2,96,768]{2,1,0:T(8,128)(2,1)}, bf16[2,96,768]{2,1,0:T(8,128)(2,1)S(1)}, u32[]{:S(2)}, u32[]{:S(2)}) collective-permute-start(bf16[2,96,768]{2,1,0:T(8,128)(2,1)} %dynamic-slice_bitcast_fusion.5), channel_id=1, source_target_pairs={{0,8},{2,10},{4,12},{6,14},{8,0},{10,2},{12,4},{14,6},{16,24},{18,... | collective-permute-start | bytes 884744 | tf_op jit(solution)/shard_map/ppermute | solution.py:65
  896.8 42.5 %collective-permute-start.73 = (bf16[2,96,768]{2,1,0:T(8,128)(2,1)}, bf16[2,96,768]{2,1,0:T(8,128)(2,1)S(1)}, u32[]{:S(2)}, u32[]{:S(2)}) collective-permute-start(bf16[2,96,768]{2,1,0:T(8,128)(2,1)} %dynamic-slice_bitcast_fusion.4), channel_id=1, source_target_pairs={{0,8},{2,10},{4,12},{6,14},{8,0},{10,2},{12,4},{14,6},{16,24},{18,... | collective-permute-start | bytes 884744 | tf_op jit(solution)/shard_map/ppermute | solution.py:65
  951.6 47.2 %collective-permute-start.81 = (bf16[1,96,4096]{2,1,0:T(8,128)(2,1)}, bf16[1,96,4096]{2,1,0:T(8,128)(2,1)}, u32[]{:S(2)}, u32[]{:S(2)}) collective-permute-start(bf16[1,96,4096]{2,1,0:T(8,128)(2,1)} %fusion.41), channel_id=1, source_target_pairs={{0,16},{2,18},{4,20},{6,22},{8,24},{10,26},{12,28},{14,30},{16,0},... | collective-permute-start | bytes 2359304 | tf_op jit(solution)/shard_map/ppermute | solution.py:65
  957.0 40.5 %collective-permute-start.49 = (bf16[2,96,1536]{2,1,0:T(8,128)(2,1)}, bf16[2,96,1536]{2,1,0:T(8,128)(2,1)}, u32[]{:S(2)}, u32[]{:S(2)}) collective-permute-start(bf16[2,96,1536]{2,1,0:T(8,128)(2,1)} %dynamic-slice_bitcast_fusion.2), channel_id=1, source_target_pairs={{0,8},{2,10},{4,12},{6,14},{8,0},{10,2},{12,4},{14,6},{16,24},{18,... | collective-permute-start | bytes 1769480 | tf_op jit(solution)/shard_map/ppermute | solution.py:65
  960.6 35.3 %collective-permute-start.56 = (bf16[1,96,896]{1,2,0:T(8,128)(2,1)S(1)}, bf16[1,96,896]{1,2,0:T(8,128)(2,1)S(1)}, u32[]{:S(2)}, u32[]{:S(2)}) collective-permute-start(bf16[1,96,896]{1,2,0:T(8,128)(2,1)S(1)} %fusion.78), channel_id=1, source_target_pairs={{0,16},{2,18},{4,20},{6,22},{8,24},{10,26},{12,28},{14,30},{16,0},... | collective-permute-start | bytes 516104 | tf_op jit(solution)/shard_map/ppermute | solution.py:65
  (125 other events, 1683.4 us)

commit v2 on v1

v2 whole, which is shorter than its diff:
```python
import functools

import jax
import jax.numpy as jnp
from jax import lax
from jax.experimental import pallas as pl
from jax.experimental.pallas import tpu as pltpu
from jax.sharding import PartitionSpec as P

EPSILON = 1e-06
LANES = 128
VMEM_LIMIT = 50 * 2**20
COST_SCALE = 0.02


def lower(values):
    return values.astype(jnp.bfloat16)


def wide(values):
    return values.astype(jnp.float32)


def matmul(left, right):
    return jnp.dot(left, right, preferred_element_type=jnp.float32)


def first_contract(left, right):
    return lax.dot_general(
        left, right, (((0,), (0,)), ((), ())), preferred_element_type=jnp.float32
    )


def second_contract(left, right):
    return lax.dot_general(
        left, right, (((1,), (1,)), ((), ())), preferred_element_type=jnp.float32
    )


def statistics(values):
    inverse = lax.rsqrt(jnp.mean(values * values, axis=-1, keepdims=True) + EPSILON)
    return (values * inverse, inverse)


def norm_backward(unit, inverse, gain, grad):
    scaled = gain * grad
    return inverse * (scaled - unit * jnp.mean(scaled * unit, axis=-1, keepdims=True))


def partner(values):
    return lax.ppermute(values, "tensor", [(0, 1), (1, 0)])


def tie(value, *others):
    if not others:
        return value
    return lax.optimization_barrier((value, *others))[0]


def small_cost(flops, size):
    return pl.CostEstimate(
        flops=int(COST_SCALE * flops), bytes_accessed=int(COST_SCALE * size), transcendentals=0
    )


class Grid:
    def __init__(self):
        self.count = lax.axis_size("dp")
        self.index = lax.axis_index("dp")
        bits = self.count.bit_length() - 1
        self.line_bits = list(range(2, bits))

    def bit(self, number):
        return (self.index >> number) & 1

    def swap(self, values, number):
        pairs = [(i, i ^ (1 << number)) for i in range(self.count)]
        return lax.ppermute(values, "dp", pairs)

    def place(self, pieces, splits):
        rows = pieces[0][1].shape[1]
        arrays = [piece for _, piece in pieces]
        codes = [code for found, _ in pieces for code in found]
        kind = arrays[0].dtype

        def body(*refs):
            inputs, results, sem = refs[: len(arrays)], refs[len(arrays) : -1], refs[-1]
            here = lax.axis_index("dp")
            copies = []
            for (found, _), ref in zip(pieces, inputs):
                for number, code in enumerate(found):
                    start = 0
                    for width, result in zip(splits, results):
                        copies.append(
                            pltpu.make_async_copy(
                                ref.at[number, :, pl.ds(start, width)],
                                result.at[here ^ code],
                                sem.at[len(copies)],
                            )
                        )
                        start += width
            for copy in copies:
                copy.start()
            for copy in copies:
                copy.wait()

        size = self.count * rows * sum(splits) * kind.itemsize
        results = pl.pallas_call(
            body,
            out_shape=[jax.ShapeDtypeStruct((self.count, rows, w), kind) for w in splits],
            in_specs=[pl.BlockSpec(memory_space=pl.ANY)] * len(arrays),
            out_specs=[pl.BlockSpec(memory_space=pltpu.VMEM)] * len(splits),
            scratch_shapes=[pltpu.SemaphoreType.DMA((len(codes) * len(splits),))],
            compiler_params=pltpu.CompilerParams(vmem_limit_bytes=VMEM_LIMIT),
            cost_estimate=small_cost(0, 2 * size),
        )(*arrays)
        return [r.reshape(self.count * rows, w) for r, w in zip(results, splits)]


class Weight:
    def __init__(self, grid, pieces, first=0, width=None):
        self.grid, self.pieces, self.first = grid, pieces, first
        self.rows = pieces[0][1].shape[1]
        self.width = width or pieces[0][1].shape[2]
        self.in_kernel = self.rows % 16 == 0

    def part(self, first, width):
        return Weight(self.grid, self.pieces, self.first + first, width)

    def arrays(self):
        return [piece for _, piece in self.pieces]

    def assembled(self):
        pieces = [
            (codes, piece[:, :, self.first : self.first + self.width])
            for codes, piece in self.pieces
        ]
        return self.grid.place(pieces, [self.width])[0]

    def copies(self, refs, target, sem, tiles):
        here = lax.axis_index("dp")
        tile = self.width // tiles
        found = []
        for step in range(tiles):
            for (codes, _), ref in zip(self.pieces, refs):
                for number, code in enumerate(codes):
                    block = here ^ code
                    source = ref.at[number, :, pl.ds(self.first + step * tile, tile)]
                    found.append(
                        pltpu.make_async_copy(source, target(step, block), sem.at[step, block])
                    )
        return found


def multiply(left, weight, tiles, epilogue, extras, outs):
    if not weight.in_kernel:
        return epilogue(matmul(left, weight.assembled()), *extras)
    grid, rows = weight.grid, weight.rows
    length, depth = left.shape
    tile = weight.width // tiles
    arrays = weight.arrays()

    def body(*refs):
        left_ref, refs = refs[0], refs[1:]
        piece_refs, refs = refs[: len(arrays)], refs[len(arrays) :]
        extra_refs, refs = refs[: len(extras)], refs[len(extras) :]
        out_refs, (held, sem) = refs[: len(outs)], refs[len(outs) :]
        step = pl.program_id(0)

        def target(place, block):
            return held.at[place, pl.ds(pl.multiple_of(block * rows, 16), rows)]

        @pl.when(step == 0)
        def _():
            for copy in weight.copies(piece_refs, target, sem, tiles):
                copy.start()

        for block in range(grid.count):
            there = target(step, block)
            pltpu.make_async_copy(there, there, sem.at[step, block]).wait()
        results = epilogue(matmul(left_ref[...], held[step]), *[ref[...] for ref in extra_refs])
        for ref, result in zip(out_refs, results):
            ref[...] = result

    def column_block(width):
        return pl.BlockSpec((length, width // tiles), lambda step: (0, step))

    size = (
        left.size * 2
        + depth * weight.width * 2
        + sum(e.size * e.dtype.itemsize for e in extras)
        + sum(length * w * jnp.dtype(kind).itemsize for w, kind in outs)
    )
    return pl.pallas_call(
        body,
        grid=(tiles,),
        in_specs=[pl.BlockSpec((length, depth), lambda step: (0, 0))]
        + [pl.BlockSpec(memory_space=pl.ANY)] * len(arrays)
        + [column_block(extra.shape[1]) for extra in extras],
        out_specs=[column_block(width) for width, _ in outs],
        out_shape=[jax.ShapeDtypeStruct((length, width), kind) for width, kind in outs],
        scratch_shapes=[
            pltpu.VMEM((tiles, depth, tile), jnp.bfloat16),
            pltpu.SemaphoreType.DMA((tiles, grid.count)),
        ],
        cost_estimate=small_cost(2 * length * depth * weight.width, size),
        compiler_params=pltpu.CompilerParams(vmem_limit_bytes=VMEM_LIMIT),
    )(left, *arrays, *extras)


def multiply_back(terms, half, tiles=4):
    grid, rows = terms[0][1].grid, terms[0][1].rows
    length = terms[0][0].shape[0] // 2
    if not terms[0][1].in_kernel:
        return sum(
            second_contract(
                lax.dynamic_slice_in_dim(left, half * length, length, 0), weight.assembled()
            )
            for left, weight in terms
        )
    depth = grid.count * rows
    tile, share = depth // tiles, grid.count // tiles
    sources, counts = [], []
    for _, weight in terms:
        sources = sources + weight.arrays()
        counts.append(len(weight.pieces))

    def body(half_ref, *refs):
        left_refs, refs = refs[: len(terms)], refs[len(terms) :]
        piece_refs, refs = refs[: len(sources)], refs[len(sources) :]
        out_ref, held, sems = refs[0], refs[1 : 1 + len(terms)], refs[1 + len(terms) :]
        step = pl.program_id(0)

        def target(number):
            def found(_, block):
                return held[number].at[pl.ds(pl.multiple_of(block * rows, 16), rows)]

            return found

        @pl.when(step == 0)
        def _():
            first = 0
            for number, (_, weight) in enumerate(terms):
                mine = piece_refs[first : first + counts[number]]
                first += counts[number]
                for copy in weight.copies(mine, target(number), sems[number], 1):
                    copy.start()

        total = None
        for number in range(len(terms)):
            for part in range(share):
                block = step * share + part
                there = target(number)(0, block)
                pltpu.make_async_copy(there, there, sems[number].at[0, block]).wait()
            found = held[number][pl.ds(pl.multiple_of(step * tile, 16), tile), :]
            product = second_contract(left_refs[number][...], found)
            total = product if total is None else total + product
        out_ref[...] = total

    size = length * depth * 4 + sum(l.size + depth * w.width * 2 for l, w in terms)
    flops = sum(2 * length * depth * w.width for _, w in terms)
    return pl.pallas_call(
        body,
        grid_spec=pltpu.PrefetchScalarGridSpec(
            num_scalar_prefetch=1,
            grid=(tiles,),
            in_specs=[
                pl.BlockSpec((length, left.shape[1]), lambda step, which: (which[0], 0))
                for left, _ in terms
            ]
            + [pl.BlockSpec(memory_space=pl.ANY)] * len(sources),
            out_specs=pl.BlockSpec((length, tile), lambda step, which: (0, step)),
            scratch_shapes=[pltpu.VMEM((depth, w.width), jnp.bfloat16) for _, w in terms]
            + [pltpu.SemaphoreType.DMA((1, grid.count)) for _ in terms],
        ),
        out_shape=jax.ShapeDtypeStruct((length, depth), jnp.float32),
        cost_estimate=small_cost(flops, size),
        compiler_params=pltpu.CompilerParams(vmem_limit_bytes=VMEM_LIMIT),
    )(jnp.reshape(half, (1,)).astype(jnp.int32), *[left for left, _ in terms], *sources)


class Gather:
    def __init__(self, grid, shard, fine=False, after_line=(), after_plane=()):
        near, codes = tie(shard[None], *after_line), [0]
        for number in reversed(grid.line_bits[1:]):
            found = grid.swap(near, number)
            near = jnp.concatenate([near, found], axis=0)
            codes = codes + [code ^ (1 << number) for code in codes]
        last = grid.line_bits[0]
        far = grid.swap(near, last)
        far_codes = [code ^ (1 << last) for code in codes]

        def moved(found, plane):
            return [code ^ plane for code in found]

        half = len(codes)
        if fine:
            near_x, near_y = grid.swap(near, 0), grid.swap(near, 1)
            far_x, far_y = grid.swap(far, 0), grid.swap(far, 1)
            sides = [
                (codes, near),
                (far_codes, far),
                (moved(codes, 1), near_x),
                (moved(codes, 2), near_y),
                (moved(far_codes, 1), far_x),
                (moved(far_codes, 2), far_y),
            ]
            self.sides_done = (near_x, near_y, far_x, far_y)
        else:
            block = tie(jnp.concatenate([near, far], axis=0), *after_plane)
            side_x, side_y = grid.swap(block, 0), grid.swap(block, 1)
            near_x, far_y = side_x[:half], side_y[half:]
            both = codes + far_codes
            sides = [(both, block), (moved(both, 1), side_x), (moved(both, 2), side_y)]
            self.sides_done = (side_x, side_y)
        near_corner, far_corner = grid.swap(near_x, 1), grid.swap(far_y, 0)
        self.line_done, self.plane_done = (far,), (near_corner, far_corner, *self.sides_done)
        self.ready = far if fine else block
        corners = [(moved(codes, 3), near_corner), (moved(far_codes, 3), far_corner)]
        self.weight = Weight(grid, sides + corners)


def gradient_parts(grid, pairs, tiles, number):
    depth, length = pairs[0][0].shape
    rows, line = depth // grid.count, grid.count // 4
    width = sum(right.shape[1] for _, right in pairs)
    lefts = []
    for left, _ in pairs:
        if not any(left is other for other in lefts):
            lefts.append(left)
    which = [[left is other for other in lefts].index(True) for left, _ in pairs]
    tile = width // tiles
    starts, first = [], 0
    for _, right in pairs:
        starts.append(first)
        first += right.shape[1]

    def body(*refs):
        left_refs, refs = refs[: len(lefts)], refs[len(lefts) :]
        right_refs, refs = refs[: len(pairs)], refs[len(pairs) :]
        away, own, total = refs
        step = pl.program_id(0)
        if tiles == 1:
            for place in range(len(pairs)):
                ahead = starts[place]
                total[:, ahead : ahead + pairs[place][1].shape[1]] = matmul(
                    left_refs[which[place]][...], right_refs[place][...]
                )
        elif len(pairs) == 1:
            total[...] = matmul(left_refs[0][...], right_refs[0][...])
        else:
            for place in range(len(pairs)):
                low = starts[place] // tile
                high = low + pairs[place][1].shape[1] // tile

                @pl.when((step >= low) & (step < high))
                def _():
                    total[...] = matmul(left_refs[which[place]][...], right_refs[place][...])

        here = (lax.axis_index("dp") >> number) & 1

        def block(place):
            return lower(total[pl.ds(pl.multiple_of(place * rows, 8), rows), :])

        other = 3 - (1 << number)
        for place in range(line):
            for side in range(2):
                base = place * 4 + side * other
                away[place, side] = block(base + ((1 - here) << number))
                own[place, side] = block(base + (here << number))

    def right_spec(place):
        columns = pairs[place][1].shape[1]
        if tiles == 1:
            return pl.BlockSpec((length, columns), lambda step: (0, 0))
        low, count = starts[place] // tile, columns // tile
        return pl.BlockSpec((length, tile), lambda step: (0, jnp.clip(step - low, 0, count - 1)))

    out = jax.ShapeDtypeStruct((line, 2, rows, width), jnp.bfloat16)
    out_spec = pl.BlockSpec((line, 2, rows, tile), lambda step: (0, 0, 0, step))
    size = depth * width * 2 + sum(l.size * 2 for l in lefts) + sum(r.size * 2 for _, r in pairs)
    return pl.pallas_call(
        body,
        grid=(tiles,),
        in_specs=[pl.BlockSpec((depth, length), lambda step: (0, 0))] * len(lefts)
        + [right_spec(place) for place in range(len(pairs))],
        out_specs=[out_spec] * 2,
        out_shape=[out] * 2,
        scratch_shapes=[pltpu.VMEM((depth, tile), jnp.float32)],
        cost_estimate=small_cost(2 * depth * length * width, size),
        compiler_params=pltpu.CompilerParams(vmem_limit_bytes=VMEM_LIMIT),
    )(*lefts, *[right for _, right in pairs])


def pick(array, axis, place):
    return lax.dynamic_index_in_dim(array, place, axis, keepdims=False)


def cut_parts(grid, array, number):
    line, rows = grid.count // 4, array.shape[0] // grid.count
    blocks = array.reshape(line, 2, 2, rows, array.shape[1])
    here, axis = grid.bit(number), 2 - number
    return pick(blocks, axis, 1 - here), pick(blocks, axis, here)


def weight_gradient(grid, pairs, tiles, number):
    rows = pairs[0][0].shape[0] // grid.count
    if rows % 16 == 0:
        return Reduce(grid, gradient_parts(grid, pairs, tiles, number), number)
    found = [lower(matmul(left, right)) for left, right in pairs]
    return Reduce(grid, cut_parts(grid, jnp.concatenate(found, axis=1), number), number)


def add_halves(terms, number):
    count, _, rows, columns = terms[0].shape
    tile = next(t for t in (512, 384, 256, 128, columns) if columns % t == 0)

    def body(*refs):
        inputs, (away, kept) = refs[: len(terms)], refs[len(terms) :]
        side = (lax.axis_index("dp") >> number) & 1
        for place in range(count):
            away[place] = lower(sum(wide(ref[place, 1 - side]) for ref in inputs))
            kept[place] = lower(sum(wide(ref[place, side]) for ref in inputs))

    block = pl.BlockSpec((count, 2, rows, tile), lambda step: (0, 0, 0, step))
    half = pl.BlockSpec((count, rows, tile), lambda step: (0, 0, step))
    size = terms[0].size * (2 * len(terms) + 2)
    return pl.pallas_call(
        body,
        grid=(columns // tile,),
        in_specs=[block] * len(terms),
        out_specs=[half] * 2,
        out_shape=[jax.ShapeDtypeStruct((count, rows, columns), jnp.bfloat16)] * 2,
        cost_estimate=small_cost(0, size),
        compiler_params=pltpu.CompilerParams(vmem_limit_bytes=VMEM_LIMIT),
    )(*terms)


def joined_rows(own, other, in_sequence):
    rows, columns = own.shape
    tile = columns // 4

    def body(own_ref, other_ref, rows_ref, turned_ref):
        first, second = own_ref[...], other_ref[...]
        if in_sequence:
            ahead = lax.axis_index("tensor") == 0
            first, second = jnp.where(ahead, first, second), jnp.where(ahead, second, first)
        rows_ref[:rows] = first
        rows_ref[rows:] = second
        turned_ref[:, :rows] = first.T
        turned_ref[:, rows:] = second.T

    block = pl.BlockSpec((rows, tile), lambda step: (0, step))
    return pl.pallas_call(
        body,
        grid=(4,),
        in_specs=[block] * 2,
        out_specs=[
            pl.BlockSpec((2 * rows, tile), lambda step: (0, step)),
            pl.BlockSpec((tile, 2 * rows), lambda step: (step, 0)),
        ],
        out_shape=[
            jax.ShapeDtypeStruct((2 * rows, columns), own.dtype),
            jax.ShapeDtypeStruct((columns, 2 * rows), own.dtype),
        ],
        cost_estimate=small_cost(0, 12 * rows * columns),
        compiler_params=pltpu.CompilerParams(vmem_limit_bytes=VMEM_LIMIT),
    )(own, other)


def row_kernel(body, inputs, outs, sums=0):
    length, columns = inputs[0].shape
    tile = length // 4

    def spec(rows):
        if rows == 1:
            return pl.BlockSpec((1, columns), lambda step: (0, 0))
        return pl.BlockSpec((tile, columns), lambda step: (step, 0))

    def kernel(*refs):
        found = body(*[ref[...] for ref in refs[: len(inputs)]])
        out_refs = refs[len(inputs) :]
        for ref, value in zip(out_refs[: len(outs)], found):
            ref[...] = value
        for ref, value in zip(out_refs[len(outs) :], found[len(outs) :]):

            @pl.when(pl.program_id(0) == 0)
            def _():
                ref[...] = jnp.zeros_like(ref)

            ref[...] += value

    size = length * columns * (sum(i.dtype.itemsize for i in inputs) + 4 * len(outs))
    return pl.pallas_call(
        kernel,
        grid=(4,),
        in_specs=[spec(i.shape[0]) for i in inputs],
        out_specs=[spec(length)] * len(outs) + [spec(1)] * sums,
        out_shape=[jax.ShapeDtypeStruct((length, columns), kind) for kind in outs]
        + [jax.ShapeDtypeStruct((1, columns), jnp.float32)] * sums,
        cost_estimate=small_cost(0, size),
        compiler_params=pltpu.CompilerParams(vmem_limit_bytes=VMEM_LIMIT),
    )(*inputs)


def norm_forward(residual, own, arrived, gain):
    middle = wide(residual) + (own + arrived)
    unit, _ = statistics(middle)
    return middle, lower(unit * gain)


def norm_gradient(source, own, arrived, base, gain):
    unit, inverse = statistics(wide(source))
    grad = own + arrived
    total = wide(base) + norm_backward(unit, inverse, gain, grad)
    return total, lower(total), jnp.sum(grad * unit, axis=0, keepdims=True)


class Reduce:
    def __init__(self, grid, parts, number):
        self.grid, self.number = grid, number
        self.sent, own = parts
        self.kind = own.dtype
        self.terms = [own]

    def start(self, *after):
        self.got = self.grid.swap(tie(self.sent, *after), self.number)
        return self

    def step(self, number, after):
        terms = self.terms + [tie(self.got, *after)]
        if number >= 2:
            terms = [t.reshape((t.shape[0] // 2, 2) + t.shape[1:]) for t in terms]
        if self.kind == jnp.bfloat16:
            self.sent, kept = add_halves(terms, number)
            self.terms = [kept]
        else:
            side = self.grid.bit(number)
            self.sent = sum(pick(t, 1, 1 - side) for t in terms)
            self.terms = [pick(t, 1, side) for t in terms]
        self.got = self.grid.swap(self.sent, number)
        return self

    def second(self, *after):
        return self.step(1 - self.number, after)

    def third(self, *after):
        return self.step(self.grid.line_bits[0], after)

    def fourth(self, *after):
        for number in self.grid.line_bits[1:]:
            self.step(number, after)
        return self

    def result(self):
        return sum(wide(term[0]) for term in self.terms + [self.got])


def running_sum(values, reverse):
    length = values.shape[1]
    place = lax.broadcasted_iota(jnp.int32, values.shape, 1)
    shift = 1
    while shift < length:
        if reverse:
            moved = jnp.where(place < length - shift, pltpu.roll(values, length - shift, 1), 0.0)
        else:
            moved = jnp.where(place >= shift, pltpu.roll(values, shift, 1), 0.0)
        values = values + moved
        shift *= 2
    return values


def decay_kernel(heads, logit_ref, bias_ref, row_ref, column_ref):
    length, lanes = logit_ref.shape
    groups, per, _ = row_ref.shape
    padded = -(-heads // 8) * 8
    logit = (logit_ref[...] + bias_ref[...]).T[:padded]
    decay = running_sum(-jnp.log1p(jnp.exp(-logit)), False)
    columns = jnp.concatenate([decay, jnp.zeros((lanes - padded, length), jnp.float32)], axis=0).T
    for group in range(groups):
        row_ref[group] = decay[group * per : (group + 1) * per]
        column_ref[group] = columns[:, group * per : (group + 1) * per]


def decays(logit, bias, heads, per):
    length = logit.shape[0]
    groups = heads // per
    return pl.pallas_call(
        functools.partial(decay_kernel, heads),
        out_shape=[
            jax.ShapeDtypeStruct((groups, per, length), jnp.float32),
            jax.ShapeDtypeStruct((groups, length, per), jnp.float32),
        ],
        compiler_params=pltpu.CompilerParams(vmem_limit_bytes=VMEM_LIMIT),
    )(logit, bias)


def forget_kernel(heads, row_ref, column_ref, logit_ref, bias_ref, grad_ref, sum_ref):
    length, lanes = logit_ref.shape
    groups, per, _ = row_ref.shape
    padded = -(-heads // 8) * 8
    rows = [row_ref[group] for group in range(groups)]
    columns = [column_ref[group] for group in range(groups)]
    columns = jnp.concatenate(
        columns + [jnp.zeros((length, lanes - heads), jnp.float32)], axis=1
    ).T[:padded]
    if padded > heads:
        rows = rows + [jnp.zeros((padded - heads, length), jnp.float32)]
    grad_log = running_sum(jnp.concatenate(rows, axis=0) - columns, True)
    grad_log = jnp.concatenate([grad_log, jnp.zeros((lanes - padded, length), jnp.float32)], axis=0).T
    grad = lower(grad_log * jax.nn.sigmoid(-(logit_ref[...] + bias_ref[...])))
    lane = lax.broadcasted_iota(jnp.int32, grad.shape, 1)
    grad = jnp.where(lane < heads, grad, jnp.bfloat16(0))
    grad_ref[...] = grad
    sum_ref[...] = jnp.sum(wide(grad), axis=0, keepdims=True)


def forget_backward(row, column, logit, bias, heads):
    return pl.pallas_call(
        functools.partial(forget_kernel, heads),
        out_shape=[
            jax.ShapeDtypeStruct(logit.shape, jnp.bfloat16),
            jax.ShapeDtypeStruct(bias.shape, jnp.float32),
        ],
        compiler_params=pltpu.CompilerParams(vmem_limit_bytes=VMEM_LIMIT),
    )(row, column, logit, bias)


def fwd_kernel(scale, head, q_ref, k_ref, v_ref, col_ref, row_ref, o_ref, lse_ref, out_t):
    length, lanes = q_ref.shape
    span = min(256, length)
    lane = lax.broadcasted_iota(jnp.int32, (span, lanes), 1) // head
    below = lax.broadcasted_iota(jnp.int32, (span, span), 0) <= lax.broadcasted_iota(jnp.int32, (span, span), 1)
    v_t = v_ref[...].T
    for h in range(lanes // head):
        for b in range(length // span):
            lo, hi = b * span, (b + 1) * span
            q = jnp.where(lane == h, q_ref[lo:hi, :] * scale, 0).astype(jnp.bfloat16)
            row = row_ref[0, h:h+1, lo:hi]
            diag = second_contract(k_ref[lo:hi, :], q) + row - col_ref[0, lo:hi, h:h+1]
            diag = jnp.where(below, diag, -1e30)
            top = jnp.max(diag, axis=0, keepdims=True)
            if lo:
                off = second_contract(k_ref[:lo, :], q) + row - col_ref[0, :lo, h:h+1]
                top = jnp.maximum(top, jnp.max(off, axis=0, keepdims=True))
            e = jnp.exp(diag - top)
            total = jnp.sum(e, axis=0, keepdims=True)
            v_h = v_t[h*head:(h+1)*head]
            acc = matmul(v_h[:, lo:hi], lower(e))
            if lo:
                e = jnp.exp(off - top)
                total = total + jnp.sum(e, axis=0, keepdims=True)
                acc = acc + matmul(v_h[:, :lo], lower(e))
            out_t[h*head:(h+1)*head, lo:hi] = acc / total
            lse_ref[0, h:h+1, lo:hi] = top + jnp.log(total)
    o_ref[...] = out_t[...].T

def bwd_kernel(scale, head, q_ref, k_ref, v_ref, do_ref, col_ref, row_ref, lse_ref, dq_ref, dk_ref, dv_ref, drow_ref, dcol_ref, dq_t, dk_acc, dv_acc):
    length, lanes = q_ref.shape
    span = min(256, length)
    heads = lanes // head
    lane = lax.broadcasted_iota(jnp.int32, (span, lanes), 1) // head
    sub = lax.broadcasted_iota(jnp.int32, (lanes, length), 0) // head
    below = lax.broadcasted_iota(jnp.int32, (span, span), 0) <= lax.broadcasted_iota(jnp.int32, (span, span), 1)
    k_t = k_ref[...].T
    one = jnp.bfloat16(1)
    for h in range(heads):
        kt_h = jnp.where(sub == h, k_t, one)
        mine = lane == h
        for b in range(length // span):
            lo, hi = b * span, (b + 1) * span
            q = q_ref[lo:hi, :] * jnp.bfloat16(scale)
            qz = jnp.where(mine, q, jnp.bfloat16(0))
            q1 = jnp.where(mine, q, one)
            do = do_ref[lo:hi, :]
            doz = jnp.where(mine, do, jnp.bfloat16(0))
            row = row_ref[0, h:h+1, lo:hi] - lse_ref[0, h:h+1, lo:hi]
            s = second_contract(k_ref[lo:hi, :], qz) + row - col_ref[0, lo:hi, h:h+1]
            p = jnp.exp(jnp.where(below, s, -1e30))
            dp = second_contract(v_ref[lo:hi, :], doz)
            centre = jnp.sum(p * dp, axis=0, keepdims=True)
            if lo:
                s0 = second_contract(k_ref[:lo, :], qz) + row - col_ref[0, :lo, h:h+1]
                p0 = jnp.exp(s0)
                dp0 = second_contract(v_ref[:lo, :], doz)
                centre = centre + jnp.sum(p0 * dp0, axis=0, keepdims=True)
            ds = lower(p * (dp - centre))
            dqt = matmul(kt_h[:, lo:hi], ds)
            dv_acc[h, lo:hi, :] = matmul(lower(p), do)
            dk_acc[h, lo:hi, :] = matmul(ds, q1)
            if lo:
                ds0 = lower(p0 * (dp0 - centre))
                dqt = dqt + matmul(kt_h[:, :lo], ds0)
                dv_acc[h, :lo, :] = dv_acc[h, :lo, :] + matmul(lower(p0), do)
                dk_acc[h, :lo, :] = dk_acc[h, :lo, :] + matmul(ds0, q1)
            dq_t[h*head:(h+1)*head, lo:hi] = dqt[h*head:(h+1)*head] * scale
            other = ((h + 1) % heads) * head
            drow_ref[0, h:h+1, lo:hi] = dqt[other:other+1]
    lane_all = lax.broadcasted_iota(jnp.int32, (length, lanes), 1) // head
    dk, dv = dk_acc[0], dv_acc[0]
    for h in range(1, heads):
        dk = jnp.where(lane_all == h, dk_acc[h], dk)
        dv = jnp.where(lane_all == h, dv_acc[h], dv)
    for h in range(heads):
        other = ((h + 1) % heads) * head
        dcol_ref[0, :, h:h+1] = dk_acc[h][:, other:other+1]
    dq_ref[...] = lower(dq_t[...].T)
    dk_ref[...] = lower(dk)
    dv_ref[...] = lower(dv)


def pair_specs(length, groups, per):
    def block(offset):
        return pl.BlockSpec((length, LANES), lambda group: (0, group + offset))

    column = pl.BlockSpec((1, length, per), lambda group: (group, 0, 0))
    row = pl.BlockSpec((1, per, length), lambda group: (group, 0, 0))
    return block, column, row


def attention_cost(length, width, head, products):
    return small_cost(products * 6 * length * length * width, 16 * length * width)


def attend(qk, values, column, row, head):
    length, width = values.shape[0], qk.shape[1] // 2
    groups, per, _ = row.shape
    block, column_spec, row_spec = pair_specs(length, groups, per)
    return pl.pallas_call(
        functools.partial(fwd_kernel, head**-0.5, head),
        grid=(groups,),
        in_specs=[block(0), block(groups), block(0), column_spec, row_spec],
        out_specs=[block(0), row_spec],
        out_shape=[
            jax.ShapeDtypeStruct((length, width), jnp.float32),
            jax.ShapeDtypeStruct(row.shape, jnp.float32),
        ],
        scratch_shapes=[pltpu.VMEM((LANES, length), jnp.float32)],
        cost_estimate=attention_cost(length, width, head, 2),
        compiler_params=pltpu.CompilerParams(vmem_limit_bytes=VMEM_LIMIT),
    )(qk, qk, values, column, row)


def attend_backward(qk, values, grad, column, row, logsum, head):
    length, width = values.shape[0], qk.shape[1] // 2
    groups, per, _ = row.shape
    block, column_spec, row_spec = pair_specs(length, groups, per)
    wide_out = jax.ShapeDtypeStruct((length, width), jnp.bfloat16)
    return pl.pallas_call(
        functools.partial(bwd_kernel, head**-0.5, head),
        grid=(groups,),
        in_specs=[block(0), block(groups), block(0), block(0), column_spec, row_spec, row_spec],
        out_specs=[block(0), block(0), block(0), row_spec, column_spec],
        out_shape=[
            wide_out,
            wide_out,
            wide_out,
            jax.ShapeDtypeStruct(row.shape, jnp.float32),
            jax.ShapeDtypeStruct(column.shape, jnp.float32),
        ],
        scratch_shapes=[
            pltpu.VMEM((LANES, length), jnp.float32),
            pltpu.VMEM((per, length, LANES), jnp.float32),
            pltpu.VMEM((per, length, LANES), jnp.float32),
        ],
        cost_estimate=attention_cost(length, width, head, 5),
        compiler_params=pltpu.CompilerParams(vmem_limit_bytes=VMEM_LIMIT),
    )(qk, qk, values, grad, column, row, logsum)


def per_device(
    tokens,
    w_query,
    w_key,
    w_value,
    w_gate_attn,
    w_forget,
    forget_bias,
    w_out,
    norm_attn,
    norm_mlp,
    w_gate,
    w_up,
    w_down,
    cotangent,
):
    grid = Grid()
    side = lax.axis_index("tensor")
    heads_here = forget_bias.shape[0]
    width = w_query.shape[1]
    head_size = width // heads_here
    hidden_here = w_gate.shape[1]
    scale = head_size ** (-0.5)
    rows_here = tokens.shape[0]

    other_cotangent = partner(cotangent)
    own_gains = jnp.stack([norm_attn, norm_mlp])
    other_gains = partner(own_gains)
    gains = jnp.where(
        side == 0,
        jnp.concatenate([own_gains, other_gains], axis=1),
        jnp.concatenate([other_gains, own_gains], axis=1),
    )[None]
    gain_codes = [0]
    for number in range(len(grid.line_bits) + 2):
        gains = jnp.concatenate([gains, grid.swap(gains, number)], axis=0)
        gain_codes = gain_codes + [code ^ (1 << number) for code in gain_codes]
    (gains,) = grid.place([(gain_codes, gains)], [gains.shape[2]])
    gains = gains.reshape(grid.count, 2, gains.shape[1])
    gain_attn = gains[:, 0].reshape(-1)
    gain_mlp = gains[:, 1].reshape(-1)

    padding = jnp.zeros((w_forget.shape[0], LANES - heads_here), jnp.bfloat16)
    forget_lanes = jnp.concatenate([lower(w_forget), padding], axis=1)
    load_qk = Gather(grid, jnp.concatenate([lower(w_query), lower(w_key)], axis=1), fine=True)
    load_vf = Gather(
        grid,
        jnp.concatenate([lower(w_value), forget_lanes], axis=1),
        after_line=load_qk.line_done,
        after_plane=load_qk.plane_done,
    )
    load_go = Gather(
        grid,
        jnp.concatenate([lower(w_gate_attn), lower(w_out).T], axis=1),
        after_line=load_vf.line_done,
        after_plane=load_vf.sides_done,
    )
    load_gate = Gather(
        grid, lower(w_gate), after_line=load_go.line_done, after_plane=load_go.sides_done
    )
    load_up = Gather(
        grid, lower(w_up), after_line=load_gate.line_done, after_plane=load_gate.sides_done
    )
    load_down = Gather(
        grid, lower(w_down).T, after_line=load_up.line_done, after_plane=load_up.sides_done
    )
    query_w, key_w = load_qk.weight.part(0, width), load_qk.weight.part(width, width)
    value_w, forget_w = load_vf.weight.part(0, width), load_vf.weight.part(width, LANES)
    gate_w, out_w = load_go.weight.part(0, width), load_go.weight.part(width, width)
    mlp_gate, mlp_up, mlp_down = load_gate.weight, load_up.weight, load_down.weight

    gain_attn, gain_mlp = gain_attn[None], gain_mlp[None]
    (own_attn,) = row_kernel(
        lambda rows, gain: (lower(statistics(wide(rows))[0] * gain),),
        [tokens, gain_attn],
        [jnp.bfloat16],
    )
    normed_attn, normed_attn_t = joined_rows(own_attn, partner(own_attn), True)
    grad_output, grad_output_t = joined_rows(cotangent, other_cotangent, False)

    low = jnp.bfloat16
    (qk,) = multiply(
        normed_attn, load_qk.weight, 3, lambda p: (lower(p),), [], [(2 * width, low)]
    )
    values_all, forget_logit = multiply(
        normed_attn,
        load_vf.weight,
        1,
        lambda p: (lower(p[:, :width]), p[:, width:]),
        [],
        [(width, low), (LANES, jnp.float32)],
    )
    bias_lanes = jnp.pad(forget_bias, (0, LANES - heads_here))[None]
    decay_row, decay_column = decays(forget_logit, bias_lanes, heads_here, LANES // head_size)
    qk = tie(qk, load_gate.ready)
    attended, logsum = attend(qk, values_all, decay_column, decay_row, head_size)

    def gate_output(product, attended):
        sigmoid = jax.nn.sigmoid(product)
        return sigmoid, lower(attended * sigmoid)

    gate_sig, gated = multiply(
        normed_attn, gate_w, 2, gate_output, [attended], [(width, jnp.float32), (width, low)]
    )
    arrived = partner(multiply_back([(gated, out_w)], 1 - side))
    middle, own_normed = row_kernel(
        norm_forward,
        [tokens, multiply_back([(gated, out_w)], side), arrived, gain_mlp],
        [jnp.float32, low],
    )
    normed_mlp, normed_mlp_t = joined_rows(own_normed, partner(own_normed), False)
    (gate_act,) = multiply(
        normed_mlp, mlp_gate, 4, lambda p: (lower(p),), [], [(hidden_here, low)]
    )

    def hidden_units(up, gate):
        gate = wide(gate)
        return lower(up), lower(gate * jax.nn.sigmoid(gate) * up)

    up_act, hidden = multiply(
        normed_mlp, mlp_up, 4, hidden_units, [gate_act], [(hidden_here, low)] * 2
    )
    sum_down = weight_gradient(grid, [(grad_output_t, hidden)], 4, 1).start()
    hidden = tie(hidden, sum_down.sent)
    other_down = multiply_back([(hidden, mlp_down)], jnp.int32(1))
    arrived_down = partner(other_down)

    def hidden_backward(grad, gate, up):
        gate, up = wide(gate), wide(up)
        sigmoid = jax.nn.sigmoid(gate)
        return (
            lower(grad * (gate * sigmoid)),
            lower(grad * up * sigmoid * (1.0 + gate * (1.0 - sigmoid))),
        )

    grad_up, grad_gate = multiply(
        tie(grad_output, other_down),
        mlp_down,
        4,
        hidden_backward,
        [gate_act, up_act],
        [(hidden_here, low)] * 2,
    )
    sum_up = weight_gradient(grid, [(normed_mlp_t, grad_up)], 4, 0).start()
    grad_gate = tie(grad_gate, sum_up.sent)
    sum_gate = weight_gradient(grid, [(normed_mlp_t, grad_gate)], 4, 1)
    grad_gate = tie(grad_gate, sum_gate.sent)
    back = [(grad_gate, mlp_gate), (grad_up, mlp_up)]
    other_part = multiply_back(back, jnp.int32(1))
    arrived = partner(other_part)
    sum_down.second(other_part)
    sum_gate.start(sum_down.sent)
    back = [(tie(grad_gate, sum_down.sent), mlp_gate), (grad_up, mlp_up)]
    grad_middle, own_branch, gain_mlp_part = row_kernel(
        norm_gradient,
        [middle, multiply_back(back, jnp.int32(0)), arrived, cotangent, gain_mlp],
        [jnp.float32, low],
        sums=1,
    )
    other_branch = partner(own_branch)
    own_down = multiply_back([(tie(hidden, own_branch), mlp_down)], jnp.int32(0))
    (mixed,) = row_kernel(
        lambda middle, own, arrived: (lower(middle + (own + arrived)),),
        [middle, own_down, arrived_down],
        [low],
    )
    grad_branch, grad_branch_t = joined_rows(own_branch, tie(other_branch, own_down), True)

    def gate_backward(grad, sigmoid, attended):
        return lower(grad * sigmoid), lower(grad * attended * sigmoid * (1.0 - sigmoid))

    grad_attended, grad_gate_logit = multiply(
        grad_branch,
        out_w,
        2,
        gate_backward,
        [gate_sig, attended],
        [(width, low)] * 2,
    )
    sum_go = weight_gradient(
        grid, [(normed_attn_t, grad_gate_logit), (grad_branch_t, gated)], 4, 0
    ).start()
    sum_up.second(sum_go.sent)
    sum_gate.second(sum_go.sent)
    sum_down.third(sum_go.sent)
    grad_attended = tie(grad_attended, sum_go.sent, sum_up.sent, sum_gate.sent, sum_down.sent)
    grad_queries, grad_keys, grad_values, row_total, column_total = attend_backward(
        qk, values_all, grad_attended, decay_column, decay_row, logsum, head_size
    )
    sum_up.third(grad_queries)
    sum_down.fourth(grad_queries)
    grad_queries = tie(grad_queries, sum_up.sent, sum_down.sent)
    sum_qk = weight_gradient(
        grid, [(normed_attn_t, grad_queries), (normed_attn_t, grad_keys)], 4, 1
    ).start()
    grad_forget, bias_part = forget_backward(
        row_total, column_total, forget_logit, bias_lanes, heads_here
    )
    sum_vf = weight_gradient(
        grid, [(normed_attn_t, tie(grad_values, sum_qk.sent)), (normed_attn_t, grad_forget)], 1, 0
    ).start()
    back = [
        (tie(grad_gate_logit, sum_qk.sent, sum_vf.sent), gate_w),
        (grad_queries, query_w),
        (grad_keys, key_w),
        (grad_values, value_w),
        (grad_forget, forget_w),
    ]
    other_part = multiply_back(back, 1 - side)
    arrived = partner(other_part)
    sum_up.fourth(other_part)
    sum_gate.third(other_part)
    back[1] = (tie(grad_queries, sum_up.sent, sum_gate.sent), query_w)
    own_part = multiply_back(back, side)
    sum_go.second(own_part)
    _, tokens_grad, gain_attn_part = row_kernel(
        norm_gradient,
        [tokens, own_part, arrived, grad_middle, gain_attn],
        [jnp.float32, low],
        sums=1,
    )
    small = jnp.concatenate(
        [
            gain_attn_part.reshape(grid.count, -1),
            gain_mlp_part.reshape(grid.count, -1),
            jnp.broadcast_to(bias_part[:, :heads_here], (grid.count, heads_here)),
        ],
        axis=1,
    )
    sum_gate.fourth(gain_attn_part)
    sum_qk.second(sum_go.sent)
    sum_vf.second(sum_go.sent)
    sum_go.third(sum_qk.sent)
    sum_qk.third(sum_go.sent, sum_vf.sent)
    sum_small = Reduce(grid, cut_parts(grid, small, 1), 1).start(sum_qk.sent)
    sum_vf.third(sum_qk.sent)
    sum_go.fourth(sum_qk.sent)
    sum_small.second(sum_vf.sent)
    sum_qk.fourth(sum_small.sent)
    sum_small.third(sum_qk.sent)
    sum_vf.fourth(sum_qk.sent)
    sum_small.fourth(sum_vf.sent)
    down_grad, up_grad, gate_grad = sum_down.result().T, sum_up.result(), sum_gate.result()
    go_grad, qk_grad, vf_grad = sum_go.result(), sum_qk.result(), sum_vf.result()
    small_sum = sum_small.result().reshape(-1)
    share = norm_attn.shape[0]
    gain_sums = small_sum[: 4 * share].reshape(2, 2, share)
    other_sums = lax.dynamic_index_in_dim(gain_sums, 1 - side, 1, keepdims=False)
    own_sums = lax.dynamic_index_in_dim(gain_sums, side, 1, keepdims=False)
    gain_grads = own_sums + partner(other_sums)
    return (
        mixed,
        tokens_grad,
        qk_grad[:, :width],
        qk_grad[:, width:],
        vf_grad[:, :width],
        go_grad[:, :width],
        vf_grad[:, width : width + heads_here],
        small_sum[4 * share :],
        go_grad[:, width:].T,
        gain_grads[0],
        gain_grads[1],
        gate_grad,
        up_grad,
        down_grad,
    )


def solution(mesh):
    return jax.shard_map(
        per_device,
        mesh=mesh,
        in_specs=(
            P(("dp", "tensor"), None),
            P("dp", "tensor"),
            P("dp", "tensor"),
            P("dp", "tensor"),
            P("dp", "tensor"),
            P("dp", "tensor"),
            P("tensor"),
            P("tensor", "dp"),
            P(("dp", "tensor")),
            P(("dp", "tensor")),
            P("dp", "tensor"),
            P("dp", "tensor"),
            P("tensor", "dp"),
            P(("dp", "tensor"), None),
        ),
        out_specs=(
            P(("dp", "tensor"), None),
            P(("dp", "tensor"), None),
            P("dp", "tensor"),
            P("dp", "tensor"),
            P("dp", "tensor"),
            P("dp", "tensor"),
            P("dp", "tensor"),
            P("tensor"),
            P("tensor", "dp"),
            P(("dp", "tensor")),
            P(("dp", "tensor")),
            P("dp", "tensor"),
            P("dp", "tensor"),
            P("tensor", "dp"),
        ),
        check_vma=False,
    )
```

time: 1050 us -> 812 us (0.77)
  Pallas kernels: 83 us -> 399 us
  waiting for transfers between devices: 464 us -> 265 us
  matrix products: 157 us -> 0 us
  other arithmetic: 115 us -> 15.1 us
  local copies, waits for them, and re-layouts: 109 us -> 40.1 us
  starting transfers between devices: 110 us -> 86.3 us
    pallas_call x6 -> x51, Pallas kernels: 27.9 us -> 343 us  [the longest x8 98.6 us: multiply_back(): pl.pallas_call(body, grid_spec=pltpu.PrefetchScalarGridSpec(num_scalar_pr...]
    ppermute x78 -> x70, waiting for transfers between devices: 463 us -> 264 us  [swap(): return lax.ppermute(values, 'dp', pairs)]
    dot_general x18 -> x0, matrix products: 157 us -> none  [the longest x6 63.1 us: matmul(): return jnp.dot(left, right, preferred_element_type=jnp.float32)]
    another operation x18 -> x1, other arithmetic: 35.6 us -> 0.01 us  [per_device(): own_gains = jnp.stack([norm_attn, norm_mlp])]
    convert_element_type x19 -> x0, other arithmetic: 27.4 us -> none  [the longest x18 22.6 us: step(): sent = self.swap(total(take(terms, axis, 1 - side)).astype(kind), number)]
    ppermute x78 -> x70, starting transfers between devices: 110 us -> 85.8 us  [swap(): return lax.ppermute(values, 'dp', pairs)]
    slice x27 -> x11, local copies, waits for them, and re-layouts: 34.4 us -> 11.3 us  [the longest x10 11.3 us: __init__(): near_x, far_y = (side_x[:half], side_y[half:])]
    squeeze x21 -> x1, local copies, waits for them, and re-layouts: 18.7 us -> 0.01 us  [pick(): return lax.dynamic_index_in_dim(array, place, axis, keepdims=False)]
  transfers between devices with their start and end apart: 88 -> 80, of which waited for: 35 -> 32; matrix products, arithmetic and copies ran while one was open for 26% -> 4% of each run, Pallas kernels for 8% -> 49%
where the time goes in v2:
time: 812 us; the launch traced here: 807 us
  Pallas kernels  399 us (49%)
  waiting for transfers between devices  265 us (33%)
  starting transfers between devices  86.3 us (11%)
  local copies, waits for them, and re-layouts  40.1 us (5%)
  other arithmetic  15.1 us (2%)
    ppermute x70, waiting for transfers between devices, swap(): return lax.ppermute(values, 'dp', pairs)  264 us
    pallas_call x8, Pallas kernels, multiply_back(): pl.pallas_call(body, grid_spec=pltpu.PrefetchScalarGridSpec(num_scalar_pr...  98.6 us
    ppermute x70, starting transfers between devices, swap(): return lax.ppermute(values, 'dp', pairs)  85.8 us
    pallas_call x7, Pallas kernels, multiply(): pl.pallas_call(body, grid=(tiles,), in_specs=[pl.BlockSpec((length, depth...  79.4 us
    pallas_call x6, Pallas kernels, gradient_parts(): pl.pallas_call(body, grid=(tiles,), in_specs=[pl.BlockSpec((depth, length...  68.1 us
    pallas_call x18, Pallas kernels, add_halves(): pl.pallas_call(body, grid=(columns // tile,), in_specs=[block] * len(term...  53.4 us
    pallas_call x1, Pallas kernels, attend_backward(): pl.pallas_call(functools.partial(bwd_kernel, head ** (-0.5), head), grid=...  32.9 us
    pallas_call x5, Pallas kernels, row_kernel(): pl.pallas_call(kernel, grid=(4,), in_specs=[spec(i.shape[0]) for i in inp...  24.6 us
  transfers between devices with their start and end apart: 80, of which 32 were waited for; matrix products, arithmetic and copies ran while one was open for 4% of the time, Pallas kernels for 49%

profile of v2, /device:TPU:0, one launch (start us, length us, event | category | flops | bytes accessed | tf_op | source)
XLA Modules:
  0.0 807.2 jit_solution(7849951432367922540)
XLA Ops:
  6.9 13.3 %collective-permute-done.6 = bf16[1,96,1536]{2,1,0:T(8,128)(2,1)S(1)} collective-permute-done((bf16[1,96,1536]{2,1,0:T(8,128)(2,1)S(1)}, bf16[1,96,1536]{2,1,0:T(8,128)(2,1)S(1)}, u32[]{:S(2)}, u32[]{:S(2)}) %collective-permute-start.6) | collective-permute-done | bytes 294944 | tf_op jit(solution)/shard_map/ppermute | solution.py:78
  21.5 13.4 %collective-permute-done.7.refs_2_.refs_11_.refs_19_ = bf16[2,96,1536]{2,1,0:T(8,128)(2,1)S(1)} collective-permute-done((bf16[2,96,1536]{2,1,0:T(8,128)(2,1)S(1)}, bf16[2,96,1536]{2,1,0:T(8,128)(2,1)S(1)}, u32[]{:S(2)}, u32[]{:S(2)}) %collective-permute-start.7) | collective-permute-done | bytes 589856 | tf_op jit(solution)/shard_map/ppermute | solution.py:78
  58.1 8.4 %collective-permute-done.2 = f32[2,2,96]{2,1,0:T(2,128)S(1)} collective-permute-done((f32[2,2,96]{2,1,0:T(2,128)S(1)}, f32[2,2,96]{2,1,0:T(2,128)S(1)}, u32[]{:S(2)}, u32[]{:S(2)}) %collective-permute-start.2) | collective-permute-done | bytes 1568 | tf_op jit(solution)/shard_map/ppermute | solution.py:78
  83.5 9.0 %collective-permute-done.15.refs_8_.refs_17_.refs_25_ = bf16[2,96,1536]{2,1,0:T(8,128)(2,1)S(1)} collective-permute-done((bf16[2,96,1536]{2,1,0:T(8,128)(2,1)S(1)}, bf16[2,96,1536]{2,1,0:T(8,128)(2,1)S(1)}, u32[]{:S(2)}, u32[]{:S(2)}) %collective-permute-start.15) | collective-permute-done | bytes 589856 | tf_op jit(solution)/shard_map/ppermute | solution.py:78
  112.9 14.8 %collective-permute-done.24 = bf16[1,96,2048]{2,1,0:T(8,128)(2,1)S(1)} collective-permute-done((bf16[1,96,2048]{2,1,0:T(8,128)(2,1)S(1)}, bf16[1,96,2048]{2,1,0:T(8,128)(2,1)S(1)}, u32[]{:S(2)}, u32[]{:S(2)}) %collective-permute-start.24) | collective-permute-done | bytes 393248 | tf_op jit(solution)/shard_map/ppermute | solution.py:78
  149.8 10.0 %shard_map.248.q_ref.k_ref = bf16[1024,1536]{1,0:T(8,128)(2,1)} custom-call(bf16[1024,1536]{1,0:T(8,128)(2,1)} %get-tuple-element.144.refs_0_, bf16[2,96,1536]{2,1,0:T(8,128)(2,1)S(1)} %copy-done.8, bf16[2,96,1536]{2,1,0:T(8,128)(2,1)S(1)} %copy-done.14, bf16[2,96,1536]{2,1,0:T(8,128)(2,1)S(1)} %copy-done.17, bf16[2,96,1536]{2,1,0:T(8,128)(2,1)S(1)} %copy-done.22, ...), custom_call_target="tpu_custom_call" | custom-call | flops 96636768 | bytes 220200 | tf_op jit(solution)/shard_map/pallas_call | solution.py:194
  159.8 10.0 %shard_map.249 = (bf16[1024,768]{1,0:T(8,128)(2,1)}, f32[1024,128]{1,0:T(8,128)S(1)}) custom-call(bf16[1024,1536]{1,0:T(8,128)(2,1)} %get-tuple-element.144.refs_0_, bf16[4,96,896]{2,1,0:T(8,128)(2,1)S(1)} %pad_maximum_fusion.7.refs_1_.refs_26_.refs_31_, bf16[4,96,896]{2,1,0:T(8,128)(2,1)S(1)} %copy-done.12, ...), custom_call_target="tpu_custom_call" | custom-call | flops 56371444 | bytes 159907 | tf_op jit(solution)/shard_map/pallas_call | solution.py:194
  181.2 22.6 %shard_map.251 = (f32[1024,768]{1,0:T(8,128)}, f32[6,2,1024]{2,1,0:T(2,128)S(1)}) custom-call(bf16[1024,1536]{1,0:T(8,128)(2,1)} %shard_map.248.q_ref.k_ref, bf16[1024,1536]{1,0:T(8,128)(2,1)} %shard_map.248.q_ref.k_ref, bf16[1024,768]{1,0:T(8,128)(2,1)S(1)} %copy-done.38, f32[6,1024,2]{2,1,0:T(8,128)} %copy-done.35, ...), custom_call_target="tpu_custom_call" | custom-call | flops 193273536 | bytes 251658 | tf_op jit(solution)/shard_map/pallas_call | solution.py:729
  203.8 9.0 %shard_map.252 = (f32[1024,768]{1,0:T(8,128)}, bf16[1024,768]{1,0:T(8,128)(2,1)}) custom-call(bf16[1024,1536]{1,0:T(8,128)(2,1)} %get-tuple-element.144.refs_0_, bf16[4,96,1536]{2,1,0:T(8,128)(2,1)S(1)} %pad_maximum_fusion.3.refs_1_.refs_5_, bf16[4,96,1536]{2,1,0:T(8,128)(2,1)S(1)} %collective-permute-done.20.refs_2_.refs_6_, ...), custom_call_target="tpu_custom_call" | custom-call | flops 48318384 | bytes 267386 | tf_op jit(solution)/shard_map/pallas_call | solution.py:194
  212.7 6.9 shard_map.254
  220.8 19.0 %collective-permute-done.31 = bf16[2,96,2048]{2,1,0:T(8,128)(2,1)S(1)} collective-permute-done((bf16[2,96,2048]{2,1,0:T(8,128)(2,1)S(1)}, bf16[2,96,2048]{2,1,0:T(8,128)(2,1)S(1)}, u32[]{:S(2)}, u32[]{:S(2)}) %collective-permute-start.31) | collective-permute-done | bytes 786464 | tf_op jit(solution)/shard_map/ppermute | solution.py:78
  242.7 17.1 %collective-permute-done.41 = bf16[1,96,2048]{2,1,0:T(8,128)(2,1)S(1)} collective-permute-done((bf16[1,96,2048]{2,1,0:T(8,128)(2,1)S(1)}, bf16[1,96,2048]{2,1,0:T(8,128)(2,1)S(1)}, u32[]{:S(2)}, u32[]{:S(2)}) %collective-permute-start.41) | collective-permute-done | bytes 393248 | tf_op jit(solution)/shard_map/ppermute | solution.py:78
  260.0 19.4 %collective-permute-done.42 = bf16[2,96,2048]{2,1,0:T(8,128)(2,1)S(1)} collective-permute-done((bf16[2,96,2048]{2,1,0:T(8,128)(2,1)S(1)}, bf16[2,96,2048]{2,1,0:T(8,128)(2,1)S(1)}, u32[]{:S(2)}, u32[]{:S(2)}) %collective-permute-start.42) | collective-permute-done | bytes 786464 | tf_op jit(solution)/shard_map/ppermute | solution.py:78
  283.3 6.4 shard_map.253.refs_1_
  289.8 5.3 shard_map.255
  300.4 18.0 %collective-permute-done.43.refs_2_ = bf16[4,96,2048]{2,1,0:T(8,128)(2,1)} collective-permute-done((bf16[4,96,2048]{2,1,0:T(8,128)(2,1)}, bf16[4,96,2048]{2,1,0:T(8,128)(2,1)}, u32[]{:S(2)}, u32[]{:S(2)}) %collective-permute-start.43) | collective-permute-done | bytes 1572896 | tf_op jit(solution)/shard_map/ppermute | solution.py:78
  325.0 11.0 %collective-permute-done.38.refs_4_.refs_5_ = bf16[2,96,2048]{2,1,0:T(8,128)(2,1)S(1)} collective-permute-done((bf16[2,96,2048]{2,1,0:T(8,128)(2,1)S(1)}, bf16[2,96,2048]{2,1,0:T(8,128)(2,1)S(1)}, u32[]{:S(2)}, u32[]{:S(2)}) %collective-permute-start.38) | collective-permute-done | bytes 786464 | tf_op jit(solution)/shard_map/ppermute | solution.py:78
  339.8 5.2 shard_map.259
  349.9 12.2 %shard_map.257.refs_6_ = bf16[1024,2048]{1,0:T(8,128)(2,1)} custom-call(bf16[1024,1536]{1,0:T(8,128)(2,1)} %get-tuple-element.160.refs_0_, bf16[4,96,2048]{2,1,0:T(8,128)(2,1)S(1)} %copy-done.3, bf16[4,96,2048]{2,1,0:T(8,128)(2,1)} %copy-done.64, bf16[4,96,2048]{2,1,0:T(8,128)(2,1)} %copy-done.66, ...), custom_call_target="tpu_custom_call" | custom-call | flops 128849016 | bytes 272629 | tf_op jit(solution)/shard_map/pallas_call | solution.py:194
  362.2 13.2 %shard_map.258 = (bf16[1024,2048]{1,0:T(8,128)(2,1)}, bf16[1024,2048]{1,0:T(8,128)(2,1)}) custom-call(bf16[1024,1536]{1,0:T(8,128)(2,1)} %get-tuple-element.160.refs_0_, bf16[4,96,2048]{2,1,0:T(8,128)(2,1)S(1)} %copy-done.5, bf16[4,96,2048]{2,1,0:T(8,128)(2,1)} %copy-done.68, bf16[4,96,2048]{2,1,0:T(8,128)(2,1)} %copy-done.70, ...), custom_call_target="tpu_custom_call" | custom-call | flops 128849016 | bytes 440401 | tf_op jit(solution)/shard_map/pallas_call | solution.py:194
  375.4 12.0 %shard_map.260 = (bf16[4,2,96,2048]{3,2,1,0:T(8,128)(2,1)S(1)}, bf16[4,2,96,2048]{3,2,1,0:T(8,128)(2,1)}) custom-call(bf16[1536,1024]{1,0:T(8,128)(2,1)} %get-tuple-element.164.refs_0_, bf16[1024,2048]{1,0:T(8,128)(2,1)} %get-tuple-element.184.refs_1_.refs_0_), custom_call_target="tpu_custom_call" | custom-call | flops 128849016 | bytes 272629 | tf_op jit(solution)/shard_map/pallas_call | solution.py:382
  387.9 9.8 %shard_map.261 = f32[512,1536]{1,0:T(8,128)} custom-call(s32[1]{0:T(128)} %constant.247.clone.1.half_ref, bf16[1024,2048]{1,0:T(8,128)(2,1)} %get-tuple-element.184.refs_1_.refs_0_, bf16[4,96,2048]{2,1,0:T(8,128)(2,1)} %pad_maximum_fusion.2.refs_1_, bf16[4,96,2048]{2,1,0:T(8,128)(2,1)} %collective-permute-done.43.refs_2_, ...), custom_call_target="tpu_custom_call" | custom-call | flops 64424508 | bytes 230686 | tf_op jit(solution)/shard_map/pallas_call | solution.py:262
  397.7 15.6 %shard_map.262 = (bf16[1024,2048]{1,0:T(8,128)(2,1)}, bf16[1024,2048]{1,0:T(8,128)(2,1)}) custom-call(bf16[1024,1536]{1,0:T(8,128)(2,1)} %get-tuple-element.170.refs_0_, bf16[4,96,2048]{2,1,0:T(8,128)(2,1)} %pad_maximum_fusion.2.refs_1_, bf16[4,96,2048]{2,1,0:T(8,128)(2,1)} %collective-permute-done.43.refs_2_, ...), custom_call_target="tpu_custom_call" | custom-call | flops 128849016 | bytes 524288 | tf_op jit(solution)/shard_map/pallas_call | solution.py:194
  413.3 12.3 %shard_map.263 = (bf16[4,2,96,2048]{3,2,1,0:T(8,128)(2,1)}, bf16[4,2,96,2048]{3,2,1,0:T(8,128)(2,1)}) custom-call(bf16[1536,1024]{1,0:T(8,128)(2,1)} %get-tuple-element.173.refs_0_, bf16[1024,2048]{1,0:T(8,128)(2,1)} %get-tuple-element.174.refs_1_), custom_call_target="tpu_custom_call" | custom-call | flops 128849016 | bytes 272629 | tf_op jit(solution)/shard_map/pallas_call | solution.py:382
  425.6 12.0 %shard_map.264 = (bf16[4,2,96,2048]{3,2,1,0:T(8,128)(2,1)S(1)}, bf16[4,2,96,2048]{3,2,1,0:T(8,128)(2,1)}) custom-call(bf16[1536,1024]{1,0:T(8,128)(2,1)} %get-tuple-element.173.refs_0_, bf16[1024,2048]{1,0:T(8,128)(2,1)} %get-tuple-element.182.refs_1_.refs_0_), custom_call_target="tpu_custom_call" | custom-call | flops 128849016 | bytes 272629 | tf_op jit(solution)/shard_map/pallas_call | solution.py:382
  437.6 18.3 %shard_map.265 = f32[512,1536]{1,0:T(8,128)} custom-call(s32[1]{0:T(128)} %constant.247.clone.1.half_ref, bf16[1024,2048]{1,0:T(8,128)(2,1)} %get-tuple-element.182.refs_1_.refs_0_, bf16[1024,2048]{1,0:T(8,128)(2,1)} %get-tuple-element.174.refs_1_, bf16[4,96,2048]{2,1,0:T(8,128)(2,1)} %copy-done.2, bf16[4,96,2048]{2,1,0:T(8,128)(2,1)} %copy-done.64, ...), custom_call_target="tpu_custom_call" | custom-call | flops 128849016 | bytes 398458 | tf_op jit(solution)/shard_map/pallas_call | solution.py:262
  457.0 4.7 shard_map.266
  463.2 17.2 %shard_map.267.refs_1_ = f32[512,1536]{1,0:T(8,128)} custom-call(s32[1]{0:T(128)} %constant.246.clone.1.half_ref, bf16[1024,2048]{1,0:T(8,128)(2,1)} %get-tuple-element.182.refs_1_.refs_0_, bf16[1024,2048]{1,0:T(8,128)(2,1)} %get-tuple-element.174.refs_1_, bf16[4,96,2048]{2,1,0:T(8,128)(2,1)} %copy-done.2, bf16[4,96,2048]{2,1,0:T(8,128)(2,1)} %copy-done.64, ...), custom_call_target="tpu_custom_call" | custom-call | flops 128849016 | bytes 398458 | tf_op jit(solution)/shard_map/pallas_call | solution.py:262
  480.4 6.8 shard_map.268
  488.3 9.9 %shard_map.269.refs_1_ = f32[512,1536]{1,0:T(8,128)} custom-call(s32[1]{0:T(128)} %constant.246.clone.1.half_ref, bf16[1024,2048]{1,0:T(8,128)(2,1)} %get-tuple-element.184.refs_1_.refs_0_, bf16[4,96,2048]{2,1,0:T(8,128)(2,1)} %pad_maximum_fusion.2.refs_1_, bf16[4,96,2048]{2,1,0:T(8,128)(2,1)} %collective-permute-done.43.refs_2_, ...), custom_call_target="tpu_custom_call" | custom-call | flops 64424508 | bytes 230686 | tf_op jit(solution)/shard_map/pallas_call | solution.py:262
  501.8 9.5 %shard_map.272 = (bf16[1024,768]{1,0:T(8,128)(2,1)}, bf16[1024,768]{1,0:T(8,128)(2,1)}) custom-call(bf16[1024,1536]{1,0:T(8,128)(2,1)} %get-tuple-element.186.refs_0_, bf16[4,96,1536]{2,1,0:T(8,128)(2,1)S(1)} %pad_maximum_fusion.3.refs_1_.refs_5_, bf16[4,96,1536]{2,1,0:T(8,128)(2,1)S(1)} %collective-permute-done.20.refs_2_.refs_6_, ...), custom_call_target="tpu_custom_call" | custom-call | flops 48318384 | bytes 298844 | tf_op jit(solution)/shard_map/pallas_call | solution.py:194
  512.8 12.3 %shard_map.273 = (bf16[4,2,96,1536]{3,2,1,0:T(8,128)(2,1)}, bf16[4,2,96,1536]{3,2,1,0:T(8,128)(2,1)}) custom-call(bf16[1536,1024]{1,0:T(8,128)(2,1)} %get-tuple-element.189.refs_0_, bf16[1536,1024]{1,0:T(8,128)(2,1)} %get-tuple-element.191.refs_1_, bf16[1024,768]{1,0:T(8,128)(2,1)S(1)} %copy-done.31, bf16[1024,768]{1,0:T(8,128)(2,1)S(1)} %copy-done.27), custom_call_target="tpu_custom_call" | custom-call | flops 96636768 | bytes 283115 | tf_op jit(solution)/shard_map/pallas_call | solution.py:382
  527.3 4.6 shard_map.274
  533.5 27.1 %collective-permute-done.53 = bf16[4,96,2048]{2,1,0:T(8,128)(2,1)} collective-permute-done((bf16[4,96,2048]{2,1,0:T(8,128)(2,1)}, bf16[4,96,2048]{2,1,0:T(8,128)(2,1)}, u32[]{:S(2)}, u32[]{:S(2)}) %collective-permute-start.53) | collective-permute-done | bytes 1572896 | tf_op jit(solution)/shard_map/ppermute | solution.py:78
  565.8 4.7 shard_map.275
  570.5 32.9 %shard_map.277 = (bf16[1024,768]{1,0:T(8,128)(2,1)S(1)}, bf16[1024,768]{1,0:T(8,128)(2,1)S(1)}, bf16[1024,768]{1,0:T(8,128)(2,1)}, f32[6,2,1024]{2,1,0:T(2,128)S(1)}, f32[6,1024,2]{2,1,0:T(8,128)}) custom-call(bf16[1024,1536]{1,0:T(8,128)(2,1)} %shard_map.248.q_ref.k_ref, bf16[1024,1536]{1,0:T(8,128)(2,1)} %shard_map.248.q_ref.k_ref, ...), custom_call_target="tpu_custom_call" | custom-call | flops 483183808 | bytes 251658 | tf_op jit(solution)/shard_map/pallas_call | solution.py:749
  611.9 11.9 %shard_map.280 = (bf16[4,2,96,1536]{3,2,1,0:T(8,128)(2,1)}, bf16[4,2,96,1536]{3,2,1,0:T(8,128)(2,1)}) custom-call(bf16[1536,1024]{1,0:T(8,128)(2,1)} %get-tuple-element.189.refs_0_, bf16[1024,768]{1,0:T(8,128)(2,1)S(1)} %get-tuple-element.228.refs_1_, bf16[1024,768]{1,0:T(8,128)(2,1)S(1)} %get-tuple-element.213.refs_2_), custom_call_target="tpu_custom_call" | custom-call | flops 96636768 | bytes 220200 | tf_op jit(solution)/shard_map/pallas_call | solution.py:382
  627.0 7.6 shard_map.282
  635.7 15.0 %shard_map.283 = f32[512,1536]{1,0:T(8,128)} custom-call(s32[1]{0:T(128)} %bitcast.11.half_ref, bf16[1024,768]{1,0:T(8,128)(2,1)} %get-tuple-element.221.refs_2_.refs_0_, bf16[1024,768]{1,0:T(8,128)(2,1)} %copy-done.32, bf16[1024,768]{1,0:T(8,128)(2,1)} %copy-done.33, bf16[1024,768]{1,0:T(8,128)(2,1)} %get-tuple-element.216.refs_1_.refs_3_, ...), custom_call_target="tpu_custom_call" | custom-call | flops 100663296 | bytes 325058 | tf_op jit(solution)/shard_map/pallas_call | solution.py:262
  657.5 15.0 %shard_map.286.refs_1_ = f32[512,1536]{1,0:T(8,128)} custom-call(s32[1]{0:T(128)} %bitcast.half_ref, bf16[1024,768]{1,0:T(8,128)(2,1)} %get-tuple-element.221.refs_2_.refs_0_, bf16[1024,768]{1,0:T(8,128)(2,1)} %copy-done.32, bf16[1024,768]{1,0:T(8,128)(2,1)} %copy-done.33, bf16[1024,768]{1,0:T(8,128)(2,1)} %get-tuple-element.216.refs_1_.refs_3_, ...), custom_call_target="tpu_custom_call" | custom-call | flops 100663296 | bytes 325058 | tf_op jit(solution)/shard_map/pallas_call | solution.py:262
  679.7 4.6 shard_map.270
  691.5 16.0 %collective-permute-done.79 = bf16[1,96,2048]{2,1,0:T(8,128)(2,1)} collective-permute-done((bf16[1,96,2048]{2,1,0:T(8,128)(2,1)}, bf16[1,96,2048]{2,1,0:T(8,128)(2,1)}, u32[]{:S(2)}, u32[]{:S(2)}) %collective-permute-start.79) | collective-permute-done | bytes 393248 | tf_op jit(solution)/shard_map/ppermute | solution.py:78
  710.7 5.0 shard_map.291
  724.2 6.9 shard_map.287
  748.3 6.6 collective-permute-done.77
  757.1 15.2 %collective-permute-done.64 = bf16[2,96,1536]{2,1,0:T(8,128)(2,1)S(1)} collective-permute-done((bf16[2,96,1536]{2,1,0:T(8,128)(2,1)S(1)}, bf16[2,96,1536]{2,1,0:T(8,128)(2,1)S(1)}, u32[]{:S(2)}, u32[]{:S(2)}) %collective-permute-start.64) | collective-permute-done | bytes 589856 | tf_op jit(solution)/shard_map/ppermute | solution.py:78
  772.9 6.7 collective-permute-done.68
  786.6 18.0 %collective-permute-done.69 = bf16[1,96,896]{2,1,0:T(8,128)(2,1)S(1)} collective-permute-done((bf16[1,96,896]{2,1,0:T(8,128)(2,1)S(1)}, bf16[1,96,896]{2,1,0:T(8,128)(2,1)S(1)}, u32[]{:S(2)}, u32[]{:S(2)}) %collective-permute-start.69) | collective-permute-done | bytes 172064 | tf_op jit(solution)/shard_map/ppermute | solution.py:78
  (427 shorter events, 222.6 us)
Async XLA Ops:
  38.0 28.9 %collective-permute-start.12 = (bf16[2,96,1536]{2,1,0:T(8,128)(2,1)S(1)}, bf16[2,96,1536]{2,1,0:T(8,128)(2,1)S(1)}, u32[]{:S(2)}, u32[]{:S(2)}) collective-permute-start(bf16[2,96,1536]{2,1,0:T(8,128)(2,1)S(1)} %pad_maximum_fusion.8.refs_1_.refs_10_.refs_18_), channel_id=1, source_target_pairs={{0,2},{2,0},{4,6},{6,4},{8,10},{10,8},{12,14},{14,12},{16,18},{18,... | collective-permute-start | bytes 1769480 | tf_op jit(solution)/shard_map/ppermute | solution.py:78
  39.6 28.9 %collective-permute-start.14 = (bf16[2,96,1536]{2,1,0:T(8,128)(2,1)S(1)}, bf16[2,96,1536]{2,1,0:T(8,128)(2,1)S(1)}, u32[]{:S(2)}, u32[]{:S(2)}) collective-permute-start(bf16[2,96,1536]{2,1,0:T(8,128)(2,1)S(1)} %collective-permute-done.7.refs_2_.refs_11_.refs_19_), channel_id=1, source_target_pairs={{0,4},{2,6},{4,0},{6,2},{8,12},{10,14},{12,8},{14,10},{16,20},{18,... | collective-permute-start | bytes 1769480 | tf_op jit(solution)/shard_map/ppermute | solution.py:78
  46.5 26.0 %collective-permute-start.16 = (bf16[2,96,1536]{2,1,0:T(8,128)(2,1)S(1)}, bf16[2,96,1536]{2,1,0:T(8,128)(2,1)S(1)}, u32[]{:S(2)}, u32[]{:S(2)}) collective-permute-start(bf16[2,96,1536]{2,1,0:T(8,128)(2,1)S(1)} %pad_maximum_fusion.8.refs_1_.refs_10_.refs_18_), channel_id=1, source_target_pairs={{0,4},{2,6},{4,0},{6,2},{8,12},{10,14},{12,8},{14,10},{16,20},{18,... | collective-permute-start | bytes 1769480 | tf_op jit(solution)/shard_map/ppermute | solution.py:78
  73.4 28.7 %collective-permute-start.11 = (bf16[2,96,1536]{2,1,0:T(8,128)(2,1)}, bf16[2,96,1536]{2,1,0:T(8,128)(2,1)}, u32[]{:S(2)}, u32[]{:S(2)}) collective-permute-start(bf16[2,96,1536]{2,1,0:T(8,128)(2,1)} %pad_maximum_fusion.9), channel_id=1, source_target_pairs={{0,8},{2,10},{4,12},{6,14},{8,0},{10,2},{12,4},{14,6},{16,24},{18,... | collective-permute-start | bytes 1769480 | tf_op jit(solution)/shard_map/ppermute | solution.py:78
  102.0 35.2 %collective-permute-start.5 = (bf16[512,1536]{1,0:T(8,128)(2,1)S(1)}, bf16[512,1536]{1,0:T(8,128)(2,1)S(1)}, u32[]{:S(2)}, u32[]{:S(2)}) collective-permute-start(bf16[512,1536]{1,0:T(8,128)(2,1)S(1)} %shard_map.246.own_ref), channel_id=1, source_target_pairs={{0,1},{1,0},{2,3},{3,2},{4,5},{5,4},{6,7},{7,6},{8,9},{9,8},{10,11... | collective-permute-start | bytes 4718600 | tf_op jit(solution)/shard_map/ppermute | solution.py:51
  108.6 27.0 %collective-permute-start.21 = (bf16[4,96,1536]{2,1,0:T(8,128)(2,1)S(1)}, bf16[4,96,1536]{2,1,0:T(8,128)(2,1)S(1)}, u32[]{:S(2)}, u32[]{:S(2)}) collective-permute-start(bf16[4,96,1536]{2,1,0:T(8,128)(2,1)S(1)} %pad_maximum_fusion.3.refs_1_.refs_5_), channel_id=1, source_target_pairs={{0,4},{2,6},{4,0},{6,2},{8,12},{10,14},{12,8},{14,10},{16,20},{18,... | collective-permute-start | bytes 3538952 | tf_op jit(solution)/shard_map/ppermute | solution.py:78
  128.7 45.3 %collective-permute-start.25 = (bf16[2,96,2048]{2,1,0:T(8,128)(2,1)}, bf16[2,96,2048]{2,1,0:T(8,128)(2,1)}, u32[]{:S(2)}, u32[]{:S(2)}) collective-permute-start(bf16[2,96,2048]{2,1,0:T(8,128)(2,1)} %pad_maximum_fusion.4), channel_id=1, source_target_pairs={{0,8},{2,10},{4,12},{6,14},{8,0},{10,2},{12,4},{14,6},{16,24},{18,... | collective-permute-start | bytes 2359304 | tf_op jit(solution)/shard_map/ppermute | solution.py:78
  129.4 30.4 %collective-permute-start.26 = (bf16[2,96,896]{2,1,0:T(8,128)(2,1)}, bf16[2,96,896]{2,1,0:T(8,128)(2,1)S(1)}, u32[]{:S(2)}, u32[]{:S(2)}) collective-permute-start(bf16[2,96,896]{2,1,0:T(8,128)(2,1)} %slice.103), channel_id=1, source_target_pairs={{0,4},{2,6},{4,0},{6,2},{8,12},{10,14},{12,8},{14,10},{16,20},{18,... | collective-permute-start | bytes 1032200 | tf_op jit(solution)/shard_map/ppermute | solution.py:78
  132.7 27.2 %collective-permute-start.27 = (bf16[2,96,896]{2,1,0:T(8,128)(2,1)}, bf16[2,96,896]{2,1,0:T(8,128)(2,1)}, u32[]{:S(2)}, u32[]{:S(2)}) collective-permute-start(bf16[2,96,896]{2,1,0:T(8,128)(2,1)} %slice.104), channel_id=1, source_target_pairs={{0,2},{2,0},{4,6},{6,4},{8,10},{10,8},{12,14},{14,12},{16,18},{18,... | collective-permute-start | bytes 1032200 | tf_op jit(solution)/shard_map/ppermute | solution.py:78
  135.6 68.2 %collective-permute-start.22 = (bf16[2,96,1536]{2,1,0:T(8,128)(2,1)}, bf16[2,96,1536]{2,1,0:T(8,128)(2,1)}, u32[]{:S(2)}, u32[]{:S(2)}) collective-permute-start(bf16[2,96,1536]{2,1,0:T(8,128)(2,1)} %slice.101), channel_id=1, source_target_pairs={{0,4},{2,6},{4,0},{6,2},{8,12},{10,14},{12,8},{14,10},{16,20},{18,... | collective-permute-start | bytes 1769480 | tf_op jit(solution)/shard_map/ppermute | solution.py:78
  138.3 65.4 %collective-permute-start.23 = (bf16[2,96,1536]{2,1,0:T(8,128)(2,1)}, bf16[2,96,1536]{2,1,0:T(8,128)(2,1)}, u32[]{:S(2)}, u32[]{:S(2)}) collective-permute-start(bf16[2,96,1536]{2,1,0:T(8,128)(2,1)} %slice.102), channel_id=1, source_target_pairs={{0,2},{2,0},{4,6},{6,4},{8,10},{10,8},{12,14},{14,12},{16,18},{18,... | collective-permute-start | bytes 1769480 | tf_op jit(solution)/shard_map/ppermute | solution.py:78
  173.9 45.8 %collective-permute-start.30 = (bf16[1,96,2048]{2,1,0:T(8,128)(2,1)S(1)}, bf16[1,96,2048]{2,1,0:T(8,128)(2,1)S(1)}, u32[]{:S(2)}, u32[]{:S(2)}) collective-permute-start(bf16[1,96,2048]{2,1,0:T(8,128)(2,1)S(1)} %copy-done.73), channel_id=1, source_target_pairs={{0,16},{2,18},{4,20},{6,22},{8,24},{10,26},{12,28},{14,30},{16,0},... | collective-permute-start | bytes 1179656 | tf_op jit(solution)/shard_map/ppermute | solution.py:78
  179.5 60.7 %collective-permute-start.32 = (bf16[4,96,2048]{2,1,0:T(8,128)(2,1)S(1)}, bf16[4,96,2048]{2,1,0:T(8,128)(2,1)S(1)}, u32[]{:S(2)}, u32[]{:S(2)}) collective-permute-start(bf16[4,96,2048]{2,1,0:T(8,128)(2,1)S(1)} %pad_maximum_fusion.refs_1_.refs_2_), channel_id=1, source_target_pairs={{0,2},{2,0},{4,6},{6,4},{8,10},{10,8},{12,14},{14,12},{16,18},{18,... | collective-permute-start | bytes 4718600 | tf_op jit(solution)/shard_map/ppermute | solution.py:78
  180.6 59.6 %collective-permute-start.33 = (bf16[4,96,2048]{2,1,0:T(8,128)(2,1)S(1)}, bf16[4,96,2048]{2,1,0:T(8,128)(2,1)S(1)}, u32[]{:S(2)}, u32[]{:S(2)}) collective-permute-start(bf16[4,96,2048]{2,1,0:T(8,128)(2,1)S(1)} %pad_maximum_fusion.refs_1_.refs_2_), channel_id=1, source_target_pairs={{0,4},{2,6},{4,0},{6,2},{8,12},{10,14},{12,8},{14,10},{16,20},{18,... | collective-permute-start | bytes 4718600 | tf_op jit(solution)/shard_map/ppermute | solution.py:78
  219.6 70.1 %collective-permute-start.28 = (f32[512,1536]{1,0:T(8,128)}, f32[512,1536]{1,0:T(8,128)}, u32[]{:S(2)}, u32[]{:S(2)}) collective-permute-start(f32[512,1536]{1,0:T(8,128)} %shard_map.254), channel_id=1, source_target_pairs={{0,1},{1,0},{2,3},{3,2},{4,5},{5,4},{6,7},{7,6},{8,9},{9,8},{10,11... | collective-permute-start | bytes 9437192 | tf_op jit(solution)/shard_map/ppermute | solution.py:51
  240.2 40.5 %collective-permute-start.34 = (bf16[4,96,2048]{2,1,0:T(8,128)(2,1)S(1)}, bf16[4,96,2048]{2,1,0:T(8,128)(2,1)S(1)}, u32[]{:S(2)}, u32[]{:S(2)}) collective-permute-start(bf16[4,96,2048]{2,1,0:T(8,128)(2,1)S(1)} %pad_maximum_fusion.1.refs_1_.refs_7_), channel_id=1, source_target_pairs={{0,2},{2,0},{4,6},{6,4},{8,10},{10,8},{12,14},{14,12},{16,18},{18,... | collective-permute-start | bytes 4718600 | tf_op jit(solution)/shard_map/ppermute | solution.py:78
  241.2 39.5 %collective-permute-start.35 = (bf16[4,96,2048]{2,1,0:T(8,128)(2,1)S(1)}, bf16[4,96,2048]{2,1,0:T(8,128)(2,1)S(1)}, u32[]{:S(2)}, u32[]{:S(2)}) collective-permute-start(bf16[4,96,2048]{2,1,0:T(8,128)(2,1)S(1)} %pad_maximum_fusion.1.refs_1_.refs_7_), channel_id=1, source_target_pairs={{0,4},{2,6},{4,0},{6,2},{8,12},{10,14},{12,8},{14,10},{16,20},{18,... | collective-permute-start | bytes 4718600 | tf_op jit(solution)/shard_map/ppermute | solution.py:78
  259.9 37.5 %collective-permute-start.40 = (bf16[512,1536]{1,0:T(8,128)(2,1)}, bf16[512,1536]{1,0:T(8,128)(2,1)}, u32[]{:S(2)}, u32[]{:S(2)}) collective-permute-start(bf16[512,1536]{1,0:T(8,128)(2,1)} %refs_3_.1), channel_id=1, source_target_pairs={{0,1},{1,0},{2,3},{3,2},{4,5},{5,4},{6,7},{7,6},{8,9},{9,8},{10,11... | collective-permute-start | bytes 4718600 | tf_op jit(solution)/shard_map/ppermute | solution.py:51
  280.7 37.7 %collective-permute-start.43 = (bf16[4,96,2048]{2,1,0:T(8,128)(2,1)}, bf16[4,96,2048]{2,1,0:T(8,128)(2,1)}, u32[]{:S(2)}, u32[]{:S(2)}) collective-permute-start(bf16[4,96,2048]{2,1,0:T(8,128)(2,1)} %pad_maximum_fusion.2.refs_1_), channel_id=1, source_target_pairs={{0,2},{2,0},{4,6},{6,4},{8,10},{10,8},{12,14},{14,12},{16,18},{18,... | collective-permute-start | bytes 4718600 | tf_op jit(solution)/shard_map/ppermute | solution.py:78
  281.7 38.2 %collective-permute-start.44 = (bf16[4,96,2048]{2,1,0:T(8,128)(2,1)}, bf16[4,96,2048]{2,1,0:T(8,128)(2,1)}, u32[]{:S(2)}, u32[]{:S(2)}) collective-permute-start(bf16[4,96,2048]{2,1,0:T(8,128)(2,1)} %pad_maximum_fusion.2.refs_1_), channel_id=1, source_target_pairs={{0,4},{2,6},{4,0},{6,2},{8,12},{10,14},{12,8},{14,10},{16,20},{18,... | collective-permute-start | bytes 4718600 | tf_op jit(solution)/shard_map/ppermute | solution.py:78
  295.0 42.6 %collective-permute-start.29 = (bf16[512,1536]{1,0:T(8,128)(2,1)S(1)}, bf16[512,1536]{1,0:T(8,128)(2,1)S(1)}, u32[]{:S(2)}, u32[]{:S(2)}) collective-permute-start(bf16[512,1536]{1,0:T(8,128)(2,1)S(1)} %get-tuple-element.159.own_ref), channel_id=1, source_target_pairs={{0,1},{1,0},{2,3},{3,2},{4,5},{5,4},{6,7},{7,6},{8,9},{9,8},{10,11... | collective-permute-start | bytes 4718600 | tf_op jit(solution)/shard_map/ppermute | solution.py:51
  295.1 40.9 %collective-permute-start.38 = (bf16[2,96,2048]{2,1,0:T(8,128)(2,1)S(1)}, bf16[2,96,2048]{2,1,0:T(8,128)(2,1)S(1)}, u32[]{:S(2)}, u32[]{:S(2)}) collective-permute-start(bf16[2,96,2048]{2,1,0:T(8,128)(2,1)S(1)} %slice.108), channel_id=1, source_target_pairs={{0,4},{2,6},{4,0},{6,2},{8,12},{10,14},{12,8},{14,10},{16,20},{18,... | collective-permute-start | bytes 2359304 | tf_op jit(solution)/shard_map/ppermute | solution.py:78
  297.4 52.5 %collective-permute-start.39 = (bf16[2,96,2048]{2,1,0:T(8,128)(2,1)}, bf16[2,96,2048]{2,1,0:T(8,128)(2,1)S(1)}, u32[]{:S(2)}, u32[]{:S(2)}) collective-permute-start(bf16[2,96,2048]{2,1,0:T(8,128)(2,1)} %slice.109), channel_id=1, source_target_pairs={{0,2},{2,0},{4,6},{6,4},{8,10},{10,8},{12,14},{14,12},{16,18},{18,... | collective-permute-start | bytes 2359304 | tf_op jit(solution)/shard_map/ppermute | solution.py:78
  318.4 43.8 %collective-permute-start.36 = (bf16[2,96,2048]{2,1,0:T(8,128)(2,1)}, bf16[2,96,2048]{2,1,0:T(8,128)(2,1)S(1)}, u32[]{:S(2)}, u32[]{:S(2)}) collective-permute-start(bf16[2,96,2048]{2,1,0:T(8,128)(2,1)} %slice.106), channel_id=1, source_target_pairs={{0,4},{2,6},{4,0},{6,2},{8,12},{10,14},{12,8},{14,10},{16,20},{18,... | collective-permute-start | bytes 2359304 | tf_op jit(solution)/shard_map/ppermute | solution.py:78
  319.9 42.3 %collective-permute-start.37 = (bf16[2,96,2048]{2,1,0:T(8,128)(2,1)}, bf16[2,96,2048]{2,1,0:T(8,128)(2,1)S(1)}, u32[]{:S(2)}, u32[]{:S(2)}) collective-permute-start(bf16[2,96,2048]{2,1,0:T(8,128)(2,1)} %slice.107), channel_id=1, source_target_pairs={{0,2},{2,0},{4,6},{6,4},{8,10},{10,8},{12,14},{14,12},{16,18},{18,... | collective-permute-start | bytes 2359304 | tf_op jit(solution)/shard_map/ppermute | solution.py:78
  336.1 51.8 %collective-permute-start.45 = (bf16[2,96,2048]{2,1,0:T(8,128)(2,1)}, bf16[2,96,2048]{2,1,0:T(8,128)(2,1)S(1)}, u32[]{:S(2)}, u32[]{:S(2)}) collective-permute-start(bf16[2,96,2048]{2,1,0:T(8,128)(2,1)} %slice.110), channel_id=1, source_target_pairs={{0,4},{2,6},{4,0},{6,2},{8,12},{10,14},{12,8},{14,10},{16,20},{18,... | collective-permute-start | bytes 2359304 | tf_op jit(solution)/shard_map/ppermute | solution.py:78
  338.7 49.1 %collective-permute-start.46 = (bf16[2,96,2048]{2,1,0:T(8,128)(2,1)}, bf16[2,96,2048]{2,1,0:T(8,128)(2,1)S(1)}, u32[]{:S(2)}, u32[]{:S(2)}) collective-permute-start(bf16[2,96,2048]{2,1,0:T(8,128)(2,1)} %slice.111), channel_id=1, source_target_pairs={{0,2},{2,0},{4,6},{6,4},{8,10},{10,8},{12,14},{14,12},{16,18},{18,... | collective-permute-start | bytes 2359304 | tf_op jit(solution)/shard_map/ppermute | solution.py:78
  387.4 69.6 %collective-permute-start.47 = (bf16[4,2,96,2048]{3,2,1,0:T(8,128)(2,1)S(1)}, bf16[4,2,96,2048]{3,2,1,0:T(8,128)(2,1)}, u32[]{:S(2)}, u32[]{:S(2)}) collective-permute-start(bf16[4,2,96,2048]{3,2,1,0:T(8,128)(2,1)S(1)} %get-tuple-element.165), channel_id=1, source_target_pairs={{0,4},{2,6},{4,0},{6,2},{8,12},{10,14},{12,8},{14,10},{16,20},{18,... | collective-permute-start | bytes 9437192 | tf_op jit(solution)/shard_map/ppermute | solution.py:78
  456.0 71.3 %collective-permute-start.51 = (bf16[4,2,96,2048]{3,2,1,0:T(8,128)(2,1)}, bf16[4,2,96,2048]{3,2,1,0:T(8,128)(2,1)}, u32[]{:S(2)}, u32[]{:S(2)}) collective-permute-start(bf16[4,2,96,2048]{3,2,1,0:T(8,128)(2,1)} %get-tuple-element.175), channel_id=1, source_target_pairs={{0,2},{2,0},{4,6},{6,4},{8,10},{10,8},{12,14},{14,12},{16,18},{18,... | collective-permute-start | bytes 9437192 | tf_op jit(solution)/shard_map/ppermute | solution.py:78
  461.7 104.1 %collective-permute-start.52 = (bf16[4,2,96,2048]{3,2,1,0:T(8,128)(2,1)}, bf16[4,2,96,2048]{3,2,1,0:T(8,128)(2,1)}, u32[]{:S(2)}, u32[]{:S(2)}) collective-permute-start(bf16[4,2,96,2048]{3,2,1,0:T(8,128)(2,1)} %copy-done.60), channel_id=1, source_target_pairs={{0,4},{2,6},{4,0},{6,2},{8,12},{10,14},{12,8},{14,10},{16,20},{18,... | collective-permute-start | bytes 9437192 | tf_op jit(solution)/shard_map/ppermute | solution.py:78
  487.2 73.4 %collective-permute-start.53 = (bf16[4,96,2048]{2,1,0:T(8,128)(2,1)}, bf16[4,96,2048]{2,1,0:T(8,128)(2,1)}, u32[]{:S(2)}, u32[]{:S(2)}) collective-permute-start(bf16[4,96,2048]{2,1,0:T(8,128)(2,1)} %get-tuple-element.181), channel_id=1, source_target_pairs={{0,2},{2,0},{4,6},{6,4},{8,10},{10,8},{12,14},{14,12},{16,18},{18,... | collective-permute-start | bytes 4718600 | tf_op jit(solution)/shard_map/ppermute | solution.py:78
  531.9 71.4 %collective-permute-start.54 = (bf16[4,96,2048]{2,1,0:T(8,128)(2,1)}, bf16[4,96,2048]{2,1,0:T(8,128)(2,1)}, u32[]{:S(2)}, u32[]{:S(2)}) collective-permute-start(bf16[4,96,2048]{2,1,0:T(8,128)(2,1)} %get-tuple-element.195), channel_id=1, source_target_pairs={{0,4},{2,6},{4,0},{6,2},{8,12},{10,14},{12,8},{14,10},{16,20},{18,... | collective-permute-start | bytes 4718600 | tf_op jit(solution)/shard_map/ppermute | solution.py:78
  533.5 146.1 %collective-permute-start.49 = (f32[512,1536]{1,0:T(8,128)}, f32[512,1536]{1,0:T(8,128)}, u32[]{:S(2)}, u32[]{:S(2)}) collective-permute-start(f32[512,1536]{1,0:T(8,128)} %shard_map.261), channel_id=1, source_target_pairs={{0,1},{1,0},{2,3},{3,2},{4,5},{5,4},{6,7},{7,6},{8,9},{9,8},{10,11... | collective-permute-start | bytes 9437192 | tf_op jit(solution)/shard_map/ppermute | solution.py:51
  564.1 45.5 %collective-permute-start.55 = (bf16[2,96,2048]{2,1,0:T(8,128)(2,1)}, bf16[2,96,2048]{2,1,0:T(8,128)(2,1)S(1)}, u32[]{:S(2)}, u32[]{:S(2)}) collective-permute-start(bf16[2,96,2048]{2,1,0:T(8,128)(2,1)} %get-tuple-element.202), channel_id=1, source_target_pairs={{0,8},{2,10},{4,12},{6,14},{8,0},{10,2},{12,4},{14,6},{16,24},{18,... | collective-permute-start | bytes 2359304 | tf_op jit(solution)/shard_map/ppermute | solution.py:78
  564.9 107.7 %collective-permute-start.60 = (bf16[4,2,96,1536]{3,2,1,0:T(8,128)(2,1)}, bf16[4,2,96,1536]{3,2,1,0:T(8,128)(2,1)}, u32[]{:S(2)}, u32[]{:S(2)}) collective-permute-start(bf16[4,2,96,1536]{3,2,1,0:T(8,128)(2,1)} %get-tuple-element.192), channel_id=1, source_target_pairs={{0,2},{2,0},{4,6},{6,4},{8,10},{10,8},{12,14},{14,12},{16,18},{18,... | collective-permute-start | bytes 7077896 | tf_op jit(solution)/shard_map/ppermute | solution.py:78
  607.2 43.5 %collective-permute-start.56 = (bf16[2,96,2048]{2,1,0:T(8,128)(2,1)}, bf16[2,96,2048]{2,1,0:T(8,128)(2,1)S(1)}, u32[]{:S(2)}, u32[]{:S(2)}) collective-permute-start(bf16[2,96,2048]{2,1,0:T(8,128)(2,1)} %get-tuple-element.208), channel_id=1, source_target_pairs={{0,8},{2,10},{4,12},{6,14},{8,0},{10,2},{12,4},{14,6},{16,24},{18,... | collective-permute-start | bytes 2359304 | tf_op jit(solution)/shard_map/ppermute | solution.py:78
  608.5 43.0 %collective-permute-start.57 = (bf16[4,96,2048]{2,1,0:T(8,128)(2,1)}, bf16[4,96,2048]{2,1,0:T(8,128)(2,1)}, u32[]{:S(2)}, u32[]{:S(2)}) collective-permute-start(bf16[4,96,2048]{2,1,0:T(8,128)(2,1)} %get-tuple-element.199), channel_id=1, source_target_pairs={{0,2},{2,0},{4,6},{6,4},{8,10},{10,8},{12,14},{14,12},{16,18},{18,... | collective-permute-start | bytes 4718600 | tf_op jit(solution)/shard_map/ppermute | solution.py:78
  623.8 60.6 %collective-permute-start.59 = (bf16[4,2,96,1536]{3,2,1,0:T(8,128)(2,1)}, bf16[4,2,96,1536]{3,2,1,0:T(8,128)(2,1)}, u32[]{:S(2)}, u32[]{:S(2)}) collective-permute-start(bf16[4,2,96,1536]{3,2,1,0:T(8,128)(2,1)} %get-tuple-element.214), channel_id=1, source_target_pairs={{0,4},{2,6},{4,0},{6,2},{8,12},{10,14},{12,8},{14,10},{16,20},{18,... | collective-permute-start | bytes 7077896 | tf_op jit(solution)/shard_map/ppermute | solution.py:78
  650.8 73.5 %collective-permute-start.58 = (f32[512,1536]{1,0:T(8,128)}, f32[512,1536]{1,0:T(8,128)}, u32[]{:S(2)}, u32[]{:S(2)}) collective-permute-start(f32[512,1536]{1,0:T(8,128)} %shard_map.283), channel_id=1, source_target_pairs={{0,1},{1,0},{2,3},{3,2},{4,5},{5,4},{6,7},{7,6},{8,9},{9,8},{10,11... | collective-permute-start | bytes 9437192 | tf_op jit(solution)/shard_map/ppermute | solution.py:51
  651.4 56.2 %collective-permute-start.63 = (bf16[4,2,96,896]{3,2,1,0:T(8,128)(2,1)}, bf16[4,2,96,896]{3,2,1,0:T(8,128)(2,1)}, u32[]{:S(2)}, u32[]{:S(2)}) collective-permute-start(bf16[4,2,96,896]{3,2,1,0:T(8,128)(2,1)} %get-tuple-element.220), channel_id=1, source_target_pairs={{0,2},{2,0},{4,6},{6,4},{8,10},{10,8},{12,14},{14,12},{16,18},{18,... | collective-permute-start | bytes 4128776 | tf_op jit(solution)/shard_map/ppermute | solution.py:78
  678.1 38.6 %collective-permute-start.62 = (bf16[4,96,1536]{2,1,0:T(8,128)(2,1)}, bf16[4,96,1536]{2,1,0:T(8,128)(2,1)}, u32[]{:S(2)}, u32[]{:S(2)}) collective-permute-start(bf16[4,96,1536]{2,1,0:T(8,128)(2,1)} %get-tuple-element.234), channel_id=1, source_target_pairs={{0,4},{2,6},{4,0},{6,2},{8,12},{10,14},{12,8},{14,10},{16,20},{18,... | collective-permute-start | bytes 3538952 | tf_op jit(solution)/shard_map/ppermute | solution.py:78
  679.6 28.0 %collective-permute-start.79 = (bf16[1,96,2048]{2,1,0:T(8,128)(2,1)}, bf16[1,96,2048]{2,1,0:T(8,128)(2,1)}, u32[]{:S(2)}, u32[]{:S(2)}) collective-permute-start(bf16[1,96,2048]{2,1,0:T(8,128)(2,1)} %get-tuple-element.211), channel_id=1, source_target_pairs={{0,16},{2,18},{4,20},{6,22},{8,24},{10,26},{12,28},{14,30},{16,0},... | collective-permute-start | bytes 1179656 | tf_op jit(solution)/shard_map/ppermute | solution.py:78
  684.4 36.8 %collective-permute-start.78 = (bf16[1,96,2048]{2,1,0:T(8,128)(2,1)S(1)}, bf16[1,96,2048]{2,1,0:T(8,128)(2,1)S(1)}, u32[]{:S(2)}, u32[]{:S(2)}) collective-permute-start(bf16[1,96,2048]{2,1,0:T(8,128)(2,1)S(1)} %copy-done.62), channel_id=1, source_target_pairs={{0,16},{2,18},{4,20},{6,22},{8,24},{10,26},{12,28},{14,30},{16,0},... | collective-permute-start | bytes 1179656 | tf_op jit(solution)/shard_map/ppermute | solution.py:78
  707.6 27.2 %collective-permute-start.61 = (bf16[4,96,1536]{2,1,0:T(8,128)(2,1)}, bf16[4,96,1536]{2,1,0:T(8,128)(2,1)S(1)}, u32[]{:S(2)}, u32[]{:S(2)}) collective-permute-start(bf16[4,96,1536]{2,1,0:T(8,128)(2,1)} %get-tuple-element.237), channel_id=1, source_target_pairs={{0,2},{2,0},{4,6},{6,4},{8,10},{10,8},{12,14},{14,12},{16,18},{18,... | collective-permute-start | bytes 3538952 | tf_op jit(solution)/shard_map/ppermute | solution.py:78
  735.4 36.9 %collective-permute-start.64 = (bf16[2,96,1536]{2,1,0:T(8,128)(2,1)S(1)}, bf16[2,96,1536]{2,1,0:T(8,128)(2,1)S(1)}, u32[]{:S(2)}, u32[]{:S(2)}) collective-permute-start(bf16[2,96,1536]{2,1,0:T(8,128)(2,1)S(1)} %get-tuple-element.246), channel_id=1, source_target_pairs={{0,8},{2,10},{4,12},{6,14},{8,0},{10,2},{12,4},{14,6},{16,24},{18,... | collective-permute-start | bytes 1769480 | tf_op jit(solution)/shard_map/ppermute | solution.py:78
  742.5 37.1 %collective-permute-start.68 = (bf16[2,96,896]{2,1,0:T(8,128)(2,1)S(1)}, bf16[2,96,896]{2,1,0:T(8,128)(2,1)S(1)}, u32[]{:S(2)}, u32[]{:S(2)}) collective-permute-start(bf16[2,96,896]{2,1,0:T(8,128)(2,1)S(1)} %get-tuple-element.253), channel_id=1, source_target_pairs={{0,8},{2,10},{4,12},{6,14},{8,0},{10,2},{12,4},{14,6},{16,24},{18,... | collective-permute-start | bytes 1032200 | tf_op jit(solution)/shard_map/ppermute | solution.py:78
  747.5 25.3 %collective-permute-start.71 = (bf16[1,96,1536]{2,1,0:T(8,128)(2,1)S(1)}, bf16[1,96,1536]{2,1,0:T(8,128)(2,1)S(1)}, u32[]{:S(2)}, u32[]{:S(2)}) collective-permute-start(bf16[1,96,1536]{2,1,0:T(8,128)(2,1)S(1)} %get-tuple-element.265), channel_id=1, source_target_pairs={{0,16},{2,18},{4,20},{6,22},{8,24},{10,26},{12,28},{14,30},{16,0},... | collective-permute-start | bytes 884744 | tf_op jit(solution)/shard_map/ppermute | solution.py:78
  781.1 25.0 %collective-permute-start.67 = (bf16[1,96,1536]{2,1,0:T(8,128)(2,1)S(1)}, bf16[1,96,1536]{2,1,0:T(8,128)(2,1)S(1)}, u32[]{:S(2)}, u32[]{:S(2)}) collective-permute-start(bf16[1,96,1536]{2,1,0:T(8,128)(2,1)S(1)} %get-tuple-element.257), channel_id=1, source_target_pairs={{0,16},{2,18},{4,20},{6,22},{8,24},{10,26},{12,28},{14,30},{16,0},... | collective-permute-start | bytes 884744 | tf_op jit(solution)/shard_map/ppermute | solution.py:78
  (123 other events, 2263.8 us)

commit v3 on v2

--- a/solution.py
+++ b/solution.py
@@ -208,18 +208,26 @@
     )(left, *arrays, *extras)
 
 
-def multiply_back(terms, half, tiles=4):
+def multiply_back(terms, half, kind=jnp.float32, parts=1, tiles=4):
     grid, rows = terms[0][1].grid, terms[0][1].rows
     length = terms[0][0].shape[0] // 2
     if not terms[0][1].in_kernel:
-        return sum(
+        total = sum(
             second_contract(
                 lax.dynamic_slice_in_dim(left, half * length, length, 0), weight.assembled()
             )
             for left, weight in terms
         )
+        return jnp.split(total.astype(kind), parts, axis=1)
     depth = grid.count * rows
     tile, share = depth // tiles, grid.count // tiles
+    run = tiles // parts
+
+    def part_spec(number):
+        return pl.BlockSpec(
+            (length, tile), lambda step, which: (0, jnp.clip(step - number * run, 0, run - 1))
+        )
+
     sources, counts = [], []
     for _, weight in terms:
         sources = sources + weight.arrays()
@@ -228,7 +236,8 @@
     def body(half_ref, *refs):
         left_refs, refs = refs[: len(terms)], refs[len(terms) :]
         piece_refs, refs = refs[: len(sources)], refs[len(sources) :]
-        out_ref, held, sems = refs[0], refs[1 : 1 + len(terms)], refs[1 + len(terms) :]
+        out_refs, refs = refs[:parts], refs[parts:]
+        held, sems = refs[: len(terms)], refs[len(terms) :]
         step = pl.program_id(0)
 
         def target(number):
@@ -255,7 +264,11 @@
             found = held[number][pl.ds(pl.multiple_of(step * tile, 16), tile), :]
             product = second_contract(left_refs[number][...], found)
             total = product if total is None else total + product
-        out_ref[...] = total
+        for number, out_ref in enumerate(out_refs):
+
+            @pl.when(step // run == number)
+            def _():
+                out_ref[...] = total.astype(kind)
 
     size = length * depth * 4 + sum(l.size + depth * w.width * 2 for l, w in terms)
     flops = sum(2 * length * depth * w.width for _, w in terms)
@@ -269,31 +282,44 @@
                 for left, _ in terms
             ]
             + [pl.BlockSpec(memory_space=pl.ANY)] * len(sources),
-            out_specs=pl.BlockSpec((length, tile), lambda step, which: (0, step)),
+            out_specs=[part_spec(number) for number in range(parts)],
             scratch_shapes=[pltpu.VMEM((depth, w.width), jnp.bfloat16) for _, w in terms]
             + [pltpu.SemaphoreType.DMA((1, grid.count)) for _ in terms],
         ),
-        out_shape=jax.ShapeDtypeStruct((length, depth), jnp.float32),
+        out_shape=[jax.ShapeDtypeStruct((length, depth // parts), kind)] * parts,
         cost_estimate=small_cost(flops, size),
         compiler_params=pltpu.CompilerParams(vmem_limit_bytes=VMEM_LIMIT),
     )(jnp.reshape(half, (1,)).astype(jnp.int32), *[left for left, _ in terms], *sources)
 
 
 class Gather:
-    def __init__(self, grid, shard, fine=False, after_line=(), after_plane=()):
-        near, codes = tie(shard[None], *after_line), [0]
+    def __init__(self, grid, shard, *after):
+        near, codes = tie(shard[None], *after), [0]
         for number in reversed(grid.line_bits[1:]):
             found = grid.swap(near, number)
             near = jnp.concatenate([near, found], axis=0)
-            codes = codes + [code ^ (1 << number) for code in codes]
-        last = grid.line_bits[0]
-        far = grid.swap(near, last)
-        far_codes = [code ^ (1 << last) for code in codes]
-
-        def moved(found, plane):
-            return [code ^ plane for code in found]
-
-        half = len(codes)
+            codes = codes + self.moved(codes, 1 << number)
+        self.grid, self.near, self.codes = grid, near, codes
+
+    def moved(self, found, plane):
+        return [code ^ plane for code in found]
+
+    def line_end(self, *after):
+        last = self.grid.line_bits[0]
+        self.near = tie(self.near, *after)
+        self.far = self.grid.swap(self.near, last)
+        self.far_codes = self.moved(self.codes, 1 << last)
+        return self
+
+    def plane(self, *after, fine=False):
+        grid, near, far, codes, far_codes = (
+            self.grid,
+            self.near,
+            self.far,
+            self.codes,
+            self.far_codes,
+        )
+        moved, both, half = self.moved, self.codes + self.far_codes, len(self.codes)
         if fine:
             near_x, near_y = grid.swap(near, 0), grid.swap(near, 1)
             far_x, far_y = grid.swap(far, 0), grid.swap(far, 1)
@@ -305,22 +331,23 @@
                 (moved(far_codes, 1), far_x),
                 (moved(far_codes, 2), far_y),
             ]
-            self.sides_done = (near_x, near_y, far_x, far_y)
+            received = (near_y, far_x)
         else:
-            block = tie(jnp.concatenate([near, far], axis=0), *after_plane)
+            block = tie(jnp.concatenate([near, far], axis=0), *after)
             side_x, side_y = grid.swap(block, 0), grid.swap(block, 1)
             near_x, far_y = side_x[:half], side_y[half:]
-            both = codes + far_codes
             sides = [(both, block), (moved(both, 1), side_x), (moved(both, 2), side_y)]
-            self.sides_done = (side_x, side_y)
+            received = ()
+            self.block = block
         near_corner, far_corner = grid.swap(near_x, 1), grid.swap(far_y, 0)
-        self.line_done, self.plane_done = (far,), (near_corner, far_corner, *self.sides_done)
-        self.ready = far if fine else block
+        self.corners = (near_corner, far_corner, *received)
+        self.corner_parts = (near_x, far_y)
         corners = [(moved(codes, 3), near_corner), (moved(far_codes, 3), far_corner)]
         self.weight = Weight(grid, sides + corners)
-
-
-def gradient_parts(grid, pairs, tiles, number):
+        return self
+
+
+def gradient_parts(grid, pairs, tiles, form):
     depth, length = pairs[0][0].shape
     rows, line = depth // grid.count, grid.count // 4
     width = sum(right.shape[1] for _, right in pairs)
@@ -338,7 +365,7 @@
     def body(*refs):
         left_refs, refs = refs[: len(lefts)], refs[len(lefts) :]
         right_refs, refs = refs[: len(pairs)], refs[len(pairs) :]
-        away, own, total = refs
+        outs, total = refs[:-1], refs[-1]
         step = pl.program_id(0)
         if tiles == 1:
             for place in range(len(pairs)):
@@ -357,17 +384,30 @@
                 def _():
                     total[...] = matmul(left_refs[which[place]][...], right_refs[place][...])
 
-        here = (lax.axis_index("dp") >> number) & 1
+        index = lax.axis_index("dp")
 
         def block(place):
             return lower(total[pl.ds(pl.multiple_of(place * rows, 8), rows), :])
 
-        other = 3 - (1 << number)
-        for place in range(line):
-            for side in range(2):
-                base = place * 4 + side * other
-                away[place, side] = block(base + ((1 - here) << number))
-                own[place, side] = block(base + (here << number))
+        if form == "line":
+            here = (index >> 2) & 1
+            for place in range(half):
+                for plane in range(4):
+                    outs[0][place, plane] = block((2 * place + 1 - here) * 4 + plane)
+                    outs[1][place, plane] = block((2 * place + here) * 4 + plane)
+            return
+
+        for number, first, count, away, own in (
+            [(form, 0, line, *outs)]
+            if form in (0, 1)
+            else [(1, 0, half, outs[0], outs[2]), (0, half, half, outs[1], outs[3])]
+        ):
+            here = (index >> number) & 1
+            for place in range(count):
+                for side in range(2):
+                    base = (first + place) * 4 + side * (3 - (1 << number))
+                    away[place, side] = block(base + ((1 - here) << number))
+                    own[place, side] = block(base + (here << number))
 
     def right_spec(place):
         columns = pairs[place][1].shape[1]
@@ -376,16 +416,18 @@
         low, count = starts[place] // tile, columns // tile
         return pl.BlockSpec((length, tile), lambda step: (0, jnp.clip(step - low, 0, count - 1)))
 
-    out = jax.ShapeDtypeStruct((line, 2, rows, width), jnp.bfloat16)
-    out_spec = pl.BlockSpec((line, 2, rows, tile), lambda step: (0, 0, 0, step))
+    half = line // 2
+    cut, parts = {"line": ((half, 4), 2), "halves": ((half, 2), 4)}.get(form, ((line, 2), 2))
+    out = jax.ShapeDtypeStruct((*cut, rows, width), jnp.bfloat16)
+    out_spec = pl.BlockSpec((*cut, rows, tile), lambda step: (0, 0, 0, step))
     size = depth * width * 2 + sum(l.size * 2 for l in lefts) + sum(r.size * 2 for _, r in pairs)
     return pl.pallas_call(
         body,
         grid=(tiles,),
         in_specs=[pl.BlockSpec((depth, length), lambda step: (0, 0))] * len(lefts)
         + [right_spec(place) for place in range(len(pairs))],
-        out_specs=[out_spec] * 2,
-        out_shape=[out] * 2,
+        out_specs=[out_spec] * parts,
+        out_shape=[out] * parts,
         scratch_shapes=[pltpu.VMEM((depth, tile), jnp.float32)],
         cost_estimate=small_cost(2 * depth * length * width, size),
         compiler_params=pltpu.CompilerParams(vmem_limit_bytes=VMEM_LIMIT),
@@ -396,19 +438,31 @@
     return lax.dynamic_index_in_dim(array, place, axis, keepdims=False)
 
 
-def cut_parts(grid, array, number):
+def cut_parts(grid, array, form):
     line, rows = grid.count // 4, array.shape[0] // grid.count
     blocks = array.reshape(line, 2, 2, rows, array.shape[1])
-    here, axis = grid.bit(number), 2 - number
-    return pick(blocks, axis, 1 - here), pick(blocks, axis, here)
-
-
-def weight_gradient(grid, pairs, tiles, number):
+
+    def cut(blocks, number):
+        here, axis = grid.bit(number), 2 - number
+        return pick(blocks, axis, 1 - here), pick(blocks, axis, here)
+
+    if form in (0, 1):
+        return cut(blocks, form)
+    if form == "line":
+        here, whole = grid.bit(2), array.reshape(line // 2, 2, 4, rows, array.shape[1])
+        return pick(whole, 1, 1 - here), pick(whole, 1, here)
+    low, high = cut(blocks[: line // 2], 1), cut(blocks[line // 2 :], 0)
+    return low[0], high[0], low[1], high[1]
+
+
+def weight_gradient(grid, pairs, tiles, form):
     rows = pairs[0][0].shape[0] // grid.count
     if rows % 16 == 0:
-        return Reduce(grid, gradient_parts(grid, pairs, tiles, number), number)
-    found = [lower(matmul(left, right)) for left, right in pairs]
-    return Reduce(grid, cut_parts(grid, jnp.concatenate(found, axis=1), number), number)
+        parts = gradient_parts(grid, pairs, tiles, form)
+    else:
+        found = [lower(matmul(left, right)) for left, right in pairs]
+        parts = cut_parts(grid, jnp.concatenate(found, axis=1), form)
+    return BitSum(grid, parts) if form == "line" else PlaneSum(grid, parts, form)
 
 
 def add_halves(terms, number):
@@ -436,12 +490,47 @@
     )(*terms)
 
 
-def joined_rows(own, other, in_sequence):
+def add_joined(packs, number):
+    rows = packs[0][0][0].shape[2]
+    widths = [pack[0][0].shape[3] for pack in packs]
+    count = sum(group[0].shape[0] for group in packs[0])
+    flat = [term for pack in packs for group in pack for term in group]
+
+    def body(*refs):
+        inputs, (away, kept) = list(refs[: len(flat)]), refs[len(flat) :]
+        side = (lax.axis_index("dp") >> number) & 1
+        start = 0
+        for pack, width in zip(packs, widths):
+            place = 0
+            for group in pack:
+                terms = [inputs.pop(0) for _ in group]
+                for row in range(group[0].shape[0]):
+                    other = sum(wide(term[row, 1 - side]) for term in terms)
+                    own = sum(wide(term[row, side]) for term in terms)
+                    away[place, :, start : start + width] = lower(other)
+                    kept[place, :, start : start + width] = lower(own)
+                    place += 1
+            start += width
+
+    out = jax.ShapeDtypeStruct((count, rows, sum(widths)), jnp.bfloat16)
+    return pl.pallas_call(
+        body,
+        out_shape=[out] * 2,
+        cost_estimate=small_cost(0, 2 * sum(term.size for term in flat)),
+        compiler_params=pltpu.CompilerParams(vmem_limit_bytes=VMEM_LIMIT),
+    )(*flat)
+
+
+def joined_rows(own, others, in_sequence):
     rows, columns = own.shape
-    tile = columns // 4
-
-    def body(own_ref, other_ref, rows_ref, turned_ref):
-        first, second = own_ref[...], other_ref[...]
+    tile, run = columns // 4, 4 // len(others)
+
+    def body(own_ref, *refs):
+        other_refs, (rows_ref, turned_ref) = refs[: len(others)], refs[len(others) :]
+        first, second = own_ref[...], other_refs[0][...]
+        for number in range(1, len(others)):
+            later = pl.program_id(0) >= number * run
+            second = jnp.where(later, other_refs[number][...], second)
         if in_sequence:
             ahead = lax.axis_index("tensor") == 0
             first, second = jnp.where(ahead, first, second), jnp.where(ahead, second, first)
@@ -450,11 +539,16 @@
         turned_ref[:, :rows] = first.T
         turned_ref[:, rows:] = second.T
 
-    block = pl.BlockSpec((rows, tile), lambda step: (0, step))
+    def part_spec(number):
+        return pl.BlockSpec(
+            (rows, tile), lambda step: (0, jnp.clip(step - number * run, 0, run - 1))
+        )
+
     return pl.pallas_call(
         body,
         grid=(4,),
-        in_specs=[block] * 2,
+        in_specs=[pl.BlockSpec((rows, tile), lambda step: (0, step))]
+        + [part_spec(number) for number in range(len(others))],
         out_specs=[
             pl.BlockSpec((2 * rows, tile), lambda step: (0, step)),
             pl.BlockSpec((tile, 2 * rows), lambda step: (step, 0)),
@@ -465,17 +559,17 @@
         ],
         cost_estimate=small_cost(0, 12 * rows * columns),
         compiler_params=pltpu.CompilerParams(vmem_limit_bytes=VMEM_LIMIT),
-    )(own, other)
+    )(own, *others)
 
 
 def row_kernel(body, inputs, outs, sums=0):
     length, columns = inputs[0].shape
     tile = length // 4
 
-    def spec(rows):
+    def spec(rows, width):
         if rows == 1:
-            return pl.BlockSpec((1, columns), lambda step: (0, 0))
-        return pl.BlockSpec((tile, columns), lambda step: (step, 0))
+            return pl.BlockSpec((1, width), lambda step: (0, 0))
+        return pl.BlockSpec((tile, width), lambda step: (step, 0))
 
     def kernel(*refs):
         found = body(*[ref[...] for ref in refs[: len(inputs)]])
@@ -494,55 +588,113 @@
     return pl.pallas_call(
         kernel,
         grid=(4,),
-        in_specs=[spec(i.shape[0]) for i in inputs],
-        out_specs=[spec(length)] * len(outs) + [spec(1)] * sums,
-        out_shape=[jax.ShapeDtypeStruct((length, columns), kind) for kind in outs]
+        in_specs=[spec(*i.shape) for i in inputs],
+        out_specs=[spec(length, width) for width, _ in outs] + [spec(1, columns)] * sums,
+        out_shape=[jax.ShapeDtypeStruct((length, width), kind) for width, kind in outs]
         + [jax.ShapeDtypeStruct((1, columns), jnp.float32)] * sums,
         cost_estimate=small_cost(0, size),
         compiler_params=pltpu.CompilerParams(vmem_limit_bytes=VMEM_LIMIT),
     )(*inputs)
 
 
-def norm_forward(residual, own, arrived, gain):
-    middle = wide(residual) + (own + arrived)
+def halves(values):
+    half = values.shape[1] // 2
+    return values, values[:, :half], values[:, half:]
+
+
+def both_parts(first, second):
+    return wide(jnp.concatenate([first, second], axis=1))
+
+
+def norm_forward(residual, own, first, second, gain):
+    middle = wide(residual) + (own + both_parts(first, second))
     unit, _ = statistics(middle)
-    return middle, lower(unit * gain)
-
-
-def norm_gradient(source, own, arrived, base, gain):
+    return middle, *halves(lower(unit * gain))
+
+
+def norm_gradient(source, own, first, second, base, gain):
     unit, inverse = statistics(wide(source))
-    grad = own + arrived
+    grad = own + both_parts(first, second)
     total = wide(base) + norm_backward(unit, inverse, gain, grad)
     return total, lower(total), jnp.sum(grad * unit, axis=0, keepdims=True)
 
 
-class Reduce:
-    def __init__(self, grid, parts, number):
-        self.grid, self.number = grid, number
-        self.sent, own = parts
-        self.kind = own.dtype
-        self.terms = [own]
+def norm_gradient_halves(*values):
+    total, rounded, summed = norm_gradient(*values)
+    return total, *halves(rounded), summed
+
+
+class PlaneSum:
+    def __init__(self, grid, parts, form):
+        half = len(parts) // 2
+        self.grid, self.sent, self.own = grid, tuple(parts[:half]), tuple(parts[half:])
+        self.numbers = (form,) if form in (0, 1) else (1, 0)
 
     def start(self, *after):
-        self.got = self.grid.swap(tie(self.sent, *after), self.number)
+        swaps = zip(self.sent, self.numbers)
+        self.got = [self.grid.swap(tie(sent, *after), number) for sent, number in swaps]
         return self
 
+    def second(self, *after):
+        sent, self.groups = [], []
+        for own, got, number in zip(self.own, self.got, self.numbers):
+            away, kept = add_halves([own, tie(got, *after)], 1 - number)
+            sent.append(away)
+            self.groups.append([kept, self.grid.swap(away, 1 - number)])
+        self.sent = tuple(sent)
+        return self
+
+
+class BitSum:
+    def __init__(self, grid, parts):
+        self.grid, self.sent, self.kept = grid, *parts
+
+    def start(self, *after):
+        self.got = self.grid.swap(tie(self.sent, *after), 2)
+        return self
+
+    def step(self, number, *after):
+        def cut(array):
+            rows, columns = array.shape[-2:]
+            count = array.size // (rows * columns)
+            if number >= 2:
+                count, rows = count // 4, rows * 4
+            else:
+                count = 1
+                rows = array.size // (2 * columns)
+            return array.reshape(count if number < 2 else count // 2, 2, rows, columns)
+
+        self.sent, self.kept = add_halves([cut(self.kept), cut(tie(self.got, *after))], number)
+        self.got = self.grid.swap(self.sent, number)
+        if number >= 2:
+            shape = (self.sent.shape[0], 4, self.sent.shape[1] // 4, self.sent.shape[2])
+            self.kept, self.got = self.kept.reshape(shape), self.got.reshape(shape)
+        return self
+
+    def line(self, *after):
+        for number in self.grid.line_bits[1:]:
+            self.step(number, *after)
+        return self
+
+    def result(self):
+        return wide(self.kept[0]) + wide(self.got[0])
+
+
+class LineSum:
+    def __init__(self, grid, sums):
+        self.grid, self.packs = grid, [found.groups for found in sums]
+
     def step(self, number, after):
-        terms = self.terms + [tie(self.got, *after)]
-        if number >= 2:
-            terms = [t.reshape((t.shape[0] // 2, 2) + t.shape[1:]) for t in terms]
-        if self.kind == jnp.bfloat16:
-            self.sent, kept = add_halves(terms, number)
-            self.terms = [kept]
-        else:
-            side = self.grid.bit(number)
-            self.sent = sum(pick(t, 1, 1 - side) for t in terms)
-            self.terms = [pick(t, 1, side) for t in terms]
-        self.got = self.grid.swap(self.sent, number)
+        packs = [
+            [
+                [t.reshape((t.shape[0] // 2, 2) + t.shape[1:]) for t in (*kept, tie(got, *after))]
+                for *kept, got in groups
+            ]
+            for groups in self.packs
+        ]
+        self.sent, kept = add_joined(packs, number)
+        self.packs = [[[kept, self.grid.swap(self.sent, number)]]]
         return self
-
-    def second(self, *after):
-        return self.step(1 - self.number, after)
 
     def third(self, *after):
         return self.step(self.grid.line_bits[0], after)
@@ -553,7 +705,24 @@
         return self
 
     def result(self):
-        return sum(wide(term[0]) for term in self.terms + [self.got])
+        return sum(wide(term[0]) for term in self.packs[0][0])
+
+
+class SmallSum:
+    def __init__(self, grid, array):
+        rows = array.shape[0] // grid.count
+        self.grid, self.terms = grid, [array.reshape(grid.count, rows, array.shape[1])]
+
+    def step(self, number, *after):
+        terms = [tie(t, *after).reshape((t.shape[0] // 2, 2) + t.shape[1:]) for t in self.terms]
+        side = self.grid.bit(number)
+        self.sent = sum(pick(t, 1, 1 - side) for t in terms)
+        kept = sum(pick(t, 1, side) for t in terms)
+        self.terms = [kept, self.grid.swap(self.sent, number)]
+        return self
+
+    def result(self):
+        return sum(term[0] for term in self.terms)
 
 
 def running_sum(values, reverse):
@@ -793,7 +962,7 @@
     scale = head_size ** (-0.5)
     rows_here = tokens.shape[0]
 
-    other_cotangent = partner(cotangent)
+    load_qk = Gather(grid, jnp.concatenate([lower(w_query), lower(w_key)], axis=1))
     own_gains = jnp.stack([norm_attn, norm_mlp])
     other_gains = partner(own_gains)
     gains = jnp.where(
@@ -805,50 +974,48 @@
     for number in range(len(grid.line_bits) + 2):
         gains = jnp.concatenate([gains, grid.swap(gains, number)], axis=0)
         gain_codes = gain_codes + [code ^ (1 << number) for code in gain_codes]
-    (gains,) = grid.place([(gain_codes, gains)], [gains.shape[2]])
-    gains = gains.reshape(grid.count, 2, gains.shape[1])
-    gain_attn = gains[:, 0].reshape(-1)
-    gain_mlp = gains[:, 1].reshape(-1)
+        if number == 1:
+            load_qk.line_end(gains)
+    (all_gains,) = grid.place([(gain_codes, gains)], [gains.shape[2]])
+    all_gains = all_gains.reshape(grid.count, 2, all_gains.shape[1])
+    gain_attn = all_gains[:, 0].reshape(-1)
+    gain_mlp = all_gains[:, 1].reshape(-1)
+    load_qk.plane(fine=True)
+    other_cotangent = partner(tie(cotangent, gains))
 
     padding = jnp.zeros((w_forget.shape[0], LANES - heads_here), jnp.bfloat16)
     forget_lanes = jnp.concatenate([lower(w_forget), padding], axis=1)
-    load_qk = Gather(grid, jnp.concatenate([lower(w_query), lower(w_key)], axis=1), fine=True)
     load_vf = Gather(
-        grid,
-        jnp.concatenate([lower(w_value), forget_lanes], axis=1),
-        after_line=load_qk.line_done,
-        after_plane=load_qk.plane_done,
-    )
+        grid, jnp.concatenate([lower(w_value), forget_lanes], axis=1), load_qk.far, gains
+    )
+    load_vf.line_end(*load_qk.corner_parts).plane(*load_qk.corners)
     load_go = Gather(
-        grid,
-        jnp.concatenate([lower(w_gate_attn), lower(w_out).T], axis=1),
-        after_line=load_vf.line_done,
-        after_plane=load_vf.sides_done,
-    )
-    load_gate = Gather(
-        grid, lower(w_gate), after_line=load_go.line_done, after_plane=load_go.sides_done
-    )
-    load_up = Gather(
-        grid, lower(w_up), after_line=load_gate.line_done, after_plane=load_gate.sides_done
-    )
-    load_down = Gather(
-        grid, lower(w_down).T, after_line=load_up.line_done, after_plane=load_up.sides_done
-    )
+        grid, jnp.concatenate([lower(w_gate_attn), lower(w_out).T], axis=1), load_vf.far
+    )
+    load_go.line_end(load_vf.block)
+    gain_attn, gain_mlp = gain_attn[None], gain_mlp[None]
+    low = jnp.bfloat16
+    columns = tokens.shape[1]
+    rounded_outs = [(columns, low), (columns // 2, low), (columns // 2, low)]
+
+    def exchanged(parts):
+        return [partner(part) for part in parts]
+
+    own_attn, *sent = row_kernel(
+        lambda rows, gain: halves(lower(statistics(wide(rows))[0] * gain)),
+        [tokens, gain_attn],
+        rounded_outs,
+    )
+    normed_attn, normed_attn_t = joined_rows(own_attn, exchanged(sent), True)
+    grad_output, grad_output_t = joined_rows(cotangent, [other_cotangent], False)
+
+    load_go.plane(*load_vf.corners, normed_attn)
+    load_gate = Gather(grid, lower(w_gate), load_go.far).line_end(load_go.block)
+    load_up = Gather(grid, lower(w_up), load_gate.far, load_go.corners[0])
+    value_w, forget_w = load_vf.weight.part(0, width), load_vf.weight.part(width, LANES)
     query_w, key_w = load_qk.weight.part(0, width), load_qk.weight.part(width, width)
-    value_w, forget_w = load_vf.weight.part(0, width), load_vf.weight.part(width, LANES)
     gate_w, out_w = load_go.weight.part(0, width), load_go.weight.part(width, width)
-    mlp_gate, mlp_up, mlp_down = load_gate.weight, load_up.weight, load_down.weight
-
-    gain_attn, gain_mlp = gain_attn[None], gain_mlp[None]
-    (own_attn,) = row_kernel(
-        lambda rows, gain: (lower(statistics(wide(rows))[0] * gain),),
-        [tokens, gain_attn],
-        [jnp.bfloat16],
-    )
-    normed_attn, normed_attn_t = joined_rows(own_attn, partner(own_attn), True)
-    grad_output, grad_output_t = joined_rows(cotangent, other_cotangent, False)
-
-    low = jnp.bfloat16
+
     (qk,) = multiply(
         normed_attn, load_qk.weight, 3, lambda p: (lower(p),), [], [(2 * width, low)]
     )
@@ -862,8 +1029,14 @@
     )
     bias_lanes = jnp.pad(forget_bias, (0, LANES - heads_here))[None]
     decay_row, decay_column = decays(forget_logit, bias_lanes, heads_here, LANES // head_size)
-    qk = tie(qk, load_gate.ready)
+    load_gate.plane(*load_go.corners, decay_row, qk)
+    load_up.line_end(load_gate.block)
+    qk = tie(qk, load_gate.block)
     attended, logsum = attend(qk, values_all, decay_column, decay_row, head_size)
+    load_up.plane(*load_gate.corners, attended)
+    load_down = Gather(grid, lower(w_down).T, load_up.far, load_gate.corners[0])
+    load_down.line_end(load_up.block)
+    mlp_gate, mlp_up = load_gate.weight, load_up.weight
 
     def gate_output(product, attended):
         sigmoid = jax.nn.sigmoid(product)
@@ -872,16 +1045,20 @@
     gate_sig, gated = multiply(
         normed_attn, gate_w, 2, gate_output, [attended], [(width, jnp.float32), (width, low)]
     )
-    arrived = partner(multiply_back([(gated, out_w)], 1 - side))
-    middle, own_normed = row_kernel(
+    arrived = exchanged(multiply_back([(gated, out_w)], 1 - side, low, 2))
+    (own_part,) = multiply_back([(gated, out_w)], side)
+    middle, own_normed, *sent = row_kernel(
         norm_forward,
-        [tokens, multiply_back([(gated, out_w)], side), arrived, gain_mlp],
-        [jnp.float32, low],
-    )
-    normed_mlp, normed_mlp_t = joined_rows(own_normed, partner(own_normed), False)
+        [tokens, own_part, *arrived, gain_mlp],
+        [(columns, jnp.float32)] + rounded_outs,
+    )
+    normed_mlp, normed_mlp_t = joined_rows(own_normed, exchanged(sent), False)
     (gate_act,) = multiply(
         normed_mlp, mlp_gate, 4, lambda p: (lower(p),), [], [(hidden_here, low)]
     )
+
+    load_down.plane(*load_up.corners, gate_act)
+    mlp_down = load_down.weight
 
     def hidden_units(up, gate):
         gate = wide(gate)
@@ -890,10 +1067,7 @@
     up_act, hidden = multiply(
         normed_mlp, mlp_up, 4, hidden_units, [gate_act], [(hidden_here, low)] * 2
     )
-    sum_down = weight_gradient(grid, [(grad_output_t, hidden)], 4, 1).start()
-    hidden = tie(hidden, sum_down.sent)
-    other_down = multiply_back([(hidden, mlp_down)], jnp.int32(1))
-    arrived_down = partner(other_down)
+    sum_down = weight_gradient(grid, [(grad_output_t, hidden)], 4, "line").start()
 
     def hidden_backward(grad, gate, up):
         gate, up = wide(gate), wide(up)
@@ -904,37 +1078,31 @@
         )
 
     grad_up, grad_gate = multiply(
-        tie(grad_output, other_down),
+        tie(grad_output, sum_down.sent),
         mlp_down,
         4,
         hidden_backward,
         [gate_act, up_act],
         [(hidden_here, low)] * 2,
     )
-    sum_up = weight_gradient(grid, [(normed_mlp_t, grad_up)], 4, 0).start()
-    grad_gate = tie(grad_gate, sum_up.sent)
-    sum_gate = weight_gradient(grid, [(normed_mlp_t, grad_gate)], 4, 1)
-    grad_gate = tie(grad_gate, sum_gate.sent)
+    sum_up = weight_gradient(grid, [(normed_mlp_t, grad_up)], 4, 0)
+    sum_up.start()
+    grad_gate = tie(grad_gate, *sum_up.sent)
+    sum_gate = weight_gradient(grid, [(normed_mlp_t, grad_gate)], 4, 1).start()
+    grad_gate = tie(grad_gate, *sum_gate.sent)
     back = [(grad_gate, mlp_gate), (grad_up, mlp_up)]
-    other_part = multiply_back(back, jnp.int32(1))
-    arrived = partner(other_part)
-    sum_down.second(other_part)
-    sum_gate.start(sum_down.sent)
-    back = [(tie(grad_gate, sum_down.sent), mlp_gate), (grad_up, mlp_up)]
-    grad_middle, own_branch, gain_mlp_part = row_kernel(
-        norm_gradient,
-        [middle, multiply_back(back, jnp.int32(0)), arrived, cotangent, gain_mlp],
-        [jnp.float32, low],
+    arrived = exchanged(multiply_back(back, jnp.int32(1), low, 2))
+    (own_part,) = multiply_back(back, jnp.int32(0))
+    sum_down.line(own_part)
+    own_part = tie(own_part, sum_down.sent)
+    grad_middle, own_branch, *sent, gain_mlp_part = row_kernel(
+        norm_gradient_halves,
+        [middle, own_part, *arrived, cotangent, gain_mlp],
+        [(columns, jnp.float32)] + rounded_outs,
         sums=1,
     )
-    other_branch = partner(own_branch)
-    own_down = multiply_back([(tie(hidden, own_branch), mlp_down)], jnp.int32(0))
-    (mixed,) = row_kernel(
-        lambda middle, own, arrived: (lower(middle + (own + arrived)),),
-        [middle, own_down, arrived_down],
-        [low],
-    )
-    grad_branch, grad_branch_t = joined_rows(own_branch, tie(other_branch, own_down), True)
+    other_branch = exchanged(sent)
+    grad_branch, grad_branch_t = joined_rows(own_branch, other_branch, True)
 
     def gate_backward(grad, sigmoid, attended):
         return lower(grad * sigmoid), lower(grad * attended * sigmoid * (1.0 - sigmoid))
@@ -947,46 +1115,60 @@
         [gate_sig, attended],
         [(width, low)] * 2,
     )
+    sum_up.second(grad_attended)
+    sum_gate.second(grad_attended)
+    grad_gate_logit = tie(grad_gate_logit, *sum_up.sent, *sum_gate.sent)
     sum_go = weight_gradient(
-        grid, [(normed_attn_t, grad_gate_logit), (grad_branch_t, gated)], 4, 0
+        grid, [(normed_attn_t, grad_gate_logit), (grad_branch_t, gated)], 4, "halves"
     ).start()
-    sum_up.second(sum_go.sent)
-    sum_gate.second(sum_go.sent)
-    sum_down.third(sum_go.sent)
-    grad_attended = tie(grad_attended, sum_go.sent, sum_up.sent, sum_gate.sent, sum_down.sent)
+    grad_attended = tie(grad_attended, *sum_go.sent)
     grad_queries, grad_keys, grad_values, row_total, column_total = attend_backward(
         qk, values_all, grad_attended, decay_column, decay_row, logsum, head_size
     )
-    sum_up.third(grad_queries)
-    sum_down.fourth(grad_queries)
-    grad_queries = tie(grad_queries, sum_up.sent, sum_down.sent)
+    line_mlp = LineSum(grid, [sum_gate, sum_up]).third(grad_queries)
+    sum_down.step(1, grad_queries)
+    grad_queries = tie(grad_queries, line_mlp.sent, sum_down.sent)
     sum_qk = weight_gradient(
-        grid, [(normed_attn_t, grad_queries), (normed_attn_t, grad_keys)], 4, 1
-    ).start()
+        grid, [(normed_attn_t, grad_queries), (normed_attn_t, grad_keys)], 4, "halves"
+    )
+    sum_qk.start()
+    sum_go.second(*sum_qk.sent)
     grad_forget, bias_part = forget_backward(
         row_total, column_total, forget_logit, bias_lanes, heads_here
     )
+    grad_values = tie(grad_values, *sum_qk.sent, *sum_go.sent)
     sum_vf = weight_gradient(
-        grid, [(normed_attn_t, tie(grad_values, sum_qk.sent)), (normed_attn_t, grad_forget)], 1, 0
-    ).start()
+        grid, [(normed_attn_t, grad_values), (normed_attn_t, grad_forget)], 1, "halves"
+    )
+    sum_down.step(0, *sum_vf.sent)
+    hidden = tie(hidden, sum_down.sent)
+    other_down = multiply_back([(hidden, mlp_down)], jnp.int32(1), low, 2)
+    arrived_down = exchanged(other_down)
     back = [
-        (tie(grad_gate_logit, sum_qk.sent, sum_vf.sent), gate_w),
+        (tie(grad_gate_logit, *other_down), gate_w),
         (grad_queries, query_w),
         (grad_keys, key_w),
         (grad_values, value_w),
         (grad_forget, forget_w),
     ]
-    other_part = multiply_back(back, 1 - side)
-    arrived = partner(other_part)
-    sum_up.fourth(other_part)
-    sum_gate.third(other_part)
-    back[1] = (tie(grad_queries, sum_up.sent, sum_gate.sent), query_w)
-    own_part = multiply_back(back, side)
-    sum_go.second(own_part)
+    other_part = multiply_back(back, 1 - side, low, 2)
+    arrived = exchanged(other_part)
+    sum_qk.second(*other_part)
+    line_mlp.fourth(*other_part)
+    back[1] = (tie(grad_queries, line_mlp.sent, *sum_qk.sent), query_w)
+    (own_part,) = multiply_back(back, side)
+    (own_down,) = multiply_back([(tie(hidden, own_part), mlp_down)], jnp.int32(0))
+    (mixed,) = row_kernel(
+        lambda middle, own, *parts: (lower(middle + (own + both_parts(*parts))),),
+        [middle, own_down, *arrived_down],
+        [(columns, low)],
+    )
+    line_go = LineSum(grid, [sum_go]).third(own_part)
+    sum_vf.start(own_part, line_go.sent)
     _, tokens_grad, gain_attn_part = row_kernel(
         norm_gradient,
-        [tokens, own_part, arrived, grad_middle, gain_attn],
-        [jnp.float32, low],
+        [tokens, own_part, *arrived, grad_middle, gain_attn],
+        [(columns, jnp.float32), (columns, low)],
         sums=1,
     )
     small = jnp.concatenate(
@@ -997,21 +1179,15 @@
         ],
         axis=1,
     )
-    sum_gate.fourth(gain_attn_part)
-    sum_qk.second(sum_go.sent)
-    sum_vf.second(sum_go.sent)
-    sum_go.third(sum_qk.sent)
-    sum_qk.third(sum_go.sent, sum_vf.sent)
-    sum_small = Reduce(grid, cut_parts(grid, small, 1), 1).start(sum_qk.sent)
-    sum_vf.third(sum_qk.sent)
-    sum_go.fourth(sum_qk.sent)
-    sum_small.second(sum_vf.sent)
-    sum_qk.fourth(sum_small.sent)
-    sum_small.third(sum_qk.sent)
-    sum_vf.fourth(sum_qk.sent)
-    sum_small.fourth(sum_vf.sent)
-    down_grad, up_grad, gate_grad = sum_down.result().T, sum_up.result(), sum_gate.result()
-    go_grad, qk_grad, vf_grad = sum_go.result(), sum_qk.result(), sum_vf.result()
+    sum_vf.second(gain_attn_part)
+    line_qkv = LineSum(grid, [sum_qk, sum_vf]).third(gain_attn_part)
+    line_go.fourth(line_qkv.sent)
+    sum_small = SmallSum(grid, small).step(0, line_qkv.sent).step(1)
+    line_qkv.fourth(sum_small.sent)
+    for number in grid.line_bits:
+        sum_small.step(number, line_qkv.sent)
+    down_grad, go_grad, qkv_grad = sum_down.result().T, line_go.result(), line_qkv.result()
+    mlp_grad = line_mlp.result()
     small_sum = sum_small.result().reshape(-1)
     share = norm_attn.shape[0]
     gain_sums = small_sum[: 4 * share].reshape(2, 2, share)
@@ -1021,17 +1197,17 @@
     return (
         mixed,
         tokens_grad,
-        qk_grad[:, :width],
-        qk_grad[:, width:],
-        vf_grad[:, :width],
+        qkv_grad[:, :width],
+        qkv_grad[:, width : 2 * width],
+        qkv_grad[:, 2 * width : 3 * width],
         go_grad[:, :width],
-        vf_grad[:, width : width + heads_here],
+        qkv_grad[:, 3 * width : 3 * width + heads_here],
         small_sum[4 * share :],
         go_grad[:, width:].T,
         gain_grads[0],
         gain_grads[1],
-        gate_grad,
-        up_grad,
+        mlp_grad[:, :hidden_here],
+        mlp_grad[:, hidden_here:],
         down_grad,
     )
 

time: 812 us -> 765 us (0.942)
  waiting for transfers between devices: 265 us -> 198 us
  starting transfers between devices: 86.3 us -> 103 us
    ppermute x70 -> x72, waiting for transfers between devices: 264 us -> 197 us  [swap(): return lax.ppermute(values, 'dp', pairs)]
    pallas_call x18 -> x11, Pallas kernels: 53.4 us -> 33.2 us  [add_halves(): pl.pallas_call(body, grid=(columns // tile,), in_specs=[block] * len(term...]
    ppermute x70 -> x72, starting transfers between devices: 85.8 us -> 98.7 us  [swap(): return lax.ppermute(values, 'dp', pairs)]
    pallas_call x9 -> x15, Pallas kernels: 40.4 us -> 52.2 us  [the longest x5 26.7 us: row_kernel(): pl.pallas_call(kernel, grid=(4,), in_specs=[spec(*i.shape) for i in input...]
    unnamed x186 -> x240, local copies, waits for them, and re-layouts: 24.4 us -> 28.9 us
  transfers between devices with their start and end apart: 80 -> 89, of which waited for: 32 -> 31; matrix products, arithmetic and copies ran while one was open for 4% -> 4% of each run, Pallas kernels for 49% -> 52%
where the time goes in v3:
time: 765 us; the launch traced here: 753 us
  Pallas kernels  392 us (51%)
  waiting for transfers between devices  198 us (26%)
  starting transfers between devices  103 us (13%)
  local copies, waits for them, and re-layouts  41.3 us (5%)
  other arithmetic  16.9 us (2%)
    ppermute x72, waiting for transfers between devices, swap(): return lax.ppermute(values, 'dp', pairs)  197 us
    pallas_call x8, Pallas kernels, multiply_back(): pl.pallas_call(body, grid_spec=pltpu.PrefetchScalarGridSpec(num_scalar_pr...  99.2 us
    ppermute x72, starting transfers between devices, swap(): return lax.ppermute(values, 'dp', pairs)  98.7 us
    pallas_call x7, Pallas kernels, multiply(): pl.pallas_call(body, grid=(tiles,), in_specs=[pl.BlockSpec((length, depth...  80.2 us
    pallas_call x6, Pallas kernels, gradient_parts(): pl.pallas_call(body, grid=(tiles,), in_specs=[pl.BlockSpec((depth, length...  68.2 us
    pallas_call x11, Pallas kernels, add_halves(): pl.pallas_call(body, grid=(columns // tile,), in_specs=[block] * len(term...  33.2 us
    pallas_call x1, Pallas kernels, attend_backward(): pl.pallas_call(functools.partial(bwd_kernel, head ** (-0.5), head), grid=...  32.9 us
    unnamed x240, local copies, waits for them, and re-layouts  28.9 us
  transfers between devices with their start and end apart: 89, of which 31 were waited for; matrix products, arithmetic and copies ran while one was open for 4% of the time, Pallas kernels for 52%

profile of v3, /device:TPU:0, one launch (start us, length us, event | category | flops | bytes accessed | tf_op | source)
XLA Modules:
  0.0 753.5 jit_solution(5474289586531833099)
XLA Ops:
  14.7 6.7 collective-permute-done.7
  25.6 11.3 %collective-permute-done.8.refs_2_.refs_11_.refs_19_ = bf16[2,96,1536]{2,1,0:T(8,128)(2,1)S(1)} collective-permute-done((bf16[2,96,1536]{2,1,0:T(8,128)(2,1)S(1)}, bf16[2,96,1536]{2,1,0:T(8,128)(2,1)S(1)}, u32[]{:S(2)}, u32[]{:S(2)}) %collective-permute-start.8) | collective-permute-done | bytes 589856 | tf_op jit(solution)/shard_map/ppermute | solution.py:78
  68.2 8.3 %collective-permute-done.14.refs_7_.refs_16_.refs_24_ = bf16[2,96,1536]{2,1,0:T(8,128)(2,1)} collective-permute-done((bf16[2,96,1536]{2,1,0:T(8,128)(2,1)S(1)}, bf16[2,96,1536]{2,1,0:T(8,128)(2,1)}, u32[]{:S(2)}, u32[]{:S(2)}) %collective-permute-start.14) | collective-permute-done | bytes 589856 | tf_op jit(solution)/shard_map/ppermute | solution.py:78
  81.7 10.2 %collective-permute-done.19.refs_2_.refs_27_.refs_32_ = bf16[4,96,896]{2,1,0:T(8,128)(2,1)S(1)} collective-permute-done((bf16[4,96,896]{2,1,0:T(8,128)(2,1)S(1)}, bf16[4,96,896]{2,1,0:T(8,128)(2,1)S(1)}, u32[]{:S(2)}, u32[]{:S(2)}) %collective-permute-start.19) | collective-permute-done | bytes 688160 | tf_op jit(solution)/shard_map/ppermute | solution.py:78
  107.0 13.8 %collective-permute-done.27 = bf16[1,96,2048]{2,1,0:T(8,128)(2,1)S(1)} collective-permute-done((bf16[1,96,2048]{2,1,0:T(8,128)(2,1)S(1)}, bf16[1,96,2048]{2,1,0:T(8,128)(2,1)S(1)}, u32[]{:S(2)}, u32[]{:S(2)}) %collective-permute-start.27) | collective-permute-done | bytes 393248 | tf_op jit(solution)/shard_map/ppermute | solution.py:78
  121.3 4.5 collective-permute-done.23.refs_2_.refs_6_
  130.1 10.2 %shard_map.248.q_ref.k_ref = bf16[1024,1536]{1,0:T(8,128)(2,1)} custom-call(bf16[1024,1536]{1,0:T(8,128)(2,1)} %get-tuple-element.179.refs_0_, bf16[2,96,1536]{2,1,0:T(8,128)(2,1)S(1)} %copy-done.13, bf16[2,96,1536]{2,1,0:T(8,128)(2,1)S(1)} %copy-done.18, bf16[2,96,1536]{2,1,0:T(8,128)(2,1)S(1)} %copy-done.21, ...), custom_call_target="tpu_custom_call" | custom-call | flops 96636768 | bytes 220200 | tf_op jit(solution)/shard_map/pallas_call | solution.py:194
  140.4 10.3 %shard_map.249 = (bf16[1024,768]{1,0:T(8,128)(2,1)}, f32[1024,128]{1,0:T(8,128)S(1)}) custom-call(bf16[1024,1536]{1,0:T(8,128)(2,1)} %get-tuple-element.179.refs_0_, bf16[4,96,896]{2,1,0:T(8,128)(2,1)S(1)} %pad_maximum_fusion.7.refs_1_.refs_26_.refs_31_, bf16[4,96,896]{2,1,0:T(8,128)(2,1)S(1)} %collective-permute-done.19.refs_2_.refs_27_.refs_32_, ...), custom_call_target="tpu_custom_call" | custom-call | flops 56371444 | bytes 159907 | tf_op jit(solution)/shard_map/pallas_call | solution.py:194
  156.2 3.9 collective-permute-start.33
  160.1 11.9 %collective-permute-done.33 = bf16[1,96,2048]{2,1,0:T(8,128)(2,1)S(1)} collective-permute-done((bf16[1,96,2048]{2,1,0:T(8,128)(2,1)S(1)}, bf16[1,96,2048]{2,1,0:T(8,128)(2,1)S(1)}, u32[]{:S(2)}, u32[]{:S(2)}) %collective-permute-start.33) | collective-permute-done | bytes 393248 | tf_op jit(solution)/shard_map/ppermute | solution.py:78
  172.5 14.9 %collective-permute-done.35.refs_2_.refs_3_ = bf16[4,96,2048]{2,1,0:T(8,128)(2,1)S(1)} collective-permute-done((bf16[4,96,2048]{2,1,0:T(8,128)(2,1)S(1)}, bf16[4,96,2048]{2,1,0:T(8,128)(2,1)S(1)}, u32[]{:S(2)}, u32[]{:S(2)}) %collective-permute-start.35) | collective-permute-done | bytes 1572896 | tf_op jit(solution)/shard_map/ppermute | solution.py:78
  191.4 23.0 %shard_map.251 = (f32[1024,768]{1,0:T(8,128)}, f32[6,2,1024]{2,1,0:T(2,128)S(1)}) custom-call(bf16[1024,1536]{1,0:T(8,128)(2,1)} %shard_map.248.q_ref.k_ref, bf16[1024,1536]{1,0:T(8,128)(2,1)} %shard_map.248.q_ref.k_ref, bf16[1024,768]{1,0:T(8,128)(2,1)S(1)} %copy-done.46, f32[6,1024,2]{2,1,0:T(8,128)} %copy-done.28, ...), custom_call_target="tpu_custom_call" | custom-call | flops 193273536 | bytes 251658 | tf_op jit(solution)/shard_map/pallas_call | solution.py:898
  220.9 8.9 %shard_map.252 = (f32[1024,768]{1,0:T(8,128)}, bf16[1024,768]{1,0:T(8,128)(2,1)}) custom-call(bf16[1024,1536]{1,0:T(8,128)(2,1)} %get-tuple-element.179.refs_0_, bf16[4,96,1536]{2,1,0:T(8,128)(2,1)S(1)} %pad_maximum_fusion.3.refs_1_.refs_5_, bf16[4,96,1536]{2,1,0:T(8,128)(2,1)S(1)} %collective-permute-done.23.refs_2_.refs_6_, ...), custom_call_target="tpu_custom_call" | custom-call | flops 48318384 | bytes 267386 | tf_op jit(solution)/shard_map/pallas_call | solution.py:194
  229.7 6.7 shard_map.254
  237.8 4.1 collective-permute-start.45
  242.7 6.3 shard_map.253.refs_1_
  249.0 5.5 shard_map.255
  255.0 5.0 collective-permute-done.45
  269.9 12.1 %shard_map.257.refs_6_ = bf16[1024,2048]{1,0:T(8,128)(2,1)} custom-call(bf16[1024,1536]{1,0:T(8,128)(2,1)} %get-tuple-element.203.refs_0_, bf16[4,96,2048]{2,1,0:T(8,128)(2,1)S(1)} %copy-done.6, bf16[4,96,2048]{2,1,0:T(8,128)(2,1)} %copy-done.107, bf16[4,96,2048]{2,1,0:T(8,128)(2,1)} %copy-done.108, bf16[2,96,2048]{2,1,0:T(8,128)(2,1)S(1)} %copy-done.39, ...), custom_call_target="tpu_custom_call" | custom-call | flops 128849016 | bytes 272629 | tf_op jit(solution)/shard_map/pallas_call | solution.py:194
  285.9 33.7 %collective-permute-done.47.refs_2_ = bf16[4,96,2048]{2,1,0:T(8,128)(2,1)S(1)} collective-permute-done((bf16[4,96,2048]{2,1,0:T(8,128)(2,1)S(1)}, bf16[4,96,2048]{2,1,0:T(8,128)(2,1)S(1)}, u32[]{:S(2)}, u32[]{:S(2)}) %collective-permute-start.47) | collective-permute-done | bytes 1572896 | tf_op jit(solution)/shard_map/ppermute | solution.py:78
  326.4 13.3 %shard_map.258 = (bf16[1024,2048]{1,0:T(8,128)(2,1)}, bf16[1024,2048]{1,0:T(8,128)(2,1)}) custom-call(bf16[1024,1536]{1,0:T(8,128)(2,1)} %get-tuple-element.203.refs_0_, bf16[4,96,2048]{2,1,0:T(8,128)(2,1)} %pad_maximum_fusion.1.refs_1_.refs_7_, bf16[4,96,2048]{2,1,0:T(8,128)(2,1)} %collective-permute-done.39.refs_2_.refs_8_, ...), custom_call_target="tpu_custom_call" | custom-call | flops 128849016 | bytes 440401 | tf_op jit(solution)/shard_map/pallas_call | solution.py:194
  339.7 12.0 %shard_map.260 = (bf16[2,4,96,2048]{3,2,1,0:T(8,128)(2,1)}, bf16[2,4,96,2048]{3,2,1,0:T(8,128)(2,1)}) custom-call(bf16[1536,1024]{1,0:T(8,128)(2,1)} %get-tuple-element.209.refs_0_, bf16[1024,2048]{1,0:T(8,128)(2,1)} %get-tuple-element.295.refs_1_.refs_0_), custom_call_target="tpu_custom_call" | custom-call | flops 128849016 | bytes 272629 | tf_op jit(solution)/shard_map/pallas_call | solution.py:424
  352.1 16.0 %shard_map.261 = (bf16[1024,2048]{1,0:T(8,128)(2,1)}, bf16[1024,2048]{1,0:T(8,128)(2,1)}) custom-call(bf16[1024,1536]{1,0:T(8,128)(2,1)} %get-tuple-element.213.refs_0_, bf16[4,96,2048]{2,1,0:T(8,128)(2,1)S(1)} %pad_maximum_fusion.2.refs_1_, bf16[4,96,2048]{2,1,0:T(8,128)(2,1)} %copy-done.105, bf16[4,96,2048]{2,1,0:T(8,128)(2,1)} %copy-done.106, ...), custom_call_target="tpu_custom_call" | custom-call | flops 128849016 | bytes 524288 | tf_op jit(solution)/shard_map/pallas_call | solution.py:194
  368.1 12.3 %shard_map.262 = (bf16[4,2,96,2048]{3,2,1,0:T(8,128)(2,1)S(1)}, bf16[4,2,96,2048]{3,2,1,0:T(8,128)(2,1)}) custom-call(bf16[1536,1024]{1,0:T(8,128)(2,1)} %get-tuple-element.219.refs_0_, bf16[1024,2048]{1,0:T(8,128)(2,1)} %get-tuple-element.220.refs_1_), custom_call_target="tpu_custom_call" | custom-call | flops 128849016 | bytes 272629 | tf_op jit(solution)/shard_map/pallas_call | solution.py:424
  380.4 12.0 %shard_map.263 = (bf16[4,2,96,2048]{3,2,1,0:T(8,128)(2,1)S(1)}, bf16[4,2,96,2048]{3,2,1,0:T(8,128)(2,1)}) custom-call(bf16[1536,1024]{1,0:T(8,128)(2,1)} %get-tuple-element.219.refs_0_, bf16[1024,2048]{1,0:T(8,128)(2,1)} %get-tuple-element.224.refs_1_.refs_0_), custom_call_target="tpu_custom_call" | custom-call | flops 128849016 | bytes 272629 | tf_op jit(solution)/shard_map/pallas_call | solution.py:424
  397.0 17.5 %shard_map.266 = (bf16[512,768]{1,0:T(8,128)(2,1)}, bf16[512,768]{1,0:T(8,128)(2,1)}) custom-call(s32[1]{0:T(128)} %constant.67.clone.1.half_ref, bf16[1024,2048]{1,0:T(8,128)(2,1)} %get-tuple-element.224.refs_1_.refs_0_, bf16[1024,2048]{1,0:T(8,128)(2,1)} %get-tuple-element.220.refs_1_, bf16[4,96,2048]{2,1,0:T(8,128)(2,1)} %copy-done.5, ...), custom_call_target="tpu_custom_call" | custom-call | flops 128849016 | bytes 398458 | tf_op jit(solution)/shard_map/pallas_call | solution.py:275
  415.0 17.5 %shard_map.264.refs_1_ = f32[512,1536]{1,0:T(8,128)} custom-call(s32[1]{0:T(128)} %constant.66.clone.1.half_ref, bf16[1024,2048]{1,0:T(8,128)(2,1)} %get-tuple-element.224.refs_1_.refs_0_, bf16[1024,2048]{1,0:T(8,128)(2,1)} %get-tuple-element.220.refs_1_, bf16[4,96,2048]{2,1,0:T(8,128)(2,1)} %copy-done.5, bf16[4,96,2048]{2,1,0:T(8,128)(2,1)} %copy-done.107, ...), custom_call_target="tpu_custom_call" | custom-call | flops 128849016 | bytes 398458 | tf_op jit(solution)/shard_map/pallas_call | solution.py:275
  440.5 6.8 shard_map.267
  450.1 4.0 collective-permute-start.51
  459.2 9.5 %shard_map.269 = (bf16[1024,768]{1,0:T(8,128)(2,1)}, bf16[1024,768]{1,0:T(8,128)(2,1)}) custom-call(bf16[1024,1536]{1,0:T(8,128)(2,1)} %get-tuple-element.234.refs_0_, bf16[4,96,1536]{2,1,0:T(8,128)(2,1)S(1)} %pad_maximum_fusion.3.refs_1_.refs_5_, bf16[4,96,1536]{2,1,0:T(8,128)(2,1)S(1)} %copy-done.2, bf16[4,96,1536]{2,1,0:T(8,128)(2,1)} %copy-done.104, ...), custom_call_target="tpu_custom_call" | custom-call | flops 48318384 | bytes 298844 | tf_op jit(solution)/shard_map/pallas_call | solution.py:194
  468.7 3.8 shard_map.270
  480.0 12.6 %shard_map.272 = (bf16[2,2,96,1536]{3,2,1,0:T(8,128)(2,1)}, bf16[2,2,96,1536]{3,2,1,0:T(8,128)(2,1)}, bf16[2,2,96,1536]{3,2,1,0:T(8,128)(2,1)S(1)}, bf16[2,2,96,1536]{3,2,1,0:T(8,128)(2,1)}) custom-call(bf16[1536,1024]{1,0:T(8,128)(2,1)} %get-tuple-element.237.refs_0_, bf16[1536,1024]{1,0:T(8,128)(2,1)} %get-tuple-element.238.refs_1_, ...), custom_call_target="tpu_custom_call" | custom-call | flops 96636768 | bytes 283115 | tf_op jit(solution)/shard_map/pallas_call | solution.py:424
  495.4 32.9 %shard_map.273 = (bf16[1024,768]{1,0:T(8,128)(2,1)S(1)}, bf16[1024,768]{1,0:T(8,128)(2,1)S(1)}, bf16[1024,768]{1,0:T(8,128)(2,1)}, f32[6,2,1024]{2,1,0:T(2,128)S(1)}, f32[6,1024,2]{2,1,0:T(8,128)}) custom-call(bf16[1024,1536]{1,0:T(8,128)(2,1)} %shard_map.248.q_ref.k_ref, bf16[1024,1536]{1,0:T(8,128)(2,1)} %shard_map.248.q_ref.k_ref, ...), custom_call_target="tpu_custom_call" | custom-call | flops 483183808 | bytes 251658 | tf_op jit(solution)/shard_map/pallas_call | solution.py:918
  534.8 4.6 shard_map.275
  542.6 11.9 %shard_map.276 = (bf16[2,2,96,1536]{3,2,1,0:T(8,128)(2,1)}, bf16[2,2,96,1536]{3,2,1,0:T(8,128)(2,1)}, bf16[2,2,96,1536]{3,2,1,0:T(8,128)(2,1)S(1)}, bf16[2,2,96,1536]{3,2,1,0:T(8,128)(2,1)}) custom-call(bf16[1536,1024]{1,0:T(8,128)(2,1)} %get-tuple-element.237.refs_0_, bf16[1024,768]{1,0:T(8,128)(2,1)} %copy-done.26, bf16[1024,768]{1,0:T(8,128)(2,1)} %copy-done.27), custom_call_target="tpu_custom_call" | custom-call | flops 96636768 | bytes 220200 | tf_op jit(solution)/shard_map/pallas_call | solution.py:424
  562.4 7.5 shard_map.280
  575.9 13.5 %collective-permute-done.88 = bf16[1,96,2048]{2,1,0:T(8,128)(2,1)} collective-permute-done((bf16[1,96,2048]{2,1,0:T(8,128)(2,1)S(1)}, bf16[1,96,2048]{2,1,0:T(8,128)(2,1)}, u32[]{:S(2)}, u32[]{:S(2)}) %collective-permute-start.88) | collective-permute-done | bytes 393248 | tf_op jit(solution)/shard_map/ppermute | solution.py:78
  589.8 10.1 %shard_map.282 = (bf16[512,768]{1,0:T(8,128)(2,1)}, bf16[512,768]{1,0:T(8,128)(2,1)}) custom-call(s32[1]{0:T(128)} %constant.67.clone.1.half_ref, bf16[1024,2048]{1,0:T(8,128)(2,1)} %get-tuple-element.295.refs_1_.refs_0_, bf16[4,96,2048]{2,1,0:T(8,128)(2,1)} %copy-done.3, bf16[4,96,2048]{2,1,0:T(8,128)(2,1)} %copy-done.105, ...), custom_call_target="tpu_custom_call" | custom-call | flops 64424508 | bytes 230686 | tf_op jit(solution)/shard_map/pallas_call | solution.py:275
  599.9 15.2 %shard_map.283 = (bf16[512,768]{1,0:T(8,128)(2,1)}, bf16[512,768]{1,0:T(8,128)(2,1)}) custom-call(s32[1]{0:T(128)} %bitcast.11.half_ref, bf16[1024,768]{1,0:T(8,128)(2,1)} %get-tuple-element.282.refs_2_.refs_0_, bf16[1024,768]{1,0:T(8,128)(2,1)} %copy-done.26, bf16[1024,768]{1,0:T(8,128)(2,1)} %copy-done.27, ...), custom_call_target="tpu_custom_call" | custom-call | flops 100663296 | bytes 325058 | tf_op jit(solution)/shard_map/pallas_call | solution.py:275
  632.8 15.6 %shard_map.287.refs_1_ = f32[512,1536]{1,0:T(8,128)} custom-call(s32[1]{0:T(128)} %bitcast.half_ref, bf16[1024,768]{1,0:T(8,128)(2,1)} %get-tuple-element.282.refs_2_.refs_0_, bf16[1024,768]{1,0:T(8,128)(2,1)} %copy-done.26, bf16[1024,768]{1,0:T(8,128)(2,1)} %copy-done.27, bf16[1024,768]{1,0:T(8,128)(2,1)} %get-tuple-element.271.refs_1_.refs_3_, ...), custom_call_target="tpu_custom_call" | custom-call | flops 100663296 | bytes 325058 | tf_op jit(solution)/shard_map/pallas_call | solution.py:275
  654.9 6.7 shard_map.290
  661.7 10.4 %shard_map.288.refs_1_ = f32[512,1536]{1,0:T(8,128)} custom-call(s32[1]{0:T(128)} %constant.66.clone.1.half_ref, bf16[1024,2048]{1,0:T(8,128)(2,1)} %get-tuple-element.295.refs_1_.refs_0_, bf16[4,96,2048]{2,1,0:T(8,128)(2,1)S(1)} %copy-done.4, bf16[4,96,2048]{2,1,0:T(8,128)(2,1)} %copy-done.105, bf16[4,96,2048]{2,1,0:T(8,128)(2,1)} %copy-done.106, ...), custom_call_target="tpu_custom_call" | custom-call | flops 64424508 | bytes 230686 | tf_op jit(solution)/shard_map/pallas_call | solution.py:275
  672.2 5.0 shard_map.289
  679.8 3.8 shard_map.293
  684.6 3.8 shard_map.292
  692.7 4.0 collective-permute-done.75
  707.3 17.4 %collective-permute-done.82 = bf16[1,96,1536]{2,1,0:T(8,128)(2,1)S(1)} collective-permute-done((bf16[1,96,1536]{2,1,0:T(8,128)(2,1)S(1)}, bf16[1,96,1536]{2,1,0:T(8,128)(2,1)S(1)}, u32[]{:S(2)}, u32[]{:S(2)}) %collective-permute-start.82) | collective-permute-done | bytes 294944 | tf_op jit(solution)/shard_map/ppermute | solution.py:78
  738.7 12.9 %collective-permute-done.80 = bf16[1,96,2432]{2,1,0:T(8,128)(2,1)S(1)} collective-permute-done((bf16[1,96,2432]{2,1,0:T(8,128)(2,1)S(1)}, bf16[1,96,2432]{2,1,0:T(8,128)(2,1)S(1)}, u32[]{:S(2)}, u32[]{:S(2)}) %collective-permute-start.80) | collective-permute-done | bytes 466976 | tf_op jit(solution)/shard_map/ppermute | solution.py:78
  (498 shorter events, 227.6 us)
Async XLA Ops:
  24.0 23.5 %collective-permute-start.10 = (bf16[2,96,1536]{2,1,0:T(8,128)(2,1)S(1)}, bf16[2,96,1536]{2,1,0:T(8,128)(2,1)S(1)}, u32[]{:S(2)}, u32[]{:S(2)}) collective-permute-start(bf16[2,96,1536]{2,1,0:T(8,128)(2,1)S(1)} %pad_maximum_fusion.8.refs_1_.refs_10_.refs_18_), channel_id=1, source_target_pairs={{0,2},{2,0},{4,6},{6,4},{8,10},{10,8},{12,14},{14,12},{16,18},{18,... | collective-permute-start | bytes 1769480 | tf_op jit(solution)/shard_map/ppermute | solution.py:78
  47.5 29.0 %collective-permute-start.14 = (bf16[2,96,1536]{2,1,0:T(8,128)(2,1)S(1)}, bf16[2,96,1536]{2,1,0:T(8,128)(2,1)}, u32[]{:S(2)}, u32[]{:S(2)}) collective-permute-start(bf16[2,96,1536]{2,1,0:T(8,128)(2,1)S(1)} %collective-permute-done.10.refs_3_.refs_12_.refs_20_), channel_id=1, source_target_pairs={{0,4},{2,6},{4,0},{6,2},{8,12},{10,14},{12,8},{14,10},{16,20},{18,... | collective-permute-start | bytes 1769480 | tf_op jit(solution)/shard_map/ppermute | solution.py:78
  54.0 22.5 %collective-permute-start.15 = (bf16[2,96,1536]{2,1,0:T(8,128)(2,1)S(1)}, bf16[2,96,1536]{2,1,0:T(8,128)(2,1)S(1)}, u32[]{:S(2)}, u32[]{:S(2)}) collective-permute-start(bf16[2,96,1536]{2,1,0:T(8,128)(2,1)S(1)} %collective-permute-done.11.refs_6_.refs_15_.refs_23_), channel_id=1, source_target_pairs={{0,2},{2,0},{4,6},{6,4},{8,10},{10,8},{12,14},{14,12},{16,18},{18,... | collective-permute-start | bytes 1769480 | tf_op jit(solution)/shard_map/ppermute | solution.py:78
  67.6 27.3 %collective-permute-start.5 = (bf16[512,768]{1,0:T(8,128)(2,1)S(1)}, bf16[512,768]{1,0:T(8,128)(2,1)S(1)}, u32[]{:S(2)}, u32[]{:S(2)}) collective-permute-start(bf16[512,768]{1,0:T(8,128)(2,1)S(1)} %get-tuple-element.177), channel_id=1, source_target_pairs={{0,1},{1,0},{2,3},{3,2},{4,5},{5,4},{6,7},{7,6},{8,9},{9,8},{10,11... | collective-permute-start | bytes 2359304 | tf_op jit(solution)/shard_map/ppermute | solution.py:51
  67.7 27.3 %collective-permute-start.6 = (bf16[512,768]{1,0:T(8,128)(2,1)S(1)}, bf16[512,768]{1,0:T(8,128)(2,1)S(1)}, u32[]{:S(2)}, u32[]{:S(2)}) collective-permute-start(bf16[512,768]{1,0:T(8,128)(2,1)S(1)} %get-tuple-element.178), channel_id=1, source_target_pairs={{0,1},{1,0},{2,3},{3,2},{4,5},{5,4},{6,7},{7,6},{8,9},{9,8},{10,11... | collective-permute-start | bytes 2359304 | tf_op jit(solution)/shard_map/ppermute | solution.py:51
  101.4 24.4 %collective-permute-start.23 = (bf16[4,96,1536]{2,1,0:T(8,128)(2,1)S(1)}, bf16[4,96,1536]{2,1,0:T(8,128)(2,1)S(1)}, u32[]{:S(2)}, u32[]{:S(2)}) collective-permute-start(bf16[4,96,1536]{2,1,0:T(8,128)(2,1)S(1)} %pad_maximum_fusion.3.refs_1_.refs_5_), channel_id=1, source_target_pairs={{0,2},{2,0},{4,6},{6,4},{8,10},{10,8},{12,14},{14,12},{16,18},{18,... | collective-permute-start | bytes 3538952 | tf_op jit(solution)/shard_map/ppermute | solution.py:78
  103.3 25.7 %collective-permute-start.24 = (bf16[4,96,1536]{2,1,0:T(8,128)(2,1)S(1)}, bf16[4,96,1536]{2,1,0:T(8,128)(2,1)S(1)}, u32[]{:S(2)}, u32[]{:S(2)}) collective-permute-start(bf16[4,96,1536]{2,1,0:T(8,128)(2,1)S(1)} %pad_maximum_fusion.3.refs_1_.refs_5_), channel_id=1, source_target_pairs={{0,4},{2,6},{4,0},{6,2},{8,12},{10,14},{12,8},{14,10},{16,20},{18,... | collective-permute-start | bytes 3538952 | tf_op jit(solution)/shard_map/ppermute | solution.py:78
  120.9 31.4 %collective-permute-start.28 = (bf16[2,96,2048]{2,1,0:T(8,128)(2,1)S(1)}, bf16[2,96,2048]{2,1,0:T(8,128)(2,1)S(1)}, u32[]{:S(2)}, u32[]{:S(2)}) collective-permute-start(bf16[2,96,2048]{2,1,0:T(8,128)(2,1)S(1)} %pad_maximum_fusion.4), channel_id=1, source_target_pairs={{0,8},{2,10},{4,12},{6,14},{8,0},{10,2},{12,4},{14,6},{16,24},{18,... | collective-permute-start | bytes 2359304 | tf_op jit(solution)/shard_map/ppermute | solution.py:78
  125.8 28.1 %collective-permute-start.25 = (bf16[2,96,1536]{2,1,0:T(8,128)(2,1)S(1)}, bf16[2,96,1536]{2,1,0:T(8,128)(2,1)S(1)}, u32[]{:S(2)}, u32[]{:S(2)}) collective-permute-start(bf16[2,96,1536]{2,1,0:T(8,128)(2,1)S(1)} %slice.108), channel_id=1, source_target_pairs={{0,4},{2,6},{4,0},{6,2},{8,12},{10,14},{12,8},{14,10},{16,20},{18,... | collective-permute-start | bytes 1769480 | tf_op jit(solution)/shard_map/ppermute | solution.py:78
  130.1 23.9 %collective-permute-start.26 = (bf16[2,96,1536]{2,1,0:T(8,128)(2,1)S(1)}, bf16[2,96,1536]{2,1,0:T(8,128)(2,1)S(1)}, u32[]{:S(2)}, u32[]{:S(2)}) collective-permute-start(bf16[2,96,1536]{2,1,0:T(8,128)(2,1)S(1)} %slice.109), channel_id=1, source_target_pairs={{0,2},{2,0},{4,6},{6,4},{8,10},{10,8},{12,14},{14,12},{16,18},{18,... | collective-permute-start | bytes 1769480 | tf_op jit(solution)/shard_map/ppermute | solution.py:78
  154.0 33.4 %collective-permute-start.35 = (bf16[4,96,2048]{2,1,0:T(8,128)(2,1)S(1)}, bf16[4,96,2048]{2,1,0:T(8,128)(2,1)S(1)}, u32[]{:S(2)}, u32[]{:S(2)}) collective-permute-start(bf16[4,96,2048]{2,1,0:T(8,128)(2,1)S(1)} %pad_maximum_fusion.refs_1_.refs_2_), channel_id=1, source_target_pairs={{0,2},{2,0},{4,6},{6,4},{8,10},{10,8},{12,14},{14,12},{16,18},{18,... | collective-permute-start | bytes 4718600 | tf_op jit(solution)/shard_map/ppermute | solution.py:78
  156.1 35.2 %collective-permute-start.37 = (bf16[4,96,2048]{2,1,0:T(8,128)(2,1)S(1)}, bf16[4,96,2048]{2,1,0:T(8,128)(2,1)S(1)}, u32[]{:S(2)}, u32[]{:S(2)}) collective-permute-start(bf16[4,96,2048]{2,1,0:T(8,128)(2,1)S(1)} %pad_maximum_fusion.refs_1_.refs_2_), channel_id=1, source_target_pairs={{0,4},{2,6},{4,0},{6,2},{8,12},{10,14},{12,8},{14,10},{16,20},{18,... | collective-permute-start | bytes 4718600 | tf_op jit(solution)/shard_map/ppermute | solution.py:78
  172.1 42.4 %collective-permute-start.34 = (bf16[2,96,2048]{2,1,0:T(8,128)(2,1)S(1)}, bf16[2,96,2048]{2,1,0:T(8,128)(2,1)}, u32[]{:S(2)}, u32[]{:S(2)}) collective-permute-start(bf16[2,96,2048]{2,1,0:T(8,128)(2,1)S(1)} %pad_maximum_fusion.5), channel_id=1, source_target_pairs={{0,8},{2,10},{4,12},{6,14},{8,0},{10,2},{12,4},{14,6},{16,24},{18,... | collective-permute-start | bytes 2359304 | tf_op jit(solution)/shard_map/ppermute | solution.py:78
  187.5 29.5 %collective-permute-start.36 = (bf16[2,96,2048]{2,1,0:T(8,128)(2,1)S(1)}, bf16[2,96,2048]{2,1,0:T(8,128)(2,1)S(1)}, u32[]{:S(2)}, u32[]{:S(2)}) collective-permute-start(bf16[2,96,2048]{2,1,0:T(8,128)(2,1)S(1)} %slice.111), channel_id=1, source_target_pairs={{0,4},{2,6},{4,0},{6,2},{8,12},{10,14},{12,8},{14,10},{16,20},{18,... | collective-permute-start | bytes 2359304 | tf_op jit(solution)/shard_map/ppermute | solution.py:78
  191.3 26.5 %collective-permute-start.38 = (bf16[2,96,2048]{2,1,0:T(8,128)(2,1)S(1)}, bf16[2,96,2048]{2,1,0:T(8,128)(2,1)S(1)}, u32[]{:S(2)}, u32[]{:S(2)}) collective-permute-start(bf16[2,96,2048]{2,1,0:T(8,128)(2,1)S(1)} %slice.112), channel_id=1, source_target_pairs={{0,2},{2,0},{4,6},{6,4},{8,10},{10,8},{12,14},{14,12},{16,18},{18,... | collective-permute-start | bytes 2359304 | tf_op jit(solution)/shard_map/ppermute | solution.py:78
  218.7 43.3 %collective-permute-start.39 = (bf16[4,96,2048]{2,1,0:T(8,128)(2,1)}, bf16[4,96,2048]{2,1,0:T(8,128)(2,1)}, u32[]{:S(2)}, u32[]{:S(2)}) collective-permute-start(bf16[4,96,2048]{2,1,0:T(8,128)(2,1)} %pad_maximum_fusion.1.refs_1_.refs_7_), channel_id=1, source_target_pairs={{0,2},{2,0},{4,6},{6,4},{8,10},{10,8},{12,14},{14,12},{16,18},{18,... | collective-permute-start | bytes 4718600 | tf_op jit(solution)/shard_map/ppermute | solution.py:78
  220.4 44.1 %collective-permute-start.40 = (bf16[4,96,2048]{2,1,0:T(8,128)(2,1)}, bf16[4,96,2048]{2,1,0:T(8,128)(2,1)}, u32[]{:S(2)}, u32[]{:S(2)}) collective-permute-start(bf16[4,96,2048]{2,1,0:T(8,128)(2,1)} %pad_maximum_fusion.1.refs_1_.refs_7_), channel_id=1, source_target_pairs={{0,4},{2,6},{4,0},{6,2},{8,12},{10,14},{12,8},{14,10},{16,20},{18,... | collective-permute-start | bytes 4718600 | tf_op jit(solution)/shard_map/ppermute | solution.py:78
  284.7 34.8 %collective-permute-start.47 = (bf16[4,96,2048]{2,1,0:T(8,128)(2,1)S(1)}, bf16[4,96,2048]{2,1,0:T(8,128)(2,1)S(1)}, u32[]{:S(2)}, u32[]{:S(2)}) collective-permute-start(bf16[4,96,2048]{2,1,0:T(8,128)(2,1)S(1)} %pad_maximum_fusion.2.refs_1_), channel_id=1, source_target_pairs={{0,2},{2,0},{4,6},{6,4},{8,10},{10,8},{12,14},{14,12},{16,18},{18,... | collective-permute-start | bytes 4718600 | tf_op jit(solution)/shard_map/ppermute | solution.py:78
  285.1 36.3 %collective-permute-start.48 = (bf16[4,96,2048]{2,1,0:T(8,128)(2,1)S(1)}, bf16[4,96,2048]{2,1,0:T(8,128)(2,1)S(1)}, u32[]{:S(2)}, u32[]{:S(2)}) collective-permute-start(bf16[4,96,2048]{2,1,0:T(8,128)(2,1)S(1)} %pad_maximum_fusion.2.refs_1_), channel_id=1, source_target_pairs={{0,4},{2,6},{4,0},{6,2},{8,12},{10,14},{12,8},{14,10},{16,20},{18,... | collective-permute-start | bytes 4718600 | tf_op jit(solution)/shard_map/ppermute | solution.py:78
  285.9 37.0 %collective-permute-start.43 = (bf16[512,1536]{1,0:T(8,128)(2,1)S(1)}, bf16[512,1536]{1,0:T(8,128)(2,1)S(1)}, u32[]{:S(2)}, u32[]{:S(2)}) collective-permute-start(bf16[512,1536]{1,0:T(8,128)(2,1)S(1)} %copy-done.44), channel_id=1, source_target_pairs={{0,1},{1,0},{2,3},{3,2},{4,5},{5,4},{6,7},{7,6},{8,9},{9,8},{10,11... | collective-permute-start | bytes 4718600 | tf_op jit(solution)/shard_map/ppermute | solution.py:51
  320.6 31.5 %collective-permute-start.49 = (bf16[2,96,2048]{2,1,0:T(8,128)(2,1)}, bf16[2,96,2048]{2,1,0:T(8,128)(2,1)S(1)}, u32[]{:S(2)}, u32[]{:S(2)}) collective-permute-start(bf16[2,96,2048]{2,1,0:T(8,128)(2,1)} %slice.115), channel_id=1, source_target_pairs={{0,4},{2,6},{4,0},{6,2},{8,12},{10,14},{12,8},{14,10},{16,20},{18,... | collective-permute-start | bytes 2359304 | tf_op jit(solution)/shard_map/ppermute | solution.py:78
  322.5 29.6 %collective-permute-start.50 = (bf16[2,96,2048]{2,1,0:T(8,128)(2,1)}, bf16[2,96,2048]{2,1,0:T(8,128)(2,1)S(1)}, u32[]{:S(2)}, u32[]{:S(2)}) collective-permute-start(bf16[2,96,2048]{2,1,0:T(8,128)(2,1)} %slice.116), channel_id=1, source_target_pairs={{0,2},{2,0},{4,6},{6,4},{8,10},{10,8},{12,14},{14,12},{16,18},{18,... | collective-permute-start | bytes 2359304 | tf_op jit(solution)/shard_map/ppermute | solution.py:78
  351.7 80.8 %collective-permute-start.44 = (bf16[2,4,96,2048]{3,2,1,0:T(8,128)(2,1)}, bf16[2,4,96,2048]{3,2,1,0:T(8,128)(2,1)}, u32[]{:S(2)}, u32[]{:S(2)}) collective-permute-start(bf16[2,4,96,2048]{3,2,1,0:T(8,128)(2,1)} %get-tuple-element.211), channel_id=1, source_target_pairs={{0,8},{2,10},{4,12},{6,14},{8,0},{10,2},{12,4},{14,6},{16,24},{18,... | collective-permute-start | bytes 9437192 | tf_op jit(solution)/shard_map/ppermute | solution.py:78
  394.1 74.6 %collective-permute-start.57 = (bf16[4,2,96,2048]{3,2,1,0:T(8,128)(2,1)}, bf16[4,2,96,2048]{3,2,1,0:T(8,128)(2,1)}, u32[]{:S(2)}, u32[]{:S(2)}) collective-permute-start(bf16[4,2,96,2048]{3,2,1,0:T(8,128)(2,1)} %copy-done.99), channel_id=1, source_target_pairs={{0,4},{2,6},{4,0},{6,2},{8,12},{10,14},{12,8},{14,10},{16,20},{18,... | collective-permute-start | bytes 9437192 | tf_op jit(solution)/shard_map/ppermute | solution.py:78
  395.3 73.4 %collective-permute-start.56 = (bf16[4,2,96,2048]{3,2,1,0:T(8,128)(2,1)S(1)}, bf16[4,2,96,2048]{3,2,1,0:T(8,128)(2,1)}, u32[]{:S(2)}, u32[]{:S(2)}) collective-permute-start(bf16[4,2,96,2048]{3,2,1,0:T(8,128)(2,1)S(1)} %get-tuple-element.221), channel_id=1, source_target_pairs={{0,2},{2,0},{4,6},{6,4},{8,10},{10,8},{12,14},{14,12},{16,18},{18,... | collective-permute-start | bytes 9437192 | tf_op jit(solution)/shard_map/ppermute | solution.py:78
  414.5 22.8 %collective-permute-start.53 = (bf16[512,768]{1,0:T(8,128)(2,1)}, bf16[512,768]{1,0:T(8,128)(2,1)S(1)}, u32[]{:S(2)}, u32[]{:S(2)}) collective-permute-start(bf16[512,768]{1,0:T(8,128)(2,1)} %get-tuple-element.230), channel_id=1, source_target_pairs={{0,1},{1,0},{2,3},{3,2},{4,5},{5,4},{6,7},{7,6},{8,9},{9,8},{10,11... | collective-permute-start | bytes 2359304 | tf_op jit(solution)/shard_map/ppermute | solution.py:51
  450.1 80.5 %collective-permute-start.51 = (bf16[1,384,2048]{2,1,0:T(8,128)(2,1)S(1)}, bf16[1,384,2048]{2,1,0:T(8,128)(2,1)}, u32[]{:S(2)}, u32[]{:S(2)}) collective-permute-start(bf16[1,384,2048]{2,1,0:T(8,128)(2,1)S(1)} %get-tuple-element.227), channel_id=1, source_target_pairs={{0,16},{2,18},{4,20},{6,22},{8,24},{10,26},{12,28},{14,30},{16,0},... | collective-permute-start | bytes 4718600 | tf_op jit(solution)/shard_map/ppermute | solution.py:78
  473.8 61.0 %collective-permute-start.60 = (bf16[4,96,2048]{2,1,0:T(8,128)(2,1)S(1)}, bf16[4,96,2048]{2,1,0:T(8,128)(2,1)}, u32[]{:S(2)}, u32[]{:S(2)}) collective-permute-start(bf16[4,96,2048]{2,1,0:T(8,128)(2,1)S(1)} %get-tuple-element.242), channel_id=1, source_target_pairs={{0,4},{2,6},{4,0},{6,2},{8,12},{10,14},{12,8},{14,10},{16,20},{18,... | collective-permute-start | bytes 4718600 | tf_op jit(solution)/shard_map/ppermute | solution.py:78
  479.6 55.2 %collective-permute-start.59 = (bf16[4,96,2048]{2,1,0:T(8,128)(2,1)S(1)}, bf16[4,96,2048]{2,1,0:T(8,128)(2,1)}, u32[]{:S(2)}, u32[]{:S(2)}) collective-permute-start(bf16[4,96,2048]{2,1,0:T(8,128)(2,1)S(1)} %get-tuple-element.245), channel_id=1, source_target_pairs={{0,2},{2,0},{4,6},{6,4},{8,10},{10,8},{12,14},{14,12},{16,18},{18,... | collective-permute-start | bytes 4718600 | tf_op jit(solution)/shard_map/ppermute | solution.py:78
  492.6 64.1 %collective-permute-start.62 = (bf16[2,2,96,1536]{3,2,1,0:T(8,128)(2,1)}, bf16[2,2,96,1536]{3,2,1,0:T(8,128)(2,1)}, u32[]{:S(2)}, u32[]{:S(2)}) collective-permute-start(bf16[2,2,96,1536]{3,2,1,0:T(8,128)(2,1)} %get-tuple-element.248), channel_id=1, source_target_pairs={{0,2},{2,0},{4,6},{6,4},{8,10},{10,8},{12,14},{14,12},{16,18},{18,... | collective-permute-start | bytes 3538952 | tf_op jit(solution)/shard_map/ppermute | solution.py:78
  494.2 62.5 %collective-permute-start.61 = (bf16[2,2,96,1536]{3,2,1,0:T(8,128)(2,1)}, bf16[2,2,96,1536]{3,2,1,0:T(8,128)(2,1)}, u32[]{:S(2)}, u32[]{:S(2)}) collective-permute-start(bf16[2,2,96,1536]{3,2,1,0:T(8,128)(2,1)} %get-tuple-element.247), channel_id=1, source_target_pairs={{0,4},{2,6},{4,0},{6,2},{8,12},{10,14},{12,8},{14,10},{16,20},{18,... | collective-permute-start | bytes 3538952 | tf_op jit(solution)/shard_map/ppermute | solution.py:78
  534.0 37.6 %collective-permute-start.58 = (bf16[1,192,2048]{2,1,0:T(8,128)(2,1)S(1)}, bf16[1,192,2048]{2,1,0:T(8,128)(2,1)S(1)}, u32[]{:S(2)}, u32[]{:S(2)}) collective-permute-start(bf16[1,192,2048]{2,1,0:T(8,128)(2,1)S(1)} %get-tuple-element.254), channel_id=1, source_target_pairs={{0,4},{2,6},{4,0},{6,2},{8,12},{10,14},{12,8},{14,10},{16,20},{18,... | collective-permute-start | bytes 2359304 | tf_op jit(solution)/shard_map/ppermute | solution.py:78
  540.7 76.6 %collective-permute-start.63 = (bf16[2,96,4096]{2,1,0:T(8,128)(2,1)}, bf16[2,96,4096]{2,1,0:T(8,128)(2,1)}, u32[]{:S(2)}, u32[]{:S(2)}) collective-permute-start(bf16[2,96,4096]{2,1,0:T(8,128)(2,1)} %get-tuple-element.260), channel_id=1, source_target_pairs={{0,8},{2,10},{4,12},{6,14},{8,0},{10,2},{12,4},{14,6},{16,24},{18,... | collective-permute-start | bytes 4718600 | tf_op jit(solution)/shard_map/ppermute | solution.py:78
  554.5 62.7 %collective-permute-start.65 = (bf16[2,2,96,1536]{3,2,1,0:T(8,128)(2,1)}, bf16[2,2,96,1536]{3,2,1,0:T(8,128)(2,1)}, u32[]{:S(2)}, u32[]{:S(2)}) collective-permute-start(bf16[2,2,96,1536]{3,2,1,0:T(8,128)(2,1)} %get-tuple-element.264), channel_id=1, source_target_pairs={{0,2},{2,0},{4,6},{6,4},{8,10},{10,8},{12,14},{14,12},{16,18},{18,... | collective-permute-start | bytes 3538952 | tf_op jit(solution)/shard_map/ppermute | solution.py:78
  573.9 48.9 %collective-permute-start.64 = (bf16[2,2,96,1536]{3,2,1,0:T(8,128)(2,1)}, bf16[2,2,96,1536]{3,2,1,0:T(8,128)(2,1)}, u32[]{:S(2)}, u32[]{:S(2)}) collective-permute-start(bf16[2,2,96,1536]{3,2,1,0:T(8,128)(2,1)} %get-tuple-element.263), channel_id=1, source_target_pairs={{0,4},{2,6},{4,0},{6,2},{8,12},{10,14},{12,8},{14,10},{16,20},{18,... | collective-permute-start | bytes 3538952 | tf_op jit(solution)/shard_map/ppermute | solution.py:78
  575.1 40.0 %collective-permute-start.73 = (bf16[2,96,1536]{2,1,0:T(8,128)(2,1)S(1)}, bf16[2,96,1536]{2,1,0:T(8,128)(2,1)S(1)}, u32[]{:S(2)}, u32[]{:S(2)}) collective-permute-start(bf16[2,96,1536]{2,1,0:T(8,128)(2,1)S(1)} %get-tuple-element.270), channel_id=1, source_target_pairs={{0,4},{2,6},{4,0},{6,2},{8,12},{10,14},{12,8},{14,10},{16,20},{18,... | collective-permute-start | bytes 1769480 | tf_op jit(solution)/shard_map/ppermute | solution.py:78
  589.4 26.6 %collective-permute-start.72 = (bf16[2,96,1536]{2,1,0:T(8,128)(2,1)S(1)}, bf16[2,96,1536]{2,1,0:T(8,128)(2,1)S(1)}, u32[]{:S(2)}, u32[]{:S(2)}) collective-permute-start(bf16[2,96,1536]{2,1,0:T(8,128)(2,1)S(1)} %get-tuple-element.267), channel_id=1, source_target_pairs={{0,2},{2,0},{4,6},{6,4},{8,10},{10,8},{12,14},{14,12},{16,18},{18,... | collective-permute-start | bytes 1769480 | tf_op jit(solution)/shard_map/ppermute | solution.py:78
  615.9 32.8 %collective-permute-start.68 = (bf16[512,768]{1,0:T(8,128)(2,1)}, bf16[512,768]{1,0:T(8,128)(2,1)}, u32[]{:S(2)}, u32[]{:S(2)}) collective-permute-start(bf16[512,768]{1,0:T(8,128)(2,1)} %get-tuple-element.284), channel_id=1, source_target_pairs={{0,1},{1,0},{2,3},{3,2},{4,5},{5,4},{6,7},{7,6},{8,9},{9,8},{10,11... | collective-permute-start | bytes 2359304 | tf_op jit(solution)/shard_map/ppermute | solution.py:51
  616.8 33.2 %collective-permute-start.69 = (bf16[512,768]{1,0:T(8,128)(2,1)}, bf16[512,768]{1,0:T(8,128)(2,1)}, u32[]{:S(2)}, u32[]{:S(2)}) collective-permute-start(bf16[512,768]{1,0:T(8,128)(2,1)} %get-tuple-element.285), channel_id=1, source_target_pairs={{0,1},{1,0},{2,3},{3,2},{4,5},{5,4},{6,7},{7,6},{8,9},{9,8},{10,11... | collective-permute-start | bytes 2359304 | tf_op jit(solution)/shard_map/ppermute | solution.py:51
  617.3 34.4 %collective-permute-start.66 = (bf16[512,768]{1,0:T(8,128)(2,1)}, bf16[512,768]{1,0:T(8,128)(2,1)}, u32[]{:S(2)}, u32[]{:S(2)}) collective-permute-start(bf16[512,768]{1,0:T(8,128)(2,1)} %get-tuple-element.280), channel_id=1, source_target_pairs={{0,1},{1,0},{2,3},{3,2},{4,5},{5,4},{6,7},{7,6},{8,9},{9,8},{10,11... | collective-permute-start | bytes 2359304 | tf_op jit(solution)/shard_map/ppermute | solution.py:51
  617.3 34.8 %collective-permute-start.67 = (bf16[512,768]{1,0:T(8,128)(2,1)}, bf16[512,768]{1,0:T(8,128)(2,1)}, u32[]{:S(2)}, u32[]{:S(2)}) collective-permute-start(bf16[512,768]{1,0:T(8,128)(2,1)} %get-tuple-element.281), channel_id=1, source_target_pairs={{0,1},{1,0},{2,3},{3,2},{4,5},{5,4},{6,7},{7,6},{8,9},{9,8},{10,11... | collective-permute-start | bytes 2359304 | tf_op jit(solution)/shard_map/ppermute | solution.py:51
  622.8 67.3 %collective-permute-start.87 = (bf16[1,96,4096]{2,1,0:T(8,128)(2,1)}, bf16[1,96,4096]{2,1,0:T(8,128)(2,1)}, u32[]{:S(2)}, u32[]{:S(2)}) collective-permute-start(bf16[1,96,4096]{2,1,0:T(8,128)(2,1)} %get-tuple-element.287), channel_id=1, source_target_pairs={{0,16},{2,18},{4,20},{6,22},{8,24},{10,26},{12,28},{14,30},{16,0},... | collective-permute-start | bytes 2359304 | tf_op jit(solution)/shard_map/ppermute | solution.py:78
  648.7 28.5 %collective-permute-start.71 = (bf16[2,96,1536]{2,1,0:T(8,128)(2,1)}, bf16[2,96,1536]{2,1,0:T(8,128)(2,1)}, u32[]{:S(2)}, u32[]{:S(2)}) collective-permute-start(bf16[2,96,1536]{2,1,0:T(8,128)(2,1)} %get-tuple-element.293), channel_id=1, source_target_pairs={{0,4},{2,6},{4,0},{6,2},{8,12},{10,14},{12,8},{14,10},{16,20},{18,... | collective-permute-start | bytes 1769480 | tf_op jit(solution)/shard_map/ppermute | solution.py:78
  650.0 28.3 %collective-permute-start.70 = (bf16[2,96,1536]{2,1,0:T(8,128)(2,1)}, bf16[2,96,1536]{2,1,0:T(8,128)(2,1)}, u32[]{:S(2)}, u32[]{:S(2)}) collective-permute-start(bf16[2,96,1536]{2,1,0:T(8,128)(2,1)} %get-tuple-element.290), channel_id=1, source_target_pairs={{0,2},{2,0},{4,6},{6,4},{8,10},{10,8},{12,14},{14,12},{16,18},{18,... | collective-permute-start | bytes 1769480 | tf_op jit(solution)/shard_map/ppermute | solution.py:78
  651.7 28.1 %collective-permute-start.76 = (bf16[2,2,96,896]{3,2,1,0:T(8,128)(2,1)}, bf16[2,2,96,896]{3,2,1,0:T(8,128)(2,1)}, u32[]{:S(2)}, u32[]{:S(2)}) collective-permute-start(bf16[2,2,96,896]{3,2,1,0:T(8,128)(2,1)} %get-tuple-element.315), channel_id=1, source_target_pairs={{0,2},{2,0},{4,6},{6,4},{8,10},{10,8},{12,14},{14,12},{16,18},{18,... | collective-permute-start | bytes 2064392 | tf_op jit(solution)/shard_map/ppermute | solution.py:78
  652.0 32.5 %collective-permute-start.74 = (bf16[2,2,96,896]{3,2,1,0:T(8,128)(2,1)}, bf16[2,2,96,896]{3,2,1,0:T(8,128)(2,1)}, u32[]{:S(2)}, u32[]{:S(2)}) collective-permute-start(bf16[2,2,96,896]{3,2,1,0:T(8,128)(2,1)} %get-tuple-element.309), channel_id=1, source_target_pairs={{0,4},{2,6},{4,0},{6,2},{8,12},{10,14},{12,8},{14,10},{16,20},{18,... | collective-permute-start | bytes 2064392 | tf_op jit(solution)/shard_map/ppermute | solution.py:78
  677.2 25.1 %collective-permute-start.81 = (bf16[2,96,1536]{2,1,0:T(8,128)(2,1)S(1)}, bf16[2,96,1536]{2,1,0:T(8,128)(2,1)S(1)}, u32[]{:S(2)}, u32[]{:S(2)}) collective-permute-start(bf16[2,96,1536]{2,1,0:T(8,128)(2,1)S(1)} %copy-done.103), channel_id=1, source_target_pairs={{0,8},{2,10},{4,12},{6,14},{8,0},{10,2},{12,4},{14,6},{16,24},{18,... | collective-permute-start | bytes 1769480 | tf_op jit(solution)/shard_map/ppermute | solution.py:78
  699.8 26.5 %collective-permute-start.78 = (bf16[2,96,2432]{2,1,0:T(8,128)(2,1)}, bf16[2,96,2432]{2,1,0:T(8,128)(2,1)S(1)}, u32[]{:S(2)}, u32[]{:S(2)}) collective-permute-start(bf16[2,96,2432]{2,1,0:T(8,128)(2,1)} %get-tuple-element.321), channel_id=1, source_target_pairs={{0,8},{2,10},{4,12},{6,14},{8,0},{10,2},{12,4},{14,6},{16,24},{18,... | collective-permute-start | bytes 2801672 | tf_op jit(solution)/shard_map/ppermute | solution.py:78
  (159 other events, 2968.7 us)

commit v4 on v3

--- a/solution.py
+++ b/solution.py
@@ -311,7 +311,7 @@
         self.far_codes = self.moved(self.codes, 1 << last)
         return self
 
-    def plane(self, *after, fine=False):
+    def plane(self, *after, fine=False, to_end=True):
         grid, near, far, codes, far_codes = (
             self.grid,
             self.near,
@@ -339,15 +339,21 @@
             sides = [(both, block), (moved(both, 1), side_x), (moved(both, 2), side_y)]
             received = ()
             self.block = block
+        self.corner_parts, self.received, self.sides = (near_x, far_y), received, sides
+        return self.plane_end() if to_end else self
+
+    def plane_end(self, *after):
+        grid, codes, far_codes = self.grid, self.codes, self.far_codes
+        moved, sides = self.moved, self.sides
+        near_x, far_y = [tie(part, *after) for part in self.corner_parts]
         near_corner, far_corner = grid.swap(near_x, 1), grid.swap(far_y, 0)
-        self.corners = (near_corner, far_corner, *received)
-        self.corner_parts = (near_x, far_y)
+        self.corners = (near_corner, far_corner, *self.received)
         corners = [(moved(codes, 3), near_corner), (moved(far_codes, 3), far_corner)]
         self.weight = Weight(grid, sides + corners)
         return self
 
 
-def gradient_parts(grid, pairs, tiles, form):
+def gradient_parts(grid, pairs, tiles, form, extra=None):
     depth, length = pairs[0][0].shape
     rows, line = depth // grid.count, grid.count // 4
     width = sum(right.shape[1] for _, right in pairs)
@@ -365,6 +371,8 @@
     def body(*refs):
         left_refs, refs = refs[: len(lefts)], refs[len(lefts) :]
         right_refs, refs = refs[: len(pairs)], refs[len(pairs) :]
+        if extra is not None:
+            extra_ref, refs = refs[0], refs[1:]
         outs, total = refs[:-1], refs[-1]
         step = pl.program_id(0)
         if tiles == 1:
@@ -384,6 +392,8 @@
                 def _():
                     total[...] = matmul(left_refs[which[place]][...], right_refs[place][...])
 
+        if extra is not None:
+            total[:, tile - extra.shape[1] :] += extra_ref[...]
         index = lax.axis_index("dp")
 
         def block(place):
@@ -425,13 +435,14 @@
         body,
         grid=(tiles,),
         in_specs=[pl.BlockSpec((depth, length), lambda step: (0, 0))] * len(lefts)
-        + [right_spec(place) for place in range(len(pairs))],
+        + [right_spec(place) for place in range(len(pairs))]
+        + ([] if extra is None else [pl.BlockSpec(extra.shape, lambda step: (0, 0))]),
         out_specs=[out_spec] * parts,
         out_shape=[out] * parts,
         scratch_shapes=[pltpu.VMEM((depth, tile), jnp.float32)],
         cost_estimate=small_cost(2 * depth * length * width, size),
         compiler_params=pltpu.CompilerParams(vmem_limit_bytes=VMEM_LIMIT),
-    )(*lefts, *[right for _, right in pairs])
+    )(*lefts, *[right for _, right in pairs], *([] if extra is None else [extra]))
 
 
 def pick(array, axis, place):
@@ -455,13 +466,15 @@
     return low[0], high[0], low[1], high[1]
 
 
-def weight_gradient(grid, pairs, tiles, form):
+def weight_gradient(grid, pairs, tiles, form, extra=None):
     rows = pairs[0][0].shape[0] // grid.count
     if rows % 16 == 0:
-        parts = gradient_parts(grid, pairs, tiles, form)
+        parts = gradient_parts(grid, pairs, tiles, form, extra)
     else:
-        found = [lower(matmul(left, right)) for left, right in pairs]
-        parts = cut_parts(grid, jnp.concatenate(found, axis=1), form)
+        found = [matmul(left, right) for left, right in pairs]
+        if extra is not None:
+            found[-1] = found[-1] + extra
+        parts = cut_parts(grid, lower(jnp.concatenate(found, axis=1)), form)
     return BitSum(grid, parts) if form == "line" else PlaneSum(grid, parts, form)
 
 
@@ -616,12 +629,12 @@
     unit, inverse = statistics(wide(source))
     grad = own + both_parts(first, second)
     total = wide(base) + norm_backward(unit, inverse, gain, grad)
-    return total, lower(total), jnp.sum(grad * unit, axis=0, keepdims=True)
+    return total, lower(total)
 
 
 def norm_gradient_halves(*values):
-    total, rounded, summed = norm_gradient(*values)
-    return total, *halves(rounded), summed
+    total, rounded = norm_gradient(*values)
+    return total, *halves(rounded)
 
 
 class PlaneSum:
@@ -706,23 +719,6 @@
 
     def result(self):
         return sum(wide(term[0]) for term in self.packs[0][0])
-
-
-class SmallSum:
-    def __init__(self, grid, array):
-        rows = array.shape[0] // grid.count
-        self.grid, self.terms = grid, [array.reshape(grid.count, rows, array.shape[1])]
-
-    def step(self, number, *after):
-        terms = [tie(t, *after).reshape((t.shape[0] // 2, 2) + t.shape[1:]) for t in self.terms]
-        side = self.grid.bit(number)
-        self.sent = sum(pick(t, 1, 1 - side) for t in terms)
-        kept = sum(pick(t, 1, side) for t in terms)
-        self.terms = [kept, self.grid.swap(self.sent, number)]
-        return self
-
-    def result(self):
-        return sum(term[0] for term in self.terms)
 
 
 def running_sum(values, reverse):
@@ -970,7 +966,7 @@
         jnp.concatenate([own_gains, other_gains], axis=1),
         jnp.concatenate([other_gains, own_gains], axis=1),
     )[None]
-    gain_codes = [0]
+    pair_gains, gain_codes = gains[0], [0]
     for number in range(len(grid.line_bits) + 2):
         gains = jnp.concatenate([gains, grid.swap(gains, number)], axis=0)
         gain_codes = gain_codes + [code ^ (1 << number) for code in gain_codes]
@@ -1029,11 +1025,12 @@
     )
     bias_lanes = jnp.pad(forget_bias, (0, LANES - heads_here))[None]
     decay_row, decay_column = decays(forget_logit, bias_lanes, heads_here, LANES // head_size)
-    load_gate.plane(*load_go.corners, decay_row, qk)
-    load_up.line_end(load_gate.block)
+    load_gate.plane(*load_go.corners, qk, to_end=False)
+    load_up.line_end(load_gate.block, decay_row, values_all)
     qk = tie(qk, load_gate.block)
     attended, logsum = attend(qk, values_all, decay_column, decay_row, head_size)
-    load_up.plane(*load_gate.corners, attended)
+    load_gate.plane_end(attended)
+    load_up.plane(*load_gate.corners)
     load_down = Gather(grid, lower(w_down).T, load_up.far, load_gate.corners[0])
     load_down.line_end(load_up.block)
     mlp_gate, mlp_up = load_gate.weight, load_up.weight
@@ -1095,11 +1092,10 @@
     (own_part,) = multiply_back(back, jnp.int32(0))
     sum_down.line(own_part)
     own_part = tie(own_part, sum_down.sent)
-    grad_middle, own_branch, *sent, gain_mlp_part = row_kernel(
+    grad_middle, own_branch, *sent = row_kernel(
         norm_gradient_halves,
         [middle, own_part, *arrived, cotangent, gain_mlp],
         [(columns, jnp.float32)] + rounded_outs,
-        sums=1,
     )
     other_branch = exchanged(sent)
     grad_branch, grad_branch_t = joined_rows(own_branch, other_branch, True)
@@ -1136,16 +1132,21 @@
     grad_forget, bias_part = forget_backward(
         row_total, column_total, forget_logit, bias_lanes, heads_here
     )
+    bias_block = jnp.pad(
+        bias_part[0, :heads_here, None],
+        ((0, w_forget.shape[0] - heads_here), (heads_here, LANES - heads_here - 1)),
+    )
+    bias_extra = jnp.tile(bias_block, (grid.count, 1))
     grad_values = tie(grad_values, *sum_qk.sent, *sum_go.sent)
     sum_vf = weight_gradient(
-        grid, [(normed_attn_t, grad_values), (normed_attn_t, grad_forget)], 1, "halves"
-    )
-    sum_down.step(0, *sum_vf.sent)
-    hidden = tie(hidden, sum_down.sent)
-    other_down = multiply_back([(hidden, mlp_down)], jnp.int32(1), low, 2)
-    arrived_down = exchanged(other_down)
+        grid,
+        [(normed_attn_t, grad_values), (normed_attn_t, grad_forget)],
+        1,
+        "halves",
+        bias_extra,
+    )
     back = [
-        (tie(grad_gate_logit, *other_down), gate_w),
+        (tie(grad_gate_logit, *sum_vf.sent), gate_w),
         (grad_queries, query_w),
         (grad_keys, key_w),
         (grad_values, value_w),
@@ -1153,47 +1154,55 @@
     ]
     other_part = multiply_back(back, 1 - side, low, 2)
     arrived = exchanged(other_part)
-    sum_qk.second(*other_part)
-    line_mlp.fourth(*other_part)
+    hidden = tie(hidden, *other_part)
+    other_down = multiply_back([(hidden, mlp_down)], jnp.int32(1), low, 2)
+    arrived_down = exchanged(other_down)
+    sum_qk.second(*other_down)
+    line_mlp.fourth(*other_down)
+    sum_vf.start(*sum_qk.sent)
     back[1] = (tie(grad_queries, line_mlp.sent, *sum_qk.sent), query_w)
     (own_part,) = multiply_back(back, side)
-    (own_down,) = multiply_back([(tie(hidden, own_part), mlp_down)], jnp.int32(0))
+    line_go = LineSum(grid, [sum_go]).third(own_part)
+    own_part = tie(own_part, line_go.sent)
+    _, tokens_grad = row_kernel(
+        norm_gradient,
+        [tokens, own_part, *arrived, grad_middle, gain_attn],
+        [(columns, jnp.float32), (columns, low)],
+    )
+    sum_vf.second(tokens_grad)
+    line_qkv = LineSum(grid, [sum_qk, sum_vf]).third()
+    (own_down,) = multiply_back([(tie(hidden, line_qkv.sent), mlp_down)], jnp.int32(0))
     (mixed,) = row_kernel(
         lambda middle, own, *parts: (lower(middle + (own + both_parts(*parts))),),
         [middle, own_down, *arrived_down],
         [(columns, low)],
     )
-    line_go = LineSum(grid, [sum_go]).third(own_part)
-    sum_vf.start(own_part, line_go.sent)
-    _, tokens_grad, gain_attn_part = row_kernel(
-        norm_gradient,
-        [tokens, own_part, *arrived, grad_middle, gain_attn],
-        [(columns, jnp.float32), (columns, low)],
-        sums=1,
-    )
-    small = jnp.concatenate(
-        [
-            gain_attn_part.reshape(grid.count, -1),
-            gain_mlp_part.reshape(grid.count, -1),
-            jnp.broadcast_to(bias_part[:, :heads_here], (grid.count, heads_here)),
-        ],
-        axis=1,
-    )
-    sum_vf.second(gain_attn_part)
-    line_qkv = LineSum(grid, [sum_qk, sum_vf]).third(gain_attn_part)
+    line_qkv.fourth(own_down)
     line_go.fourth(line_qkv.sent)
-    sum_small = SmallSum(grid, small).step(0, line_qkv.sent).step(1)
-    line_qkv.fourth(sum_small.sent)
-    for number in grid.line_bits:
-        sum_small.step(number, line_qkv.sent)
+    sum_down.step(0, line_qkv.sent)
     down_grad, go_grad, qkv_grad = sum_down.result().T, line_go.result(), line_qkv.result()
     mlp_grad = line_mlp.result()
-    small_sum = sum_small.result().reshape(-1)
-    share = norm_attn.shape[0]
-    gain_sums = small_sum[: 4 * share].reshape(2, 2, share)
-    other_sums = lax.dynamic_index_in_dim(gain_sums, 1 - side, 1, keepdims=False)
-    own_sums = lax.dynamic_index_in_dim(gain_sums, side, 1, keepdims=False)
-    gain_grads = own_sums + partner(other_sums)
+
+    def gain_gradient(gain, *pairs):
+        return sum(jnp.sum(wide(lower(w)) * grad, axis=1) for w, grad in pairs) / gain
+
+    forget_at = 3 * width
+    parts = jnp.stack(
+        [
+            gain_gradient(
+                pair_gains[0],
+                (w_query, qkv_grad[:, :width]),
+                (w_key, qkv_grad[:, width : 2 * width]),
+                (w_value, qkv_grad[:, 2 * width : forget_at]),
+                (w_forget, qkv_grad[:, forget_at : forget_at + heads_here]),
+                (w_gate_attn, go_grad[:, :width]),
+            ),
+            gain_gradient(
+                pair_gains[1], (w_gate, mlp_grad[:, :hidden_here]), (w_up, mlp_grad[:, hidden_here:])
+            ),
+        ]
+    ).reshape(2, 2, norm_attn.shape[0])
+    gain_grads = pick(parts, 1, side) + partner(pick(parts, 1, 1 - side))
     return (
         mixed,
         tokens_grad,
@@ -1202,7 +1211,7 @@
         qkv_grad[:, 2 * width : 3 * width],
         go_grad[:, :width],
         qkv_grad[:, 3 * width : 3 * width + heads_here],
-        small_sum[4 * share :],
+        qkv_grad[:heads_here, forget_at + heads_here],
         go_grad[:, width:].T,
         gain_grads[0],
         gain_grads[1],

time: 765 us -> 737 us (0.963)
  waiting for transfers between devices: 198 us -> 186 us
  starting transfers between devices: 103 us -> 93.8 us
    ppermute x72 -> x68, waiting for transfers between devices: 197 us -> 184 us  [swap(): return lax.ppermute(values, 'dp', pairs)]
    ppermute x72 -> x68, starting transfers between devices: 98.7 us -> 90 us  [swap(): return lax.ppermute(values, 'dp', pairs)]
    unnamed x240 -> x244, local copies, waits for them, and re-layouts: 28.9 us -> 26.7 us
  transfers between devices with their start and end apart: 89 -> 85, of which waited for: 31 -> 29; matrix products, arithmetic and copies ran while one was open for 4% -> 4% of each run, Pallas kernels for 52% -> 53%
where the time goes in v4:
time: 737 us; the launch traced here: 724 us
  Pallas kernels  386 us (52%)
  waiting for transfers between devices  186 us (25%)
  starting transfers between devices  93.8 us (13%)
  local copies, waits for them, and re-layouts  36.9 us (5%)
  other arithmetic  18.3 us (2%)
    ppermute x68, waiting for transfers between devices, swap(): return lax.ppermute(values, 'dp', pairs)  184 us
    pallas_call x8, Pallas kernels, multiply_back(): pl.pallas_call(body, grid_spec=pltpu.PrefetchScalarGridSpec(num_scalar_pr...  98.2 us
    ppermute x68, starting transfers between devices, swap(): return lax.ppermute(values, 'dp', pairs)  90 us
    pallas_call x7, Pallas kernels, multiply(): pl.pallas_call(body, grid=(tiles,), in_specs=[pl.BlockSpec((length, depth...  80.2 us
    pallas_call x6, Pallas kernels, gradient_parts(): pl.pallas_call(body, grid=(tiles,), in_specs=[pl.BlockSpec((depth, length...  67.6 us
    pallas_call x1, Pallas kernels, attend_backward(): pl.pallas_call(functools.partial(bwd_kernel, head ** (-0.5), head), grid=...  32.9 us
    pallas_call x11, Pallas kernels, add_halves(): pl.pallas_call(body, grid=(columns // tile,), in_specs=[block] * len(term...  28.9 us
    unnamed x244, local copies, waits for them, and re-layouts  26.7 us
  transfers between devices with their start and end apart: 85, of which 29 were waited for; matrix products, arithmetic and copies ran while one was open for 4% of the time, Pallas kernels for 53%

profile of v4, /device:TPU:0, one launch (start us, length us, event | category | flops | bytes accessed | tf_op | source)
XLA Modules:
  0.0 724.0 jit_solution(13458069678822224162)
XLA Ops:
  14.8 6.7 collective-permute-done.7
  25.6 11.3 %collective-permute-done.8.refs_2_.refs_11_.refs_19_ = bf16[2,96,1536]{2,1,0:T(8,128)(2,1)S(1)} collective-permute-done((bf16[2,96,1536]{2,1,0:T(8,128)(2,1)S(1)}, bf16[2,96,1536]{2,1,0:T(8,128)(2,1)S(1)}, u32[]{:S(2)}, u32[]{:S(2)}) %collective-permute-start.8) | collective-permute-done | bytes 589856 | tf_op jit(solution)/shard_map/ppermute | solution.py:78
  57.2 3.8 collective-permute-done.12
  68.2 8.3 %collective-permute-done.14.refs_7_.refs_16_.refs_24_ = bf16[2,96,1536]{2,1,0:T(8,128)(2,1)} collective-permute-done((bf16[2,96,1536]{2,1,0:T(8,128)(2,1)S(1)}, bf16[2,96,1536]{2,1,0:T(8,128)(2,1)}, u32[]{:S(2)}, u32[]{:S(2)}) %collective-permute-start.14) | collective-permute-done | bytes 589856 | tf_op jit(solution)/shard_map/ppermute | solution.py:78
  81.7 10.2 %collective-permute-done.19.refs_2_.refs_27_.refs_32_ = bf16[4,96,896]{2,1,0:T(8,128)(2,1)S(1)} collective-permute-done((bf16[4,96,896]{2,1,0:T(8,128)(2,1)S(1)}, bf16[4,96,896]{2,1,0:T(8,128)(2,1)S(1)}, u32[]{:S(2)}, u32[]{:S(2)}) %collective-permute-start.19) | collective-permute-done | bytes 688160 | tf_op jit(solution)/shard_map/ppermute | solution.py:78
  94.9 3.7 shard_map.247
  107.0 13.8 %collective-permute-done.27 = bf16[1,96,2048]{2,1,0:T(8,128)(2,1)S(1)} collective-permute-done((bf16[1,96,2048]{2,1,0:T(8,128)(2,1)S(1)}, bf16[1,96,2048]{2,1,0:T(8,128)(2,1)S(1)}, u32[]{:S(2)}, u32[]{:S(2)}) %collective-permute-start.27) | collective-permute-done | bytes 393248 | tf_op jit(solution)/shard_map/ppermute | solution.py:78
  121.3 4.5 collective-permute-done.23.refs_2_.refs_6_
  130.5 10.2 %shard_map.248.q_ref.k_ref = bf16[1024,1536]{1,0:T(8,128)(2,1)} custom-call(bf16[1024,1536]{1,0:T(8,128)(2,1)} %get-tuple-element.171.refs_0_, bf16[2,96,1536]{2,1,0:T(8,128)(2,1)S(1)} %copy-done.13, bf16[2,96,1536]{2,1,0:T(8,128)(2,1)S(1)} %copy-done.18, bf16[2,96,1536]{2,1,0:T(8,128)(2,1)S(1)} %copy-done.21, ...), custom_call_target="tpu_custom_call" | custom-call | flops 96636768 | bytes 220200 | tf_op jit(solution)/shard_map/pallas_call | solution.py:194
  143.6 4.8 collective-permute-start.33
  148.5 10.3 %shard_map.249 = (bf16[1024,768]{1,0:T(8,128)(2,1)}, f32[1024,128]{1,0:T(8,128)S(1)}) custom-call(bf16[1024,1536]{1,0:T(8,128)(2,1)} %get-tuple-element.171.refs_0_, bf16[4,96,896]{2,1,0:T(8,128)(2,1)S(1)} %pad_maximum_fusion.7.refs_1_.refs_26_.refs_31_, bf16[4,96,896]{2,1,0:T(8,128)(2,1)S(1)} %collective-permute-done.19.refs_2_.refs_27_.refs_32_, ...), custom_call_target="tpu_custom_call" | custom-call | flops 56371444 | bytes 159907 | tf_op jit(solution)/shard_map/pallas_call | solution.py:194
  165.1 22.6 %shard_map.251 = (f32[1024,768]{1,0:T(8,128)}, f32[6,2,1024]{2,1,0:T(2,128)S(1)}) custom-call(bf16[1024,1536]{1,0:T(8,128)(2,1)} %shard_map.248.q_ref.k_ref, bf16[1024,1536]{1,0:T(8,128)(2,1)} %shard_map.248.q_ref.k_ref, bf16[1024,768]{1,0:T(8,128)(2,1)S(1)} %copy-done.44, f32[6,1024,2]{2,1,0:T(8,128)} %copy-done.28, ...), custom_call_target="tpu_custom_call" | custom-call | flops 193273536 | bytes 251658 | tf_op jit(solution)/shard_map/pallas_call | solution.py:894
  192.6 10.0 %collective-permute-done.36.refs_4_.refs_5_ = bf16[2,96,2048]{2,1,0:T(8,128)(2,1)S(1)} collective-permute-done((bf16[2,96,2048]{2,1,0:T(8,128)(2,1)S(1)}, bf16[2,96,2048]{2,1,0:T(8,128)(2,1)S(1)}, u32[]{:S(2)}, u32[]{:S(2)}) %collective-permute-start.36) | collective-permute-done | bytes 786464 | tf_op jit(solution)/shard_map/ppermute | solution.py:78
  209.1 8.9 %shard_map.252 = (f32[1024,768]{1,0:T(8,128)}, bf16[1024,768]{1,0:T(8,128)(2,1)}) custom-call(bf16[1024,1536]{1,0:T(8,128)(2,1)} %get-tuple-element.171.refs_0_, bf16[4,96,1536]{2,1,0:T(8,128)(2,1)S(1)} %pad_maximum_fusion.3.refs_1_.refs_5_, bf16[4,96,1536]{2,1,0:T(8,128)(2,1)S(1)} %collective-permute-done.23.refs_2_.refs_6_, ...), custom_call_target="tpu_custom_call" | custom-call | flops 48318384 | bytes 267386 | tf_op jit(solution)/shard_map/pallas_call | solution.py:194
  218.0 6.7 shard_map.254
  226.9 6.2 shard_map.253.refs_1_
  233.1 5.5 shard_map.255
  239.2 7.6 %collective-permute-done.44 = bf16[1,96,2048]{2,1,0:T(8,128)(2,1)} collective-permute-done((bf16[1,96,2048]{2,1,0:T(8,128)(2,1)}, bf16[1,96,2048]{2,1,0:T(8,128)(2,1)}, u32[]{:S(2)}, u32[]{:S(2)}) %collective-permute-start.44) | collective-permute-done | bytes 393248 | tf_op jit(solution)/shard_map/ppermute | solution.py:78
  256.4 12.1 %shard_map.257.refs_6_ = bf16[1024,2048]{1,0:T(8,128)(2,1)} custom-call(bf16[1024,1536]{1,0:T(8,128)(2,1)} %get-tuple-element.195.refs_0_, bf16[4,96,2048]{2,1,0:T(8,128)(2,1)S(1)} %copy-done.6, bf16[4,96,2048]{2,1,0:T(8,128)(2,1)} %copy-done.96, bf16[4,96,2048]{2,1,0:T(8,128)(2,1)} %collective-permute-done.37.refs_3_.refs_4_, ...), custom_call_target="tpu_custom_call" | custom-call | flops 128849016 | bytes 272629 | tf_op jit(solution)/shard_map/pallas_call | solution.py:194
  273.6 32.1 %collective-permute-done.46.refs_2_ = bf16[4,96,2048]{2,1,0:T(8,128)(2,1)S(1)} collective-permute-done((bf16[4,96,2048]{2,1,0:T(8,128)(2,1)S(1)}, bf16[4,96,2048]{2,1,0:T(8,128)(2,1)S(1)}, u32[]{:S(2)}, u32[]{:S(2)}) %collective-permute-start.46) | collective-permute-done | bytes 1572896 | tf_op jit(solution)/shard_map/ppermute | solution.py:78
  314.6 13.4 %shard_map.258 = (bf16[1024,2048]{1,0:T(8,128)(2,1)}, bf16[1024,2048]{1,0:T(8,128)(2,1)}) custom-call(bf16[1024,1536]{1,0:T(8,128)(2,1)} %get-tuple-element.195.refs_0_, bf16[4,96,2048]{2,1,0:T(8,128)(2,1)} %pad_maximum_fusion.1.refs_1_.refs_7_, bf16[4,96,2048]{2,1,0:T(8,128)(2,1)} %collective-permute-done.39.refs_2_.refs_8_, ...), custom_call_target="tpu_custom_call" | custom-call | flops 128849016 | bytes 440401 | tf_op jit(solution)/shard_map/pallas_call | solution.py:194
  328.0 12.0 %shard_map.260 = (bf16[2,4,96,2048]{3,2,1,0:T(8,128)(2,1)}, bf16[2,4,96,2048]{3,2,1,0:T(8,128)(2,1)}) custom-call(bf16[1536,1024]{1,0:T(8,128)(2,1)} %get-tuple-element.204.refs_0_, bf16[1024,2048]{1,0:T(8,128)(2,1)} %get-tuple-element.308.refs_1_.refs_0_), custom_call_target="tpu_custom_call" | custom-call | flops 128849016 | bytes 272629 | tf_op jit(solution)/shard_map/pallas_call | solution.py:434
  341.4 16.0 %shard_map.261 = (bf16[1024,2048]{1,0:T(8,128)(2,1)}, bf16[1024,2048]{1,0:T(8,128)(2,1)}) custom-call(bf16[1024,1536]{1,0:T(8,128)(2,1)} %get-tuple-element.206.refs_0_, bf16[4,96,2048]{2,1,0:T(8,128)(2,1)S(1)} %pad_maximum_fusion.2.refs_1_, bf16[4,96,2048]{2,1,0:T(8,128)(2,1)} %copy-done.94, bf16[4,96,2048]{2,1,0:T(8,128)(2,1)} %copy-done.95, ...), custom_call_target="tpu_custom_call" | custom-call | flops 128849016 | bytes 524288 | tf_op jit(solution)/shard_map/pallas_call | solution.py:194
  357.4 12.3 %shard_map.262 = (bf16[4,2,96,2048]{3,2,1,0:T(8,128)(2,1)S(1)}, bf16[4,2,96,2048]{3,2,1,0:T(8,128)(2,1)}) custom-call(bf16[1536,1024]{1,0:T(8,128)(2,1)} %get-tuple-element.212.refs_0_, bf16[1024,2048]{1,0:T(8,128)(2,1)} %get-tuple-element.213.refs_1_), custom_call_target="tpu_custom_call" | custom-call | flops 128849016 | bytes 272629 | tf_op jit(solution)/shard_map/pallas_call | solution.py:434
  369.7 12.1 %shard_map.263 = (bf16[4,2,96,2048]{3,2,1,0:T(8,128)(2,1)}, bf16[4,2,96,2048]{3,2,1,0:T(8,128)(2,1)}) custom-call(bf16[1536,1024]{1,0:T(8,128)(2,1)} %get-tuple-element.212.refs_0_, bf16[1024,2048]{1,0:T(8,128)(2,1)} %get-tuple-element.217.refs_1_.refs_0_), custom_call_target="tpu_custom_call" | custom-call | flops 128849016 | bytes 272629 | tf_op jit(solution)/shard_map/pallas_call | solution.py:434
  383.2 16.7 %shard_map.266 = (bf16[512,768]{1,0:T(8,128)(2,1)S(1)}, bf16[512,768]{1,0:T(8,128)(2,1)S(1)}) custom-call(s32[1]{0:T(128)} %constant.23.clone.1.half_ref, bf16[1024,2048]{1,0:T(8,128)(2,1)} %get-tuple-element.217.refs_1_.refs_0_, bf16[1024,2048]{1,0:T(8,128)(2,1)} %get-tuple-element.213.refs_1_, bf16[4,96,2048]{2,1,0:T(8,128)(2,1)} %copy-done.5, ...), custom_call_target="tpu_custom_call" | custom-call | flops 128849016 | bytes 398458 | tf_op jit(solution)/shard_map/pallas_call | solution.py:275
  400.5 17.4 %shard_map.264.refs_1_ = f32[512,1536]{1,0:T(8,128)} custom-call(s32[1]{0:T(128)} %constant.22.clone.1.half_ref, bf16[1024,2048]{1,0:T(8,128)(2,1)} %get-tuple-element.217.refs_1_.refs_0_, bf16[1024,2048]{1,0:T(8,128)(2,1)} %get-tuple-element.213.refs_1_, bf16[4,96,2048]{2,1,0:T(8,128)(2,1)} %copy-done.5, bf16[4,96,2048]{2,1,0:T(8,128)(2,1)} %copy-done.96, ...), custom_call_target="tpu_custom_call" | custom-call | flops 128849016 | bytes 398458 | tf_op jit(solution)/shard_map/pallas_call | solution.py:275
  417.9 3.8 shard_map.265
  421.8 6.3 shard_map.267
  436.6 9.4 %shard_map.269 = (bf16[1024,768]{1,0:T(8,128)(2,1)}, bf16[1024,768]{1,0:T(8,128)(2,1)}) custom-call(bf16[1024,1536]{1,0:T(8,128)(2,1)} %get-tuple-element.227.refs_0_, bf16[4,96,1536]{2,1,0:T(8,128)(2,1)S(1)} %pad_maximum_fusion.3.refs_1_.refs_5_, bf16[4,96,1536]{2,1,0:T(8,128)(2,1)S(1)} %copy-done.2, bf16[4,96,1536]{2,1,0:T(8,128)(2,1)} %copy-done.93, ...), custom_call_target="tpu_custom_call" | custom-call | flops 48318384 | bytes 298844 | tf_op jit(solution)/shard_map/pallas_call | solution.py:194
  448.9 3.8 shard_map.270
  455.4 4.7 shard_map.271
  462.9 12.6 %shard_map.272 = (bf16[2,2,96,1536]{3,2,1,0:T(8,128)(2,1)}, bf16[2,2,96,1536]{3,2,1,0:T(8,128)(2,1)}, bf16[2,2,96,1536]{3,2,1,0:T(8,128)(2,1)S(1)}, bf16[2,2,96,1536]{3,2,1,0:T(8,128)(2,1)}) custom-call(bf16[1536,1024]{1,0:T(8,128)(2,1)} %get-tuple-element.238.refs_0_, bf16[1536,1024]{1,0:T(8,128)(2,1)} %get-tuple-element.239.refs_1_, ...), custom_call_target="tpu_custom_call" | custom-call | flops 96636768 | bytes 283115 | tf_op jit(solution)/shard_map/pallas_call | solution.py:434
  476.3 32.9 %shard_map.273 = (bf16[1024,768]{1,0:T(8,128)(2,1)S(1)}, bf16[1024,768]{1,0:T(8,128)(2,1)S(1)}, bf16[1024,768]{1,0:T(8,128)(2,1)}, f32[6,2,1024]{2,1,0:T(2,128)S(1)}, f32[6,1024,2]{2,1,0:T(8,128)}) custom-call(bf16[1024,1536]{1,0:T(8,128)(2,1)} %shard_map.248.q_ref.k_ref, bf16[1024,1536]{1,0:T(8,128)(2,1)} %shard_map.248.q_ref.k_ref, ...), custom_call_target="tpu_custom_call" | custom-call | flops 483183808 | bytes 251658 | tf_op jit(solution)/shard_map/pallas_call | solution.py:914
  515.8 4.6 shard_map.274
  521.5 11.9 %shard_map.276 = (bf16[2,2,96,1536]{3,2,1,0:T(8,128)(2,1)}, bf16[2,2,96,1536]{3,2,1,0:T(8,128)(2,1)}, bf16[2,2,96,1536]{3,2,1,0:T(8,128)(2,1)S(1)}, bf16[2,2,96,1536]{3,2,1,0:T(8,128)(2,1)}) custom-call(bf16[1536,1024]{1,0:T(8,128)(2,1)} %get-tuple-element.238.refs_0_, bf16[1024,768]{1,0:T(8,128)(2,1)} %copy-done.26, bf16[1024,768]{1,0:T(8,128)(2,1)} %copy-done.27), custom_call_target="tpu_custom_call" | custom-call | flops 96636768 | bytes 220200 | tf_op jit(solution)/shard_map/pallas_call | solution.py:434
  545.5 6.7 shard_map.280
  553.1 15.5 %shard_map.281 = (bf16[512,768]{1,0:T(8,128)(2,1)}, bf16[512,768]{1,0:T(8,128)(2,1)}) custom-call(s32[1]{0:T(128)} %bitcast.11.half_ref, bf16[1024,768]{1,0:T(8,128)(2,1)} %get-tuple-element.271.refs_2_.refs_0_, bf16[1024,768]{1,0:T(8,128)(2,1)} %copy-done.26, bf16[1024,768]{1,0:T(8,128)(2,1)} %copy-done.27, ...), custom_call_target="tpu_custom_call" | custom-call | flops 100663296 | bytes 325058 | tf_op jit(solution)/shard_map/pallas_call | solution.py:275
  569.2 10.0 %shard_map.282 = (bf16[512,768]{1,0:T(8,128)(2,1)}, bf16[512,768]{1,0:T(8,128)(2,1)}) custom-call(s32[1]{0:T(128)} %constant.23.clone.1.half_ref, bf16[1024,2048]{1,0:T(8,128)(2,1)} %get-tuple-element.308.refs_1_.refs_0_, bf16[4,96,2048]{2,1,0:T(8,128)(2,1)} %copy-done.3, bf16[4,96,2048]{2,1,0:T(8,128)(2,1)} %copy-done.94, bf16[4,96,2048]{2,1,0:T(8,128)(2,1)} %copy-done.95, ...), custom_call_target="tpu_custom_call" | custom-call | flops 64424508 | bytes 230686 | tf_op jit(solution)/shard_map/pallas_call | solution.py:275
  594.1 11.6 %collective-permute-done.73.refs_1_ = bf16[2,2,96,896]{3,2,1,0:T(8,128)(2,1)S(1)} collective-permute-done((bf16[2,2,96,896]{3,2,1,0:T(8,128)(2,1)S(1)}, bf16[2,2,96,896]{3,2,1,0:T(8,128)(2,1)S(1)}, u32[]{:S(2)}, u32[]{:S(2)}) %collective-permute-start.73) | collective-permute-done | bytes 688160 | tf_op jit(solution)/shard_map/ppermute | solution.py:78
  608.0 15.4 %shard_map.286.refs_1_ = f32[512,1536]{1,0:T(8,128)} custom-call(s32[1]{0:T(128)} %bitcast.half_ref, bf16[1024,768]{1,0:T(8,128)(2,1)} %get-tuple-element.271.refs_2_.refs_0_, bf16[1024,768]{1,0:T(8,128)(2,1)} %copy-done.26, bf16[1024,768]{1,0:T(8,128)(2,1)} %copy-done.27, bf16[1024,768]{1,0:T(8,128)(2,1)} %get-tuple-element.264.refs_1_.refs_3_, ...), custom_call_target="tpu_custom_call" | custom-call | flops 100663296 | bytes 325058 | tf_op jit(solution)/shard_map/pallas_call | solution.py:275
  625.2 6.2 shard_map.288
  641.0 7.0 collective-permute-done.74
  656.1 10.4 %shard_map.292.refs_1_ = f32[512,1536]{1,0:T(8,128)} custom-call(s32[1]{0:T(128)} %constant.22.clone.1.half_ref, bf16[1024,2048]{1,0:T(8,128)(2,1)} %get-tuple-element.308.refs_1_.refs_0_, bf16[4,96,2048]{2,1,0:T(8,128)(2,1)S(1)} %copy-done.4, bf16[4,96,2048]{2,1,0:T(8,128)(2,1)} %copy-done.94, bf16[4,96,2048]{2,1,0:T(8,128)(2,1)} %copy-done.95, ...), custom_call_target="tpu_custom_call" | custom-call | flops 64424508 | bytes 230686 | tf_op jit(solution)/shard_map/pallas_call | solution.py:275
  667.4 4.8 shard_map.293
  673.6 13.3 %collective-permute-done.77 = bf16[2,96,2432]{2,1,0:T(8,128)(2,1)S(1)} collective-permute-done((bf16[2,96,2432]{2,1,0:T(8,128)(2,1)S(1)}, bf16[2,96,2432]{2,1,0:T(8,128)(2,1)S(1)}, u32[]{:S(2)}, u32[]{:S(2)}) %collective-permute-start.77) | collective-permute-done | bytes 933920 | tf_op jit(solution)/shard_map/ppermute | solution.py:78
  695.2 16.4 %collective-permute-done.80 = bf16[1,96,1536]{2,1,0:T(8,128)(2,1)S(1)} collective-permute-done((bf16[1,96,1536]{2,1,0:T(8,128)(2,1)S(1)}, bf16[1,96,1536]{2,1,0:T(8,128)(2,1)S(1)}, u32[]{:S(2)}, u32[]{:S(2)}) %collective-permute-start.80) | collective-permute-done | bytes 294944 | tf_op jit(solution)/shard_map/ppermute | solution.py:78
  713.6 6.6 collective-permute-done.78
  (485 shorter events, 208.5 us)
Async XLA Ops:
  24.0 23.5 %collective-permute-start.10 = (bf16[2,96,1536]{2,1,0:T(8,128)(2,1)S(1)}, bf16[2,96,1536]{2,1,0:T(8,128)(2,1)S(1)}, u32[]{:S(2)}, u32[]{:S(2)}) collective-permute-start(bf16[2,96,1536]{2,1,0:T(8,128)(2,1)S(1)} %pad_maximum_fusion.8.refs_1_.refs_10_.refs_18_), channel_id=1, source_target_pairs={{0,2},{2,0},{4,6},{6,4},{8,10},{10,8},{12,14},{14,12},{16,18},{18,... | collective-permute-start | bytes 1769480 | tf_op jit(solution)/shard_map/ppermute | solution.py:78
  45.5 22.1 %collective-permute-start.16 = (bf16[2,96,1536]{2,1,0:T(8,128)(2,1)S(1)}, bf16[2,96,1536]{2,1,0:T(8,128)(2,1)}, u32[]{:S(2)}, u32[]{:S(2)}) collective-permute-start(bf16[2,96,1536]{2,1,0:T(8,128)(2,1)S(1)} %pad_maximum_fusion.8.refs_1_.refs_10_.refs_18_), channel_id=1, source_target_pairs={{0,4},{2,6},{4,0},{6,2},{8,12},{10,14},{12,8},{14,10},{16,20},{18,... | collective-permute-start | bytes 1769480 | tf_op jit(solution)/shard_map/ppermute | solution.py:78
  46.0 21.7 %collective-permute-start.17 = (bf16[2,96,1536]{2,1,0:T(8,128)(2,1)S(1)}, bf16[2,96,1536]{2,1,0:T(8,128)(2,1)}, u32[]{:S(2)}, u32[]{:S(2)}) collective-permute-start(bf16[2,96,1536]{2,1,0:T(8,128)(2,1)S(1)} %collective-permute-done.8.refs_2_.refs_11_.refs_19_), channel_id=1, source_target_pairs={{0,2},{2,0},{4,6},{6,4},{8,10},{10,8},{12,14},{14,12},{16,18},{18,... | collective-permute-start | bytes 1769480 | tf_op jit(solution)/shard_map/ppermute | solution.py:78
  47.5 29.0 %collective-permute-start.14 = (bf16[2,96,1536]{2,1,0:T(8,128)(2,1)S(1)}, bf16[2,96,1536]{2,1,0:T(8,128)(2,1)}, u32[]{:S(2)}, u32[]{:S(2)}) collective-permute-start(bf16[2,96,1536]{2,1,0:T(8,128)(2,1)S(1)} %collective-permute-done.10.refs_3_.refs_12_.refs_20_), channel_id=1, source_target_pairs={{0,4},{2,6},{4,0},{6,2},{8,12},{10,14},{12,8},{14,10},{16,20},{18,... | collective-permute-start | bytes 1769480 | tf_op jit(solution)/shard_map/ppermute | solution.py:78
  54.0 22.5 %collective-permute-start.15 = (bf16[2,96,1536]{2,1,0:T(8,128)(2,1)S(1)}, bf16[2,96,1536]{2,1,0:T(8,128)(2,1)}, u32[]{:S(2)}, u32[]{:S(2)}) collective-permute-start(bf16[2,96,1536]{2,1,0:T(8,128)(2,1)S(1)} %collective-permute-done.11.refs_6_.refs_15_.refs_23_), channel_id=1, source_target_pairs={{0,2},{2,0},{4,6},{6,4},{8,10},{10,8},{12,14},{14,12},{16,18},{18,... | collective-permute-start | bytes 1769480 | tf_op jit(solution)/shard_map/ppermute | solution.py:78
  67.6 27.3 %collective-permute-start.5 = (bf16[512,768]{1,0:T(8,128)(2,1)S(1)}, bf16[512,768]{1,0:T(8,128)(2,1)S(1)}, u32[]{:S(2)}, u32[]{:S(2)}) collective-permute-start(bf16[512,768]{1,0:T(8,128)(2,1)S(1)} %get-tuple-element.169), channel_id=1, source_target_pairs={{0,1},{1,0},{2,3},{3,2},{4,5},{5,4},{6,7},{7,6},{8,9},{9,8},{10,11... | collective-permute-start | bytes 2359304 | tf_op jit(solution)/shard_map/ppermute | solution.py:51
  67.7 27.3 %collective-permute-start.6 = (bf16[512,768]{1,0:T(8,128)(2,1)S(1)}, bf16[512,768]{1,0:T(8,128)(2,1)S(1)}, u32[]{:S(2)}, u32[]{:S(2)}) collective-permute-start(bf16[512,768]{1,0:T(8,128)(2,1)S(1)} %get-tuple-element.170), channel_id=1, source_target_pairs={{0,1},{1,0},{2,3},{3,2},{4,5},{5,4},{6,7},{7,6},{8,9},{9,8},{10,11... | collective-permute-start | bytes 2359304 | tf_op jit(solution)/shard_map/ppermute | solution.py:51
  101.4 24.4 %collective-permute-start.23 = (bf16[4,96,1536]{2,1,0:T(8,128)(2,1)S(1)}, bf16[4,96,1536]{2,1,0:T(8,128)(2,1)S(1)}, u32[]{:S(2)}, u32[]{:S(2)}) collective-permute-start(bf16[4,96,1536]{2,1,0:T(8,128)(2,1)S(1)} %pad_maximum_fusion.3.refs_1_.refs_5_), channel_id=1, source_target_pairs={{0,2},{2,0},{4,6},{6,4},{8,10},{10,8},{12,14},{14,12},{16,18},{18,... | collective-permute-start | bytes 3538952 | tf_op jit(solution)/shard_map/ppermute | solution.py:78
  103.3 24.9 %collective-permute-start.24 = (bf16[4,96,1536]{2,1,0:T(8,128)(2,1)S(1)}, bf16[4,96,1536]{2,1,0:T(8,128)(2,1)S(1)}, u32[]{:S(2)}, u32[]{:S(2)}) collective-permute-start(bf16[4,96,1536]{2,1,0:T(8,128)(2,1)S(1)} %pad_maximum_fusion.3.refs_1_.refs_5_), channel_id=1, source_target_pairs={{0,4},{2,6},{4,0},{6,2},{8,12},{10,14},{12,8},{14,10},{16,20},{18,... | collective-permute-start | bytes 3538952 | tf_op jit(solution)/shard_map/ppermute | solution.py:78
  140.9 46.7 %collective-permute-start.35 = (bf16[4,96,2048]{2,1,0:T(8,128)(2,1)S(1)}, bf16[4,96,2048]{2,1,0:T(8,128)(2,1)S(1)}, u32[]{:S(2)}, u32[]{:S(2)}) collective-permute-start(bf16[4,96,2048]{2,1,0:T(8,128)(2,1)S(1)} %pad_maximum_fusion.refs_1_.refs_2_), channel_id=1, source_target_pairs={{0,2},{2,0},{4,6},{6,4},{8,10},{10,8},{12,14},{14,12},{16,18},{18,... | collective-permute-start | bytes 4718600 | tf_op jit(solution)/shard_map/ppermute | solution.py:78
  142.7 45.6 %collective-permute-start.37 = (bf16[4,96,2048]{2,1,0:T(8,128)(2,1)S(1)}, bf16[4,96,2048]{2,1,0:T(8,128)(2,1)}, u32[]{:S(2)}, u32[]{:S(2)}) collective-permute-start(bf16[4,96,2048]{2,1,0:T(8,128)(2,1)S(1)} %pad_maximum_fusion.refs_1_.refs_2_), channel_id=1, source_target_pairs={{0,4},{2,6},{4,0},{6,2},{8,12},{10,14},{12,8},{14,10},{16,20},{18,... | collective-permute-start | bytes 4718600 | tf_op jit(solution)/shard_map/ppermute | solution.py:78
  163.2 28.0 %collective-permute-start.34 = (bf16[2,96,2048]{2,1,0:T(8,128)(2,1)S(1)}, bf16[2,96,2048]{2,1,0:T(8,128)(2,1)S(1)}, u32[]{:S(2)}, u32[]{:S(2)}) collective-permute-start(bf16[2,96,2048]{2,1,0:T(8,128)(2,1)S(1)} %pad_maximum_fusion.5), channel_id=1, source_target_pairs={{0,8},{2,10},{4,12},{6,14},{8,0},{10,2},{12,4},{14,6},{16,24},{18,... | collective-permute-start | bytes 2359304 | tf_op jit(solution)/shard_map/ppermute | solution.py:78
  207.1 41.0 %collective-permute-start.39 = (bf16[4,96,2048]{2,1,0:T(8,128)(2,1)}, bf16[4,96,2048]{2,1,0:T(8,128)(2,1)}, u32[]{:S(2)}, u32[]{:S(2)}) collective-permute-start(bf16[4,96,2048]{2,1,0:T(8,128)(2,1)} %pad_maximum_fusion.1.refs_1_.refs_7_), channel_id=1, source_target_pairs={{0,2},{2,0},{4,6},{6,4},{8,10},{10,8},{12,14},{14,12},{16,18},{18,... | collective-permute-start | bytes 4718600 | tf_op jit(solution)/shard_map/ppermute | solution.py:78
  207.4 42.4 %collective-permute-start.40 = (bf16[4,96,2048]{2,1,0:T(8,128)(2,1)}, bf16[4,96,2048]{2,1,0:T(8,128)(2,1)}, u32[]{:S(2)}, u32[]{:S(2)}) collective-permute-start(bf16[4,96,2048]{2,1,0:T(8,128)(2,1)} %pad_maximum_fusion.1.refs_1_.refs_7_), channel_id=1, source_target_pairs={{0,4},{2,6},{4,0},{6,2},{8,12},{10,14},{12,8},{14,10},{16,20},{18,... | collective-permute-start | bytes 4718600 | tf_op jit(solution)/shard_map/ppermute | solution.py:78
  226.1 20.7 %collective-permute-start.44 = (bf16[1,96,2048]{2,1,0:T(8,128)(2,1)}, bf16[1,96,2048]{2,1,0:T(8,128)(2,1)}, u32[]{:S(2)}, u32[]{:S(2)}) collective-permute-start(bf16[1,96,2048]{2,1,0:T(8,128)(2,1)} %convert_bitcast_fusion), channel_id=1, source_target_pairs={{0,16},{2,18},{4,20},{6,22},{8,24},{10,26},{12,28},{14,30},{16,0},... | collective-permute-start | bytes 1179656 | tf_op jit(solution)/shard_map/ppermute | solution.py:78
  248.0 20.5 %collective-permute-start.45 = (bf16[2,96,2048]{2,1,0:T(8,128)(2,1)S(1)}, bf16[2,96,2048]{2,1,0:T(8,128)(2,1)}, u32[]{:S(2)}, u32[]{:S(2)}) collective-permute-start(bf16[2,96,2048]{2,1,0:T(8,128)(2,1)S(1)} %pad_maximum_fusion.6), channel_id=1, source_target_pairs={{0,8},{2,10},{4,12},{6,14},{8,0},{10,2},{12,4},{14,6},{16,24},{18,... | collective-permute-start | bytes 2359304 | tf_op jit(solution)/shard_map/ppermute | solution.py:78
  249.4 20.6 %collective-permute-start.41 = (bf16[2,96,2048]{2,1,0:T(8,128)(2,1)S(1)}, bf16[2,96,2048]{2,1,0:T(8,128)(2,1)S(1)}, u32[]{:S(2)}, u32[]{:S(2)}) collective-permute-start(bf16[2,96,2048]{2,1,0:T(8,128)(2,1)S(1)} %slice.119), channel_id=1, source_target_pairs={{0,4},{2,6},{4,0},{6,2},{8,12},{10,14},{12,8},{14,10},{16,20},{18,... | collective-permute-start | bytes 2359304 | tf_op jit(solution)/shard_map/ppermute | solution.py:78
  270.2 35.6 %collective-permute-start.46 = (bf16[4,96,2048]{2,1,0:T(8,128)(2,1)S(1)}, bf16[4,96,2048]{2,1,0:T(8,128)(2,1)S(1)}, u32[]{:S(2)}, u32[]{:S(2)}) collective-permute-start(bf16[4,96,2048]{2,1,0:T(8,128)(2,1)S(1)} %pad_maximum_fusion.2.refs_1_), channel_id=1, source_target_pairs={{0,2},{2,0},{4,6},{6,4},{8,10},{10,8},{12,14},{14,12},{16,18},{18,... | collective-permute-start | bytes 4718600 | tf_op jit(solution)/shard_map/ppermute | solution.py:78
  271.9 36.7 %collective-permute-start.47 = (bf16[4,96,2048]{2,1,0:T(8,128)(2,1)S(1)}, bf16[4,96,2048]{2,1,0:T(8,128)(2,1)S(1)}, u32[]{:S(2)}, u32[]{:S(2)}) collective-permute-start(bf16[4,96,2048]{2,1,0:T(8,128)(2,1)S(1)} %pad_maximum_fusion.2.refs_1_), channel_id=1, source_target_pairs={{0,4},{2,6},{4,0},{6,2},{8,12},{10,14},{12,8},{14,10},{16,20},{18,... | collective-permute-start | bytes 4718600 | tf_op jit(solution)/shard_map/ppermute | solution.py:78
  273.6 37.5 %collective-permute-start.43 = (bf16[512,1536]{1,0:T(8,128)(2,1)S(1)}, bf16[512,1536]{1,0:T(8,128)(2,1)S(1)}, u32[]{:S(2)}, u32[]{:S(2)}) collective-permute-start(bf16[512,1536]{1,0:T(8,128)(2,1)S(1)} %copy-done.43), channel_id=1, source_target_pairs={{0,1},{1,0},{2,3},{3,2},{4,5},{5,4},{6,7},{7,6},{8,9},{9,8},{10,11... | collective-permute-start | bytes 4718600 | tf_op jit(solution)/shard_map/ppermute | solution.py:51
  306.8 34.5 %collective-permute-start.48 = (bf16[2,96,2048]{2,1,0:T(8,128)(2,1)}, bf16[2,96,2048]{2,1,0:T(8,128)(2,1)S(1)}, u32[]{:S(2)}, u32[]{:S(2)}) collective-permute-start(bf16[2,96,2048]{2,1,0:T(8,128)(2,1)} %slice.121), channel_id=1, source_target_pairs={{0,4},{2,6},{4,0},{6,2},{8,12},{10,14},{12,8},{14,10},{16,20},{18,... | collective-permute-start | bytes 2359304 | tf_op jit(solution)/shard_map/ppermute | solution.py:78
  310.0 31.4 %collective-permute-start.49 = (bf16[2,96,2048]{2,1,0:T(8,128)(2,1)}, bf16[2,96,2048]{2,1,0:T(8,128)(2,1)S(1)}, u32[]{:S(2)}, u32[]{:S(2)}) collective-permute-start(bf16[2,96,2048]{2,1,0:T(8,128)(2,1)} %slice.122), channel_id=1, source_target_pairs={{0,2},{2,0},{4,6},{6,4},{8,10},{10,8},{12,14},{14,12},{16,18},{18,... | collective-permute-start | bytes 2359304 | tf_op jit(solution)/shard_map/ppermute | solution.py:78
  340.0 77.9 %collective-permute-start.50 = (bf16[2,4,96,2048]{3,2,1,0:T(8,128)(2,1)}, bf16[2,4,96,2048]{3,2,1,0:T(8,128)(2,1)}, u32[]{:S(2)}, u32[]{:S(2)}) collective-permute-start(bf16[2,4,96,2048]{3,2,1,0:T(8,128)(2,1)} %get-tuple-element.205), channel_id=1, source_target_pairs={{0,8},{2,10},{4,12},{6,14},{8,0},{10,2},{12,4},{14,6},{16,24},{18,... | collective-permute-start | bytes 9437192 | tf_op jit(solution)/shard_map/ppermute | solution.py:78
  381.8 67.1 %collective-permute-start.56 = (bf16[4,2,96,2048]{3,2,1,0:T(8,128)(2,1)}, bf16[4,2,96,2048]{3,2,1,0:T(8,128)(2,1)}, u32[]{:S(2)}, u32[]{:S(2)}) collective-permute-start(bf16[4,2,96,2048]{3,2,1,0:T(8,128)(2,1)} %get-tuple-element.216), channel_id=1, source_target_pairs={{0,4},{2,6},{4,0},{6,2},{8,12},{10,14},{12,8},{14,10},{16,20},{18,... | collective-permute-start | bytes 9437192 | tf_op jit(solution)/shard_map/ppermute | solution.py:78
  382.1 66.8 %collective-permute-start.55 = (bf16[4,2,96,2048]{3,2,1,0:T(8,128)(2,1)S(1)}, bf16[4,2,96,2048]{3,2,1,0:T(8,128)(2,1)}, u32[]{:S(2)}, u32[]{:S(2)}) collective-permute-start(bf16[4,2,96,2048]{3,2,1,0:T(8,128)(2,1)S(1)} %get-tuple-element.214), channel_id=1, source_target_pairs={{0,2},{2,0},{4,6},{6,4},{8,10},{10,8},{12,14},{14,12},{16,18},{18,... | collective-permute-start | bytes 9437192 | tf_op jit(solution)/shard_map/ppermute | solution.py:78
  399.9 21.9 %collective-permute-start.51 = (bf16[512,768]{1,0:T(8,128)(2,1)S(1)}, bf16[512,768]{1,0:T(8,128)(2,1)S(1)}, u32[]{:S(2)}, u32[]{:S(2)}) collective-permute-start(bf16[512,768]{1,0:T(8,128)(2,1)S(1)} %get-tuple-element.222), channel_id=1, source_target_pairs={{0,1},{1,0},{2,3},{3,2},{4,5},{5,4},{6,7},{7,6},{8,9},{9,8},{10,11... | collective-permute-start | bytes 2359304 | tf_op jit(solution)/shard_map/ppermute | solution.py:51
  400.0 21.8 %collective-permute-start.52 = (bf16[512,768]{1,0:T(8,128)(2,1)S(1)}, bf16[512,768]{1,0:T(8,128)(2,1)S(1)}, u32[]{:S(2)}, u32[]{:S(2)}) collective-permute-start(bf16[512,768]{1,0:T(8,128)(2,1)S(1)} %get-tuple-element.223), channel_id=1, source_target_pairs={{0,1},{1,0},{2,3},{3,2},{4,5},{5,4},{6,7},{7,6},{8,9},{9,8},{10,11... | collective-permute-start | bytes 2359304 | tf_op jit(solution)/shard_map/ppermute | solution.py:51
  428.6 82.8 %collective-permute-start.59 = (bf16[1,384,2048]{2,1,0:T(8,128)(2,1)S(1)}, bf16[1,384,2048]{2,1,0:T(8,128)(2,1)}, u32[]{:S(2)}, u32[]{:S(2)}) collective-permute-start(bf16[1,384,2048]{2,1,0:T(8,128)(2,1)S(1)} %get-tuple-element.220), channel_id=1, source_target_pairs={{0,16},{2,18},{4,20},{6,22},{8,24},{10,26},{12,28},{14,30},{16,0},... | collective-permute-start | bytes 4718600 | tf_op jit(solution)/shard_map/ppermute | solution.py:78
  453.9 61.9 %collective-permute-start.58 = (bf16[4,96,2048]{2,1,0:T(8,128)(2,1)S(1)}, bf16[4,96,2048]{2,1,0:T(8,128)(2,1)}, u32[]{:S(2)}, u32[]{:S(2)}) collective-permute-start(bf16[4,96,2048]{2,1,0:T(8,128)(2,1)S(1)} %get-tuple-element.233), channel_id=1, source_target_pairs={{0,4},{2,6},{4,0},{6,2},{8,12},{10,14},{12,8},{14,10},{16,20},{18,... | collective-permute-start | bytes 4718600 | tf_op jit(solution)/shard_map/ppermute | solution.py:78
  461.2 54.5 %collective-permute-start.57 = (bf16[4,96,2048]{2,1,0:T(8,128)(2,1)}, bf16[4,96,2048]{2,1,0:T(8,128)(2,1)}, u32[]{:S(2)}, u32[]{:S(2)}) collective-permute-start(bf16[4,96,2048]{2,1,0:T(8,128)(2,1)} %get-tuple-element.236), channel_id=1, source_target_pairs={{0,2},{2,0},{4,6},{6,4},{8,10},{10,8},{12,14},{14,12},{16,18},{18,... | collective-permute-start | bytes 4718600 | tf_op jit(solution)/shard_map/ppermute | solution.py:78
  475.5 62.8 %collective-permute-start.61 = (bf16[2,2,96,1536]{3,2,1,0:T(8,128)(2,1)}, bf16[2,2,96,1536]{3,2,1,0:T(8,128)(2,1)S(1)}, u32[]{:S(2)}, u32[]{:S(2)}) collective-permute-start(bf16[2,2,96,1536]{3,2,1,0:T(8,128)(2,1)} %get-tuple-element.241), channel_id=1, source_target_pairs={{0,2},{2,0},{4,6},{6,4},{8,10},{10,8},{12,14},{14,12},{16,18},{18,... | collective-permute-start | bytes 3538952 | tf_op jit(solution)/shard_map/ppermute | solution.py:78
  475.8 62.5 %collective-permute-start.60 = (bf16[2,2,96,1536]{3,2,1,0:T(8,128)(2,1)}, bf16[2,2,96,1536]{3,2,1,0:T(8,128)(2,1)S(1)}, u32[]{:S(2)}, u32[]{:S(2)}) collective-permute-start(bf16[2,2,96,1536]{3,2,1,0:T(8,128)(2,1)} %get-tuple-element.240), channel_id=1, source_target_pairs={{0,4},{2,6},{4,0},{6,2},{8,12},{10,14},{12,8},{14,10},{16,20},{18,... | collective-permute-start | bytes 3538952 | tf_op jit(solution)/shard_map/ppermute | solution.py:78
  534.5 34.2 %collective-permute-start.64 = (bf16[2,2,96,1536]{3,2,1,0:T(8,128)(2,1)}, bf16[2,2,96,1536]{3,2,1,0:T(8,128)(2,1)}, u32[]{:S(2)}, u32[]{:S(2)}) collective-permute-start(bf16[2,2,96,1536]{3,2,1,0:T(8,128)(2,1)} %get-tuple-element.257), channel_id=1, source_target_pairs={{0,2},{2,0},{4,6},{6,4},{8,10},{10,8},{12,14},{14,12},{16,18},{18,... | collective-permute-start | bytes 3538952 | tf_op jit(solution)/shard_map/ppermute | solution.py:78
  536.2 32.6 %collective-permute-start.62 = (bf16[2,2,96,1536]{3,2,1,0:T(8,128)(2,1)}, bf16[2,2,96,1536]{3,2,1,0:T(8,128)(2,1)}, u32[]{:S(2)}, u32[]{:S(2)}) collective-permute-start(bf16[2,2,96,1536]{3,2,1,0:T(8,128)(2,1)} %get-tuple-element.256), channel_id=1, source_target_pairs={{0,4},{2,6},{4,0},{6,2},{8,12},{10,14},{12,8},{14,10},{16,20},{18,... | collective-permute-start | bytes 3538952 | tf_op jit(solution)/shard_map/ppermute | solution.py:78
  537.7 53.1 %collective-permute-start.67 = (bf16[2,96,4096]{2,1,0:T(8,128)(2,1)}, bf16[2,96,4096]{2,1,0:T(8,128)(2,1)}, u32[]{:S(2)}, u32[]{:S(2)}) collective-permute-start(bf16[2,96,4096]{2,1,0:T(8,128)(2,1)} %get-tuple-element.250), channel_id=1, source_target_pairs={{0,8},{2,10},{4,12},{6,14},{8,0},{10,2},{12,4},{14,6},{16,24},{18,... | collective-permute-start | bytes 4718600 | tf_op jit(solution)/shard_map/ppermute | solution.py:78
  540.7 46.7 %collective-permute-start.69 = (bf16[2,96,1536]{2,1,0:T(8,128)(2,1)}, bf16[2,96,1536]{2,1,0:T(8,128)(2,1)}, u32[]{:S(2)}, u32[]{:S(2)}) collective-permute-start(bf16[2,96,1536]{2,1,0:T(8,128)(2,1)} %get-tuple-element.263), channel_id=1, source_target_pairs={{0,4},{2,6},{4,0},{6,2},{8,12},{10,14},{12,8},{14,10},{16,20},{18,... | collective-permute-start | bytes 1769480 | tf_op jit(solution)/shard_map/ppermute | solution.py:78
  542.9 45.9 %collective-permute-start.68 = (bf16[2,96,1536]{2,1,0:T(8,128)(2,1)}, bf16[2,96,1536]{2,1,0:T(8,128)(2,1)}, u32[]{:S(2)}, u32[]{:S(2)}) collective-permute-start(bf16[2,96,1536]{2,1,0:T(8,128)(2,1)} %get-tuple-element.260), channel_id=1, source_target_pairs={{0,2},{2,0},{4,6},{6,4},{8,10},{10,8},{12,14},{14,12},{16,18},{18,... | collective-permute-start | bytes 1769480 | tf_op jit(solution)/shard_map/ppermute | solution.py:78
  568.7 21.7 %collective-permute-start.70 = (bf16[512,768]{1,0:T(8,128)(2,1)}, bf16[512,768]{1,0:T(8,128)(2,1)S(1)}, u32[]{:S(2)}, u32[]{:S(2)}) collective-permute-start(bf16[512,768]{1,0:T(8,128)(2,1)} %get-tuple-element.272), channel_id=1, source_target_pairs={{0,1},{1,0},{2,3},{3,2},{4,5},{5,4},{6,7},{7,6},{8,9},{9,8},{10,11... | collective-permute-start | bytes 2359304 | tf_op jit(solution)/shard_map/ppermute | solution.py:51
  568.8 25.4 %collective-permute-start.71 = (bf16[512,768]{1,0:T(8,128)(2,1)}, bf16[512,768]{1,0:T(8,128)(2,1)S(1)}, u32[]{:S(2)}, u32[]{:S(2)}) collective-permute-start(bf16[512,768]{1,0:T(8,128)(2,1)} %get-tuple-element.273), channel_id=1, source_target_pairs={{0,1},{1,0},{2,3},{3,2},{4,5},{5,4},{6,7},{7,6},{8,9},{9,8},{10,11... | collective-permute-start | bytes 2359304 | tf_op jit(solution)/shard_map/ppermute | solution.py:51
  590.3 48.2 %collective-permute-start.65 = (bf16[2,96,1536]{2,1,0:T(8,128)(2,1)}, bf16[2,96,1536]{2,1,0:T(8,128)(2,1)}, u32[]{:S(2)}, u32[]{:S(2)}) collective-permute-start(bf16[2,96,1536]{2,1,0:T(8,128)(2,1)} %copy-done.92), channel_id=1, source_target_pairs={{0,4},{2,6},{4,0},{6,2},{8,12},{10,14},{12,8},{14,10},{16,20},{18,... | collective-permute-start | bytes 1769480 | tf_op jit(solution)/shard_map/ppermute | solution.py:78
  590.8 49.2 %collective-permute-start.63 = (bf16[2,96,1536]{2,1,0:T(8,128)(2,1)}, bf16[2,96,1536]{2,1,0:T(8,128)(2,1)}, u32[]{:S(2)}, u32[]{:S(2)}) collective-permute-start(bf16[2,96,1536]{2,1,0:T(8,128)(2,1)} %copy-done.91), channel_id=1, source_target_pairs={{0,2},{2,0},{4,6},{6,4},{8,10},{10,8},{12,14},{14,12},{16,18},{18,... | collective-permute-start | bytes 1769480 | tf_op jit(solution)/shard_map/ppermute | solution.py:78
  594.1 72.4 %collective-permute-start.75 = (bf16[512,768]{1,0:T(8,128)(2,1)}, bf16[512,768]{1,0:T(8,128)(2,1)}, u32[]{:S(2)}, u32[]{:S(2)}) collective-permute-start(bf16[512,768]{1,0:T(8,128)(2,1)} %get-tuple-element.276), channel_id=1, source_target_pairs={{0,1},{1,0},{2,3},{3,2},{4,5},{5,4},{6,7},{7,6},{8,9},{9,8},{10,11... | collective-permute-start | bytes 2359304 | tf_op jit(solution)/shard_map/ppermute | solution.py:51
  605.7 61.6 %collective-permute-start.76 = (bf16[512,768]{1,0:T(8,128)(2,1)}, bf16[512,768]{1,0:T(8,128)(2,1)}, u32[]{:S(2)}, u32[]{:S(2)}) collective-permute-start(bf16[512,768]{1,0:T(8,128)(2,1)} %get-tuple-element.277), channel_id=1, source_target_pairs={{0,1},{1,0},{2,3},{3,2},{4,5},{5,4},{6,7},{7,6},{8,9},{9,8},{10,11... | collective-permute-start | bytes 2359304 | tf_op jit(solution)/shard_map/ppermute | solution.py:51
  608.0 64.2 %collective-permute-start.81 = (bf16[1,96,4096]{2,1,0:T(8,128)(2,1)}, bf16[1,96,4096]{2,1,0:T(8,128)(2,1)}, u32[]{:S(2)}, u32[]{:S(2)}) collective-permute-start(bf16[1,96,4096]{2,1,0:T(8,128)(2,1)} %get-tuple-element.289), channel_id=1, source_target_pairs={{0,16},{2,18},{4,20},{6,22},{8,24},{10,26},{12,28},{14,30},{16,0},... | collective-permute-start | bytes 2359304 | tf_op jit(solution)/shard_map/ppermute | solution.py:78
  647.9 44.3 %collective-permute-start.83 = (bf16[1,192,2048]{2,1,0:T(8,128)(2,1)}, bf16[1,192,2048]{2,1,0:T(8,128)(2,1)S(1)}, u32[]{:S(2)}, u32[]{:S(2)}) collective-permute-start(bf16[1,192,2048]{2,1,0:T(8,128)(2,1)} %copy-done.89), channel_id=1, source_target_pairs={{0,4},{2,6},{4,0},{6,2},{8,12},{10,14},{12,8},{14,10},{16,20},{18,... | collective-permute-start | bytes 2359304 | tf_op jit(solution)/shard_map/ppermute | solution.py:78
  649.5 37.7 %collective-permute-start.79 = (bf16[2,96,1536]{2,1,0:T(8,128)(2,1)}, bf16[2,96,1536]{2,1,0:T(8,128)(2,1)S(1)}, u32[]{:S(2)}, u32[]{:S(2)}) collective-permute-start(bf16[2,96,1536]{2,1,0:T(8,128)(2,1)} %copy-done.90), channel_id=1, source_target_pairs={{0,8},{2,10},{4,12},{6,14},{8,0},{10,2},{12,4},{14,6},{16,24},{18,... | collective-permute-start | bytes 1769480 | tf_op jit(solution)/shard_map/ppermute | solution.py:78
  687.3 24.2 %collective-permute-start.80 = (bf16[1,96,1536]{2,1,0:T(8,128)(2,1)S(1)}, bf16[1,96,1536]{2,1,0:T(8,128)(2,1)S(1)}, u32[]{:S(2)}, u32[]{:S(2)}) collective-permute-start(bf16[1,96,1536]{2,1,0:T(8,128)(2,1)S(1)} %get-tuple-element.316), channel_id=1, source_target_pairs={{0,16},{2,18},{4,20},{6,22},{8,24},{10,26},{12,28},{14,30},{16,0},... | collective-permute-start | bytes 884744 | tf_op jit(solution)/shard_map/ppermute | solution.py:78
  692.2 28.1 %collective-permute-start.78 = (bf16[1,96,2432]{2,1,0:T(8,128)(2,1)S(1)}, bf16[1,96,2432]{2,1,0:T(8,128)(2,1)S(1)}, u32[]{:S(2)}, u32[]{:S(2)}) collective-permute-start(bf16[1,96,2432]{2,1,0:T(8,128)(2,1)S(1)} %get-tuple-element.312), channel_id=1, source_target_pairs={{0,16},{2,18},{4,20},{6,22},{8,24},{10,26},{12,28},{14,30},{16,0},... | collective-permute-start | bytes 1400840 | tf_op jit(solution)/shard_map/ppermute | solution.py:78
  (156 other events, 2327.3 us)

commit v5 on v4

--- a/solution.py
+++ b/solution.py
@@ -1054,8 +1054,7 @@
         normed_mlp, mlp_gate, 4, lambda p: (lower(p),), [], [(hidden_here, low)]
     )
 
-    load_down.plane(*load_up.corners, gate_act)
-    mlp_down = load_down.weight
+    load_down.plane(*load_up.corners, gate_act, to_end=False)
 
     def hidden_units(up, gate):
         gate = wide(gate)
@@ -1065,6 +1064,7 @@
         normed_mlp, mlp_up, 4, hidden_units, [gate_act], [(hidden_here, low)] * 2
     )
     sum_down = weight_gradient(grid, [(grad_output_t, hidden)], 4, "line").start()
+    mlp_down = load_down.plane_end(sum_down.sent).weight
 
     def hidden_backward(grad, gate, up):
         gate, up = wide(gate), wide(up)

time: 737 us -> 727 us (0.986)
  waiting for transfers between devices: 186 us -> 178 us
  transfers between devices with their start and end apart: 85 -> 85, of which waited for: 29 -> 33; matrix products, arithmetic and copies ran while one was open for 4% -> 4% of each run, Pallas kernels for 53% -> 54%
where the time goes in v5:
time: 727 us; the launch traced here: 715 us
  Pallas kernels  387 us (53%)
  waiting for transfers between devices  178 us (24%)
  starting transfers between devices  93.5 us (13%)
  local copies, waits for them, and re-layouts  36.4 us (5%)
  other arithmetic  18.2 us (3%)
    ppermute x68, waiting for transfers between devices, swap(): return lax.ppermute(values, 'dp', pairs)  176 us
    pallas_call x8, Pallas kernels, multiply_back(): pl.pallas_call(body, grid_spec=pltpu.PrefetchScalarGridSpec(num_scalar_pr...  98.1 us
    ppermute x68, starting transfers between devices, swap(): return lax.ppermute(values, 'dp', pairs)  89.7 us
    pallas_call x7, Pallas kernels, multiply(): pl.pallas_call(body, grid=(tiles,), in_specs=[pl.BlockSpec((length, depth...  80 us
    pallas_call x6, Pallas kernels, gradient_parts(): pl.pallas_call(body, grid=(tiles,), in_specs=[pl.BlockSpec((depth, length...  67.6 us
    pallas_call x1, Pallas kernels, attend_backward(): pl.pallas_call(functools.partial(bwd_kernel, head ** (-0.5), head), grid=...  32.9 us
    pallas_call x11, Pallas kernels, add_halves(): pl.pallas_call(body, grid=(columns // tile,), in_specs=[block] * len(term...  28.9 us
    unnamed x244, local copies, waits for them, and re-layouts  26.4 us
  transfers between devices with their start and end apart: 85, of which 33 were waited for; matrix products, arithmetic and copies ran while one was open for 4% of the time, Pallas kernels for 54%

profile of v5, /device:TPU:0, one launch (start us, length us, event | category | flops | bytes accessed | tf_op | source)
XLA Modules:
  0.0 715.2 jit_solution(10559276567730988223)
XLA Ops:
  14.8 6.7 collective-permute-done.7
  25.6 11.3 %collective-permute-done.8.refs_2_.refs_11_.refs_19_ = bf16[2,96,1536]{2,1,0:T(8,128)(2,1)S(1)} collective-permute-done((bf16[2,96,1536]{2,1,0:T(8,128)(2,1)S(1)}, bf16[2,96,1536]{2,1,0:T(8,128)(2,1)S(1)}, u32[]{:S(2)}, u32[]{:S(2)}) %collective-permute-start.8) | collective-permute-done | bytes 589856 | tf_op jit(solution)/shard_map/ppermute | solution.py:78
  57.2 3.8 collective-permute-done.12
  68.2 8.3 %collective-permute-done.14.refs_7_.refs_16_.refs_24_ = bf16[2,96,1536]{2,1,0:T(8,128)(2,1)} collective-permute-done((bf16[2,96,1536]{2,1,0:T(8,128)(2,1)S(1)}, bf16[2,96,1536]{2,1,0:T(8,128)(2,1)}, u32[]{:S(2)}, u32[]{:S(2)}) %collective-permute-start.14) | collective-permute-done | bytes 589856 | tf_op jit(solution)/shard_map/ppermute | solution.py:78
  81.7 10.2 %collective-permute-done.19.refs_2_.refs_27_.refs_32_ = bf16[4,96,896]{2,1,0:T(8,128)(2,1)S(1)} collective-permute-done((bf16[4,96,896]{2,1,0:T(8,128)(2,1)S(1)}, bf16[4,96,896]{2,1,0:T(8,128)(2,1)S(1)}, u32[]{:S(2)}, u32[]{:S(2)}) %collective-permute-start.19) | collective-permute-done | bytes 688160 | tf_op jit(solution)/shard_map/ppermute | solution.py:78
  107.0 13.8 %collective-permute-done.27 = bf16[1,96,2048]{2,1,0:T(8,128)(2,1)S(1)} collective-permute-done((bf16[1,96,2048]{2,1,0:T(8,128)(2,1)S(1)}, bf16[1,96,2048]{2,1,0:T(8,128)(2,1)S(1)}, u32[]{:S(2)}, u32[]{:S(2)}) %collective-permute-start.27) | collective-permute-done | bytes 393248 | tf_op jit(solution)/shard_map/ppermute | solution.py:78
  121.3 4.5 collective-permute-done.23.refs_2_.refs_6_
  130.5 10.2 %shard_map.248.q_ref.k_ref = bf16[1024,1536]{1,0:T(8,128)(2,1)} custom-call(bf16[1024,1536]{1,0:T(8,128)(2,1)} %get-tuple-element.173.refs_0_, bf16[2,96,1536]{2,1,0:T(8,128)(2,1)S(1)} %copy-done.13, bf16[2,96,1536]{2,1,0:T(8,128)(2,1)S(1)} %copy-done.18, bf16[2,96,1536]{2,1,0:T(8,128)(2,1)S(1)} %copy-done.21, ...), custom_call_target="tpu_custom_call" | custom-call | flops 96636768 | bytes 220200 | tf_op jit(solution)/shard_map/pallas_call | solution.py:194
  143.6 4.8 collective-permute-start.33
  148.5 10.3 %shard_map.249 = (bf16[1024,768]{1,0:T(8,128)(2,1)}, f32[1024,128]{1,0:T(8,128)S(1)}) custom-call(bf16[1024,1536]{1,0:T(8,128)(2,1)} %get-tuple-element.173.refs_0_, bf16[4,96,896]{2,1,0:T(8,128)(2,1)S(1)} %pad_maximum_fusion.7.refs_1_.refs_26_.refs_31_, bf16[4,96,896]{2,1,0:T(8,128)(2,1)S(1)} %collective-permute-done.19.refs_2_.refs_27_.refs_32_, ...), custom_call_target="tpu_custom_call" | custom-call | flops 56371444 | bytes 159907 | tf_op jit(solution)/shard_map/pallas_call | solution.py:194
  165.1 22.6 %shard_map.251 = (f32[1024,768]{1,0:T(8,128)}, f32[6,2,1024]{2,1,0:T(2,128)S(1)}) custom-call(bf16[1024,1536]{1,0:T(8,128)(2,1)} %shard_map.248.q_ref.k_ref, bf16[1024,1536]{1,0:T(8,128)(2,1)} %shard_map.248.q_ref.k_ref, bf16[1024,768]{1,0:T(8,128)(2,1)S(1)} %copy-done.44, f32[6,1024,2]{2,1,0:T(8,128)} %copy-done.28, ...), custom_call_target="tpu_custom_call" | custom-call | flops 193273536 | bytes 251658 | tf_op jit(solution)/shard_map/pallas_call | solution.py:894
  192.6 10.0 %collective-permute-done.36.refs_4_.refs_5_ = bf16[2,96,2048]{2,1,0:T(8,128)(2,1)S(1)} collective-permute-done((bf16[2,96,2048]{2,1,0:T(8,128)(2,1)S(1)}, bf16[2,96,2048]{2,1,0:T(8,128)(2,1)S(1)}, u32[]{:S(2)}, u32[]{:S(2)}) %collective-permute-start.36) | collective-permute-done | bytes 786464 | tf_op jit(solution)/shard_map/ppermute | solution.py:78
  209.1 8.9 %shard_map.252 = (f32[1024,768]{1,0:T(8,128)}, bf16[1024,768]{1,0:T(8,128)(2,1)}) custom-call(bf16[1024,1536]{1,0:T(8,128)(2,1)} %get-tuple-element.173.refs_0_, bf16[4,96,1536]{2,1,0:T(8,128)(2,1)S(1)} %pad_maximum_fusion.3.refs_1_.refs_5_, bf16[4,96,1536]{2,1,0:T(8,128)(2,1)S(1)} %collective-permute-done.23.refs_2_.refs_6_, ...), custom_call_target="tpu_custom_call" | custom-call | flops 48318384 | bytes 267386 | tf_op jit(solution)/shard_map/pallas_call | solution.py:194
  218.0 6.7 shard_map.254
  226.9 6.2 shard_map.253.refs_1_
  233.1 5.5 shard_map.255
  239.2 7.6 %collective-permute-done.44 = bf16[1,96,2048]{2,1,0:T(8,128)(2,1)} collective-permute-done((bf16[1,96,2048]{2,1,0:T(8,128)(2,1)}, bf16[1,96,2048]{2,1,0:T(8,128)(2,1)}, u32[]{:S(2)}, u32[]{:S(2)}) %collective-permute-start.44) | collective-permute-done | bytes 393248 | tf_op jit(solution)/shard_map/ppermute | solution.py:78
  258.1 12.1 %shard_map.257.refs_6_ = bf16[1024,2048]{1,0:T(8,128)(2,1)} custom-call(bf16[1024,1536]{1,0:T(8,128)(2,1)} %get-tuple-element.197.refs_0_, bf16[4,96,2048]{2,1,0:T(8,128)(2,1)S(1)} %copy-done.6, bf16[4,96,2048]{2,1,0:T(8,128)(2,1)} %copy-done.96, bf16[4,96,2048]{2,1,0:T(8,128)(2,1)} %collective-permute-done.37.refs_3_.refs_4_, ...), custom_call_target="tpu_custom_call" | custom-call | flops 128849016 | bytes 272629 | tf_op jit(solution)/shard_map/pallas_call | solution.py:194
  275.5 4.8 shard_map.259
  280.4 13.3 %shard_map.258 = (bf16[1024,2048]{1,0:T(8,128)(2,1)}, bf16[1024,2048]{1,0:T(8,128)(2,1)}) custom-call(bf16[1024,1536]{1,0:T(8,128)(2,1)} %get-tuple-element.197.refs_0_, bf16[4,96,2048]{2,1,0:T(8,128)(2,1)} %pad_maximum_fusion.1.refs_1_.refs_7_, bf16[4,96,2048]{2,1,0:T(8,128)(2,1)} %collective-permute-done.39.refs_2_.refs_8_, ...), custom_call_target="tpu_custom_call" | custom-call | flops 128849016 | bytes 440401 | tf_op jit(solution)/shard_map/pallas_call | solution.py:194
  293.7 12.0 %shard_map.260 = (bf16[2,4,96,2048]{3,2,1,0:T(8,128)(2,1)}, bf16[2,4,96,2048]{3,2,1,0:T(8,128)(2,1)}) custom-call(bf16[1536,1024]{1,0:T(8,128)(2,1)} %get-tuple-element.206.refs_0_, bf16[1024,2048]{1,0:T(8,128)(2,1)} %get-tuple-element.312.refs_1_.refs_0_), custom_call_target="tpu_custom_call" | custom-call | flops 128849016 | bytes 272629 | tf_op jit(solution)/shard_map/pallas_call | solution.py:434
  313.2 14.0 %collective-permute-done.49.refs_5_ = bf16[2,96,2048]{2,1,0:T(8,128)(2,1)S(1)} collective-permute-done((bf16[2,96,2048]{2,1,0:T(8,128)(2,1)S(1)}, bf16[2,96,2048]{2,1,0:T(8,128)(2,1)S(1)}, u32[]{:S(2)}, u32[]{:S(2)}) %collective-permute-start.49) | collective-permute-done | bytes 786464 | tf_op jit(solution)/shard_map/ppermute | solution.py:78
  328.3 15.8 %shard_map.261 = (bf16[1024,2048]{1,0:T(8,128)(2,1)}, bf16[1024,2048]{1,0:T(8,128)(2,1)}) custom-call(bf16[1024,1536]{1,0:T(8,128)(2,1)} %get-tuple-element.208.refs_0_, bf16[4,96,2048]{2,1,0:T(8,128)(2,1)S(1)} %pad_maximum_fusion.2.refs_1_, bf16[4,96,2048]{2,1,0:T(8,128)(2,1)} %copy-done.95, bf16[4,96,2048]{2,1,0:T(8,128)(2,1)} %copy-done.94, ...), custom_call_target="tpu_custom_call" | custom-call | flops 128849016 | bytes 524288 | tf_op jit(solution)/shard_map/pallas_call | solution.py:194
  344.1 12.3 %shard_map.262 = (bf16[4,2,96,2048]{3,2,1,0:T(8,128)(2,1)S(1)}, bf16[4,2,96,2048]{3,2,1,0:T(8,128)(2,1)}) custom-call(bf16[1536,1024]{1,0:T(8,128)(2,1)} %get-tuple-element.216.refs_0_, bf16[1024,2048]{1,0:T(8,128)(2,1)} %get-tuple-element.217.refs_1_), custom_call_target="tpu_custom_call" | custom-call | flops 128849016 | bytes 272629 | tf_op jit(solution)/shard_map/pallas_call | solution.py:434
  356.4 12.1 %shard_map.263 = (bf16[4,2,96,2048]{3,2,1,0:T(8,128)(2,1)}, bf16[4,2,96,2048]{3,2,1,0:T(8,128)(2,1)}) custom-call(bf16[1536,1024]{1,0:T(8,128)(2,1)} %get-tuple-element.216.refs_0_, bf16[1024,2048]{1,0:T(8,128)(2,1)} %get-tuple-element.221.refs_1_.refs_0_), custom_call_target="tpu_custom_call" | custom-call | flops 128849016 | bytes 272629 | tf_op jit(solution)/shard_map/pallas_call | solution.py:434
  371.0 16.7 %shard_map.266 = (bf16[512,768]{1,0:T(8,128)(2,1)S(1)}, bf16[512,768]{1,0:T(8,128)(2,1)S(1)}) custom-call(s32[1]{0:T(128)} %constant.23.clone.1.half_ref, bf16[1024,2048]{1,0:T(8,128)(2,1)} %get-tuple-element.221.refs_1_.refs_0_, bf16[1024,2048]{1,0:T(8,128)(2,1)} %get-tuple-element.217.refs_1_, bf16[4,96,2048]{2,1,0:T(8,128)(2,1)} %copy-done.5, ...), custom_call_target="tpu_custom_call" | custom-call | flops 128849016 | bytes 398458 | tf_op jit(solution)/shard_map/pallas_call | solution.py:275
  388.2 17.4 %shard_map.264.refs_1_ = f32[512,1536]{1,0:T(8,128)} custom-call(s32[1]{0:T(128)} %constant.22.clone.1.half_ref, bf16[1024,2048]{1,0:T(8,128)(2,1)} %get-tuple-element.221.refs_1_.refs_0_, bf16[1024,2048]{1,0:T(8,128)(2,1)} %get-tuple-element.217.refs_1_, bf16[4,96,2048]{2,1,0:T(8,128)(2,1)} %copy-done.5, bf16[4,96,2048]{2,1,0:T(8,128)(2,1)} %copy-done.96, ...), custom_call_target="tpu_custom_call" | custom-call | flops 128849016 | bytes 398458 | tf_op jit(solution)/shard_map/pallas_call | solution.py:275
  405.7 3.8 shard_map.265
  409.5 6.3 shard_map.267
  424.3 9.4 %shard_map.269 = (bf16[1024,768]{1,0:T(8,128)(2,1)}, bf16[1024,768]{1,0:T(8,128)(2,1)}) custom-call(bf16[1024,1536]{1,0:T(8,128)(2,1)} %get-tuple-element.231.refs_0_, bf16[4,96,1536]{2,1,0:T(8,128)(2,1)S(1)} %pad_maximum_fusion.3.refs_1_.refs_5_, bf16[4,96,1536]{2,1,0:T(8,128)(2,1)S(1)} %copy-done.2, bf16[4,96,1536]{2,1,0:T(8,128)(2,1)} %copy-done.93, ...), custom_call_target="tpu_custom_call" | custom-call | flops 48318384 | bytes 298844 | tf_op jit(solution)/shard_map/pallas_call | solution.py:194
  438.3 3.8 shard_map.270
  443.8 4.7 shard_map.271
  450.2 12.6 %shard_map.272 = (bf16[2,2,96,1536]{3,2,1,0:T(8,128)(2,1)}, bf16[2,2,96,1536]{3,2,1,0:T(8,128)(2,1)}, bf16[2,2,96,1536]{3,2,1,0:T(8,128)(2,1)S(1)}, bf16[2,2,96,1536]{3,2,1,0:T(8,128)(2,1)}) custom-call(bf16[1536,1024]{1,0:T(8,128)(2,1)} %get-tuple-element.242.refs_0_, bf16[1536,1024]{1,0:T(8,128)(2,1)} %get-tuple-element.243.refs_1_, ...), custom_call_target="tpu_custom_call" | custom-call | flops 96636768 | bytes 283115 | tf_op jit(solution)/shard_map/pallas_call | solution.py:434
  465.7 32.9 %shard_map.273 = (bf16[1024,768]{1,0:T(8,128)(2,1)S(1)}, bf16[1024,768]{1,0:T(8,128)(2,1)S(1)}, bf16[1024,768]{1,0:T(8,128)(2,1)}, f32[6,2,1024]{2,1,0:T(2,128)S(1)}, f32[6,1024,2]{2,1,0:T(8,128)}) custom-call(bf16[1024,1536]{1,0:T(8,128)(2,1)} %shard_map.248.q_ref.k_ref, bf16[1024,1536]{1,0:T(8,128)(2,1)} %shard_map.248.q_ref.k_ref, ...), custom_call_target="tpu_custom_call" | custom-call | flops 483183808 | bytes 251658 | tf_op jit(solution)/shard_map/pallas_call | solution.py:914
  505.2 4.6 shard_map.274
  510.9 11.9 %shard_map.276 = (bf16[2,2,96,1536]{3,2,1,0:T(8,128)(2,1)}, bf16[2,2,96,1536]{3,2,1,0:T(8,128)(2,1)}, bf16[2,2,96,1536]{3,2,1,0:T(8,128)(2,1)S(1)}, bf16[2,2,96,1536]{3,2,1,0:T(8,128)(2,1)}) custom-call(bf16[1536,1024]{1,0:T(8,128)(2,1)} %get-tuple-element.242.refs_0_, bf16[1024,768]{1,0:T(8,128)(2,1)} %copy-done.26, bf16[1024,768]{1,0:T(8,128)(2,1)} %copy-done.27), custom_call_target="tpu_custom_call" | custom-call | flops 96636768 | bytes 220200 | tf_op jit(solution)/shard_map/pallas_call | solution.py:434
  536.5 6.7 shard_map.280
  544.1 15.5 %shard_map.281 = (bf16[512,768]{1,0:T(8,128)(2,1)}, bf16[512,768]{1,0:T(8,128)(2,1)}) custom-call(s32[1]{0:T(128)} %bitcast.11.half_ref, bf16[1024,768]{1,0:T(8,128)(2,1)} %get-tuple-element.275.refs_2_.refs_0_, bf16[1024,768]{1,0:T(8,128)(2,1)} %copy-done.26, bf16[1024,768]{1,0:T(8,128)(2,1)} %copy-done.27, ...), custom_call_target="tpu_custom_call" | custom-call | flops 100663296 | bytes 325058 | tf_op jit(solution)/shard_map/pallas_call | solution.py:275
  560.2 10.0 %shard_map.282 = (bf16[512,768]{1,0:T(8,128)(2,1)}, bf16[512,768]{1,0:T(8,128)(2,1)}) custom-call(s32[1]{0:T(128)} %constant.23.clone.1.half_ref, bf16[1024,2048]{1,0:T(8,128)(2,1)} %get-tuple-element.312.refs_1_.refs_0_, bf16[4,96,2048]{2,1,0:T(8,128)(2,1)} %copy-done.3, bf16[4,96,2048]{2,1,0:T(8,128)(2,1)} %copy-done.95, bf16[4,96,2048]{2,1,0:T(8,128)(2,1)} %copy-done.94, ...), custom_call_target="tpu_custom_call" | custom-call | flops 64424508 | bytes 230686 | tf_op jit(solution)/shard_map/pallas_call | solution.py:275
  585.1 11.6 %collective-permute-done.73.refs_1_ = bf16[2,2,96,896]{3,2,1,0:T(8,128)(2,1)S(1)} collective-permute-done((bf16[2,2,96,896]{3,2,1,0:T(8,128)(2,1)S(1)}, bf16[2,2,96,896]{3,2,1,0:T(8,128)(2,1)S(1)}, u32[]{:S(2)}, u32[]{:S(2)}) %collective-permute-start.73) | collective-permute-done | bytes 688160 | tf_op jit(solution)/shard_map/ppermute | solution.py:78
  598.5 15.2 %shard_map.286.refs_1_ = f32[512,1536]{1,0:T(8,128)} custom-call(s32[1]{0:T(128)} %bitcast.half_ref, bf16[1024,768]{1,0:T(8,128)(2,1)} %get-tuple-element.275.refs_2_.refs_0_, bf16[1024,768]{1,0:T(8,128)(2,1)} %copy-done.26, bf16[1024,768]{1,0:T(8,128)(2,1)} %copy-done.27, bf16[1024,768]{1,0:T(8,128)(2,1)} %get-tuple-element.268.refs_1_.refs_3_, ...), custom_call_target="tpu_custom_call" | custom-call | flops 100663296 | bytes 325058 | tf_op jit(solution)/shard_map/pallas_call | solution.py:275
  615.5 6.2 shard_map.288
  631.1 7.9 %collective-permute-done.74 = bf16[2,96,896]{2,1,0:T(8,128)(2,1)} collective-permute-done((bf16[2,96,896]{2,1,0:T(8,128)(2,1)}, bf16[2,96,896]{2,1,0:T(8,128)(2,1)}, u32[]{:S(2)}, u32[]{:S(2)}) %collective-permute-start.74) | collective-permute-done | bytes 344096 | tf_op jit(solution)/shard_map/ppermute | solution.py:78
  646.3 10.4 %shard_map.292.refs_1_ = f32[512,1536]{1,0:T(8,128)} custom-call(s32[1]{0:T(128)} %constant.22.clone.1.half_ref, bf16[1024,2048]{1,0:T(8,128)(2,1)} %get-tuple-element.312.refs_1_.refs_0_, bf16[4,96,2048]{2,1,0:T(8,128)(2,1)S(1)} %copy-done.4, bf16[4,96,2048]{2,1,0:T(8,128)(2,1)} %copy-done.95, bf16[4,96,2048]{2,1,0:T(8,128)(2,1)} %copy-done.94, ...), custom_call_target="tpu_custom_call" | custom-call | flops 64424508 | bytes 230686 | tf_op jit(solution)/shard_map/pallas_call | solution.py:275
  657.3 4.8 shard_map.293
  663.6 14.0 %collective-permute-done.77 = bf16[2,96,2432]{2,1,0:T(8,128)(2,1)S(1)} collective-permute-done((bf16[2,96,2432]{2,1,0:T(8,128)(2,1)S(1)}, bf16[2,96,2432]{2,1,0:T(8,128)(2,1)S(1)}, u32[]{:S(2)}, u32[]{:S(2)}) %collective-permute-start.77) | collective-permute-done | bytes 933920 | tf_op jit(solution)/shard_map/ppermute | solution.py:78
  683.0 19.0 %collective-permute-done.80 = bf16[1,96,1536]{2,1,0:T(8,128)(2,1)S(1)} collective-permute-done((bf16[1,96,1536]{2,1,0:T(8,128)(2,1)S(1)}, bf16[1,96,1536]{2,1,0:T(8,128)(2,1)S(1)}, u32[]{:S(2)}, u32[]{:S(2)}) %collective-permute-start.80) | collective-permute-done | bytes 294944 | tf_op jit(solution)/shard_map/ppermute | solution.py:78
  704.1 7.3 %collective-permute-done.78 = bf16[1,96,2432]{2,1,0:T(8,128)(2,1)S(1)} collective-permute-done((bf16[1,96,2432]{2,1,0:T(8,128)(2,1)S(1)}, bf16[1,96,2432]{2,1,0:T(8,128)(2,1)S(1)}, u32[]{:S(2)}, u32[]{:S(2)}) %collective-permute-start.78) | collective-permute-done | bytes 466976 | tf_op jit(solution)/shard_map/ppermute | solution.py:78
  (485 shorter events, 212.3 us)
Async XLA Ops:
  24.0 23.5 %collective-permute-start.10 = (bf16[2,96,1536]{2,1,0:T(8,128)(2,1)S(1)}, bf16[2,96,1536]{2,1,0:T(8,128)(2,1)S(1)}, u32[]{:S(2)}, u32[]{:S(2)}) collective-permute-start(bf16[2,96,1536]{2,1,0:T(8,128)(2,1)S(1)} %pad_maximum_fusion.8.refs_1_.refs_10_.refs_18_), channel_id=1, source_target_pairs={{0,2},{2,0},{4,6},{6,4},{8,10},{10,8},{12,14},{14,12},{16,18},{18,... | collective-permute-start | bytes 1769480 | tf_op jit(solution)/shard_map/ppermute | solution.py:78
  45.5 22.1 %collective-permute-start.16 = (bf16[2,96,1536]{2,1,0:T(8,128)(2,1)S(1)}, bf16[2,96,1536]{2,1,0:T(8,128)(2,1)}, u32[]{:S(2)}, u32[]{:S(2)}) collective-permute-start(bf16[2,96,1536]{2,1,0:T(8,128)(2,1)S(1)} %pad_maximum_fusion.8.refs_1_.refs_10_.refs_18_), channel_id=1, source_target_pairs={{0,4},{2,6},{4,0},{6,2},{8,12},{10,14},{12,8},{14,10},{16,20},{18,... | collective-permute-start | bytes 1769480 | tf_op jit(solution)/shard_map/ppermute | solution.py:78
  46.0 21.7 %collective-permute-start.17 = (bf16[2,96,1536]{2,1,0:T(8,128)(2,1)S(1)}, bf16[2,96,1536]{2,1,0:T(8,128)(2,1)}, u32[]{:S(2)}, u32[]{:S(2)}) collective-permute-start(bf16[2,96,1536]{2,1,0:T(8,128)(2,1)S(1)} %collective-permute-done.8.refs_2_.refs_11_.refs_19_), channel_id=1, source_target_pairs={{0,2},{2,0},{4,6},{6,4},{8,10},{10,8},{12,14},{14,12},{16,18},{18,... | collective-permute-start | bytes 1769480 | tf_op jit(solution)/shard_map/ppermute | solution.py:78
  47.5 29.0 %collective-permute-start.14 = (bf16[2,96,1536]{2,1,0:T(8,128)(2,1)S(1)}, bf16[2,96,1536]{2,1,0:T(8,128)(2,1)}, u32[]{:S(2)}, u32[]{:S(2)}) collective-permute-start(bf16[2,96,1536]{2,1,0:T(8,128)(2,1)S(1)} %collective-permute-done.10.refs_3_.refs_12_.refs_20_), channel_id=1, source_target_pairs={{0,4},{2,6},{4,0},{6,2},{8,12},{10,14},{12,8},{14,10},{16,20},{18,... | collective-permute-start | bytes 1769480 | tf_op jit(solution)/shard_map/ppermute | solution.py:78
  54.0 22.5 %collective-permute-start.15 = (bf16[2,96,1536]{2,1,0:T(8,128)(2,1)S(1)}, bf16[2,96,1536]{2,1,0:T(8,128)(2,1)}, u32[]{:S(2)}, u32[]{:S(2)}) collective-permute-start(bf16[2,96,1536]{2,1,0:T(8,128)(2,1)S(1)} %collective-permute-done.11.refs_6_.refs_15_.refs_23_), channel_id=1, source_target_pairs={{0,2},{2,0},{4,6},{6,4},{8,10},{10,8},{12,14},{14,12},{16,18},{18,... | collective-permute-start | bytes 1769480 | tf_op jit(solution)/shard_map/ppermute | solution.py:78
  67.6 27.3 %collective-permute-start.5 = (bf16[512,768]{1,0:T(8,128)(2,1)S(1)}, bf16[512,768]{1,0:T(8,128)(2,1)S(1)}, u32[]{:S(2)}, u32[]{:S(2)}) collective-permute-start(bf16[512,768]{1,0:T(8,128)(2,1)S(1)} %get-tuple-element.171), channel_id=1, source_target_pairs={{0,1},{1,0},{2,3},{3,2},{4,5},{5,4},{6,7},{7,6},{8,9},{9,8},{10,11... | collective-permute-start | bytes 2359304 | tf_op jit(solution)/shard_map/ppermute | solution.py:51
  67.7 27.3 %collective-permute-start.6 = (bf16[512,768]{1,0:T(8,128)(2,1)S(1)}, bf16[512,768]{1,0:T(8,128)(2,1)S(1)}, u32[]{:S(2)}, u32[]{:S(2)}) collective-permute-start(bf16[512,768]{1,0:T(8,128)(2,1)S(1)} %get-tuple-element.172), channel_id=1, source_target_pairs={{0,1},{1,0},{2,3},{3,2},{4,5},{5,4},{6,7},{7,6},{8,9},{9,8},{10,11... | collective-permute-start | bytes 2359304 | tf_op jit(solution)/shard_map/ppermute | solution.py:51
  101.4 24.4 %collective-permute-start.23 = (bf16[4,96,1536]{2,1,0:T(8,128)(2,1)S(1)}, bf16[4,96,1536]{2,1,0:T(8,128)(2,1)S(1)}, u32[]{:S(2)}, u32[]{:S(2)}) collective-permute-start(bf16[4,96,1536]{2,1,0:T(8,128)(2,1)S(1)} %pad_maximum_fusion.3.refs_1_.refs_5_), channel_id=1, source_target_pairs={{0,2},{2,0},{4,6},{6,4},{8,10},{10,8},{12,14},{14,12},{16,18},{18,... | collective-permute-start | bytes 3538952 | tf_op jit(solution)/shard_map/ppermute | solution.py:78
  103.3 24.9 %collective-permute-start.24 = (bf16[4,96,1536]{2,1,0:T(8,128)(2,1)S(1)}, bf16[4,96,1536]{2,1,0:T(8,128)(2,1)S(1)}, u32[]{:S(2)}, u32[]{:S(2)}) collective-permute-start(bf16[4,96,1536]{2,1,0:T(8,128)(2,1)S(1)} %pad_maximum_fusion.3.refs_1_.refs_5_), channel_id=1, source_target_pairs={{0,4},{2,6},{4,0},{6,2},{8,12},{10,14},{12,8},{14,10},{16,20},{18,... | collective-permute-start | bytes 3538952 | tf_op jit(solution)/shard_map/ppermute | solution.py:78
  140.9 46.7 %collective-permute-start.35 = (bf16[4,96,2048]{2,1,0:T(8,128)(2,1)S(1)}, bf16[4,96,2048]{2,1,0:T(8,128)(2,1)S(1)}, u32[]{:S(2)}, u32[]{:S(2)}) collective-permute-start(bf16[4,96,2048]{2,1,0:T(8,128)(2,1)S(1)} %pad_maximum_fusion.refs_1_.refs_2_), channel_id=1, source_target_pairs={{0,2},{2,0},{4,6},{6,4},{8,10},{10,8},{12,14},{14,12},{16,18},{18,... | collective-permute-start | bytes 4718600 | tf_op jit(solution)/shard_map/ppermute | solution.py:78
  142.7 45.6 %collective-permute-start.37 = (bf16[4,96,2048]{2,1,0:T(8,128)(2,1)S(1)}, bf16[4,96,2048]{2,1,0:T(8,128)(2,1)}, u32[]{:S(2)}, u32[]{:S(2)}) collective-permute-start(bf16[4,96,2048]{2,1,0:T(8,128)(2,1)S(1)} %pad_maximum_fusion.refs_1_.refs_2_), channel_id=1, source_target_pairs={{0,4},{2,6},{4,0},{6,2},{8,12},{10,14},{12,8},{14,10},{16,20},{18,... | collective-permute-start | bytes 4718600 | tf_op jit(solution)/shard_map/ppermute | solution.py:78
  163.2 28.0 %collective-permute-start.34 = (bf16[2,96,2048]{2,1,0:T(8,128)(2,1)S(1)}, bf16[2,96,2048]{2,1,0:T(8,128)(2,1)S(1)}, u32[]{:S(2)}, u32[]{:S(2)}) collective-permute-start(bf16[2,96,2048]{2,1,0:T(8,128)(2,1)S(1)} %pad_maximum_fusion.5), channel_id=1, source_target_pairs={{0,8},{2,10},{4,12},{6,14},{8,0},{10,2},{12,4},{14,6},{16,24},{18,... | collective-permute-start | bytes 2359304 | tf_op jit(solution)/shard_map/ppermute | solution.py:78
  207.1 41.0 %collective-permute-start.39 = (bf16[4,96,2048]{2,1,0:T(8,128)(2,1)}, bf16[4,96,2048]{2,1,0:T(8,128)(2,1)}, u32[]{:S(2)}, u32[]{:S(2)}) collective-permute-start(bf16[4,96,2048]{2,1,0:T(8,128)(2,1)} %pad_maximum_fusion.1.refs_1_.refs_7_), channel_id=1, source_target_pairs={{0,2},{2,0},{4,6},{6,4},{8,10},{10,8},{12,14},{14,12},{16,18},{18,... | collective-permute-start | bytes 4718600 | tf_op jit(solution)/shard_map/ppermute | solution.py:78
  207.4 43.3 %collective-permute-start.40 = (bf16[4,96,2048]{2,1,0:T(8,128)(2,1)}, bf16[4,96,2048]{2,1,0:T(8,128)(2,1)}, u32[]{:S(2)}, u32[]{:S(2)}) collective-permute-start(bf16[4,96,2048]{2,1,0:T(8,128)(2,1)} %pad_maximum_fusion.1.refs_1_.refs_7_), channel_id=1, source_target_pairs={{0,4},{2,6},{4,0},{6,2},{8,12},{10,14},{12,8},{14,10},{16,20},{18,... | collective-permute-start | bytes 4718600 | tf_op jit(solution)/shard_map/ppermute | solution.py:78
  226.1 20.7 %collective-permute-start.44 = (bf16[1,96,2048]{2,1,0:T(8,128)(2,1)}, bf16[1,96,2048]{2,1,0:T(8,128)(2,1)}, u32[]{:S(2)}, u32[]{:S(2)}) collective-permute-start(bf16[1,96,2048]{2,1,0:T(8,128)(2,1)} %convert_bitcast_fusion), channel_id=1, source_target_pairs={{0,16},{2,18},{4,20},{6,22},{8,24},{10,26},{12,28},{14,30},{16,0},... | collective-permute-start | bytes 1179656 | tf_op jit(solution)/shard_map/ppermute | solution.py:78
  248.0 22.2 %collective-permute-start.45 = (bf16[2,96,2048]{2,1,0:T(8,128)(2,1)S(1)}, bf16[2,96,2048]{2,1,0:T(8,128)(2,1)}, u32[]{:S(2)}, u32[]{:S(2)}) collective-permute-start(bf16[2,96,2048]{2,1,0:T(8,128)(2,1)S(1)} %pad_maximum_fusion.6), channel_id=1, source_target_pairs={{0,8},{2,10},{4,12},{6,14},{8,0},{10,2},{12,4},{14,6},{16,24},{18,... | collective-permute-start | bytes 2359304 | tf_op jit(solution)/shard_map/ppermute | solution.py:78
  250.4 21.2 %collective-permute-start.41 = (bf16[2,96,2048]{2,1,0:T(8,128)(2,1)}, bf16[2,96,2048]{2,1,0:T(8,128)(2,1)S(1)}, u32[]{:S(2)}, u32[]{:S(2)}) collective-permute-start(bf16[2,96,2048]{2,1,0:T(8,128)(2,1)} %slice.119), channel_id=1, source_target_pairs={{0,4},{2,6},{4,0},{6,2},{8,12},{10,14},{12,8},{14,10},{16,20},{18,... | collective-permute-start | bytes 2359304 | tf_op jit(solution)/shard_map/ppermute | solution.py:78
  254.5 21.0 %collective-permute-start.43 = (bf16[512,1536]{1,0:T(8,128)(2,1)S(1)}, bf16[512,1536]{1,0:T(8,128)(2,1)}, u32[]{:S(2)}, u32[]{:S(2)}) collective-permute-start(bf16[512,1536]{1,0:T(8,128)(2,1)S(1)} %copy-done.43), channel_id=1, source_target_pairs={{0,1},{1,0},{2,3},{3,2},{4,5},{5,4},{6,7},{7,6},{8,9},{9,8},{10,11... | collective-permute-start | bytes 4718600 | tf_op jit(solution)/shard_map/ppermute | solution.py:51
  272.1 36.3 %collective-permute-start.47 = (bf16[4,96,2048]{2,1,0:T(8,128)(2,1)S(1)}, bf16[4,96,2048]{2,1,0:T(8,128)(2,1)S(1)}, u32[]{:S(2)}, u32[]{:S(2)}) collective-permute-start(bf16[4,96,2048]{2,1,0:T(8,128)(2,1)S(1)} %pad_maximum_fusion.2.refs_1_), channel_id=1, source_target_pairs={{0,4},{2,6},{4,0},{6,2},{8,12},{10,14},{12,8},{14,10},{16,20},{18,... | collective-permute-start | bytes 4718600 | tf_op jit(solution)/shard_map/ppermute | solution.py:78
  273.8 36.0 %collective-permute-start.46 = (bf16[4,96,2048]{2,1,0:T(8,128)(2,1)S(1)}, bf16[4,96,2048]{2,1,0:T(8,128)(2,1)S(1)}, u32[]{:S(2)}, u32[]{:S(2)}) collective-permute-start(bf16[4,96,2048]{2,1,0:T(8,128)(2,1)S(1)} %pad_maximum_fusion.2.refs_1_), channel_id=1, source_target_pairs={{0,2},{2,0},{4,6},{6,4},{8,10},{10,8},{12,14},{14,12},{16,18},{18,... | collective-permute-start | bytes 4718600 | tf_op jit(solution)/shard_map/ppermute | solution.py:78
  311.3 94.3 %collective-permute-start.50 = (bf16[2,4,96,2048]{3,2,1,0:T(8,128)(2,1)}, bf16[2,4,96,2048]{3,2,1,0:T(8,128)(2,1)}, u32[]{:S(2)}, u32[]{:S(2)}) collective-permute-start(bf16[2,4,96,2048]{3,2,1,0:T(8,128)(2,1)} %get-tuple-element.207), channel_id=1, source_target_pairs={{0,8},{2,10},{4,12},{6,14},{8,0},{10,2},{12,4},{14,6},{16,24},{18,... | collective-permute-start | bytes 9437192 | tf_op jit(solution)/shard_map/ppermute | solution.py:78
  368.5 68.5 %collective-permute-start.56 = (bf16[4,2,96,2048]{3,2,1,0:T(8,128)(2,1)}, bf16[4,2,96,2048]{3,2,1,0:T(8,128)(2,1)}, u32[]{:S(2)}, u32[]{:S(2)}) collective-permute-start(bf16[4,2,96,2048]{3,2,1,0:T(8,128)(2,1)} %get-tuple-element.220), channel_id=1, source_target_pairs={{0,4},{2,6},{4,0},{6,2},{8,12},{10,14},{12,8},{14,10},{16,20},{18,... | collective-permute-start | bytes 9437192 | tf_op jit(solution)/shard_map/ppermute | solution.py:78
  370.1 68.2 %collective-permute-start.55 = (bf16[4,2,96,2048]{3,2,1,0:T(8,128)(2,1)S(1)}, bf16[4,2,96,2048]{3,2,1,0:T(8,128)(2,1)}, u32[]{:S(2)}, u32[]{:S(2)}) collective-permute-start(bf16[4,2,96,2048]{3,2,1,0:T(8,128)(2,1)S(1)} %get-tuple-element.218), channel_id=1, source_target_pairs={{0,2},{2,0},{4,6},{6,4},{8,10},{10,8},{12,14},{14,12},{16,18},{18,... | collective-permute-start | bytes 9437192 | tf_op jit(solution)/shard_map/ppermute | solution.py:78
  387.6 21.9 %collective-permute-start.51 = (bf16[512,768]{1,0:T(8,128)(2,1)S(1)}, bf16[512,768]{1,0:T(8,128)(2,1)S(1)}, u32[]{:S(2)}, u32[]{:S(2)}) collective-permute-start(bf16[512,768]{1,0:T(8,128)(2,1)S(1)} %get-tuple-element.226), channel_id=1, source_target_pairs={{0,1},{1,0},{2,3},{3,2},{4,5},{5,4},{6,7},{7,6},{8,9},{9,8},{10,11... | collective-permute-start | bytes 2359304 | tf_op jit(solution)/shard_map/ppermute | solution.py:51
  387.7 21.8 %collective-permute-start.52 = (bf16[512,768]{1,0:T(8,128)(2,1)S(1)}, bf16[512,768]{1,0:T(8,128)(2,1)S(1)}, u32[]{:S(2)}, u32[]{:S(2)}) collective-permute-start(bf16[512,768]{1,0:T(8,128)(2,1)S(1)} %get-tuple-element.227), channel_id=1, source_target_pairs={{0,1},{1,0},{2,3},{3,2},{4,5},{5,4},{6,7},{7,6},{8,9},{9,8},{10,11... | collective-permute-start | bytes 2359304 | tf_op jit(solution)/shard_map/ppermute | solution.py:51
  416.4 84.5 %collective-permute-start.59 = (bf16[1,384,2048]{2,1,0:T(8,128)(2,1)S(1)}, bf16[1,384,2048]{2,1,0:T(8,128)(2,1)}, u32[]{:S(2)}, u32[]{:S(2)}) collective-permute-start(bf16[1,384,2048]{2,1,0:T(8,128)(2,1)S(1)} %get-tuple-element.224), channel_id=1, source_target_pairs={{0,16},{2,18},{4,20},{6,22},{8,24},{10,26},{12,28},{14,30},{16,0},... | collective-permute-start | bytes 4718600 | tf_op jit(solution)/shard_map/ppermute | solution.py:78
  443.3 61.9 %collective-permute-start.58 = (bf16[4,96,2048]{2,1,0:T(8,128)(2,1)S(1)}, bf16[4,96,2048]{2,1,0:T(8,128)(2,1)}, u32[]{:S(2)}, u32[]{:S(2)}) collective-permute-start(bf16[4,96,2048]{2,1,0:T(8,128)(2,1)S(1)} %get-tuple-element.237), channel_id=1, source_target_pairs={{0,4},{2,6},{4,0},{6,2},{8,12},{10,14},{12,8},{14,10},{16,20},{18,... | collective-permute-start | bytes 4718600 | tf_op jit(solution)/shard_map/ppermute | solution.py:78
  449.6 55.6 %collective-permute-start.57 = (bf16[4,96,2048]{2,1,0:T(8,128)(2,1)}, bf16[4,96,2048]{2,1,0:T(8,128)(2,1)}, u32[]{:S(2)}, u32[]{:S(2)}) collective-permute-start(bf16[4,96,2048]{2,1,0:T(8,128)(2,1)} %get-tuple-element.240), channel_id=1, source_target_pairs={{0,2},{2,0},{4,6},{6,4},{8,10},{10,8},{12,14},{14,12},{16,18},{18,... | collective-permute-start | bytes 4718600 | tf_op jit(solution)/shard_map/ppermute | solution.py:78
  462.7 64.7 %collective-permute-start.61 = (bf16[2,2,96,1536]{3,2,1,0:T(8,128)(2,1)}, bf16[2,2,96,1536]{3,2,1,0:T(8,128)(2,1)S(1)}, u32[]{:S(2)}, u32[]{:S(2)}) collective-permute-start(bf16[2,2,96,1536]{3,2,1,0:T(8,128)(2,1)} %get-tuple-element.245), channel_id=1, source_target_pairs={{0,2},{2,0},{4,6},{6,4},{8,10},{10,8},{12,14},{14,12},{16,18},{18,... | collective-permute-start | bytes 3538952 | tf_op jit(solution)/shard_map/ppermute | solution.py:78
  464.2 63.3 %collective-permute-start.60 = (bf16[2,2,96,1536]{3,2,1,0:T(8,128)(2,1)}, bf16[2,2,96,1536]{3,2,1,0:T(8,128)(2,1)S(1)}, u32[]{:S(2)}, u32[]{:S(2)}) collective-permute-start(bf16[2,2,96,1536]{3,2,1,0:T(8,128)(2,1)} %get-tuple-element.244), channel_id=1, source_target_pairs={{0,4},{2,6},{4,0},{6,2},{8,12},{10,14},{12,8},{14,10},{16,20},{18,... | collective-permute-start | bytes 3538952 | tf_op jit(solution)/shard_map/ppermute | solution.py:78
  523.8 35.8 %collective-permute-start.64 = (bf16[2,2,96,1536]{3,2,1,0:T(8,128)(2,1)}, bf16[2,2,96,1536]{3,2,1,0:T(8,128)(2,1)}, u32[]{:S(2)}, u32[]{:S(2)}) collective-permute-start(bf16[2,2,96,1536]{3,2,1,0:T(8,128)(2,1)} %get-tuple-element.261), channel_id=1, source_target_pairs={{0,2},{2,0},{4,6},{6,4},{8,10},{10,8},{12,14},{14,12},{16,18},{18,... | collective-permute-start | bytes 3538952 | tf_op jit(solution)/shard_map/ppermute | solution.py:78
  524.4 35.3 %collective-permute-start.62 = (bf16[2,2,96,1536]{3,2,1,0:T(8,128)(2,1)}, bf16[2,2,96,1536]{3,2,1,0:T(8,128)(2,1)}, u32[]{:S(2)}, u32[]{:S(2)}) collective-permute-start(bf16[2,2,96,1536]{3,2,1,0:T(8,128)(2,1)} %get-tuple-element.260), channel_id=1, source_target_pairs={{0,4},{2,6},{4,0},{6,2},{8,12},{10,14},{12,8},{14,10},{16,20},{18,... | collective-permute-start | bytes 3538952 | tf_op jit(solution)/shard_map/ppermute | solution.py:78
  524.9 56.1 %collective-permute-start.67 = (bf16[2,96,4096]{2,1,0:T(8,128)(2,1)}, bf16[2,96,4096]{2,1,0:T(8,128)(2,1)}, u32[]{:S(2)}, u32[]{:S(2)}) collective-permute-start(bf16[2,96,4096]{2,1,0:T(8,128)(2,1)} %get-tuple-element.254), channel_id=1, source_target_pairs={{0,8},{2,10},{4,12},{6,14},{8,0},{10,2},{12,4},{14,6},{16,24},{18,... | collective-permute-start | bytes 4718600 | tf_op jit(solution)/shard_map/ppermute | solution.py:78
  529.9 48.5 %collective-permute-start.69 = (bf16[2,96,1536]{2,1,0:T(8,128)(2,1)}, bf16[2,96,1536]{2,1,0:T(8,128)(2,1)}, u32[]{:S(2)}, u32[]{:S(2)}) collective-permute-start(bf16[2,96,1536]{2,1,0:T(8,128)(2,1)} %get-tuple-element.267), channel_id=1, source_target_pairs={{0,4},{2,6},{4,0},{6,2},{8,12},{10,14},{12,8},{14,10},{16,20},{18,... | collective-permute-start | bytes 1769480 | tf_op jit(solution)/shard_map/ppermute | solution.py:78
  533.1 45.9 %collective-permute-start.68 = (bf16[2,96,1536]{2,1,0:T(8,128)(2,1)}, bf16[2,96,1536]{2,1,0:T(8,128)(2,1)}, u32[]{:S(2)}, u32[]{:S(2)}) collective-permute-start(bf16[2,96,1536]{2,1,0:T(8,128)(2,1)} %get-tuple-element.264), channel_id=1, source_target_pairs={{0,2},{2,0},{4,6},{6,4},{8,10},{10,8},{12,14},{14,12},{16,18},{18,... | collective-permute-start | bytes 1769480 | tf_op jit(solution)/shard_map/ppermute | solution.py:78
  559.6 19.9 %collective-permute-start.70 = (bf16[512,768]{1,0:T(8,128)(2,1)}, bf16[512,768]{1,0:T(8,128)(2,1)S(1)}, u32[]{:S(2)}, u32[]{:S(2)}) collective-permute-start(bf16[512,768]{1,0:T(8,128)(2,1)} %get-tuple-element.276), channel_id=1, source_target_pairs={{0,1},{1,0},{2,3},{3,2},{4,5},{5,4},{6,7},{7,6},{8,9},{9,8},{10,11... | collective-permute-start | bytes 2359304 | tf_op jit(solution)/shard_map/ppermute | solution.py:51
  559.7 25.4 %collective-permute-start.71 = (bf16[512,768]{1,0:T(8,128)(2,1)}, bf16[512,768]{1,0:T(8,128)(2,1)S(1)}, u32[]{:S(2)}, u32[]{:S(2)}) collective-permute-start(bf16[512,768]{1,0:T(8,128)(2,1)} %get-tuple-element.277), channel_id=1, source_target_pairs={{0,1},{1,0},{2,3},{3,2},{4,5},{5,4},{6,7},{7,6},{8,9},{9,8},{10,11... | collective-permute-start | bytes 2359304 | tf_op jit(solution)/shard_map/ppermute | solution.py:51
  579.5 49.3 %collective-permute-start.65 = (bf16[2,96,1536]{2,1,0:T(8,128)(2,1)}, bf16[2,96,1536]{2,1,0:T(8,128)(2,1)}, u32[]{:S(2)}, u32[]{:S(2)}) collective-permute-start(bf16[2,96,1536]{2,1,0:T(8,128)(2,1)} %copy-done.92), channel_id=1, source_target_pairs={{0,4},{2,6},{4,0},{6,2},{8,12},{10,14},{12,8},{14,10},{16,20},{18,... | collective-permute-start | bytes 1769480 | tf_op jit(solution)/shard_map/ppermute | solution.py:78
  581.1 48.3 %collective-permute-start.63 = (bf16[2,96,1536]{2,1,0:T(8,128)(2,1)}, bf16[2,96,1536]{2,1,0:T(8,128)(2,1)}, u32[]{:S(2)}, u32[]{:S(2)}) collective-permute-start(bf16[2,96,1536]{2,1,0:T(8,128)(2,1)} %copy-done.91), channel_id=1, source_target_pairs={{0,2},{2,0},{4,6},{6,4},{8,10},{10,8},{12,14},{14,12},{16,18},{18,... | collective-permute-start | bytes 1769480 | tf_op jit(solution)/shard_map/ppermute | solution.py:78
  585.1 71.6 %collective-permute-start.75 = (bf16[512,768]{1,0:T(8,128)(2,1)}, bf16[512,768]{1,0:T(8,128)(2,1)}, u32[]{:S(2)}, u32[]{:S(2)}) collective-permute-start(bf16[512,768]{1,0:T(8,128)(2,1)} %get-tuple-element.280), channel_id=1, source_target_pairs={{0,1},{1,0},{2,3},{3,2},{4,5},{5,4},{6,7},{7,6},{8,9},{9,8},{10,11... | collective-permute-start | bytes 2359304 | tf_op jit(solution)/shard_map/ppermute | solution.py:51
  596.7 60.6 %collective-permute-start.76 = (bf16[512,768]{1,0:T(8,128)(2,1)}, bf16[512,768]{1,0:T(8,128)(2,1)}, u32[]{:S(2)}, u32[]{:S(2)}) collective-permute-start(bf16[512,768]{1,0:T(8,128)(2,1)} %get-tuple-element.281), channel_id=1, source_target_pairs={{0,1},{1,0},{2,3},{3,2},{4,5},{5,4},{6,7},{7,6},{8,9},{9,8},{10,11... | collective-permute-start | bytes 2359304 | tf_op jit(solution)/shard_map/ppermute | solution.py:51
  598.2 63.9 %collective-permute-start.81 = (bf16[1,96,4096]{2,1,0:T(8,128)(2,1)}, bf16[1,96,4096]{2,1,0:T(8,128)(2,1)}, u32[]{:S(2)}, u32[]{:S(2)}) collective-permute-start(bf16[1,96,4096]{2,1,0:T(8,128)(2,1)} %get-tuple-element.293), channel_id=1, source_target_pairs={{0,16},{2,18},{4,20},{6,22},{8,24},{10,26},{12,28},{14,30},{16,0},... | collective-permute-start | bytes 2359304 | tf_op jit(solution)/shard_map/ppermute | solution.py:78
  638.9 43.6 %collective-permute-start.83 = (bf16[1,192,2048]{2,1,0:T(8,128)(2,1)}, bf16[1,192,2048]{2,1,0:T(8,128)(2,1)S(1)}, u32[]{:S(2)}, u32[]{:S(2)}) collective-permute-start(bf16[1,192,2048]{2,1,0:T(8,128)(2,1)} %copy-done.89), channel_id=1, source_target_pairs={{0,4},{2,6},{4,0},{6,2},{8,12},{10,14},{12,8},{14,10},{16,20},{18,... | collective-permute-start | bytes 2359304 | tf_op jit(solution)/shard_map/ppermute | solution.py:78
  639.4 38.4 %collective-permute-start.79 = (bf16[2,96,1536]{2,1,0:T(8,128)(2,1)}, bf16[2,96,1536]{2,1,0:T(8,128)(2,1)S(1)}, u32[]{:S(2)}, u32[]{:S(2)}) collective-permute-start(bf16[2,96,1536]{2,1,0:T(8,128)(2,1)} %copy-done.90), channel_id=1, source_target_pairs={{0,8},{2,10},{4,12},{6,14},{8,0},{10,2},{12,4},{14,6},{16,24},{18,... | collective-permute-start | bytes 1769480 | tf_op jit(solution)/shard_map/ppermute | solution.py:78
  656.7 20.8 %collective-permute-start.77 = (bf16[2,96,2432]{2,1,0:T(8,128)(2,1)S(1)}, bf16[2,96,2432]{2,1,0:T(8,128)(2,1)S(1)}, u32[]{:S(2)}, u32[]{:S(2)}) collective-permute-start(bf16[2,96,2432]{2,1,0:T(8,128)(2,1)S(1)} %copy-done.117), channel_id=1, source_target_pairs={{0,8},{2,10},{4,12},{6,14},{8,0},{10,2},{12,4},{14,6},{16,24},{18,... | collective-permute-start | bytes 2801672 | tf_op jit(solution)/shard_map/ppermute | solution.py:78
  678.0 24.1 %collective-permute-start.80 = (bf16[1,96,1536]{2,1,0:T(8,128)(2,1)S(1)}, bf16[1,96,1536]{2,1,0:T(8,128)(2,1)S(1)}, u32[]{:S(2)}, u32[]{:S(2)}) collective-permute-start(bf16[1,96,1536]{2,1,0:T(8,128)(2,1)S(1)} %get-tuple-element.320), channel_id=1, source_target_pairs={{0,16},{2,18},{4,20},{6,22},{8,24},{10,26},{12,28},{14,30},{16,0},... | collective-permute-start | bytes 884744 | tf_op jit(solution)/shard_map/ppermute | solution.py:78
  681.0 30.5 %collective-permute-start.78 = (bf16[1,96,2432]{2,1,0:T(8,128)(2,1)S(1)}, bf16[1,96,2432]{2,1,0:T(8,128)(2,1)S(1)}, u32[]{:S(2)}, u32[]{:S(2)}) collective-permute-start(bf16[1,96,2432]{2,1,0:T(8,128)(2,1)S(1)} %get-tuple-element.316), channel_id=1, source_target_pairs={{0,16},{2,18},{4,20},{6,22},{8,24},{10,26},{12,28},{14,30},{16,0},... | collective-permute-start | bytes 1400840 | tf_op jit(solution)/shard_map/ppermute | solution.py:78
  683.0 20.1 %collective-permute-start.84 = (bf16[1,96,2048]{2,1,0:T(8,128)(2,1)S(1)}, bf16[1,96,2048]{2,1,0:T(8,128)(2,1)S(1)}, u32[]{:S(2)}, u32[]{:S(2)}) collective-permute-start(bf16[1,96,2048]{2,1,0:T(8,128)(2,1)S(1)} %get-tuple-element.325), channel_id=1, source_target_pairs={{0,2},{2,0},{4,6},{6,4},{8,10},{10,8},{12,14},{14,12},{16,18},{18,... | collective-permute-start | bytes 1179656 | tf_op jit(solution)/shard_map/ppermute | solution.py:78
  (156 other events, 2276.2 us)

commit v6 on v5

--- a/solution.py
+++ b/solution.py
@@ -1155,7 +1155,7 @@
     other_part = multiply_back(back, 1 - side, low, 2)
     arrived = exchanged(other_part)
     hidden = tie(hidden, *other_part)
-    other_down = multiply_back([(hidden, mlp_down)], jnp.int32(1), low, 2)
+    other_down = multiply_back([(hidden, mlp_down)], jnp.int32(1), low)
     arrived_down = exchanged(other_down)
     sum_qk.second(*other_down)
     line_mlp.fourth(*other_down)
@@ -1171,13 +1171,13 @@
     )
     sum_vf.second(tokens_grad)
     line_qkv = LineSum(grid, [sum_qk, sum_vf]).third()
+    line_qkv.fourth()
     (own_down,) = multiply_back([(tie(hidden, line_qkv.sent), mlp_down)], jnp.int32(0))
     (mixed,) = row_kernel(
-        lambda middle, own, *parts: (lower(middle + (own + both_parts(*parts))),),
+        lambda middle, own, part: (lower(middle + (own + wide(part))),),
         [middle, own_down, *arrived_down],
         [(columns, low)],
     )
-    line_qkv.fourth(own_down)
     line_go.fourth(line_qkv.sent)
     sum_down.step(0, line_qkv.sent)
     down_grad, go_grad, qkv_grad = sum_down.result().T, line_go.result(), line_qkv.result()

time: 727 us -> 712 us (0.979)
  waiting for transfers between devices: 178 us -> 153 us
    ppermute x68, waiting for transfers between devices: 176 us -> 151 us  [swap(): return lax.ppermute(values, 'dp', pairs)]
    unnamed x244 -> x234, local copies, waits for them, and re-layouts: 26.4 us -> 25.7 us
  transfers between devices with their start and end apart: 85 -> 84, of which waited for: 33 -> 32; matrix products, arithmetic and copies ran while one was open for 4% -> 4% of each run, Pallas kernels for 54% -> 56%
where the time goes in v6:
time: 712 us; the launch traced here: 700 us
  Pallas kernels  392 us (55%)
  waiting for transfers between devices  153 us (21%)
  starting transfers between devices  95.2 us (13%)
  local copies, waits for them, and re-layouts  37.7 us (5%)
  other arithmetic  19.4 us (3%)
    ppermute x68, waiting for transfers between devices, swap(): return lax.ppermute(values, 'dp', pairs)  151 us
    pallas_call x8, Pallas kernels, multiply_back(): pl.pallas_call(body, grid_spec=pltpu.PrefetchScalarGridSpec(num_scalar_pr...  97.7 us
    ppermute x68, starting transfers between devices, swap(): return lax.ppermute(values, 'dp', pairs)  91.4 us
    pallas_call x7, Pallas kernels, multiply(): pl.pallas_call(body, grid=(tiles,), in_specs=[pl.BlockSpec((length, depth...  79.7 us
    pallas_call x6, Pallas kernels, gradient_parts(): pl.pallas_call(body, grid=(tiles,), in_specs=[pl.BlockSpec((depth, length...  68.2 us
    pallas_call x11, Pallas kernels, add_halves(): pl.pallas_call(body, grid=(columns // tile,), in_specs=[block] * len(term...  35 us
    pallas_call x1, Pallas kernels, attend_backward(): pl.pallas_call(functools.partial(bwd_kernel, head ** (-0.5), head), grid=...  32.9 us
    unnamed x234, local copies, waits for them, and re-layouts  25.7 us
  transfers between devices with their start and end apart: 84, of which 32 were waited for; matrix products, arithmetic and copies ran while one was open for 4% of the time, Pallas kernels for 56%

profile of v6, /device:TPU:0, one launch (start us, length us, event | category | flops | bytes accessed | tf_op | source)
XLA Modules:
  0.0 699.7 jit_solution(10327264241910433856)
XLA Ops:
  14.8 6.7 collective-permute-done.7
  26.2 10.7 %collective-permute-done.8.refs_2_.refs_11_.refs_19_ = bf16[2,96,1536]{2,1,0:T(8,128)(2,1)S(1)} collective-permute-done((bf16[2,96,1536]{2,1,0:T(8,128)(2,1)S(1)}, bf16[2,96,1536]{2,1,0:T(8,128)(2,1)S(1)}, u32[]{:S(2)}, u32[]{:S(2)}) %collective-permute-start.8) | collective-permute-done | bytes 589856 | tf_op jit(solution)/shard_map/ppermute | solution.py:78
  68.2 8.3 %collective-permute-done.14.refs_7_.refs_16_.refs_24_ = bf16[2,96,1536]{2,1,0:T(8,128)(2,1)} collective-permute-done((bf16[2,96,1536]{2,1,0:T(8,128)(2,1)S(1)}, bf16[2,96,1536]{2,1,0:T(8,128)(2,1)}, u32[]{:S(2)}, u32[]{:S(2)}) %collective-permute-start.14) | collective-permute-done | bytes 589856 | tf_op jit(solution)/shard_map/ppermute | solution.py:78
  81.7 10.2 %collective-permute-done.19.refs_2_.refs_27_.refs_32_ = bf16[4,96,896]{2,1,0:T(8,128)(2,1)S(1)} collective-permute-done((bf16[4,96,896]{2,1,0:T(8,128)(2,1)S(1)}, bf16[4,96,896]{2,1,0:T(8,128)(2,1)S(1)}, u32[]{:S(2)}, u32[]{:S(2)}) %collective-permute-start.19) | collective-permute-done | bytes 688160 | tf_op jit(solution)/shard_map/ppermute | solution.py:78
  107.0 13.8 %collective-permute-done.27 = bf16[1,96,2048]{2,1,0:T(8,128)(2,1)S(1)} collective-permute-done((bf16[1,96,2048]{2,1,0:T(8,128)(2,1)S(1)}, bf16[1,96,2048]{2,1,0:T(8,128)(2,1)S(1)}, u32[]{:S(2)}, u32[]{:S(2)}) %collective-permute-start.27) | collective-permute-done | bytes 393248 | tf_op jit(solution)/shard_map/ppermute | solution.py:78
  121.3 4.5 collective-permute-done.23.refs_2_.refs_6_
  131.0 10.1 %shard_map.248.q_ref.k_ref = bf16[1024,1536]{1,0:T(8,128)(2,1)} custom-call(bf16[1024,1536]{1,0:T(8,128)(2,1)} %get-tuple-element.170.refs_0_, bf16[2,96,1536]{2,1,0:T(8,128)(2,1)S(1)} %copy-done.13, bf16[2,96,1536]{2,1,0:T(8,128)(2,1)S(1)} %copy-done.18, bf16[2,96,1536]{2,1,0:T(8,128)(2,1)S(1)} %copy-done.21, ...), custom_call_target="tpu_custom_call" | custom-call | flops 96636768 | bytes 220200 | tf_op jit(solution)/shard_map/pallas_call | solution.py:194
  143.5 4.9 collective-permute-start.33
  148.4 10.3 %shard_map.249 = (bf16[1024,768]{1,0:T(8,128)(2,1)}, f32[1024,128]{1,0:T(8,128)S(1)}) custom-call(bf16[1024,1536]{1,0:T(8,128)(2,1)} %get-tuple-element.170.refs_0_, bf16[4,96,896]{2,1,0:T(8,128)(2,1)S(1)} %pad_maximum_fusion.7.refs_1_.refs_26_.refs_31_, bf16[4,96,896]{2,1,0:T(8,128)(2,1)S(1)} %collective-permute-done.19.refs_2_.refs_27_.refs_32_, ...), custom_call_target="tpu_custom_call" | custom-call | flops 56371444 | bytes 159907 | tf_op jit(solution)/shard_map/pallas_call | solution.py:194
  164.3 22.6 %shard_map.251 = (f32[1024,768]{1,0:T(8,128)}, f32[6,2,1024]{2,1,0:T(2,128)S(1)}) custom-call(bf16[1024,1536]{1,0:T(8,128)(2,1)} %shard_map.248.q_ref.k_ref, bf16[1024,1536]{1,0:T(8,128)(2,1)} %shard_map.248.q_ref.k_ref, bf16[1024,768]{1,0:T(8,128)(2,1)S(1)} %copy-done.44, f32[6,1024,2]{2,1,0:T(8,128)} %copy-done.28, ...), custom_call_target="tpu_custom_call" | custom-call | flops 193273536 | bytes 251658 | tf_op jit(solution)/shard_map/pallas_call | solution.py:894
  193.8 9.2 %collective-permute-done.36.refs_4_.refs_5_ = bf16[2,96,2048]{2,1,0:T(8,128)(2,1)S(1)} collective-permute-done((bf16[2,96,2048]{2,1,0:T(8,128)(2,1)S(1)}, bf16[2,96,2048]{2,1,0:T(8,128)(2,1)S(1)}, u32[]{:S(2)}, u32[]{:S(2)}) %collective-permute-start.36) | collective-permute-done | bytes 786464 | tf_op jit(solution)/shard_map/ppermute | solution.py:78
  208.7 8.9 %shard_map.252 = (f32[1024,768]{1,0:T(8,128)}, bf16[1024,768]{1,0:T(8,128)(2,1)}) custom-call(bf16[1024,1536]{1,0:T(8,128)(2,1)} %get-tuple-element.170.refs_0_, bf16[4,96,1536]{2,1,0:T(8,128)(2,1)S(1)} %pad_maximum_fusion.3.refs_1_.refs_5_, bf16[4,96,1536]{2,1,0:T(8,128)(2,1)S(1)} %collective-permute-done.23.refs_2_.refs_6_, ...), custom_call_target="tpu_custom_call" | custom-call | flops 48318384 | bytes 267386 | tf_op jit(solution)/shard_map/pallas_call | solution.py:194
  217.6 6.7 shard_map.254
  227.2 6.2 shard_map.253.refs_1_
  233.5 5.6 shard_map.255
  239.6 6.8 collective-permute-done.44
  259.5 12.1 %shard_map.257.refs_6_ = bf16[1024,2048]{1,0:T(8,128)(2,1)} custom-call(bf16[1024,1536]{1,0:T(8,128)(2,1)} %get-tuple-element.194.refs_0_, bf16[4,96,2048]{2,1,0:T(8,128)(2,1)S(1)} %copy-done.6, bf16[4,96,2048]{2,1,0:T(8,128)(2,1)} %copy-done.92, bf16[4,96,2048]{2,1,0:T(8,128)(2,1)} %collective-permute-done.37.refs_3_.refs_4_, ...), custom_call_target="tpu_custom_call" | custom-call | flops 128849016 | bytes 272629 | tf_op jit(solution)/shard_map/pallas_call | solution.py:194
  275.6 4.8 shard_map.259
  280.4 13.3 %shard_map.258 = (bf16[1024,2048]{1,0:T(8,128)(2,1)}, bf16[1024,2048]{1,0:T(8,128)(2,1)}) custom-call(bf16[1024,1536]{1,0:T(8,128)(2,1)} %get-tuple-element.194.refs_0_, bf16[4,96,2048]{2,1,0:T(8,128)(2,1)} %pad_maximum_fusion.1.refs_1_.refs_7_, bf16[4,96,2048]{2,1,0:T(8,128)(2,1)} %collective-permute-done.39.refs_2_.refs_8_, ...), custom_call_target="tpu_custom_call" | custom-call | flops 128849016 | bytes 440401 | tf_op jit(solution)/shard_map/pallas_call | solution.py:194
  293.7 11.9 %shard_map.260 = (bf16[2,4,96,2048]{3,2,1,0:T(8,128)(2,1)S(1)}, bf16[2,4,96,2048]{3,2,1,0:T(8,128)(2,1)}) custom-call(bf16[1536,1024]{1,0:T(8,128)(2,1)} %get-tuple-element.203.refs_0_, bf16[1024,2048]{1,0:T(8,128)(2,1)} %get-tuple-element.309.refs_1_.refs_0_), custom_call_target="tpu_custom_call" | custom-call | flops 128849016 | bytes 272629 | tf_op jit(solution)/shard_map/pallas_call | solution.py:434
  305.6 4.3 collective-permute-done.47.refs_3_
  315.0 14.4 %collective-permute-done.49.refs_5_ = bf16[2,96,2048]{2,1,0:T(8,128)(2,1)S(1)} collective-permute-done((bf16[2,96,2048]{2,1,0:T(8,128)(2,1)S(1)}, bf16[2,96,2048]{2,1,0:T(8,128)(2,1)S(1)}, u32[]{:S(2)}, u32[]{:S(2)}) %collective-permute-start.49) | collective-permute-done | bytes 786464 | tf_op jit(solution)/shard_map/ppermute | solution.py:78
  331.1 15.7 %shard_map.261 = (bf16[1024,2048]{1,0:T(8,128)(2,1)}, bf16[1024,2048]{1,0:T(8,128)(2,1)}) custom-call(bf16[1024,1536]{1,0:T(8,128)(2,1)} %get-tuple-element.205.refs_0_, bf16[4,96,2048]{2,1,0:T(8,128)(2,1)S(1)} %pad_maximum_fusion.2.refs_1_, bf16[4,96,2048]{2,1,0:T(8,128)(2,1)} %collective-permute-done.46.refs_2_, bf16[4,96,2048]{2,1,0:T(8,128)(2,1)} %copy-done.91, ...), custom_call_target="tpu_custom_call" | custom-call | flops 128849016 | bytes 524288 | tf_op jit(solution)/shard_map/pallas_call | solution.py:194
  346.8 12.3 %shard_map.262 = (bf16[4,2,96,2048]{3,2,1,0:T(8,128)(2,1)S(1)}, bf16[4,2,96,2048]{3,2,1,0:T(8,128)(2,1)}) custom-call(bf16[1536,1024]{1,0:T(8,128)(2,1)} %get-tuple-element.213.refs_0_, bf16[1024,2048]{1,0:T(8,128)(2,1)} %get-tuple-element.214.refs_1_), custom_call_target="tpu_custom_call" | custom-call | flops 128849016 | bytes 272629 | tf_op jit(solution)/shard_map/pallas_call | solution.py:434
  360.8 12.1 %shard_map.263 = (bf16[4,2,96,2048]{3,2,1,0:T(8,128)(2,1)}, bf16[4,2,96,2048]{3,2,1,0:T(8,128)(2,1)}) custom-call(bf16[1536,1024]{1,0:T(8,128)(2,1)} %get-tuple-element.213.refs_0_, bf16[1024,2048]{1,0:T(8,128)(2,1)} %get-tuple-element.218.refs_1_.refs_0_), custom_call_target="tpu_custom_call" | custom-call | flops 128849016 | bytes 272629 | tf_op jit(solution)/shard_map/pallas_call | solution.py:434
  374.9 16.7 %shard_map.266 = (bf16[512,768]{1,0:T(8,128)(2,1)S(1)}, bf16[512,768]{1,0:T(8,128)(2,1)S(1)}) custom-call(s32[1]{0:T(128)} %constant.23.clone.1.half_ref, bf16[1024,2048]{1,0:T(8,128)(2,1)} %get-tuple-element.218.refs_1_.refs_0_, bf16[1024,2048]{1,0:T(8,128)(2,1)} %get-tuple-element.214.refs_1_, bf16[4,96,2048]{2,1,0:T(8,128)(2,1)} %copy-done.5, ...), custom_call_target="tpu_custom_call" | custom-call | flops 128849016 | bytes 398458 | tf_op jit(solution)/shard_map/pallas_call | solution.py:275
  392.1 17.4 %shard_map.264.refs_1_ = f32[512,1536]{1,0:T(8,128)} custom-call(s32[1]{0:T(128)} %constant.22.clone.1.half_ref, bf16[1024,2048]{1,0:T(8,128)(2,1)} %get-tuple-element.218.refs_1_.refs_0_, bf16[1024,2048]{1,0:T(8,128)(2,1)} %get-tuple-element.214.refs_1_, bf16[4,96,2048]{2,1,0:T(8,128)(2,1)} %copy-done.5, bf16[4,96,2048]{2,1,0:T(8,128)(2,1)} %copy-done.92, ...), custom_call_target="tpu_custom_call" | custom-call | flops 128849016 | bytes 398458 | tf_op jit(solution)/shard_map/pallas_call | solution.py:275
  409.5 4.7 shard_map.265
  414.2 6.3 shard_map.267
  428.9 9.4 %shard_map.269 = (bf16[1024,768]{1,0:T(8,128)(2,1)}, bf16[1024,768]{1,0:T(8,128)(2,1)}) custom-call(bf16[1024,1536]{1,0:T(8,128)(2,1)} %get-tuple-element.228.refs_0_, bf16[4,96,1536]{2,1,0:T(8,128)(2,1)S(1)} %pad_maximum_fusion.3.refs_1_.refs_5_, bf16[4,96,1536]{2,1,0:T(8,128)(2,1)S(1)} %copy-done.2, bf16[4,96,1536]{2,1,0:T(8,128)(2,1)} %copy-done.90, ...), custom_call_target="tpu_custom_call" | custom-call | flops 48318384 | bytes 298844 | tf_op jit(solution)/shard_map/pallas_call | solution.py:194
  438.3 3.9 collective-permute-done.56.refs_1_
  448.9 4.7 shard_map.271
  455.8 12.5 %shard_map.272 = (bf16[2,2,96,1536]{3,2,1,0:T(8,128)(2,1)}, bf16[2,2,96,1536]{3,2,1,0:T(8,128)(2,1)}, bf16[2,2,96,1536]{3,2,1,0:T(8,128)(2,1)S(1)}, bf16[2,2,96,1536]{3,2,1,0:T(8,128)(2,1)}) custom-call(bf16[1536,1024]{1,0:T(8,128)(2,1)} %get-tuple-element.239.refs_0_, bf16[1536,1024]{1,0:T(8,128)(2,1)} %get-tuple-element.240.refs_1_, ...), custom_call_target="tpu_custom_call" | custom-call | flops 96636768 | bytes 283115 | tf_op jit(solution)/shard_map/pallas_call | solution.py:434
  469.7 32.9 %shard_map.273 = (bf16[1024,768]{1,0:T(8,128)(2,1)S(1)}, bf16[1024,768]{1,0:T(8,128)(2,1)S(1)}, bf16[1024,768]{1,0:T(8,128)(2,1)}, f32[6,2,1024]{2,1,0:T(2,128)S(1)}, f32[6,1024,2]{2,1,0:T(8,128)}) custom-call(bf16[1024,1536]{1,0:T(8,128)(2,1)} %shard_map.248.q_ref.k_ref, bf16[1024,1536]{1,0:T(8,128)(2,1)} %shard_map.248.q_ref.k_ref, ...), custom_call_target="tpu_custom_call" | custom-call | flops 483183808 | bytes 251658 | tf_op jit(solution)/shard_map/pallas_call | solution.py:914
  514.5 11.9 %shard_map.276 = (bf16[2,2,96,1536]{3,2,1,0:T(8,128)(2,1)}, bf16[2,2,96,1536]{3,2,1,0:T(8,128)(2,1)}, bf16[2,2,96,1536]{3,2,1,0:T(8,128)(2,1)S(1)}, bf16[2,2,96,1536]{3,2,1,0:T(8,128)(2,1)}) custom-call(bf16[1536,1024]{1,0:T(8,128)(2,1)} %get-tuple-element.239.refs_0_, bf16[1024,768]{1,0:T(8,128)(2,1)} %copy-done.26, bf16[1024,768]{1,0:T(8,128)(2,1)} %copy-done.27), custom_call_target="tpu_custom_call" | custom-call | flops 96636768 | bytes 220200 | tf_op jit(solution)/shard_map/pallas_call | solution.py:434
  538.5 7.6 %shard_map.280 = (bf16[2,2,96,896]{3,2,1,0:T(8,128)(2,1)}, bf16[2,2,96,896]{3,2,1,0:T(8,128)(2,1)}, bf16[2,2,96,896]{3,2,1,0:T(8,128)(2,1)S(1)}, bf16[2,2,96,896]{3,2,1,0:T(8,128)(2,1)S(1)}) custom-call(bf16[1536,1024]{1,0:T(8,128)(2,1)} %get-tuple-element.239.refs_0_, bf16[1024,768]{1,0:T(8,128)(2,1)} %get-tuple-element.265.refs_1_.refs_3_, ...), custom_call_target="tpu_custom_call" | custom-call | flops 56371444 | bytes 154664 | tf_op jit(solution)/shard_map/pallas_call | solution.py:434
  547.0 15.5 %shard_map.281 = (bf16[512,768]{1,0:T(8,128)(2,1)}, bf16[512,768]{1,0:T(8,128)(2,1)}) custom-call(s32[1]{0:T(128)} %bitcast.11.half_ref, bf16[1024,768]{1,0:T(8,128)(2,1)} %get-tuple-element.272.refs_2_.refs_0_, bf16[1024,768]{1,0:T(8,128)(2,1)} %copy-done.26, bf16[1024,768]{1,0:T(8,128)(2,1)} %copy-done.27, ...), custom_call_target="tpu_custom_call" | custom-call | flops 100663296 | bytes 325058 | tf_op jit(solution)/shard_map/pallas_call | solution.py:275
  563.1 9.8 %shard_map.282 = bf16[512,1536]{1,0:T(8,128)(2,1)} custom-call(s32[1]{0:T(128)} %constant.23.clone.1.half_ref, bf16[1024,2048]{1,0:T(8,128)(2,1)} %get-tuple-element.309.refs_1_.refs_0_, bf16[4,96,2048]{2,1,0:T(8,128)(2,1)} %copy-done.3, bf16[4,96,2048]{2,1,0:T(8,128)(2,1)} %collective-permute-done.46.refs_2_, bf16[4,96,2048]{2,1,0:T(8,128)(2,1)} %copy-done.91, ...), custom_call_target="tpu_custom_call" | custom-call | flops 64424508 | bytes 230686 | tf_op jit(solution)/shard_map/pallas_call | solution.py:275
  586.7 15.3 %shard_map.286.refs_1_ = f32[512,1536]{1,0:T(8,128)} custom-call(s32[1]{0:T(128)} %bitcast.half_ref, bf16[1024,768]{1,0:T(8,128)(2,1)} %get-tuple-element.272.refs_2_.refs_0_, bf16[1024,768]{1,0:T(8,128)(2,1)} %copy-done.26, bf16[1024,768]{1,0:T(8,128)(2,1)} %copy-done.27, bf16[1024,768]{1,0:T(8,128)(2,1)} %get-tuple-element.265.refs_1_.refs_3_, ...), custom_call_target="tpu_custom_call" | custom-call | flops 100663296 | bytes 325058 | tf_op jit(solution)/shard_map/pallas_call | solution.py:275
  604.5 6.1 shard_map.288
  610.7 4.7 shard_map.290
  617.1 4.7 shard_map.289
  626.6 5.0 collective-permute-done.72
  641.1 19.1 %collective-permute-done.75 = bf16[2,96,2432]{2,1,0:T(8,128)(2,1)S(1)} collective-permute-done((bf16[2,96,2432]{2,1,0:T(8,128)(2,1)}, bf16[2,96,2432]{2,1,0:T(8,128)(2,1)S(1)}, u32[]{:S(2)}, u32[]{:S(2)}) %collective-permute-start.75) | collective-permute-done | bytes 933920 | tf_op jit(solution)/shard_map/ppermute | solution.py:78
  666.8 10.3 %shard_map.293.refs_1_ = f32[512,1536]{1,0:T(8,128)} custom-call(s32[1]{0:T(128)} %constant.22.clone.1.half_ref, bf16[1024,2048]{1,0:T(8,128)(2,1)} %get-tuple-element.309.refs_1_.refs_0_, bf16[4,96,2048]{2,1,0:T(8,128)(2,1)S(1)} %copy-done.4, bf16[4,96,2048]{2,1,0:T(8,128)(2,1)} %collective-permute-done.46.refs_2_, bf16[4,96,2048]{2,1,0:T(8,128)(2,1)} %copy-done.91, ...), custom_call_target="tpu_custom_call" | custom-call | flops 64424508 | bytes 230686 | tf_op jit(solution)/shard_map/pallas_call | solution.py:275
  677.0 4.6 shard_map.294
  681.6 5.2 collective-permute-done.79
  688.9 7.0 collective-permute-done.77
  (473 shorter events, 215.9 us)
Async XLA Ops:
  24.6 22.9 %collective-permute-start.10 = (bf16[2,96,1536]{2,1,0:T(8,128)(2,1)S(1)}, bf16[2,96,1536]{2,1,0:T(8,128)(2,1)S(1)}, u32[]{:S(2)}, u32[]{:S(2)}) collective-permute-start(bf16[2,96,1536]{2,1,0:T(8,128)(2,1)S(1)} %pad_maximum_fusion.8.refs_1_.refs_10_.refs_18_), channel_id=1, source_target_pairs={{0,2},{2,0},{4,6},{6,4},{8,10},{10,8},{12,14},{14,12},{16,18},{18,... | collective-permute-start | bytes 1769480 | tf_op jit(solution)/shard_map/ppermute | solution.py:78
  45.5 22.1 %collective-permute-start.16 = (bf16[2,96,1536]{2,1,0:T(8,128)(2,1)S(1)}, bf16[2,96,1536]{2,1,0:T(8,128)(2,1)}, u32[]{:S(2)}, u32[]{:S(2)}) collective-permute-start(bf16[2,96,1536]{2,1,0:T(8,128)(2,1)S(1)} %pad_maximum_fusion.8.refs_1_.refs_10_.refs_18_), channel_id=1, source_target_pairs={{0,4},{2,6},{4,0},{6,2},{8,12},{10,14},{12,8},{14,10},{16,20},{18,... | collective-permute-start | bytes 1769480 | tf_op jit(solution)/shard_map/ppermute | solution.py:78
  46.0 21.7 %collective-permute-start.17 = (bf16[2,96,1536]{2,1,0:T(8,128)(2,1)S(1)}, bf16[2,96,1536]{2,1,0:T(8,128)(2,1)}, u32[]{:S(2)}, u32[]{:S(2)}) collective-permute-start(bf16[2,96,1536]{2,1,0:T(8,128)(2,1)S(1)} %collective-permute-done.8.refs_2_.refs_11_.refs_19_), channel_id=1, source_target_pairs={{0,2},{2,0},{4,6},{6,4},{8,10},{10,8},{12,14},{14,12},{16,18},{18,... | collective-permute-start | bytes 1769480 | tf_op jit(solution)/shard_map/ppermute | solution.py:78
  47.5 29.0 %collective-permute-start.14 = (bf16[2,96,1536]{2,1,0:T(8,128)(2,1)S(1)}, bf16[2,96,1536]{2,1,0:T(8,128)(2,1)}, u32[]{:S(2)}, u32[]{:S(2)}) collective-permute-start(bf16[2,96,1536]{2,1,0:T(8,128)(2,1)S(1)} %collective-permute-done.10.refs_3_.refs_12_.refs_20_), channel_id=1, source_target_pairs={{0,4},{2,6},{4,0},{6,2},{8,12},{10,14},{12,8},{14,10},{16,20},{18,... | collective-permute-start | bytes 1769480 | tf_op jit(solution)/shard_map/ppermute | solution.py:78
  54.0 22.5 %collective-permute-start.15 = (bf16[2,96,1536]{2,1,0:T(8,128)(2,1)S(1)}, bf16[2,96,1536]{2,1,0:T(8,128)(2,1)}, u32[]{:S(2)}, u32[]{:S(2)}) collective-permute-start(bf16[2,96,1536]{2,1,0:T(8,128)(2,1)S(1)} %collective-permute-done.11.refs_6_.refs_15_.refs_23_), channel_id=1, source_target_pairs={{0,2},{2,0},{4,6},{6,4},{8,10},{10,8},{12,14},{14,12},{16,18},{18,... | collective-permute-start | bytes 1769480 | tf_op jit(solution)/shard_map/ppermute | solution.py:78
  67.6 27.3 %collective-permute-start.5 = (bf16[512,768]{1,0:T(8,128)(2,1)S(1)}, bf16[512,768]{1,0:T(8,128)(2,1)S(1)}, u32[]{:S(2)}, u32[]{:S(2)}) collective-permute-start(bf16[512,768]{1,0:T(8,128)(2,1)S(1)} %get-tuple-element.168), channel_id=1, source_target_pairs={{0,1},{1,0},{2,3},{3,2},{4,5},{5,4},{6,7},{7,6},{8,9},{9,8},{10,11... | collective-permute-start | bytes 2359304 | tf_op jit(solution)/shard_map/ppermute | solution.py:51
  67.7 27.3 %collective-permute-start.6 = (bf16[512,768]{1,0:T(8,128)(2,1)S(1)}, bf16[512,768]{1,0:T(8,128)(2,1)S(1)}, u32[]{:S(2)}, u32[]{:S(2)}) collective-permute-start(bf16[512,768]{1,0:T(8,128)(2,1)S(1)} %get-tuple-element.169), channel_id=1, source_target_pairs={{0,1},{1,0},{2,3},{3,2},{4,5},{5,4},{6,7},{7,6},{8,9},{9,8},{10,11... | collective-permute-start | bytes 2359304 | tf_op jit(solution)/shard_map/ppermute | solution.py:51
  101.4 24.4 %collective-permute-start.23 = (bf16[4,96,1536]{2,1,0:T(8,128)(2,1)S(1)}, bf16[4,96,1536]{2,1,0:T(8,128)(2,1)S(1)}, u32[]{:S(2)}, u32[]{:S(2)}) collective-permute-start(bf16[4,96,1536]{2,1,0:T(8,128)(2,1)S(1)} %pad_maximum_fusion.3.refs_1_.refs_5_), channel_id=1, source_target_pairs={{0,2},{2,0},{4,6},{6,4},{8,10},{10,8},{12,14},{14,12},{16,18},{18,... | collective-permute-start | bytes 3538952 | tf_op jit(solution)/shard_map/ppermute | solution.py:78
  103.3 25.7 %collective-permute-start.24 = (bf16[4,96,1536]{2,1,0:T(8,128)(2,1)S(1)}, bf16[4,96,1536]{2,1,0:T(8,128)(2,1)S(1)}, u32[]{:S(2)}, u32[]{:S(2)}) collective-permute-start(bf16[4,96,1536]{2,1,0:T(8,128)(2,1)S(1)} %pad_maximum_fusion.3.refs_1_.refs_5_), channel_id=1, source_target_pairs={{0,4},{2,6},{4,0},{6,2},{8,12},{10,14},{12,8},{14,10},{16,20},{18,... | collective-permute-start | bytes 3538952 | tf_op jit(solution)/shard_map/ppermute | solution.py:78
  141.6 45.3 %collective-permute-start.35 = (bf16[4,96,2048]{2,1,0:T(8,128)(2,1)S(1)}, bf16[4,96,2048]{2,1,0:T(8,128)(2,1)S(1)}, u32[]{:S(2)}, u32[]{:S(2)}) collective-permute-start(bf16[4,96,2048]{2,1,0:T(8,128)(2,1)S(1)} %pad_maximum_fusion.refs_1_.refs_2_), channel_id=1, source_target_pairs={{0,2},{2,0},{4,6},{6,4},{8,10},{10,8},{12,14},{14,12},{16,18},{18,... | collective-permute-start | bytes 4718600 | tf_op jit(solution)/shard_map/ppermute | solution.py:78
  143.4 45.8 %collective-permute-start.37 = (bf16[4,96,2048]{2,1,0:T(8,128)(2,1)S(1)}, bf16[4,96,2048]{2,1,0:T(8,128)(2,1)}, u32[]{:S(2)}, u32[]{:S(2)}) collective-permute-start(bf16[4,96,2048]{2,1,0:T(8,128)(2,1)S(1)} %pad_maximum_fusion.refs_1_.refs_2_), channel_id=1, source_target_pairs={{0,4},{2,6},{4,0},{6,2},{8,12},{10,14},{12,8},{14,10},{16,20},{18,... | collective-permute-start | bytes 4718600 | tf_op jit(solution)/shard_map/ppermute | solution.py:78
  163.1 29.4 %collective-permute-start.34 = (bf16[2,96,2048]{2,1,0:T(8,128)(2,1)S(1)}, bf16[2,96,2048]{2,1,0:T(8,128)(2,1)S(1)}, u32[]{:S(2)}, u32[]{:S(2)}) collective-permute-start(bf16[2,96,2048]{2,1,0:T(8,128)(2,1)S(1)} %pad_maximum_fusion.5), channel_id=1, source_target_pairs={{0,8},{2,10},{4,12},{6,14},{8,0},{10,2},{12,4},{14,6},{16,24},{18,... | collective-permute-start | bytes 2359304 | tf_op jit(solution)/shard_map/ppermute | solution.py:78
  207.6 40.9 %collective-permute-start.39 = (bf16[4,96,2048]{2,1,0:T(8,128)(2,1)}, bf16[4,96,2048]{2,1,0:T(8,128)(2,1)}, u32[]{:S(2)}, u32[]{:S(2)}) collective-permute-start(bf16[4,96,2048]{2,1,0:T(8,128)(2,1)} %pad_maximum_fusion.1.refs_1_.refs_7_), channel_id=1, source_target_pairs={{0,2},{2,0},{4,6},{6,4},{8,10},{10,8},{12,14},{14,12},{16,18},{18,... | collective-permute-start | bytes 4718600 | tf_op jit(solution)/shard_map/ppermute | solution.py:78
  207.9 44.1 %collective-permute-start.40 = (bf16[4,96,2048]{2,1,0:T(8,128)(2,1)}, bf16[4,96,2048]{2,1,0:T(8,128)(2,1)}, u32[]{:S(2)}, u32[]{:S(2)}) collective-permute-start(bf16[4,96,2048]{2,1,0:T(8,128)(2,1)} %pad_maximum_fusion.1.refs_1_.refs_7_), channel_id=1, source_target_pairs={{0,4},{2,6},{4,0},{6,2},{8,12},{10,14},{12,8},{14,10},{16,20},{18,... | collective-permute-start | bytes 4718600 | tf_op jit(solution)/shard_map/ppermute | solution.py:78
  225.6 20.7 %collective-permute-start.44 = (bf16[1,96,2048]{2,1,0:T(8,128)(2,1)}, bf16[1,96,2048]{2,1,0:T(8,128)(2,1)}, u32[]{:S(2)}, u32[]{:S(2)}) collective-permute-start(bf16[1,96,2048]{2,1,0:T(8,128)(2,1)} %convert_bitcast_fusion), channel_id=1, source_target_pairs={{0,16},{2,18},{4,20},{6,22},{8,24},{10,26},{12,28},{14,30},{16,0},... | collective-permute-start | bytes 1179656 | tf_op jit(solution)/shard_map/ppermute | solution.py:78
  248.5 23.0 %collective-permute-start.45 = (bf16[2,96,2048]{2,1,0:T(8,128)(2,1)}, bf16[2,96,2048]{2,1,0:T(8,128)(2,1)}, u32[]{:S(2)}, u32[]{:S(2)}) collective-permute-start(bf16[2,96,2048]{2,1,0:T(8,128)(2,1)} %pad_maximum_fusion.6), channel_id=1, source_target_pairs={{0,8},{2,10},{4,12},{6,14},{8,0},{10,2},{12,4},{14,6},{16,24},{18,... | collective-permute-start | bytes 2359304 | tf_op jit(solution)/shard_map/ppermute | solution.py:78
  250.8 22.3 %collective-permute-start.41 = (bf16[2,96,2048]{2,1,0:T(8,128)(2,1)}, bf16[2,96,2048]{2,1,0:T(8,128)(2,1)S(1)}, u32[]{:S(2)}, u32[]{:S(2)}) collective-permute-start(bf16[2,96,2048]{2,1,0:T(8,128)(2,1)} %slice.119), channel_id=1, source_target_pairs={{0,4},{2,6},{4,0},{6,2},{8,12},{10,14},{12,8},{14,10},{16,20},{18,... | collective-permute-start | bytes 2359304 | tf_op jit(solution)/shard_map/ppermute | solution.py:78
  273.1 36.8 %collective-permute-start.47 = (bf16[4,96,2048]{2,1,0:T(8,128)(2,1)S(1)}, bf16[4,96,2048]{2,1,0:T(8,128)(2,1)S(1)}, u32[]{:S(2)}, u32[]{:S(2)}) collective-permute-start(bf16[4,96,2048]{2,1,0:T(8,128)(2,1)S(1)} %pad_maximum_fusion.2.refs_1_), channel_id=1, source_target_pairs={{0,4},{2,6},{4,0},{6,2},{8,12},{10,14},{12,8},{14,10},{16,20},{18,... | collective-permute-start | bytes 4718600 | tf_op jit(solution)/shard_map/ppermute | solution.py:78
  273.9 36.6 %collective-permute-start.46 = (bf16[4,96,2048]{2,1,0:T(8,128)(2,1)S(1)}, bf16[4,96,2048]{2,1,0:T(8,128)(2,1)}, u32[]{:S(2)}, u32[]{:S(2)}) collective-permute-start(bf16[4,96,2048]{2,1,0:T(8,128)(2,1)S(1)} %pad_maximum_fusion.2.refs_1_), channel_id=1, source_target_pairs={{0,2},{2,0},{4,6},{6,4},{8,10},{10,8},{12,14},{14,12},{16,18},{18,... | collective-permute-start | bytes 4718600 | tf_op jit(solution)/shard_map/ppermute | solution.py:78
  313.1 96.5 %collective-permute-start.50 = (bf16[2,4,96,2048]{3,2,1,0:T(8,128)(2,1)}, bf16[2,4,96,2048]{3,2,1,0:T(8,128)(2,1)}, u32[]{:S(2)}, u32[]{:S(2)}) collective-permute-start(bf16[2,4,96,2048]{3,2,1,0:T(8,128)(2,1)} %copy-done.86), channel_id=1, source_target_pairs={{0,8},{2,10},{4,12},{6,14},{8,0},{10,2},{12,4},{14,6},{16,24},{18,... | collective-permute-start | bytes 9437192 | tf_op jit(solution)/shard_map/ppermute | solution.py:78
  372.8 69.3 %collective-permute-start.56 = (bf16[4,2,96,2048]{3,2,1,0:T(8,128)(2,1)}, bf16[4,2,96,2048]{3,2,1,0:T(8,128)(2,1)}, u32[]{:S(2)}, u32[]{:S(2)}) collective-permute-start(bf16[4,2,96,2048]{3,2,1,0:T(8,128)(2,1)} %get-tuple-element.217), channel_id=1, source_target_pairs={{0,4},{2,6},{4,0},{6,2},{8,12},{10,14},{12,8},{14,10},{16,20},{18,... | collective-permute-start | bytes 9437192 | tf_op jit(solution)/shard_map/ppermute | solution.py:78
  373.7 68.6 %collective-permute-start.55 = (bf16[4,2,96,2048]{3,2,1,0:T(8,128)(2,1)}, bf16[4,2,96,2048]{3,2,1,0:T(8,128)(2,1)}, u32[]{:S(2)}, u32[]{:S(2)}) collective-permute-start(bf16[4,2,96,2048]{3,2,1,0:T(8,128)(2,1)} %copy-done.85), channel_id=1, source_target_pairs={{0,2},{2,0},{4,6},{6,4},{8,10},{10,8},{12,14},{14,12},{16,18},{18,... | collective-permute-start | bytes 9437192 | tf_op jit(solution)/shard_map/ppermute | solution.py:78
  391.5 22.7 %collective-permute-start.51 = (bf16[512,768]{1,0:T(8,128)(2,1)S(1)}, bf16[512,768]{1,0:T(8,128)(2,1)S(1)}, u32[]{:S(2)}, u32[]{:S(2)}) collective-permute-start(bf16[512,768]{1,0:T(8,128)(2,1)S(1)} %get-tuple-element.223), channel_id=1, source_target_pairs={{0,1},{1,0},{2,3},{3,2},{4,5},{5,4},{6,7},{7,6},{8,9},{9,8},{10,11... | collective-permute-start | bytes 2359304 | tf_op jit(solution)/shard_map/ppermute | solution.py:51
  391.6 22.6 %collective-permute-start.52 = (bf16[512,768]{1,0:T(8,128)(2,1)S(1)}, bf16[512,768]{1,0:T(8,128)(2,1)S(1)}, u32[]{:S(2)}, u32[]{:S(2)}) collective-permute-start(bf16[512,768]{1,0:T(8,128)(2,1)S(1)} %get-tuple-element.224), channel_id=1, source_target_pairs={{0,1},{1,0},{2,3},{3,2},{4,5},{5,4},{6,7},{7,6},{8,9},{9,8},{10,11... | collective-permute-start | bytes 2359304 | tf_op jit(solution)/shard_map/ppermute | solution.py:51
  421.0 83.9 %collective-permute-start.59 = (bf16[1,384,2048]{2,1,0:T(8,128)(2,1)}, bf16[1,384,2048]{2,1,0:T(8,128)(2,1)}, u32[]{:S(2)}, u32[]{:S(2)}) collective-permute-start(bf16[1,384,2048]{2,1,0:T(8,128)(2,1)} %get-tuple-element.221), channel_id=1, source_target_pairs={{0,16},{2,18},{4,20},{6,22},{8,24},{10,26},{12,28},{14,30},{16,0},... | collective-permute-start | bytes 4718600 | tf_op jit(solution)/shard_map/ppermute | solution.py:78
  447.2 61.1 %collective-permute-start.58 = (bf16[4,96,2048]{2,1,0:T(8,128)(2,1)S(1)}, bf16[4,96,2048]{2,1,0:T(8,128)(2,1)}, u32[]{:S(2)}, u32[]{:S(2)}) collective-permute-start(bf16[4,96,2048]{2,1,0:T(8,128)(2,1)S(1)} %get-tuple-element.234), channel_id=1, source_target_pairs={{0,4},{2,6},{4,0},{6,2},{8,12},{10,14},{12,8},{14,10},{16,20},{18,... | collective-permute-start | bytes 4718600 | tf_op jit(solution)/shard_map/ppermute | solution.py:78
  454.8 53.5 %collective-permute-start.57 = (bf16[4,96,2048]{2,1,0:T(8,128)(2,1)}, bf16[4,96,2048]{2,1,0:T(8,128)(2,1)}, u32[]{:S(2)}, u32[]{:S(2)}) collective-permute-start(bf16[4,96,2048]{2,1,0:T(8,128)(2,1)} %get-tuple-element.237), channel_id=1, source_target_pairs={{0,2},{2,0},{4,6},{6,4},{8,10},{10,8},{12,14},{14,12},{16,18},{18,... | collective-permute-start | bytes 4718600 | tf_op jit(solution)/shard_map/ppermute | solution.py:78
  468.3 64.4 %collective-permute-start.61 = (bf16[2,2,96,1536]{3,2,1,0:T(8,128)(2,1)}, bf16[2,2,96,1536]{3,2,1,0:T(8,128)(2,1)S(1)}, u32[]{:S(2)}, u32[]{:S(2)}) collective-permute-start(bf16[2,2,96,1536]{3,2,1,0:T(8,128)(2,1)} %get-tuple-element.242), channel_id=1, source_target_pairs={{0,2},{2,0},{4,6},{6,4},{8,10},{10,8},{12,14},{14,12},{16,18},{18,... | collective-permute-start | bytes 3538952 | tf_op jit(solution)/shard_map/ppermute | solution.py:78
  469.4 63.3 %collective-permute-start.60 = (bf16[2,2,96,1536]{3,2,1,0:T(8,128)(2,1)}, bf16[2,2,96,1536]{3,2,1,0:T(8,128)(2,1)S(1)}, u32[]{:S(2)}, u32[]{:S(2)}) collective-permute-start(bf16[2,2,96,1536]{3,2,1,0:T(8,128)(2,1)} %get-tuple-element.241), channel_id=1, source_target_pairs={{0,4},{2,6},{4,0},{6,2},{8,12},{10,14},{12,8},{14,10},{16,20},{18,... | collective-permute-start | bytes 3538952 | tf_op jit(solution)/shard_map/ppermute | solution.py:78
  526.4 36.1 %collective-permute-start.64 = (bf16[2,2,96,1536]{3,2,1,0:T(8,128)(2,1)}, bf16[2,2,96,1536]{3,2,1,0:T(8,128)(2,1)}, u32[]{:S(2)}, u32[]{:S(2)}) collective-permute-start(bf16[2,2,96,1536]{3,2,1,0:T(8,128)(2,1)} %get-tuple-element.258), channel_id=1, source_target_pairs={{0,2},{2,0},{4,6},{6,4},{8,10},{10,8},{12,14},{14,12},{16,18},{18,... | collective-permute-start | bytes 3538952 | tf_op jit(solution)/shard_map/ppermute | solution.py:78
  527.9 34.8 %collective-permute-start.62 = (bf16[2,2,96,1536]{3,2,1,0:T(8,128)(2,1)}, bf16[2,2,96,1536]{3,2,1,0:T(8,128)(2,1)}, u32[]{:S(2)}, u32[]{:S(2)}) collective-permute-start(bf16[2,2,96,1536]{3,2,1,0:T(8,128)(2,1)} %get-tuple-element.257), channel_id=1, source_target_pairs={{0,4},{2,6},{4,0},{6,2},{8,12},{10,14},{12,8},{14,10},{16,20},{18,... | collective-permute-start | bytes 3538952 | tf_op jit(solution)/shard_map/ppermute | solution.py:78
  529.1 53.4 %collective-permute-start.67 = (bf16[2,96,4096]{2,1,0:T(8,128)(2,1)}, bf16[2,96,4096]{2,1,0:T(8,128)(2,1)}, u32[]{:S(2)}, u32[]{:S(2)}) collective-permute-start(bf16[2,96,4096]{2,1,0:T(8,128)(2,1)} %copy-done.87), channel_id=1, source_target_pairs={{0,8},{2,10},{4,12},{6,14},{8,0},{10,2},{12,4},{14,6},{16,24},{18,... | collective-permute-start | bytes 4718600 | tf_op jit(solution)/shard_map/ppermute | solution.py:78
  534.4 45.6 %collective-permute-start.69 = (bf16[2,96,1536]{2,1,0:T(8,128)(2,1)}, bf16[2,96,1536]{2,1,0:T(8,128)(2,1)}, u32[]{:S(2)}, u32[]{:S(2)}) collective-permute-start(bf16[2,96,1536]{2,1,0:T(8,128)(2,1)} %get-tuple-element.264), channel_id=1, source_target_pairs={{0,4},{2,6},{4,0},{6,2},{8,12},{10,14},{12,8},{14,10},{16,20},{18,... | collective-permute-start | bytes 1769480 | tf_op jit(solution)/shard_map/ppermute | solution.py:78
  537.5 43.7 %collective-permute-start.68 = (bf16[2,96,1536]{2,1,0:T(8,128)(2,1)}, bf16[2,96,1536]{2,1,0:T(8,128)(2,1)}, u32[]{:S(2)}, u32[]{:S(2)}) collective-permute-start(bf16[2,96,1536]{2,1,0:T(8,128)(2,1)} %get-tuple-element.261), channel_id=1, source_target_pairs={{0,2},{2,0},{4,6},{6,4},{8,10},{10,8},{12,14},{14,12},{16,18},{18,... | collective-permute-start | bytes 1769480 | tf_op jit(solution)/shard_map/ppermute | solution.py:78
  562.5 23.4 %collective-permute-start.70 = (bf16[512,768]{1,0:T(8,128)(2,1)}, bf16[512,768]{1,0:T(8,128)(2,1)S(1)}, u32[]{:S(2)}, u32[]{:S(2)}) collective-permute-start(bf16[512,768]{1,0:T(8,128)(2,1)} %get-tuple-element.273), channel_id=1, source_target_pairs={{0,1},{1,0},{2,3},{3,2},{4,5},{5,4},{6,7},{7,6},{8,9},{9,8},{10,11... | collective-permute-start | bytes 2359304 | tf_op jit(solution)/shard_map/ppermute | solution.py:51
  562.6 23.4 %collective-permute-start.71 = (bf16[512,768]{1,0:T(8,128)(2,1)}, bf16[512,768]{1,0:T(8,128)(2,1)S(1)}, u32[]{:S(2)}, u32[]{:S(2)}) collective-permute-start(bf16[512,768]{1,0:T(8,128)(2,1)} %get-tuple-element.274), channel_id=1, source_target_pairs={{0,1},{1,0},{2,3},{3,2},{4,5},{5,4},{6,7},{7,6},{8,9},{9,8},{10,11... | collective-permute-start | bytes 2359304 | tf_op jit(solution)/shard_map/ppermute | solution.py:51
  579.9 30.8 %collective-permute-start.73 = (bf16[2,2,96,896]{3,2,1,0:T(8,128)(2,1)}, bf16[2,2,96,896]{3,2,1,0:T(8,128)(2,1)}, u32[]{:S(2)}, u32[]{:S(2)}) collective-permute-start(bf16[2,2,96,896]{3,2,1,0:T(8,128)(2,1)} %get-tuple-element.302), channel_id=1, source_target_pairs={{0,2},{2,0},{4,6},{6,4},{8,10},{10,8},{12,14},{14,12},{16,18},{18,... | collective-permute-start | bytes 2064392 | tf_op jit(solution)/shard_map/ppermute | solution.py:78
  581.3 35.9 %collective-permute-start.66 = (bf16[2,2,96,896]{3,2,1,0:T(8,128)(2,1)}, bf16[2,2,96,896]{3,2,1,0:T(8,128)(2,1)}, u32[]{:S(2)}, u32[]{:S(2)}) collective-permute-start(bf16[2,2,96,896]{3,2,1,0:T(8,128)(2,1)} %get-tuple-element.285), channel_id=1, source_target_pairs={{0,4},{2,6},{4,0},{6,2},{8,12},{10,14},{12,8},{14,10},{16,20},{18,... | collective-permute-start | bytes 2064392 | tf_op jit(solution)/shard_map/ppermute | solution.py:78
  582.6 40.9 %collective-permute-start.65 = (bf16[2,96,1536]{2,1,0:T(8,128)(2,1)}, bf16[2,96,1536]{2,1,0:T(8,128)(2,1)}, u32[]{:S(2)}, u32[]{:S(2)}) collective-permute-start(bf16[2,96,1536]{2,1,0:T(8,128)(2,1)} %get-tuple-element.283), channel_id=1, source_target_pairs={{0,4},{2,6},{4,0},{6,2},{8,12},{10,14},{12,8},{14,10},{16,20},{18,... | collective-permute-start | bytes 1769480 | tf_op jit(solution)/shard_map/ppermute | solution.py:78
  585.9 53.8 %collective-permute-start.80 = (bf16[1,96,4096]{2,1,0:T(8,128)(2,1)}, bf16[1,96,4096]{2,1,0:T(8,128)(2,1)}, u32[]{:S(2)}, u32[]{:S(2)}) collective-permute-start(bf16[1,96,4096]{2,1,0:T(8,128)(2,1)} %get-tuple-element.288), channel_id=1, source_target_pairs={{0,16},{2,18},{4,20},{6,22},{8,24},{10,26},{12,28},{14,30},{16,0},... | collective-permute-start | bytes 2359304 | tf_op jit(solution)/shard_map/ppermute | solution.py:78
  586.0 37.7 %collective-permute-start.63 = (bf16[2,96,1536]{2,1,0:T(8,128)(2,1)}, bf16[2,96,1536]{2,1,0:T(8,128)(2,1)}, u32[]{:S(2)}, u32[]{:S(2)}) collective-permute-start(bf16[2,96,1536]{2,1,0:T(8,128)(2,1)} %get-tuple-element.279), channel_id=1, source_target_pairs={{0,2},{2,0},{4,6},{6,4},{8,10},{10,8},{12,14},{14,12},{16,18},{18,... | collective-permute-start | bytes 1769480 | tf_op jit(solution)/shard_map/ppermute | solution.py:78
  623.5 53.5 %collective-permute-start.76 = (bf16[512,1536]{1,0:T(8,128)(2,1)}, bf16[512,1536]{1,0:T(8,128)(2,1)S(1)}, u32[]{:S(2)}, u32[]{:S(2)}) collective-permute-start(bf16[512,1536]{1,0:T(8,128)(2,1)} %shard_map.282), channel_id=1, source_target_pairs={{0,1},{1,0},{2,3},{3,2},{4,5},{5,4},{6,7},{7,6},{8,9},{9,8},{10,11... | collective-permute-start | bytes 4718600 | tf_op jit(solution)/shard_map/ppermute | solution.py:51
  623.7 41.5 %collective-permute-start.82 = (bf16[1,192,2048]{2,1,0:T(8,128)(2,1)}, bf16[1,192,2048]{2,1,0:T(8,128)(2,1)S(1)}, u32[]{:S(2)}, u32[]{:S(2)}) collective-permute-start(bf16[1,192,2048]{2,1,0:T(8,128)(2,1)} %copy-done.88), channel_id=1, source_target_pairs={{0,4},{2,6},{4,0},{6,2},{8,12},{10,14},{12,8},{14,10},{16,20},{18,... | collective-permute-start | bytes 2359304 | tf_op jit(solution)/shard_map/ppermute | solution.py:78
  624.8 35.7 %collective-permute-start.78 = (bf16[2,96,1536]{2,1,0:T(8,128)(2,1)}, bf16[2,96,1536]{2,1,0:T(8,128)(2,1)S(1)}, u32[]{:S(2)}, u32[]{:S(2)}) collective-permute-start(bf16[2,96,1536]{2,1,0:T(8,128)(2,1)} %copy-done.89), channel_id=1, source_target_pairs={{0,8},{2,10},{4,12},{6,14},{8,0},{10,2},{12,4},{14,6},{16,24},{18,... | collective-permute-start | bytes 1769480 | tf_op jit(solution)/shard_map/ppermute | solution.py:78
  637.9 22.4 %collective-permute-start.75 = (bf16[2,96,2432]{2,1,0:T(8,128)(2,1)}, bf16[2,96,2432]{2,1,0:T(8,128)(2,1)S(1)}, u32[]{:S(2)}, u32[]{:S(2)}) collective-permute-start(bf16[2,96,2432]{2,1,0:T(8,128)(2,1)} %get-tuple-element.307), channel_id=1, source_target_pairs={{0,8},{2,10},{4,12},{6,14},{8,0},{10,2},{12,4},{14,6},{16,24},{18,... | collective-permute-start | bytes 2801672 | tf_op jit(solution)/shard_map/ppermute | solution.py:78
  660.7 26.1 %collective-permute-start.79 = (bf16[1,96,1536]{2,1,0:T(8,128)(2,1)S(1)}, bf16[1,96,1536]{2,1,0:T(8,128)(2,1)S(1)}, u32[]{:S(2)}, u32[]{:S(2)}) collective-permute-start(bf16[1,96,1536]{2,1,0:T(8,128)(2,1)S(1)} %get-tuple-element.314), channel_id=1, source_target_pairs={{0,16},{2,18},{4,20},{6,22},{8,24},{10,26},{12,28},{14,30},{16,0},... | collective-permute-start | bytes 884744 | tf_op jit(solution)/shard_map/ppermute | solution.py:78
  665.0 30.9 %collective-permute-start.77 = (bf16[1,96,2432]{2,1,0:T(8,128)(2,1)S(1)}, bf16[1,96,2432]{2,1,0:T(8,128)(2,1)S(1)}, u32[]{:S(2)}, u32[]{:S(2)}) collective-permute-start(bf16[1,96,2432]{2,1,0:T(8,128)(2,1)S(1)} %get-tuple-element.308), channel_id=1, source_target_pairs={{0,16},{2,18},{4,20},{6,22},{8,24},{10,26},{12,28},{14,30},{16,0},... | collective-permute-start | bytes 1400840 | tf_op jit(solution)/shard_map/ppermute | solution.py:78
  665.7 22.2 %collective-permute-start.83 = (bf16[1,96,2048]{2,1,0:T(8,128)(2,1)S(1)}, bf16[1,96,2048]{2,1,0:T(8,128)(2,1)S(1)}, u32[]{:S(2)}, u32[]{:S(2)}) collective-permute-start(bf16[1,96,2048]{2,1,0:T(8,128)(2,1)S(1)} %get-tuple-element.319), channel_id=1, source_target_pairs={{0,2},{2,0},{4,6},{6,4},{8,10},{10,8},{12,14},{14,12},{16,18},{18,... | collective-permute-start | bytes 1179656 | tf_op jit(solution)/shard_map/ppermute | solution.py:78
  (150 other events, 2242.6 us)

commit v7 on v6

--- a/solution.py
+++ b/solution.py
@@ -1154,11 +1154,11 @@
     ]
     other_part = multiply_back(back, 1 - side, low, 2)
     arrived = exchanged(other_part)
-    hidden = tie(hidden, *other_part)
+    line_mlp.fourth(*other_part)
+    sum_qk.second(*other_part)
+    hidden = tie(hidden, line_mlp.sent, *sum_qk.sent)
     other_down = multiply_back([(hidden, mlp_down)], jnp.int32(1), low)
     arrived_down = exchanged(other_down)
-    sum_qk.second(*other_down)
-    line_mlp.fourth(*other_down)
     sum_vf.start(*sum_qk.sent)
     back[1] = (tie(grad_queries, line_mlp.sent, *sum_qk.sent), query_w)
     (own_part,) = multiply_back(back, side)

time: 712 us -> 706 us (level)
    unnamed x234 -> x232, local copies, waits for them, and re-layouts: 25.7 us -> 21.7 us
  transfers between devices with their start and end apart: 84 -> 84, of which waited for: 32 -> 29; matrix products, arithmetic and copies ran while one was open for 4% -> 4% of each run, Pallas kernels for 56% -> 56%
where the time goes in v7:
time: 706 us; the launch traced here: 694 us
  Pallas kernels  391 us (55%)
  waiting for transfers between devices  155 us (22%)
  starting transfers between devices  95 us (13%)
  local copies, waits for them, and re-layouts  31.7 us (4%)
  other arithmetic  18.2 us (3%)
    ppermute x68, waiting for transfers between devices, swap(): return lax.ppermute(values, 'dp', pairs)  154 us
    pallas_call x8, Pallas kernels, multiply_back(): pl.pallas_call(body, grid_spec=pltpu.PrefetchScalarGridSpec(num_scalar_pr...  97.2 us
    ppermute x68, starting transfers between devices, swap(): return lax.ppermute(values, 'dp', pairs)  91.2 us
    pallas_call x7, Pallas kernels, multiply(): pl.pallas_call(body, grid=(tiles,), in_specs=[pl.BlockSpec((length, depth...  79.8 us
    pallas_call x6, Pallas kernels, gradient_parts(): pl.pallas_call(body, grid=(tiles,), in_specs=[pl.BlockSpec((depth, length...  67.6 us
    pallas_call x11, Pallas kernels, add_halves(): pl.pallas_call(body, grid=(columns // tile,), in_specs=[block] * len(term...  33.9 us
    pallas_call x1, Pallas kernels, attend_backward(): pl.pallas_call(functools.partial(bwd_kernel, head ** (-0.5), head), grid=...  32.9 us
    pallas_call x5, Pallas kernels, row_kernel(): pl.pallas_call(kernel, grid=(4,), in_specs=[spec(*i.shape) for i in input...  25.8 us
  transfers between devices with their start and end apart: 84, of which 29 were waited for; matrix products, arithmetic and copies ran while one was open for 4% of the time, Pallas kernels for 56%

profile of v7, /device:TPU:0, one launch (start us, length us, event | category | flops | bytes accessed | tf_op | source)
XLA Modules:
  0.0 693.5 jit_solution(1273083006995957666)
XLA Ops:
  14.8 6.7 collective-permute-done.7
  25.6 11.3 %collective-permute-done.8.refs_2_.refs_11_.refs_19_ = bf16[2,96,1536]{2,1,0:T(8,128)(2,1)S(1)} collective-permute-done((bf16[2,96,1536]{2,1,0:T(8,128)(2,1)S(1)}, bf16[2,96,1536]{2,1,0:T(8,128)(2,1)S(1)}, u32[]{:S(2)}, u32[]{:S(2)}) %collective-permute-start.8) | collective-permute-done | bytes 589856 | tf_op jit(solution)/shard_map/ppermute | solution.py:78
  57.2 3.8 collective-permute-done.12
  68.2 8.3 %collective-permute-done.14.refs_7_.refs_16_.refs_24_ = bf16[2,96,1536]{2,1,0:T(8,128)(2,1)} collective-permute-done((bf16[2,96,1536]{2,1,0:T(8,128)(2,1)S(1)}, bf16[2,96,1536]{2,1,0:T(8,128)(2,1)}, u32[]{:S(2)}, u32[]{:S(2)}) %collective-permute-start.14) | collective-permute-done | bytes 589856 | tf_op jit(solution)/shard_map/ppermute | solution.py:78
  81.7 10.2 %collective-permute-done.19.refs_2_.refs_27_.refs_32_ = bf16[4,96,896]{2,1,0:T(8,128)(2,1)S(1)} collective-permute-done((bf16[4,96,896]{2,1,0:T(8,128)(2,1)S(1)}, bf16[4,96,896]{2,1,0:T(8,128)(2,1)S(1)}, u32[]{:S(2)}, u32[]{:S(2)}) %collective-permute-start.19) | collective-permute-done | bytes 688160 | tf_op jit(solution)/shard_map/ppermute | solution.py:78
  107.0 13.8 %collective-permute-done.27 = bf16[1,96,2048]{2,1,0:T(8,128)(2,1)S(1)} collective-permute-done((bf16[1,96,2048]{2,1,0:T(8,128)(2,1)S(1)}, bf16[1,96,2048]{2,1,0:T(8,128)(2,1)S(1)}, u32[]{:S(2)}, u32[]{:S(2)}) %collective-permute-start.27) | collective-permute-done | bytes 393248 | tf_op jit(solution)/shard_map/ppermute | solution.py:78
  121.3 4.5 collective-permute-done.23.refs_2_.refs_6_
  130.5 10.2 %shard_map.248.q_ref.k_ref = bf16[1024,1536]{1,0:T(8,128)(2,1)} custom-call(bf16[1024,1536]{1,0:T(8,128)(2,1)} %get-tuple-element.170.refs_0_, bf16[2,96,1536]{2,1,0:T(8,128)(2,1)S(1)} %copy-done.13, bf16[2,96,1536]{2,1,0:T(8,128)(2,1)S(1)} %copy-done.18, bf16[2,96,1536]{2,1,0:T(8,128)(2,1)S(1)} %copy-done.21, ...), custom_call_target="tpu_custom_call" | custom-call | flops 96636768 | bytes 220200 | tf_op jit(solution)/shard_map/pallas_call | solution.py:194
  143.6 4.7 collective-permute-start.33
  148.4 10.3 %shard_map.249 = (bf16[1024,768]{1,0:T(8,128)(2,1)}, f32[1024,128]{1,0:T(8,128)S(1)}) custom-call(bf16[1024,1536]{1,0:T(8,128)(2,1)} %get-tuple-element.170.refs_0_, bf16[4,96,896]{2,1,0:T(8,128)(2,1)S(1)} %pad_maximum_fusion.7.refs_1_.refs_26_.refs_31_, bf16[4,96,896]{2,1,0:T(8,128)(2,1)S(1)} %collective-permute-done.19.refs_2_.refs_27_.refs_32_, ...), custom_call_target="tpu_custom_call" | custom-call | flops 56371444 | bytes 159907 | tf_op jit(solution)/shard_map/pallas_call | solution.py:194
  164.9 22.6 %shard_map.251 = (f32[1024,768]{1,0:T(8,128)}, f32[6,2,1024]{2,1,0:T(2,128)S(1)}) custom-call(bf16[1024,1536]{1,0:T(8,128)(2,1)} %shard_map.248.q_ref.k_ref, bf16[1024,1536]{1,0:T(8,128)(2,1)} %shard_map.248.q_ref.k_ref, bf16[1024,768]{1,0:T(8,128)(2,1)S(1)} %copy-done.44, f32[6,1024,2]{2,1,0:T(8,128)} %copy-done.28, ...), custom_call_target="tpu_custom_call" | custom-call | flops 193273536 | bytes 251658 | tf_op jit(solution)/shard_map/pallas_call | solution.py:894
  192.4 10.3 %collective-permute-done.36.refs_4_.refs_5_ = bf16[2,96,2048]{2,1,0:T(8,128)(2,1)S(1)} collective-permute-done((bf16[2,96,2048]{2,1,0:T(8,128)(2,1)S(1)}, bf16[2,96,2048]{2,1,0:T(8,128)(2,1)S(1)}, u32[]{:S(2)}, u32[]{:S(2)}) %collective-permute-start.36) | collective-permute-done | bytes 786464 | tf_op jit(solution)/shard_map/ppermute | solution.py:78
  209.0 8.9 %shard_map.252 = (f32[1024,768]{1,0:T(8,128)}, bf16[1024,768]{1,0:T(8,128)(2,1)}) custom-call(bf16[1024,1536]{1,0:T(8,128)(2,1)} %get-tuple-element.170.refs_0_, bf16[4,96,1536]{2,1,0:T(8,128)(2,1)S(1)} %pad_maximum_fusion.3.refs_1_.refs_5_, bf16[4,96,1536]{2,1,0:T(8,128)(2,1)S(1)} %collective-permute-done.23.refs_2_.refs_6_, ...), custom_call_target="tpu_custom_call" | custom-call | flops 48318384 | bytes 267386 | tf_op jit(solution)/shard_map/pallas_call | solution.py:194
  217.9 6.7 shard_map.254
  227.0 6.3 shard_map.253.refs_1_
  233.3 5.6 shard_map.255
  239.4 7.3 %collective-permute-done.44 = bf16[1,96,2048]{2,1,0:T(8,128)(2,1)} collective-permute-done((bf16[1,96,2048]{2,1,0:T(8,128)(2,1)}, bf16[1,96,2048]{2,1,0:T(8,128)(2,1)}, u32[]{:S(2)}, u32[]{:S(2)}) %collective-permute-start.44) | collective-permute-done | bytes 393248 | tf_op jit(solution)/shard_map/ppermute | solution.py:78
  258.0 12.1 %shard_map.257.refs_6_ = bf16[1024,2048]{1,0:T(8,128)(2,1)} custom-call(bf16[1024,1536]{1,0:T(8,128)(2,1)} %get-tuple-element.194.refs_0_, bf16[4,96,2048]{2,1,0:T(8,128)(2,1)S(1)} %copy-done.6, bf16[4,96,2048]{2,1,0:T(8,128)(2,1)} %copy-done.90, bf16[4,96,2048]{2,1,0:T(8,128)(2,1)} %collective-permute-done.37.refs_3_.refs_4_, ...), custom_call_target="tpu_custom_call" | custom-call | flops 128849016 | bytes 272629 | tf_op jit(solution)/shard_map/pallas_call | solution.py:194
  275.4 4.8 shard_map.259
  280.2 13.3 %shard_map.258 = (bf16[1024,2048]{1,0:T(8,128)(2,1)}, bf16[1024,2048]{1,0:T(8,128)(2,1)}) custom-call(bf16[1024,1536]{1,0:T(8,128)(2,1)} %get-tuple-element.194.refs_0_, bf16[4,96,2048]{2,1,0:T(8,128)(2,1)} %pad_maximum_fusion.1.refs_1_.refs_7_, bf16[4,96,2048]{2,1,0:T(8,128)(2,1)} %collective-permute-done.39.refs_2_.refs_8_, ...), custom_call_target="tpu_custom_call" | custom-call | flops 128849016 | bytes 440401 | tf_op jit(solution)/shard_map/pallas_call | solution.py:194
  293.5 11.9 %shard_map.260 = (bf16[2,4,96,2048]{3,2,1,0:T(8,128)(2,1)S(1)}, bf16[2,4,96,2048]{3,2,1,0:T(8,128)(2,1)}) custom-call(bf16[1536,1024]{1,0:T(8,128)(2,1)} %get-tuple-element.204.refs_0_, bf16[1024,2048]{1,0:T(8,128)(2,1)} %get-tuple-element.309.refs_1_.refs_0_), custom_call_target="tpu_custom_call" | custom-call | flops 128849016 | bytes 272629 | tf_op jit(solution)/shard_map/pallas_call | solution.py:434
  313.1 14.0 %collective-permute-done.49.refs_5_ = bf16[2,96,2048]{2,1,0:T(8,128)(2,1)S(1)} collective-permute-done((bf16[2,96,2048]{2,1,0:T(8,128)(2,1)S(1)}, bf16[2,96,2048]{2,1,0:T(8,128)(2,1)S(1)}, u32[]{:S(2)}, u32[]{:S(2)}) %collective-permute-start.49) | collective-permute-done | bytes 786464 | tf_op jit(solution)/shard_map/ppermute | solution.py:78
  328.3 15.7 %shard_map.261 = (bf16[1024,2048]{1,0:T(8,128)(2,1)}, bf16[1024,2048]{1,0:T(8,128)(2,1)}) custom-call(bf16[1024,1536]{1,0:T(8,128)(2,1)} %get-tuple-element.206.refs_0_, bf16[4,96,2048]{2,1,0:T(8,128)(2,1)S(1)} %pad_maximum_fusion.2.refs_1_, bf16[4,96,2048]{2,1,0:T(8,128)(2,1)} %copy-done.89, bf16[4,96,2048]{2,1,0:T(8,128)(2,1)} %copy-done.88, ...), custom_call_target="tpu_custom_call" | custom-call | flops 128849016 | bytes 524288 | tf_op jit(solution)/shard_map/pallas_call | solution.py:194
  344.0 12.3 %shard_map.262 = (bf16[4,2,96,2048]{3,2,1,0:T(8,128)(2,1)}, bf16[4,2,96,2048]{3,2,1,0:T(8,128)(2,1)}) custom-call(bf16[1536,1024]{1,0:T(8,128)(2,1)} %get-tuple-element.201.refs_0_, bf16[1024,2048]{1,0:T(8,128)(2,1)} %get-tuple-element.214.refs_1_), custom_call_target="tpu_custom_call" | custom-call | flops 128849016 | bytes 272629 | tf_op jit(solution)/shard_map/pallas_call | solution.py:434
  357.1 12.1 %shard_map.263 = (bf16[4,2,96,2048]{3,2,1,0:T(8,128)(2,1)}, bf16[4,2,96,2048]{3,2,1,0:T(8,128)(2,1)}) custom-call(bf16[1536,1024]{1,0:T(8,128)(2,1)} %get-tuple-element.201.refs_0_, bf16[1024,2048]{1,0:T(8,128)(2,1)} %get-tuple-element.219.refs_1_.refs_0_), custom_call_target="tpu_custom_call" | custom-call | flops 128849016 | bytes 272629 | tf_op jit(solution)/shard_map/pallas_call | solution.py:434
  371.0 16.7 %shard_map.266 = (bf16[512,768]{1,0:T(8,128)(2,1)S(1)}, bf16[512,768]{1,0:T(8,128)(2,1)S(1)}) custom-call(s32[1]{0:T(128)} %constant.23.clone.1.half_ref, bf16[1024,2048]{1,0:T(8,128)(2,1)} %get-tuple-element.219.refs_1_.refs_0_, bf16[1024,2048]{1,0:T(8,128)(2,1)} %get-tuple-element.214.refs_1_, bf16[4,96,2048]{2,1,0:T(8,128)(2,1)} %copy-done.5, ...), custom_call_target="tpu_custom_call" | custom-call | flops 128849016 | bytes 398458 | tf_op jit(solution)/shard_map/pallas_call | solution.py:275
  388.2 17.5 %shard_map.264.refs_1_ = f32[512,1536]{1,0:T(8,128)} custom-call(s32[1]{0:T(128)} %constant.22.clone.1.half_ref, bf16[1024,2048]{1,0:T(8,128)(2,1)} %get-tuple-element.219.refs_1_.refs_0_, bf16[1024,2048]{1,0:T(8,128)(2,1)} %get-tuple-element.214.refs_1_, bf16[4,96,2048]{2,1,0:T(8,128)(2,1)} %copy-done.5, bf16[4,96,2048]{2,1,0:T(8,128)(2,1)} %copy-done.90, ...), custom_call_target="tpu_custom_call" | custom-call | flops 128849016 | bytes 398458 | tf_op jit(solution)/shard_map/pallas_call | solution.py:275
  405.8 3.8 shard_map.265
  409.7 6.3 shard_map.267
  424.4 9.3 %shard_map.269 = (bf16[1024,768]{1,0:T(8,128)(2,1)}, bf16[1024,768]{1,0:T(8,128)(2,1)}) custom-call(bf16[1024,1536]{1,0:T(8,128)(2,1)} %get-tuple-element.229.refs_0_, bf16[4,96,1536]{2,1,0:T(8,128)(2,1)S(1)} %pad_maximum_fusion.3.refs_1_.refs_5_, bf16[4,96,1536]{2,1,0:T(8,128)(2,1)S(1)} %copy-done.2, bf16[4,96,1536]{2,1,0:T(8,128)(2,1)} %copy-done.87, ...), custom_call_target="tpu_custom_call" | custom-call | flops 48318384 | bytes 298844 | tf_op jit(solution)/shard_map/pallas_call | solution.py:194
  439.1 3.8 shard_map.271
  445.9 3.8 shard_map.270
  452.3 12.6 %shard_map.272 = (bf16[2,2,96,1536]{3,2,1,0:T(8,128)(2,1)}, bf16[2,2,96,1536]{3,2,1,0:T(8,128)(2,1)}, bf16[2,2,96,1536]{3,2,1,0:T(8,128)(2,1)S(1)}, bf16[2,2,96,1536]{3,2,1,0:T(8,128)(2,1)}) custom-call(bf16[1536,1024]{1,0:T(8,128)(2,1)} %get-tuple-element.235.refs_0_, bf16[1536,1024]{1,0:T(8,128)(2,1)} %get-tuple-element.236.refs_1_, ...), custom_call_target="tpu_custom_call" | custom-call | flops 96636768 | bytes 283115 | tf_op jit(solution)/shard_map/pallas_call | solution.py:434
  465.8 32.9 %shard_map.273 = (bf16[1024,768]{1,0:T(8,128)(2,1)S(1)}, bf16[1024,768]{1,0:T(8,128)(2,1)S(1)}, bf16[1024,768]{1,0:T(8,128)(2,1)}, f32[6,2,1024]{2,1,0:T(2,128)S(1)}, f32[6,1024,2]{2,1,0:T(8,128)}) custom-call(bf16[1024,1536]{1,0:T(8,128)(2,1)} %shard_map.248.q_ref.k_ref, bf16[1024,1536]{1,0:T(8,128)(2,1)} %shard_map.248.q_ref.k_ref, ...), custom_call_target="tpu_custom_call" | custom-call | flops 483183808 | bytes 251658 | tf_op jit(solution)/shard_map/pallas_call | solution.py:914
  503.5 4.1 shard_map.274
  508.9 11.9 %shard_map.276 = (bf16[2,2,96,1536]{3,2,1,0:T(8,128)(2,1)}, bf16[2,2,96,1536]{3,2,1,0:T(8,128)(2,1)}, bf16[2,2,96,1536]{3,2,1,0:T(8,128)(2,1)S(1)}, bf16[2,2,96,1536]{3,2,1,0:T(8,128)(2,1)}) custom-call(bf16[1536,1024]{1,0:T(8,128)(2,1)} %get-tuple-element.235.refs_0_, bf16[1024,768]{1,0:T(8,128)(2,1)} %copy-done.26, bf16[1024,768]{1,0:T(8,128)(2,1)} %copy-done.27), custom_call_target="tpu_custom_call" | custom-call | flops 96636768 | bytes 220200 | tf_op jit(solution)/shard_map/pallas_call | solution.py:434
  534.8 6.7 shard_map.280
  541.7 15.4 %shard_map.281 = (bf16[512,768]{1,0:T(8,128)(2,1)}, bf16[512,768]{1,0:T(8,128)(2,1)}) custom-call(s32[1]{0:T(128)} %bitcast.11.half_ref, bf16[1024,768]{1,0:T(8,128)(2,1)} %get-tuple-element.273.refs_2_.refs_0_, bf16[1024,768]{1,0:T(8,128)(2,1)} %copy-done.26, bf16[1024,768]{1,0:T(8,128)(2,1)} %copy-done.27, ...), custom_call_target="tpu_custom_call" | custom-call | flops 100663296 | bytes 325058 | tf_op jit(solution)/shard_map/pallas_call | solution.py:275
  571.8 15.1 %shard_map.285.refs_1_ = f32[512,1536]{1,0:T(8,128)} custom-call(s32[1]{0:T(128)} %bitcast.half_ref, bf16[1024,768]{1,0:T(8,128)(2,1)} %get-tuple-element.273.refs_2_.refs_0_, bf16[1024,768]{1,0:T(8,128)(2,1)} %copy-done.26, bf16[1024,768]{1,0:T(8,128)(2,1)} %copy-done.27, bf16[1024,768]{1,0:T(8,128)(2,1)} %get-tuple-element.266.refs_1_.refs_3_, ...), custom_call_target="tpu_custom_call" | custom-call | flops 100663296 | bytes 325058 | tf_op jit(solution)/shard_map/pallas_call | solution.py:275
  588.7 6.3 shard_map.287
  595.1 4.8 shard_map.289
  601.6 4.7 shard_map.288
  607.8 9.2 %shard_map.293 = bf16[512,1536]{1,0:T(8,128)(2,1)S(1)} custom-call(s32[1]{0:T(128)} %constant.23.clone.1.half_ref, bf16[1024,2048]{1,0:T(8,128)(2,1)} %get-tuple-element.309.refs_1_.refs_0_, bf16[4,96,2048]{2,1,0:T(8,128)(2,1)} %copy-done.3, bf16[4,96,2048]{2,1,0:T(8,128)(2,1)} %copy-done.89, bf16[4,96,2048]{2,1,0:T(8,128)(2,1)} %copy-done.88, ...), custom_call_target="tpu_custom_call" | custom-call | flops 64424508 | bytes 230686 | tf_op jit(solution)/shard_map/pallas_call | solution.py:275
  627.4 26.2 %collective-permute-done.75 = bf16[2,96,2432]{2,1,0:T(8,128)(2,1)S(1)} collective-permute-done((bf16[2,96,2432]{2,1,0:T(8,128)(2,1)}, bf16[2,96,2432]{2,1,0:T(8,128)(2,1)S(1)}, u32[]{:S(2)}, u32[]{:S(2)}) %collective-permute-start.75) | collective-permute-done | bytes 933920 | tf_op jit(solution)/shard_map/ppermute | solution.py:78
  659.6 10.3 %shard_map.292.refs_1_ = f32[512,1536]{1,0:T(8,128)} custom-call(s32[1]{0:T(128)} %constant.22.clone.1.half_ref, bf16[1024,2048]{1,0:T(8,128)(2,1)} %get-tuple-element.309.refs_1_.refs_0_, bf16[4,96,2048]{2,1,0:T(8,128)(2,1)S(1)} %copy-done.4, bf16[4,96,2048]{2,1,0:T(8,128)(2,1)} %copy-done.89, bf16[4,96,2048]{2,1,0:T(8,128)(2,1)} %copy-done.88, ...), custom_call_target="tpu_custom_call" | custom-call | flops 64424508 | bytes 230686 | tf_op jit(solution)/shard_map/pallas_call | solution.py:275
  670.0 4.9 shard_map.294
  674.9 5.9 collective-permute-done.79
  682.9 6.9 collective-permute-done.77
  (471 shorter events, 204.0 us)
Async XLA Ops:
  24.0 23.5 %collective-permute-start.10 = (bf16[2,96,1536]{2,1,0:T(8,128)(2,1)S(1)}, bf16[2,96,1536]{2,1,0:T(8,128)(2,1)S(1)}, u32[]{:S(2)}, u32[]{:S(2)}) collective-permute-start(bf16[2,96,1536]{2,1,0:T(8,128)(2,1)S(1)} %pad_maximum_fusion.8.refs_1_.refs_10_.refs_18_), channel_id=1, source_target_pairs={{0,2},{2,0},{4,6},{6,4},{8,10},{10,8},{12,14},{14,12},{16,18},{18,... | collective-permute-start | bytes 1769480 | tf_op jit(solution)/shard_map/ppermute | solution.py:78
  45.5 22.1 %collective-permute-start.16 = (bf16[2,96,1536]{2,1,0:T(8,128)(2,1)S(1)}, bf16[2,96,1536]{2,1,0:T(8,128)(2,1)}, u32[]{:S(2)}, u32[]{:S(2)}) collective-permute-start(bf16[2,96,1536]{2,1,0:T(8,128)(2,1)S(1)} %pad_maximum_fusion.8.refs_1_.refs_10_.refs_18_), channel_id=1, source_target_pairs={{0,4},{2,6},{4,0},{6,2},{8,12},{10,14},{12,8},{14,10},{16,20},{18,... | collective-permute-start | bytes 1769480 | tf_op jit(solution)/shard_map/ppermute | solution.py:78
  46.0 21.7 %collective-permute-start.17 = (bf16[2,96,1536]{2,1,0:T(8,128)(2,1)S(1)}, bf16[2,96,1536]{2,1,0:T(8,128)(2,1)}, u32[]{:S(2)}, u32[]{:S(2)}) collective-permute-start(bf16[2,96,1536]{2,1,0:T(8,128)(2,1)S(1)} %collective-permute-done.8.refs_2_.refs_11_.refs_19_), channel_id=1, source_target_pairs={{0,2},{2,0},{4,6},{6,4},{8,10},{10,8},{12,14},{14,12},{16,18},{18,... | collective-permute-start | bytes 1769480 | tf_op jit(solution)/shard_map/ppermute | solution.py:78
  47.5 29.0 %collective-permute-start.14 = (bf16[2,96,1536]{2,1,0:T(8,128)(2,1)S(1)}, bf16[2,96,1536]{2,1,0:T(8,128)(2,1)}, u32[]{:S(2)}, u32[]{:S(2)}) collective-permute-start(bf16[2,96,1536]{2,1,0:T(8,128)(2,1)S(1)} %collective-permute-done.10.refs_3_.refs_12_.refs_20_), channel_id=1, source_target_pairs={{0,4},{2,6},{4,0},{6,2},{8,12},{10,14},{12,8},{14,10},{16,20},{18,... | collective-permute-start | bytes 1769480 | tf_op jit(solution)/shard_map/ppermute | solution.py:78
  54.0 22.5 %collective-permute-start.15 = (bf16[2,96,1536]{2,1,0:T(8,128)(2,1)S(1)}, bf16[2,96,1536]{2,1,0:T(8,128)(2,1)}, u32[]{:S(2)}, u32[]{:S(2)}) collective-permute-start(bf16[2,96,1536]{2,1,0:T(8,128)(2,1)S(1)} %collective-permute-done.11.refs_6_.refs_15_.refs_23_), channel_id=1, source_target_pairs={{0,2},{2,0},{4,6},{6,4},{8,10},{10,8},{12,14},{14,12},{16,18},{18,... | collective-permute-start | bytes 1769480 | tf_op jit(solution)/shard_map/ppermute | solution.py:78
  67.6 27.3 %collective-permute-start.5 = (bf16[512,768]{1,0:T(8,128)(2,1)S(1)}, bf16[512,768]{1,0:T(8,128)(2,1)S(1)}, u32[]{:S(2)}, u32[]{:S(2)}) collective-permute-start(bf16[512,768]{1,0:T(8,128)(2,1)S(1)} %get-tuple-element.168), channel_id=1, source_target_pairs={{0,1},{1,0},{2,3},{3,2},{4,5},{5,4},{6,7},{7,6},{8,9},{9,8},{10,11... | collective-permute-start | bytes 2359304 | tf_op jit(solution)/shard_map/ppermute | solution.py:51
  67.7 27.3 %collective-permute-start.6 = (bf16[512,768]{1,0:T(8,128)(2,1)S(1)}, bf16[512,768]{1,0:T(8,128)(2,1)S(1)}, u32[]{:S(2)}, u32[]{:S(2)}) collective-permute-start(bf16[512,768]{1,0:T(8,128)(2,1)S(1)} %get-tuple-element.169), channel_id=1, source_target_pairs={{0,1},{1,0},{2,3},{3,2},{4,5},{5,4},{6,7},{7,6},{8,9},{9,8},{10,11... | collective-permute-start | bytes 2359304 | tf_op jit(solution)/shard_map/ppermute | solution.py:51
  101.4 24.4 %collective-permute-start.23 = (bf16[4,96,1536]{2,1,0:T(8,128)(2,1)S(1)}, bf16[4,96,1536]{2,1,0:T(8,128)(2,1)S(1)}, u32[]{:S(2)}, u32[]{:S(2)}) collective-permute-start(bf16[4,96,1536]{2,1,0:T(8,128)(2,1)S(1)} %pad_maximum_fusion.3.refs_1_.refs_5_), channel_id=1, source_target_pairs={{0,2},{2,0},{4,6},{6,4},{8,10},{10,8},{12,14},{14,12},{16,18},{18,... | collective-permute-start | bytes 3538952 | tf_op jit(solution)/shard_map/ppermute | solution.py:78
  103.3 24.9 %collective-permute-start.24 = (bf16[4,96,1536]{2,1,0:T(8,128)(2,1)S(1)}, bf16[4,96,1536]{2,1,0:T(8,128)(2,1)S(1)}, u32[]{:S(2)}, u32[]{:S(2)}) collective-permute-start(bf16[4,96,1536]{2,1,0:T(8,128)(2,1)S(1)} %pad_maximum_fusion.3.refs_1_.refs_5_), channel_id=1, source_target_pairs={{0,4},{2,6},{4,0},{6,2},{8,12},{10,14},{12,8},{14,10},{16,20},{18,... | collective-permute-start | bytes 3538952 | tf_op jit(solution)/shard_map/ppermute | solution.py:78
  120.9 19.8 %collective-permute-start.28 = (bf16[2,96,2048]{2,1,0:T(8,128)(2,1)S(1)}, bf16[2,96,2048]{2,1,0:T(8,128)(2,1)S(1)}, u32[]{:S(2)}, u32[]{:S(2)}) collective-permute-start(bf16[2,96,2048]{2,1,0:T(8,128)(2,1)S(1)} %pad_maximum_fusion.4), channel_id=1, source_target_pairs={{0,8},{2,10},{4,12},{6,14},{8,0},{10,2},{12,4},{14,6},{16,24},{18,... | collective-permute-start | bytes 2359304 | tf_op jit(solution)/shard_map/ppermute | solution.py:78
  141.0 46.6 %collective-permute-start.35 = (bf16[4,96,2048]{2,1,0:T(8,128)(2,1)S(1)}, bf16[4,96,2048]{2,1,0:T(8,128)(2,1)S(1)}, u32[]{:S(2)}, u32[]{:S(2)}) collective-permute-start(bf16[4,96,2048]{2,1,0:T(8,128)(2,1)S(1)} %pad_maximum_fusion.refs_1_.refs_2_), channel_id=1, source_target_pairs={{0,2},{2,0},{4,6},{6,4},{8,10},{10,8},{12,14},{14,12},{16,18},{18,... | collective-permute-start | bytes 4718600 | tf_op jit(solution)/shard_map/ppermute | solution.py:78
  142.7 45.5 %collective-permute-start.37 = (bf16[4,96,2048]{2,1,0:T(8,128)(2,1)S(1)}, bf16[4,96,2048]{2,1,0:T(8,128)(2,1)}, u32[]{:S(2)}, u32[]{:S(2)}) collective-permute-start(bf16[4,96,2048]{2,1,0:T(8,128)(2,1)S(1)} %pad_maximum_fusion.refs_1_.refs_2_), channel_id=1, source_target_pairs={{0,4},{2,6},{4,0},{6,2},{8,12},{10,14},{12,8},{14,10},{16,20},{18,... | collective-permute-start | bytes 4718600 | tf_op jit(solution)/shard_map/ppermute | solution.py:78
  163.1 28.1 %collective-permute-start.34 = (bf16[2,96,2048]{2,1,0:T(8,128)(2,1)S(1)}, bf16[2,96,2048]{2,1,0:T(8,128)(2,1)S(1)}, u32[]{:S(2)}, u32[]{:S(2)}) collective-permute-start(bf16[2,96,2048]{2,1,0:T(8,128)(2,1)S(1)} %pad_maximum_fusion.5), channel_id=1, source_target_pairs={{0,8},{2,10},{4,12},{6,14},{8,0},{10,2},{12,4},{14,6},{16,24},{18,... | collective-permute-start | bytes 2359304 | tf_op jit(solution)/shard_map/ppermute | solution.py:78
  207.0 41.0 %collective-permute-start.39 = (bf16[4,96,2048]{2,1,0:T(8,128)(2,1)}, bf16[4,96,2048]{2,1,0:T(8,128)(2,1)}, u32[]{:S(2)}, u32[]{:S(2)}) collective-permute-start(bf16[4,96,2048]{2,1,0:T(8,128)(2,1)} %pad_maximum_fusion.1.refs_1_.refs_7_), channel_id=1, source_target_pairs={{0,2},{2,0},{4,6},{6,4},{8,10},{10,8},{12,14},{14,12},{16,18},{18,... | collective-permute-start | bytes 4718600 | tf_op jit(solution)/shard_map/ppermute | solution.py:78
  207.3 43.3 %collective-permute-start.40 = (bf16[4,96,2048]{2,1,0:T(8,128)(2,1)}, bf16[4,96,2048]{2,1,0:T(8,128)(2,1)}, u32[]{:S(2)}, u32[]{:S(2)}) collective-permute-start(bf16[4,96,2048]{2,1,0:T(8,128)(2,1)} %pad_maximum_fusion.1.refs_1_.refs_7_), channel_id=1, source_target_pairs={{0,4},{2,6},{4,0},{6,2},{8,12},{10,14},{12,8},{14,10},{16,20},{18,... | collective-permute-start | bytes 4718600 | tf_op jit(solution)/shard_map/ppermute | solution.py:78
  226.0 20.7 %collective-permute-start.44 = (bf16[1,96,2048]{2,1,0:T(8,128)(2,1)}, bf16[1,96,2048]{2,1,0:T(8,128)(2,1)}, u32[]{:S(2)}, u32[]{:S(2)}) collective-permute-start(bf16[1,96,2048]{2,1,0:T(8,128)(2,1)} %convert_bitcast_fusion), channel_id=1, source_target_pairs={{0,16},{2,18},{4,20},{6,22},{8,24},{10,26},{12,28},{14,30},{16,0},... | collective-permute-start | bytes 1179656 | tf_op jit(solution)/shard_map/ppermute | solution.py:78
  247.9 22.2 %collective-permute-start.45 = (bf16[2,96,2048]{2,1,0:T(8,128)(2,1)S(1)}, bf16[2,96,2048]{2,1,0:T(8,128)(2,1)}, u32[]{:S(2)}, u32[]{:S(2)}) collective-permute-start(bf16[2,96,2048]{2,1,0:T(8,128)(2,1)S(1)} %pad_maximum_fusion.6), channel_id=1, source_target_pairs={{0,8},{2,10},{4,12},{6,14},{8,0},{10,2},{12,4},{14,6},{16,24},{18,... | collective-permute-start | bytes 2359304 | tf_op jit(solution)/shard_map/ppermute | solution.py:78
  250.2 21.2 %collective-permute-start.41 = (bf16[2,96,2048]{2,1,0:T(8,128)(2,1)}, bf16[2,96,2048]{2,1,0:T(8,128)(2,1)S(1)}, u32[]{:S(2)}, u32[]{:S(2)}) collective-permute-start(bf16[2,96,2048]{2,1,0:T(8,128)(2,1)} %slice.119), channel_id=1, source_target_pairs={{0,4},{2,6},{4,0},{6,2},{8,12},{10,14},{12,8},{14,10},{16,20},{18,... | collective-permute-start | bytes 2359304 | tf_op jit(solution)/shard_map/ppermute | solution.py:78
  254.4 21.0 %collective-permute-start.43 = (bf16[512,1536]{1,0:T(8,128)(2,1)S(1)}, bf16[512,1536]{1,0:T(8,128)(2,1)}, u32[]{:S(2)}, u32[]{:S(2)}) collective-permute-start(bf16[512,1536]{1,0:T(8,128)(2,1)S(1)} %copy-done.43), channel_id=1, source_target_pairs={{0,1},{1,0},{2,3},{3,2},{4,5},{5,4},{6,7},{7,6},{8,9},{9,8},{10,11... | collective-permute-start | bytes 4718600 | tf_op jit(solution)/shard_map/ppermute | solution.py:51
  271.9 36.4 %collective-permute-start.47 = (bf16[4,96,2048]{2,1,0:T(8,128)(2,1)S(1)}, bf16[4,96,2048]{2,1,0:T(8,128)(2,1)S(1)}, u32[]{:S(2)}, u32[]{:S(2)}) collective-permute-start(bf16[4,96,2048]{2,1,0:T(8,128)(2,1)S(1)} %pad_maximum_fusion.2.refs_1_), channel_id=1, source_target_pairs={{0,4},{2,6},{4,0},{6,2},{8,12},{10,14},{12,8},{14,10},{16,20},{18,... | collective-permute-start | bytes 4718600 | tf_op jit(solution)/shard_map/ppermute | solution.py:78
  273.7 36.1 %collective-permute-start.46 = (bf16[4,96,2048]{2,1,0:T(8,128)(2,1)S(1)}, bf16[4,96,2048]{2,1,0:T(8,128)(2,1)S(1)}, u32[]{:S(2)}, u32[]{:S(2)}) collective-permute-start(bf16[4,96,2048]{2,1,0:T(8,128)(2,1)S(1)} %pad_maximum_fusion.2.refs_1_), channel_id=1, source_target_pairs={{0,2},{2,0},{4,6},{6,4},{8,10},{10,8},{12,14},{14,12},{16,18},{18,... | collective-permute-start | bytes 4718600 | tf_op jit(solution)/shard_map/ppermute | solution.py:78
  311.2 94.5 %collective-permute-start.51 = (bf16[2,4,96,2048]{3,2,1,0:T(8,128)(2,1)}, bf16[2,4,96,2048]{3,2,1,0:T(8,128)(2,1)}, u32[]{:S(2)}, u32[]{:S(2)}) collective-permute-start(bf16[2,4,96,2048]{3,2,1,0:T(8,128)(2,1)} %copy-done.79), channel_id=1, source_target_pairs={{0,8},{2,10},{4,12},{6,14},{8,0},{10,2},{12,4},{14,6},{16,24},{18,... | collective-permute-start | bytes 9437192 | tf_op jit(solution)/shard_map/ppermute | solution.py:78
  356.4 77.4 %collective-permute-start.57 = (bf16[4,2,96,2048]{3,2,1,0:T(8,128)(2,1)}, bf16[4,2,96,2048]{3,2,1,0:T(8,128)(2,1)}, u32[]{:S(2)}, u32[]{:S(2)}) collective-permute-start(bf16[4,2,96,2048]{3,2,1,0:T(8,128)(2,1)} %get-tuple-element.215), channel_id=1, source_target_pairs={{0,2},{2,0},{4,6},{6,4},{8,10},{10,8},{12,14},{14,12},{16,18},{18,... | collective-permute-start | bytes 9437192 | tf_op jit(solution)/shard_map/ppermute | solution.py:78
  369.2 68.1 %collective-permute-start.50 = (bf16[4,2,96,2048]{3,2,1,0:T(8,128)(2,1)}, bf16[4,2,96,2048]{3,2,1,0:T(8,128)(2,1)S(1)}, u32[]{:S(2)}, u32[]{:S(2)}) collective-permute-start(bf16[4,2,96,2048]{3,2,1,0:T(8,128)(2,1)} %get-tuple-element.218), channel_id=1, source_target_pairs={{0,4},{2,6},{4,0},{6,2},{8,12},{10,14},{12,8},{14,10},{16,20},{18,... | collective-permute-start | bytes 9437192 | tf_op jit(solution)/shard_map/ppermute | solution.py:78
  387.6 22.0 %collective-permute-start.52 = (bf16[512,768]{1,0:T(8,128)(2,1)S(1)}, bf16[512,768]{1,0:T(8,128)(2,1)S(1)}, u32[]{:S(2)}, u32[]{:S(2)}) collective-permute-start(bf16[512,768]{1,0:T(8,128)(2,1)S(1)} %get-tuple-element.224), channel_id=1, source_target_pairs={{0,1},{1,0},{2,3},{3,2},{4,5},{5,4},{6,7},{7,6},{8,9},{9,8},{10,11... | collective-permute-start | bytes 2359304 | tf_op jit(solution)/shard_map/ppermute | solution.py:51
  387.7 21.9 %collective-permute-start.53 = (bf16[512,768]{1,0:T(8,128)(2,1)S(1)}, bf16[512,768]{1,0:T(8,128)(2,1)S(1)}, u32[]{:S(2)}, u32[]{:S(2)}) collective-permute-start(bf16[512,768]{1,0:T(8,128)(2,1)S(1)} %get-tuple-element.225), channel_id=1, source_target_pairs={{0,1},{1,0},{2,3},{3,2},{4,5},{5,4},{6,7},{7,6},{8,9},{9,8},{10,11... | collective-permute-start | bytes 2359304 | tf_op jit(solution)/shard_map/ppermute | solution.py:51
  416.4 84.5 %collective-permute-start.60 = (bf16[1,384,2048]{2,1,0:T(8,128)(2,1)S(1)}, bf16[1,384,2048]{2,1,0:T(8,128)(2,1)}, u32[]{:S(2)}, u32[]{:S(2)}) collective-permute-start(bf16[1,384,2048]{2,1,0:T(8,128)(2,1)S(1)} %get-tuple-element.222), channel_id=1, source_target_pairs={{0,16},{2,18},{4,20},{6,22},{8,24},{10,26},{12,28},{14,30},{16,0},... | collective-permute-start | bytes 4718600 | tf_op jit(solution)/shard_map/ppermute | solution.py:78
  444.2 59.4 %collective-permute-start.58 = (bf16[4,96,2048]{2,1,0:T(8,128)(2,1)S(1)}, bf16[4,96,2048]{2,1,0:T(8,128)(2,1)}, u32[]{:S(2)}, u32[]{:S(2)}) collective-permute-start(bf16[4,96,2048]{2,1,0:T(8,128)(2,1)S(1)} %get-tuple-element.240), channel_id=1, source_target_pairs={{0,4},{2,6},{4,0},{6,2},{8,12},{10,14},{12,8},{14,10},{16,20},{18,... | collective-permute-start | bytes 4718600 | tf_op jit(solution)/shard_map/ppermute | solution.py:78
  450.9 52.7 %collective-permute-start.56 = (bf16[4,96,2048]{2,1,0:T(8,128)(2,1)S(1)}, bf16[4,96,2048]{2,1,0:T(8,128)(2,1)}, u32[]{:S(2)}, u32[]{:S(2)}) collective-permute-start(bf16[4,96,2048]{2,1,0:T(8,128)(2,1)S(1)} %get-tuple-element.234), channel_id=1, source_target_pairs={{0,2},{2,0},{4,6},{6,4},{8,10},{10,8},{12,14},{14,12},{16,18},{18,... | collective-permute-start | bytes 4718600 | tf_op jit(solution)/shard_map/ppermute | solution.py:78
  464.9 63.3 %collective-permute-start.62 = (bf16[2,2,96,1536]{3,2,1,0:T(8,128)(2,1)}, bf16[2,2,96,1536]{3,2,1,0:T(8,128)(2,1)}, u32[]{:S(2)}, u32[]{:S(2)}) collective-permute-start(bf16[2,2,96,1536]{3,2,1,0:T(8,128)(2,1)} %get-tuple-element.243), channel_id=1, source_target_pairs={{0,2},{2,0},{4,6},{6,4},{8,10},{10,8},{12,14},{14,12},{16,18},{18,... | collective-permute-start | bytes 3538952 | tf_op jit(solution)/shard_map/ppermute | solution.py:78
  465.5 62.7 %collective-permute-start.61 = (bf16[2,2,96,1536]{3,2,1,0:T(8,128)(2,1)}, bf16[2,2,96,1536]{3,2,1,0:T(8,128)(2,1)S(1)}, u32[]{:S(2)}, u32[]{:S(2)}) collective-permute-start(bf16[2,2,96,1536]{3,2,1,0:T(8,128)(2,1)} %get-tuple-element.242), channel_id=1, source_target_pairs={{0,4},{2,6},{4,0},{6,2},{8,12},{10,14},{12,8},{14,10},{16,20},{18,... | collective-permute-start | bytes 3538952 | tf_op jit(solution)/shard_map/ppermute | solution.py:78
  520.8 36.3 %collective-permute-start.64 = (bf16[2,2,96,1536]{3,2,1,0:T(8,128)(2,1)}, bf16[2,2,96,1536]{3,2,1,0:T(8,128)(2,1)}, u32[]{:S(2)}, u32[]{:S(2)}) collective-permute-start(bf16[2,2,96,1536]{3,2,1,0:T(8,128)(2,1)} %get-tuple-element.259), channel_id=1, source_target_pairs={{0,2},{2,0},{4,6},{6,4},{8,10},{10,8},{12,14},{14,12},{16,18},{18,... | collective-permute-start | bytes 3538952 | tf_op jit(solution)/shard_map/ppermute | solution.py:78
  522.3 34.9 %collective-permute-start.63 = (bf16[2,2,96,1536]{3,2,1,0:T(8,128)(2,1)}, bf16[2,2,96,1536]{3,2,1,0:T(8,128)(2,1)}, u32[]{:S(2)}, u32[]{:S(2)}) collective-permute-start(bf16[2,2,96,1536]{3,2,1,0:T(8,128)(2,1)} %get-tuple-element.258), channel_id=1, source_target_pairs={{0,4},{2,6},{4,0},{6,2},{8,12},{10,14},{12,8},{14,10},{16,20},{18,... | collective-permute-start | bytes 3538952 | tf_op jit(solution)/shard_map/ppermute | solution.py:78
  524.0 44.0 %collective-permute-start.59 = (bf16[2,96,4096]{2,1,0:T(8,128)(2,1)}, bf16[2,96,4096]{2,1,0:T(8,128)(2,1)}, u32[]{:S(2)}, u32[]{:S(2)}) collective-permute-start(bf16[2,96,4096]{2,1,0:T(8,128)(2,1)} %copy-done.80), channel_id=1, source_target_pairs={{0,8},{2,10},{4,12},{6,14},{8,0},{10,2},{12,4},{14,6},{16,24},{18,... | collective-permute-start | bytes 4718600 | tf_op jit(solution)/shard_map/ppermute | solution.py:78
  531.2 33.6 %collective-permute-start.69 = (bf16[2,96,1536]{2,1,0:T(8,128)(2,1)}, bf16[2,96,1536]{2,1,0:T(8,128)(2,1)}, u32[]{:S(2)}, u32[]{:S(2)}) collective-permute-start(bf16[2,96,1536]{2,1,0:T(8,128)(2,1)} %get-tuple-element.265), channel_id=1, source_target_pairs={{0,4},{2,6},{4,0},{6,2},{8,12},{10,14},{12,8},{14,10},{16,20},{18,... | collective-permute-start | bytes 1769480 | tf_op jit(solution)/shard_map/ppermute | solution.py:78
  533.9 32.4 %collective-permute-start.68 = (bf16[2,96,1536]{2,1,0:T(8,128)(2,1)}, bf16[2,96,1536]{2,1,0:T(8,128)(2,1)}, u32[]{:S(2)}, u32[]{:S(2)}) collective-permute-start(bf16[2,96,1536]{2,1,0:T(8,128)(2,1)} %get-tuple-element.262), channel_id=1, source_target_pairs={{0,2},{2,0},{4,6},{6,4},{8,10},{10,8},{12,14},{14,12},{16,18},{18,... | collective-permute-start | bytes 1769480 | tf_op jit(solution)/shard_map/ppermute | solution.py:78
  564.8 30.3 %collective-permute-start.73 = (bf16[2,2,96,896]{3,2,1,0:T(8,128)(2,1)S(1)}, bf16[2,2,96,896]{3,2,1,0:T(8,128)(2,1)}, u32[]{:S(2)}, u32[]{:S(2)}) collective-permute-start(bf16[2,2,96,896]{3,2,1,0:T(8,128)(2,1)S(1)} %copy-done.83), channel_id=1, source_target_pairs={{0,2},{2,0},{4,6},{6,4},{8,10},{10,8},{12,14},{14,12},{16,18},{18,... | collective-permute-start | bytes 2064392 | tf_op jit(solution)/shard_map/ppermute | solution.py:78
  566.3 35.3 %collective-permute-start.67 = (bf16[2,2,96,896]{3,2,1,0:T(8,128)(2,1)S(1)}, bf16[2,2,96,896]{3,2,1,0:T(8,128)(2,1)}, u32[]{:S(2)}, u32[]{:S(2)}) collective-permute-start(bf16[2,2,96,896]{3,2,1,0:T(8,128)(2,1)S(1)} %get-tuple-element.288), channel_id=1, source_target_pairs={{0,4},{2,6},{4,0},{6,2},{8,12},{10,14},{12,8},{14,10},{16,20},{18,... | collective-permute-start | bytes 2064392 | tf_op jit(solution)/shard_map/ppermute | solution.py:78
  568.1 48.9 %collective-permute-start.66 = (bf16[2,96,1536]{2,1,0:T(8,128)(2,1)S(1)}, bf16[2,96,1536]{2,1,0:T(8,128)(2,1)}, u32[]{:S(2)}, u32[]{:S(2)}) collective-permute-start(bf16[2,96,1536]{2,1,0:T(8,128)(2,1)S(1)} %copy-done.86), channel_id=1, source_target_pairs={{0,4},{2,6},{4,0},{6,2},{8,12},{10,14},{12,8},{14,10},{16,20},{18,... | collective-permute-start | bytes 1769480 | tf_op jit(solution)/shard_map/ppermute | solution.py:78
  571.0 54.9 %collective-permute-start.80 = (bf16[1,96,4096]{2,1,0:T(8,128)(2,1)}, bf16[1,96,4096]{2,1,0:T(8,128)(2,1)}, u32[]{:S(2)}, u32[]{:S(2)}) collective-permute-start(bf16[1,96,4096]{2,1,0:T(8,128)(2,1)} %get-tuple-element.277), channel_id=1, source_target_pairs={{0,16},{2,18},{4,20},{6,22},{8,24},{10,26},{12,28},{14,30},{16,0},... | collective-permute-start | bytes 2359304 | tf_op jit(solution)/shard_map/ppermute | solution.py:78
  571.2 46.1 %collective-permute-start.65 = (bf16[2,96,1536]{2,1,0:T(8,128)(2,1)}, bf16[2,96,1536]{2,1,0:T(8,128)(2,1)}, u32[]{:S(2)}, u32[]{:S(2)}) collective-permute-start(bf16[2,96,1536]{2,1,0:T(8,128)(2,1)} %get-tuple-element.280), channel_id=1, source_target_pairs={{0,2},{2,0},{4,6},{6,4},{8,10},{10,8},{12,14},{14,12},{16,18},{18,... | collective-permute-start | bytes 1769480 | tf_op jit(solution)/shard_map/ppermute | solution.py:78
  617.0 53.0 %collective-permute-start.76 = (bf16[512,1536]{1,0:T(8,128)(2,1)S(1)}, bf16[512,1536]{1,0:T(8,128)(2,1)}, u32[]{:S(2)}, u32[]{:S(2)}) collective-permute-start(bf16[512,1536]{1,0:T(8,128)(2,1)S(1)} %shard_map.293), channel_id=1, source_target_pairs={{0,1},{1,0},{2,3},{3,2},{4,5},{5,4},{6,7},{7,6},{8,9},{9,8},{10,11... | collective-permute-start | bytes 4718600 | tf_op jit(solution)/shard_map/ppermute | solution.py:51
  617.3 41.1 %collective-permute-start.82 = (bf16[1,192,2048]{2,1,0:T(8,128)(2,1)}, bf16[1,192,2048]{2,1,0:T(8,128)(2,1)S(1)}, u32[]{:S(2)}, u32[]{:S(2)}) collective-permute-start(bf16[1,192,2048]{2,1,0:T(8,128)(2,1)} %copy-done.81), channel_id=1, source_target_pairs={{0,4},{2,6},{4,0},{6,2},{8,12},{10,14},{12,8},{14,10},{16,20},{18,... | collective-permute-start | bytes 2359304 | tf_op jit(solution)/shard_map/ppermute | solution.py:78
  617.6 36.1 %collective-permute-start.78 = (bf16[2,96,1536]{2,1,0:T(8,128)(2,1)}, bf16[2,96,1536]{2,1,0:T(8,128)(2,1)S(1)}, u32[]{:S(2)}, u32[]{:S(2)}) collective-permute-start(bf16[2,96,1536]{2,1,0:T(8,128)(2,1)} %copy-done.84), channel_id=1, source_target_pairs={{0,8},{2,10},{4,12},{6,14},{8,0},{10,2},{12,4},{14,6},{16,24},{18,... | collective-permute-start | bytes 1769480 | tf_op jit(solution)/shard_map/ppermute | solution.py:78
  625.9 27.7 %collective-permute-start.75 = (bf16[2,96,2432]{2,1,0:T(8,128)(2,1)}, bf16[2,96,2432]{2,1,0:T(8,128)(2,1)S(1)}, u32[]{:S(2)}, u32[]{:S(2)}) collective-permute-start(bf16[2,96,2432]{2,1,0:T(8,128)(2,1)} %get-tuple-element.307), channel_id=1, source_target_pairs={{0,8},{2,10},{4,12},{6,14},{8,0},{10,2},{12,4},{14,6},{16,24},{18,... | collective-permute-start | bytes 2801672 | tf_op jit(solution)/shard_map/ppermute | solution.py:78
  653.9 26.9 %collective-permute-start.79 = (bf16[1,96,1536]{2,1,0:T(8,128)(2,1)S(1)}, bf16[1,96,1536]{2,1,0:T(8,128)(2,1)S(1)}, u32[]{:S(2)}, u32[]{:S(2)}) collective-permute-start(bf16[1,96,1536]{2,1,0:T(8,128)(2,1)S(1)} %get-tuple-element.314), channel_id=1, source_target_pairs={{0,16},{2,18},{4,20},{6,22},{8,24},{10,26},{12,28},{14,30},{16,0},... | collective-permute-start | bytes 884744 | tf_op jit(solution)/shard_map/ppermute | solution.py:78
  658.2 31.6 %collective-permute-start.77 = (bf16[1,96,2432]{2,1,0:T(8,128)(2,1)S(1)}, bf16[1,96,2432]{2,1,0:T(8,128)(2,1)S(1)}, u32[]{:S(2)}, u32[]{:S(2)}) collective-permute-start(bf16[1,96,2432]{2,1,0:T(8,128)(2,1)S(1)} %get-tuple-element.308), channel_id=1, source_target_pairs={{0,16},{2,18},{4,20},{6,22},{8,24},{10,26},{12,28},{14,30},{16,0},... | collective-permute-start | bytes 1400840 | tf_op jit(solution)/shard_map/ppermute | solution.py:78
  658.9 23.0 %collective-permute-start.83 = (bf16[1,96,2048]{2,1,0:T(8,128)(2,1)S(1)}, bf16[1,96,2048]{2,1,0:T(8,128)(2,1)S(1)}, u32[]{:S(2)}, u32[]{:S(2)}) collective-permute-start(bf16[1,96,2048]{2,1,0:T(8,128)(2,1)S(1)} %get-tuple-element.319), channel_id=1, source_target_pairs={{0,2},{2,0},{4,6},{6,4},{8,10},{10,8},{12,14},{14,12},{16,18},{18,... | collective-permute-start | bytes 1179656 | tf_op jit(solution)/shard_map/ppermute | solution.py:78
  (149 other events, 2266.5 us)

commit v8 on v7

--- a/solution.py
+++ b/solution.py
@@ -1171,6 +1171,7 @@
     )
     sum_vf.second(tokens_grad)
     line_qkv = LineSum(grid, [sum_qk, sum_vf]).third()
+    line_go.fourth(line_qkv.sent)
     line_qkv.fourth()
     (own_down,) = multiply_back([(tie(hidden, line_qkv.sent), mlp_down)], jnp.int32(0))
     (mixed,) = row_kernel(
@@ -1178,7 +1179,6 @@
         [middle, own_down, *arrived_down],
         [(columns, low)],
     )
-    line_go.fourth(line_qkv.sent)
     sum_down.step(0, line_qkv.sent)
     down_grad, go_grad, qkv_grad = sum_down.result().T, line_go.result(), line_qkv.result()
     mlp_grad = line_mlp.result()

time: 706 us -> 696 us (0.986)
  waiting for transfers between devices: 155 us -> 145 us
    ppermute x68, waiting for transfers between devices: 154 us -> 144 us  [swap(): return lax.ppermute(values, 'dp', pairs)]
    unnamed x232 -> x234, local copies, waits for them, and re-layouts: 21.7 us -> 21.2 us
  transfers between devices with their start and end apart: 84 -> 84, of which waited for: 29 -> 28; matrix products, arithmetic and copies ran while one was open for 4% -> 4% of each run, Pallas kernels for 56% -> 57%
where the time goes in v8:
time: 696 us; the launch traced here: 684 us
  Pallas kernels  391 us (56%)
  waiting for transfers between devices  145 us (21%)
  starting transfers between devices  96.5 us (14%)
  local copies, waits for them, and re-layouts  31.2 us (4%)
  other arithmetic  18.3 us (3%)
    ppermute x68, waiting for transfers between devices, swap(): return lax.ppermute(values, 'dp', pairs)  144 us
    pallas_call x8, Pallas kernels, multiply_back(): pl.pallas_call(body, grid_spec=pltpu.PrefetchScalarGridSpec(num_scalar_pr...  97.2 us
    ppermute x68, starting transfers between devices, swap(): return lax.ppermute(values, 'dp', pairs)  92.7 us
    pallas_call x7, Pallas kernels, multiply(): pl.pallas_call(body, grid=(tiles,), in_specs=[pl.BlockSpec((length, depth...  79.7 us
    pallas_call x6, Pallas kernels, gradient_parts(): pl.pallas_call(body, grid=(tiles,), in_specs=[pl.BlockSpec((depth, length...  67.6 us
    pallas_call x11, Pallas kernels, add_halves(): pl.pallas_call(body, grid=(columns // tile,), in_specs=[block] * len(term...  33.9 us
    pallas_call x1, Pallas kernels, attend_backward(): pl.pallas_call(functools.partial(bwd_kernel, head ** (-0.5), head), grid=...  32.9 us
    pallas_call x5, Pallas kernels, row_kernel(): pl.pallas_call(kernel, grid=(4,), in_specs=[spec(*i.shape) for i in input...  25.2 us
  transfers between devices with their start and end apart: 84, of which 28 were waited for; matrix products, arithmetic and copies ran while one was open for 4% of the time, Pallas kernels for 57%

profile of v8, /device:TPU:0, one launch (start us, length us, event | category | flops | bytes accessed | tf_op | source)
XLA Modules:
  0.0 684.2 jit_solution(9861006816624066862)
XLA Ops:
  14.8 6.7 collective-permute-done.7
  25.6 11.3 %collective-permute-done.8.refs_2_.refs_11_.refs_19_ = bf16[2,96,1536]{2,1,0:T(8,128)(2,1)S(1)} collective-permute-done((bf16[2,96,1536]{2,1,0:T(8,128)(2,1)S(1)}, bf16[2,96,1536]{2,1,0:T(8,128)(2,1)S(1)}, u32[]{:S(2)}, u32[]{:S(2)}) %collective-permute-start.8) | collective-permute-done | bytes 589856 | tf_op jit(solution)/shard_map/ppermute | solution.py:78
  57.2 3.8 collective-permute-done.12
  68.2 8.3 %collective-permute-done.14.refs_7_.refs_16_.refs_24_ = bf16[2,96,1536]{2,1,0:T(8,128)(2,1)} collective-permute-done((bf16[2,96,1536]{2,1,0:T(8,128)(2,1)S(1)}, bf16[2,96,1536]{2,1,0:T(8,128)(2,1)}, u32[]{:S(2)}, u32[]{:S(2)}) %collective-permute-start.14) | collective-permute-done | bytes 589856 | tf_op jit(solution)/shard_map/ppermute | solution.py:78
  81.7 10.2 %collective-permute-done.19.refs_2_.refs_27_.refs_32_ = bf16[4,96,896]{2,1,0:T(8,128)(2,1)S(1)} collective-permute-done((bf16[4,96,896]{2,1,0:T(8,128)(2,1)S(1)}, bf16[4,96,896]{2,1,0:T(8,128)(2,1)S(1)}, u32[]{:S(2)}, u32[]{:S(2)}) %collective-permute-start.19) | collective-permute-done | bytes 688160 | tf_op jit(solution)/shard_map/ppermute | solution.py:78
  107.0 13.8 %collective-permute-done.27 = bf16[1,96,2048]{2,1,0:T(8,128)(2,1)S(1)} collective-permute-done((bf16[1,96,2048]{2,1,0:T(8,128)(2,1)S(1)}, bf16[1,96,2048]{2,1,0:T(8,128)(2,1)S(1)}, u32[]{:S(2)}, u32[]{:S(2)}) %collective-permute-start.27) | collective-permute-done | bytes 393248 | tf_op jit(solution)/shard_map/ppermute | solution.py:78
  121.3 4.5 collective-permute-done.23.refs_2_.refs_6_
  130.6 10.1 %shard_map.248.q_ref.k_ref = bf16[1024,1536]{1,0:T(8,128)(2,1)} custom-call(bf16[1024,1536]{1,0:T(8,128)(2,1)} %get-tuple-element.170.refs_0_, bf16[2,96,1536]{2,1,0:T(8,128)(2,1)S(1)} %copy-done.13, bf16[2,96,1536]{2,1,0:T(8,128)(2,1)S(1)} %copy-done.18, bf16[2,96,1536]{2,1,0:T(8,128)(2,1)S(1)} %copy-done.21, ...), custom_call_target="tpu_custom_call" | custom-call | flops 96636768 | bytes 220200 | tf_op jit(solution)/shard_map/pallas_call | solution.py:194
  143.6 4.9 collective-permute-start.33
  148.6 10.3 %shard_map.249 = (bf16[1024,768]{1,0:T(8,128)(2,1)}, f32[1024,128]{1,0:T(8,128)S(1)}) custom-call(bf16[1024,1536]{1,0:T(8,128)(2,1)} %get-tuple-element.170.refs_0_, bf16[4,96,896]{2,1,0:T(8,128)(2,1)S(1)} %pad_maximum_fusion.7.refs_1_.refs_26_.refs_31_, bf16[4,96,896]{2,1,0:T(8,128)(2,1)S(1)} %collective-permute-done.19.refs_2_.refs_27_.refs_32_, ...), custom_call_target="tpu_custom_call" | custom-call | flops 56371444 | bytes 159907 | tf_op jit(solution)/shard_map/pallas_call | solution.py:194
  165.1 22.6 %shard_map.251 = (f32[1024,768]{1,0:T(8,128)}, f32[6,2,1024]{2,1,0:T(2,128)S(1)}) custom-call(bf16[1024,1536]{1,0:T(8,128)(2,1)} %shard_map.248.q_ref.k_ref, bf16[1024,1536]{1,0:T(8,128)(2,1)} %shard_map.248.q_ref.k_ref, bf16[1024,768]{1,0:T(8,128)(2,1)S(1)} %copy-done.44, f32[6,1024,2]{2,1,0:T(8,128)} %copy-done.28, ...), custom_call_target="tpu_custom_call" | custom-call | flops 193273536 | bytes 251658 | tf_op jit(solution)/shard_map/pallas_call | solution.py:894
  192.6 9.9 %collective-permute-done.36.refs_4_.refs_5_ = bf16[2,96,2048]{2,1,0:T(8,128)(2,1)S(1)} collective-permute-done((bf16[2,96,2048]{2,1,0:T(8,128)(2,1)S(1)}, bf16[2,96,2048]{2,1,0:T(8,128)(2,1)S(1)}, u32[]{:S(2)}, u32[]{:S(2)}) %collective-permute-start.36) | collective-permute-done | bytes 786464 | tf_op jit(solution)/shard_map/ppermute | solution.py:78
  209.2 8.9 %shard_map.252 = (f32[1024,768]{1,0:T(8,128)}, bf16[1024,768]{1,0:T(8,128)(2,1)}) custom-call(bf16[1024,1536]{1,0:T(8,128)(2,1)} %get-tuple-element.170.refs_0_, bf16[4,96,1536]{2,1,0:T(8,128)(2,1)S(1)} %pad_maximum_fusion.3.refs_1_.refs_5_, bf16[4,96,1536]{2,1,0:T(8,128)(2,1)S(1)} %collective-permute-done.23.refs_2_.refs_6_, ...), custom_call_target="tpu_custom_call" | custom-call | flops 48318384 | bytes 267386 | tf_op jit(solution)/shard_map/pallas_call | solution.py:194
  218.1 6.7 shard_map.254
  227.0 6.3 shard_map.253.refs_1_
  233.4 5.6 shard_map.255
  239.5 7.4 %collective-permute-done.44 = bf16[1,96,2048]{2,1,0:T(8,128)(2,1)} collective-permute-done((bf16[1,96,2048]{2,1,0:T(8,128)(2,1)}, bf16[1,96,2048]{2,1,0:T(8,128)(2,1)}, u32[]{:S(2)}, u32[]{:S(2)}) %collective-permute-start.44) | collective-permute-done | bytes 393248 | tf_op jit(solution)/shard_map/ppermute | solution.py:78
  258.2 12.1 %shard_map.257.refs_6_ = bf16[1024,2048]{1,0:T(8,128)(2,1)} custom-call(bf16[1024,1536]{1,0:T(8,128)(2,1)} %get-tuple-element.194.refs_0_, bf16[4,96,2048]{2,1,0:T(8,128)(2,1)S(1)} %copy-done.6, bf16[4,96,2048]{2,1,0:T(8,128)(2,1)} %copy-done.91, bf16[4,96,2048]{2,1,0:T(8,128)(2,1)} %collective-permute-done.37.refs_3_.refs_4_, ...), custom_call_target="tpu_custom_call" | custom-call | flops 128849016 | bytes 272629 | tf_op jit(solution)/shard_map/pallas_call | solution.py:194
  275.6 4.9 shard_map.259
  280.4 13.2 %shard_map.258 = (bf16[1024,2048]{1,0:T(8,128)(2,1)}, bf16[1024,2048]{1,0:T(8,128)(2,1)}) custom-call(bf16[1024,1536]{1,0:T(8,128)(2,1)} %get-tuple-element.194.refs_0_, bf16[4,96,2048]{2,1,0:T(8,128)(2,1)} %pad_maximum_fusion.1.refs_1_.refs_7_, bf16[4,96,2048]{2,1,0:T(8,128)(2,1)} %collective-permute-done.39.refs_2_.refs_8_, ...), custom_call_target="tpu_custom_call" | custom-call | flops 128849016 | bytes 440401 | tf_op jit(solution)/shard_map/pallas_call | solution.py:194
  293.7 11.9 %shard_map.260 = (bf16[2,4,96,2048]{3,2,1,0:T(8,128)(2,1)S(1)}, bf16[2,4,96,2048]{3,2,1,0:T(8,128)(2,1)}) custom-call(bf16[1536,1024]{1,0:T(8,128)(2,1)} %get-tuple-element.204.refs_0_, bf16[1024,2048]{1,0:T(8,128)(2,1)} %get-tuple-element.309.refs_1_.refs_0_), custom_call_target="tpu_custom_call" | custom-call | flops 128849016 | bytes 272629 | tf_op jit(solution)/shard_map/pallas_call | solution.py:434
  313.3 14.1 %collective-permute-done.49.refs_5_ = bf16[2,96,2048]{2,1,0:T(8,128)(2,1)S(1)} collective-permute-done((bf16[2,96,2048]{2,1,0:T(8,128)(2,1)S(1)}, bf16[2,96,2048]{2,1,0:T(8,128)(2,1)S(1)}, u32[]{:S(2)}, u32[]{:S(2)}) %collective-permute-start.49) | collective-permute-done | bytes 786464 | tf_op jit(solution)/shard_map/ppermute | solution.py:78
  328.6 15.7 %shard_map.261 = (bf16[1024,2048]{1,0:T(8,128)(2,1)}, bf16[1024,2048]{1,0:T(8,128)(2,1)}) custom-call(bf16[1024,1536]{1,0:T(8,128)(2,1)} %get-tuple-element.206.refs_0_, bf16[4,96,2048]{2,1,0:T(8,128)(2,1)S(1)} %pad_maximum_fusion.2.refs_1_, bf16[4,96,2048]{2,1,0:T(8,128)(2,1)} %copy-done.90, bf16[4,96,2048]{2,1,0:T(8,128)(2,1)} %copy-done.89, ...), custom_call_target="tpu_custom_call" | custom-call | flops 128849016 | bytes 524288 | tf_op jit(solution)/shard_map/pallas_call | solution.py:194
  344.3 12.4 %shard_map.262 = (bf16[4,2,96,2048]{3,2,1,0:T(8,128)(2,1)}, bf16[4,2,96,2048]{3,2,1,0:T(8,128)(2,1)}) custom-call(bf16[1536,1024]{1,0:T(8,128)(2,1)} %get-tuple-element.201.refs_0_, bf16[1024,2048]{1,0:T(8,128)(2,1)} %get-tuple-element.214.refs_1_), custom_call_target="tpu_custom_call" | custom-call | flops 128849016 | bytes 272629 | tf_op jit(solution)/shard_map/pallas_call | solution.py:434
  357.4 12.1 %shard_map.263 = (bf16[4,2,96,2048]{3,2,1,0:T(8,128)(2,1)}, bf16[4,2,96,2048]{3,2,1,0:T(8,128)(2,1)}) custom-call(bf16[1536,1024]{1,0:T(8,128)(2,1)} %get-tuple-element.201.refs_0_, bf16[1024,2048]{1,0:T(8,128)(2,1)} %get-tuple-element.219.refs_1_.refs_0_), custom_call_target="tpu_custom_call" | custom-call | flops 128849016 | bytes 272629 | tf_op jit(solution)/shard_map/pallas_call | solution.py:434
  371.2 16.7 %shard_map.266 = (bf16[512,768]{1,0:T(8,128)(2,1)S(1)}, bf16[512,768]{1,0:T(8,128)(2,1)S(1)}) custom-call(s32[1]{0:T(128)} %constant.23.clone.1.half_ref, bf16[1024,2048]{1,0:T(8,128)(2,1)} %get-tuple-element.219.refs_1_.refs_0_, bf16[1024,2048]{1,0:T(8,128)(2,1)} %get-tuple-element.214.refs_1_, bf16[4,96,2048]{2,1,0:T(8,128)(2,1)} %copy-done.5, ...), custom_call_target="tpu_custom_call" | custom-call | flops 128849016 | bytes 398458 | tf_op jit(solution)/shard_map/pallas_call | solution.py:275
  388.4 17.4 %shard_map.264.refs_1_ = f32[512,1536]{1,0:T(8,128)} custom-call(s32[1]{0:T(128)} %constant.22.clone.1.half_ref, bf16[1024,2048]{1,0:T(8,128)(2,1)} %get-tuple-element.219.refs_1_.refs_0_, bf16[1024,2048]{1,0:T(8,128)(2,1)} %get-tuple-element.214.refs_1_, bf16[4,96,2048]{2,1,0:T(8,128)(2,1)} %copy-done.5, bf16[4,96,2048]{2,1,0:T(8,128)(2,1)} %copy-done.91, ...), custom_call_target="tpu_custom_call" | custom-call | flops 128849016 | bytes 398458 | tf_op jit(solution)/shard_map/pallas_call | solution.py:275
  405.9 3.8 shard_map.265
  409.8 6.3 shard_map.267
  424.5 9.4 %shard_map.269 = (bf16[1024,768]{1,0:T(8,128)(2,1)}, bf16[1024,768]{1,0:T(8,128)(2,1)}) custom-call(bf16[1024,1536]{1,0:T(8,128)(2,1)} %get-tuple-element.229.refs_0_, bf16[4,96,1536]{2,1,0:T(8,128)(2,1)S(1)} %pad_maximum_fusion.3.refs_1_.refs_5_, bf16[4,96,1536]{2,1,0:T(8,128)(2,1)S(1)} %copy-done.2, bf16[4,96,1536]{2,1,0:T(8,128)(2,1)} %copy-done.88, ...), custom_call_target="tpu_custom_call" | custom-call | flops 48318384 | bytes 298844 | tf_op jit(solution)/shard_map/pallas_call | solution.py:194
  433.9 3.7 collective-permute-done.50.refs_1_
  439.2 3.8 shard_map.271
  445.9 3.8 shard_map.270
  452.4 12.6 %shard_map.272 = (bf16[2,2,96,1536]{3,2,1,0:T(8,128)(2,1)}, bf16[2,2,96,1536]{3,2,1,0:T(8,128)(2,1)}, bf16[2,2,96,1536]{3,2,1,0:T(8,128)(2,1)S(1)}, bf16[2,2,96,1536]{3,2,1,0:T(8,128)(2,1)}) custom-call(bf16[1536,1024]{1,0:T(8,128)(2,1)} %get-tuple-element.235.refs_0_, bf16[1536,1024]{1,0:T(8,128)(2,1)} %get-tuple-element.236.refs_1_, ...), custom_call_target="tpu_custom_call" | custom-call | flops 96636768 | bytes 283115 | tf_op jit(solution)/shard_map/pallas_call | solution.py:434
  465.9 32.9 %shard_map.273 = (bf16[1024,768]{1,0:T(8,128)(2,1)S(1)}, bf16[1024,768]{1,0:T(8,128)(2,1)S(1)}, bf16[1024,768]{1,0:T(8,128)(2,1)}, f32[6,2,1024]{2,1,0:T(2,128)S(1)}, f32[6,1024,2]{2,1,0:T(8,128)}) custom-call(bf16[1024,1536]{1,0:T(8,128)(2,1)} %shard_map.248.q_ref.k_ref, bf16[1024,1536]{1,0:T(8,128)(2,1)} %shard_map.248.q_ref.k_ref, ...), custom_call_target="tpu_custom_call" | custom-call | flops 483183808 | bytes 251658 | tf_op jit(solution)/shard_map/pallas_call | solution.py:914
  503.6 4.1 shard_map.274
  508.9 11.9 %shard_map.276 = (bf16[2,2,96,1536]{3,2,1,0:T(8,128)(2,1)S(1)}, bf16[2,2,96,1536]{3,2,1,0:T(8,128)(2,1)}, bf16[2,2,96,1536]{3,2,1,0:T(8,128)(2,1)S(1)}, bf16[2,2,96,1536]{3,2,1,0:T(8,128)(2,1)}) custom-call(bf16[1536,1024]{1,0:T(8,128)(2,1)} %get-tuple-element.235.refs_0_, bf16[1024,768]{1,0:T(8,128)(2,1)} %copy-done.26, bf16[1024,768]{1,0:T(8,128)(2,1)} %copy-done.27), custom_call_target="tpu_custom_call" | custom-call | flops 96636768 | bytes 220200 | tf_op jit(solution)/shard_map/pallas_call | solution.py:434
  537.7 6.7 shard_map.280
  544.5 15.5 %shard_map.281 = (bf16[512,768]{1,0:T(8,128)(2,1)}, bf16[512,768]{1,0:T(8,128)(2,1)}) custom-call(s32[1]{0:T(128)} %bitcast.11.half_ref, bf16[1024,768]{1,0:T(8,128)(2,1)} %get-tuple-element.273.refs_2_.refs_0_, bf16[1024,768]{1,0:T(8,128)(2,1)} %copy-done.26, bf16[1024,768]{1,0:T(8,128)(2,1)} %copy-done.27, ...), custom_call_target="tpu_custom_call" | custom-call | flops 100663296 | bytes 325058 | tf_op jit(solution)/shard_map/pallas_call | solution.py:275
  573.7 15.0 %shard_map.285.refs_1_ = f32[512,1536]{1,0:T(8,128)} custom-call(s32[1]{0:T(128)} %bitcast.half_ref, bf16[1024,768]{1,0:T(8,128)(2,1)} %get-tuple-element.273.refs_2_.refs_0_, bf16[1024,768]{1,0:T(8,128)(2,1)} %copy-done.26, bf16[1024,768]{1,0:T(8,128)(2,1)} %copy-done.27, bf16[1024,768]{1,0:T(8,128)(2,1)} %get-tuple-element.266.refs_1_.refs_3_, ...), custom_call_target="tpu_custom_call" | custom-call | flops 100663296 | bytes 325058 | tf_op jit(solution)/shard_map/pallas_call | solution.py:275
  592.7 6.2 shard_map.287
  598.9 4.8 shard_map.289
  605.1 4.7 shard_map.288
  612.2 9.3 %shard_map.293 = bf16[512,1536]{1,0:T(8,128)(2,1)S(1)} custom-call(s32[1]{0:T(128)} %constant.23.clone.1.half_ref, bf16[1024,2048]{1,0:T(8,128)(2,1)} %get-tuple-element.309.refs_1_.refs_0_, bf16[4,96,2048]{2,1,0:T(8,128)(2,1)} %copy-done.3, bf16[4,96,2048]{2,1,0:T(8,128)(2,1)} %copy-done.90, bf16[4,96,2048]{2,1,0:T(8,128)(2,1)} %copy-done.89, ...), custom_call_target="tpu_custom_call" | custom-call | flops 64424508 | bytes 230686 | tf_op jit(solution)/shard_map/pallas_call | solution.py:275
  632.4 22.6 %collective-permute-done.75 = bf16[2,96,2432]{2,1,0:T(8,128)(2,1)S(1)} collective-permute-done((bf16[2,96,2432]{2,1,0:T(8,128)(2,1)}, bf16[2,96,2432]{2,1,0:T(8,128)(2,1)S(1)}, u32[]{:S(2)}, u32[]{:S(2)}) %collective-permute-start.75) | collective-permute-done | bytes 933920 | tf_op jit(solution)/shard_map/ppermute | solution.py:78
  658.8 10.3 %shard_map.292.refs_1_ = f32[512,1536]{1,0:T(8,128)} custom-call(s32[1]{0:T(128)} %constant.22.clone.1.half_ref, bf16[1024,2048]{1,0:T(8,128)(2,1)} %get-tuple-element.309.refs_1_.refs_0_, bf16[4,96,2048]{2,1,0:T(8,128)(2,1)S(1)} %copy-done.4, bf16[4,96,2048]{2,1,0:T(8,128)(2,1)} %copy-done.90, bf16[4,96,2048]{2,1,0:T(8,128)(2,1)} %copy-done.89, ...), custom_call_target="tpu_custom_call" | custom-call | flops 64424508 | bytes 230686 | tf_op jit(solution)/shard_map/pallas_call | solution.py:275
  669.1 4.5 shard_map.294
  674.7 5.8 collective-permute-done.77
  (473 shorter events, 202.2 us)
Async XLA Ops:
  24.0 23.5 %collective-permute-start.10 = (bf16[2,96,1536]{2,1,0:T(8,128)(2,1)S(1)}, bf16[2,96,1536]{2,1,0:T(8,128)(2,1)S(1)}, u32[]{:S(2)}, u32[]{:S(2)}) collective-permute-start(bf16[2,96,1536]{2,1,0:T(8,128)(2,1)S(1)} %pad_maximum_fusion.8.refs_1_.refs_10_.refs_18_), channel_id=1, source_target_pairs={{0,2},{2,0},{4,6},{6,4},{8,10},{10,8},{12,14},{14,12},{16,18},{18,... | collective-permute-start | bytes 1769480 | tf_op jit(solution)/shard_map/ppermute | solution.py:78
  45.5 22.1 %collective-permute-start.16 = (bf16[2,96,1536]{2,1,0:T(8,128)(2,1)S(1)}, bf16[2,96,1536]{2,1,0:T(8,128)(2,1)}, u32[]{:S(2)}, u32[]{:S(2)}) collective-permute-start(bf16[2,96,1536]{2,1,0:T(8,128)(2,1)S(1)} %pad_maximum_fusion.8.refs_1_.refs_10_.refs_18_), channel_id=1, source_target_pairs={{0,4},{2,6},{4,0},{6,2},{8,12},{10,14},{12,8},{14,10},{16,20},{18,... | collective-permute-start | bytes 1769480 | tf_op jit(solution)/shard_map/ppermute | solution.py:78
  46.0 21.7 %collective-permute-start.17 = (bf16[2,96,1536]{2,1,0:T(8,128)(2,1)S(1)}, bf16[2,96,1536]{2,1,0:T(8,128)(2,1)}, u32[]{:S(2)}, u32[]{:S(2)}) collective-permute-start(bf16[2,96,1536]{2,1,0:T(8,128)(2,1)S(1)} %collective-permute-done.8.refs_2_.refs_11_.refs_19_), channel_id=1, source_target_pairs={{0,2},{2,0},{4,6},{6,4},{8,10},{10,8},{12,14},{14,12},{16,18},{18,... | collective-permute-start | bytes 1769480 | tf_op jit(solution)/shard_map/ppermute | solution.py:78
  47.5 29.0 %collective-permute-start.14 = (bf16[2,96,1536]{2,1,0:T(8,128)(2,1)S(1)}, bf16[2,96,1536]{2,1,0:T(8,128)(2,1)}, u32[]{:S(2)}, u32[]{:S(2)}) collective-permute-start(bf16[2,96,1536]{2,1,0:T(8,128)(2,1)S(1)} %collective-permute-done.10.refs_3_.refs_12_.refs_20_), channel_id=1, source_target_pairs={{0,4},{2,6},{4,0},{6,2},{8,12},{10,14},{12,8},{14,10},{16,20},{18,... | collective-permute-start | bytes 1769480 | tf_op jit(solution)/shard_map/ppermute | solution.py:78
  54.0 22.5 %collective-permute-start.15 = (bf16[2,96,1536]{2,1,0:T(8,128)(2,1)S(1)}, bf16[2,96,1536]{2,1,0:T(8,128)(2,1)}, u32[]{:S(2)}, u32[]{:S(2)}) collective-permute-start(bf16[2,96,1536]{2,1,0:T(8,128)(2,1)S(1)} %collective-permute-done.11.refs_6_.refs_15_.refs_23_), channel_id=1, source_target_pairs={{0,2},{2,0},{4,6},{6,4},{8,10},{10,8},{12,14},{14,12},{16,18},{18,... | collective-permute-start | bytes 1769480 | tf_op jit(solution)/shard_map/ppermute | solution.py:78
  67.6 27.3 %collective-permute-start.5 = (bf16[512,768]{1,0:T(8,128)(2,1)S(1)}, bf16[512,768]{1,0:T(8,128)(2,1)S(1)}, u32[]{:S(2)}, u32[]{:S(2)}) collective-permute-start(bf16[512,768]{1,0:T(8,128)(2,1)S(1)} %get-tuple-element.168), channel_id=1, source_target_pairs={{0,1},{1,0},{2,3},{3,2},{4,5},{5,4},{6,7},{7,6},{8,9},{9,8},{10,11... | collective-permute-start | bytes 2359304 | tf_op jit(solution)/shard_map/ppermute | solution.py:51
  67.7 27.3 %collective-permute-start.6 = (bf16[512,768]{1,0:T(8,128)(2,1)S(1)}, bf16[512,768]{1,0:T(8,128)(2,1)S(1)}, u32[]{:S(2)}, u32[]{:S(2)}) collective-permute-start(bf16[512,768]{1,0:T(8,128)(2,1)S(1)} %get-tuple-element.169), channel_id=1, source_target_pairs={{0,1},{1,0},{2,3},{3,2},{4,5},{5,4},{6,7},{7,6},{8,9},{9,8},{10,11... | collective-permute-start | bytes 2359304 | tf_op jit(solution)/shard_map/ppermute | solution.py:51
  101.4 24.4 %collective-permute-start.23 = (bf16[4,96,1536]{2,1,0:T(8,128)(2,1)S(1)}, bf16[4,96,1536]{2,1,0:T(8,128)(2,1)S(1)}, u32[]{:S(2)}, u32[]{:S(2)}) collective-permute-start(bf16[4,96,1536]{2,1,0:T(8,128)(2,1)S(1)} %pad_maximum_fusion.3.refs_1_.refs_5_), channel_id=1, source_target_pairs={{0,2},{2,0},{4,6},{6,4},{8,10},{10,8},{12,14},{14,12},{16,18},{18,... | collective-permute-start | bytes 3538952 | tf_op jit(solution)/shard_map/ppermute | solution.py:78
  103.3 24.9 %collective-permute-start.24 = (bf16[4,96,1536]{2,1,0:T(8,128)(2,1)S(1)}, bf16[4,96,1536]{2,1,0:T(8,128)(2,1)S(1)}, u32[]{:S(2)}, u32[]{:S(2)}) collective-permute-start(bf16[4,96,1536]{2,1,0:T(8,128)(2,1)S(1)} %pad_maximum_fusion.3.refs_1_.refs_5_), channel_id=1, source_target_pairs={{0,4},{2,6},{4,0},{6,2},{8,12},{10,14},{12,8},{14,10},{16,20},{18,... | collective-permute-start | bytes 3538952 | tf_op jit(solution)/shard_map/ppermute | solution.py:78
  120.9 19.8 %collective-permute-start.28 = (bf16[2,96,2048]{2,1,0:T(8,128)(2,1)S(1)}, bf16[2,96,2048]{2,1,0:T(8,128)(2,1)S(1)}, u32[]{:S(2)}, u32[]{:S(2)}) collective-permute-start(bf16[2,96,2048]{2,1,0:T(8,128)(2,1)S(1)} %pad_maximum_fusion.4), channel_id=1, source_target_pairs={{0,8},{2,10},{4,12},{6,14},{8,0},{10,2},{12,4},{14,6},{16,24},{18,... | collective-permute-start | bytes 2359304 | tf_op jit(solution)/shard_map/ppermute | solution.py:78
  140.9 46.8 %collective-permute-start.35 = (bf16[4,96,2048]{2,1,0:T(8,128)(2,1)S(1)}, bf16[4,96,2048]{2,1,0:T(8,128)(2,1)S(1)}, u32[]{:S(2)}, u32[]{:S(2)}) collective-permute-start(bf16[4,96,2048]{2,1,0:T(8,128)(2,1)S(1)} %pad_maximum_fusion.refs_1_.refs_2_), channel_id=1, source_target_pairs={{0,2},{2,0},{4,6},{6,4},{8,10},{10,8},{12,14},{14,12},{16,18},{18,... | collective-permute-start | bytes 4718600 | tf_op jit(solution)/shard_map/ppermute | solution.py:78
  142.7 45.7 %collective-permute-start.37 = (bf16[4,96,2048]{2,1,0:T(8,128)(2,1)S(1)}, bf16[4,96,2048]{2,1,0:T(8,128)(2,1)}, u32[]{:S(2)}, u32[]{:S(2)}) collective-permute-start(bf16[4,96,2048]{2,1,0:T(8,128)(2,1)S(1)} %pad_maximum_fusion.refs_1_.refs_2_), channel_id=1, source_target_pairs={{0,4},{2,6},{4,0},{6,2},{8,12},{10,14},{12,8},{14,10},{16,20},{18,... | collective-permute-start | bytes 4718600 | tf_op jit(solution)/shard_map/ppermute | solution.py:78
  163.3 28.0 %collective-permute-start.34 = (bf16[2,96,2048]{2,1,0:T(8,128)(2,1)S(1)}, bf16[2,96,2048]{2,1,0:T(8,128)(2,1)S(1)}, u32[]{:S(2)}, u32[]{:S(2)}) collective-permute-start(bf16[2,96,2048]{2,1,0:T(8,128)(2,1)S(1)} %pad_maximum_fusion.5), channel_id=1, source_target_pairs={{0,8},{2,10},{4,12},{6,14},{8,0},{10,2},{12,4},{14,6},{16,24},{18,... | collective-permute-start | bytes 2359304 | tf_op jit(solution)/shard_map/ppermute | solution.py:78
  207.1 41.0 %collective-permute-start.39 = (bf16[4,96,2048]{2,1,0:T(8,128)(2,1)}, bf16[4,96,2048]{2,1,0:T(8,128)(2,1)}, u32[]{:S(2)}, u32[]{:S(2)}) collective-permute-start(bf16[4,96,2048]{2,1,0:T(8,128)(2,1)} %pad_maximum_fusion.1.refs_1_.refs_7_), channel_id=1, source_target_pairs={{0,2},{2,0},{4,6},{6,4},{8,10},{10,8},{12,14},{14,12},{16,18},{18,... | collective-permute-start | bytes 4718600 | tf_op jit(solution)/shard_map/ppermute | solution.py:78
  207.4 43.3 %collective-permute-start.40 = (bf16[4,96,2048]{2,1,0:T(8,128)(2,1)}, bf16[4,96,2048]{2,1,0:T(8,128)(2,1)}, u32[]{:S(2)}, u32[]{:S(2)}) collective-permute-start(bf16[4,96,2048]{2,1,0:T(8,128)(2,1)} %pad_maximum_fusion.1.refs_1_.refs_7_), channel_id=1, source_target_pairs={{0,4},{2,6},{4,0},{6,2},{8,12},{10,14},{12,8},{14,10},{16,20},{18,... | collective-permute-start | bytes 4718600 | tf_op jit(solution)/shard_map/ppermute | solution.py:78
  226.1 20.7 %collective-permute-start.44 = (bf16[1,96,2048]{2,1,0:T(8,128)(2,1)}, bf16[1,96,2048]{2,1,0:T(8,128)(2,1)}, u32[]{:S(2)}, u32[]{:S(2)}) collective-permute-start(bf16[1,96,2048]{2,1,0:T(8,128)(2,1)} %convert_bitcast_fusion), channel_id=1, source_target_pairs={{0,16},{2,18},{4,20},{6,22},{8,24},{10,26},{12,28},{14,30},{16,0},... | collective-permute-start | bytes 1179656 | tf_op jit(solution)/shard_map/ppermute | solution.py:78
  248.1 22.3 %collective-permute-start.45 = (bf16[2,96,2048]{2,1,0:T(8,128)(2,1)S(1)}, bf16[2,96,2048]{2,1,0:T(8,128)(2,1)}, u32[]{:S(2)}, u32[]{:S(2)}) collective-permute-start(bf16[2,96,2048]{2,1,0:T(8,128)(2,1)S(1)} %pad_maximum_fusion.6), channel_id=1, source_target_pairs={{0,8},{2,10},{4,12},{6,14},{8,0},{10,2},{12,4},{14,6},{16,24},{18,... | collective-permute-start | bytes 2359304 | tf_op jit(solution)/shard_map/ppermute | solution.py:78
  250.4 21.2 %collective-permute-start.41 = (bf16[2,96,2048]{2,1,0:T(8,128)(2,1)}, bf16[2,96,2048]{2,1,0:T(8,128)(2,1)S(1)}, u32[]{:S(2)}, u32[]{:S(2)}) collective-permute-start(bf16[2,96,2048]{2,1,0:T(8,128)(2,1)} %slice.119), channel_id=1, source_target_pairs={{0,4},{2,6},{4,0},{6,2},{8,12},{10,14},{12,8},{14,10},{16,20},{18,... | collective-permute-start | bytes 2359304 | tf_op jit(solution)/shard_map/ppermute | solution.py:78
  252.8 19.3 %collective-permute-start.42 = (bf16[2,96,2048]{2,1,0:T(8,128)(2,1)}, bf16[2,96,2048]{2,1,0:T(8,128)(2,1)S(1)}, u32[]{:S(2)}, u32[]{:S(2)}) collective-permute-start(bf16[2,96,2048]{2,1,0:T(8,128)(2,1)} %slice.120), channel_id=1, source_target_pairs={{0,2},{2,0},{4,6},{6,4},{8,10},{10,8},{12,14},{14,12},{16,18},{18,... | collective-permute-start | bytes 2359304 | tf_op jit(solution)/shard_map/ppermute | solution.py:78
  254.5 21.1 %collective-permute-start.43 = (bf16[512,1536]{1,0:T(8,128)(2,1)S(1)}, bf16[512,1536]{1,0:T(8,128)(2,1)}, u32[]{:S(2)}, u32[]{:S(2)}) collective-permute-start(bf16[512,1536]{1,0:T(8,128)(2,1)S(1)} %copy-done.43), channel_id=1, source_target_pairs={{0,1},{1,0},{2,3},{3,2},{4,5},{5,4},{6,7},{7,6},{8,9},{9,8},{10,11... | collective-permute-start | bytes 4718600 | tf_op jit(solution)/shard_map/ppermute | solution.py:51
  272.1 36.4 %collective-permute-start.47 = (bf16[4,96,2048]{2,1,0:T(8,128)(2,1)S(1)}, bf16[4,96,2048]{2,1,0:T(8,128)(2,1)S(1)}, u32[]{:S(2)}, u32[]{:S(2)}) collective-permute-start(bf16[4,96,2048]{2,1,0:T(8,128)(2,1)S(1)} %pad_maximum_fusion.2.refs_1_), channel_id=1, source_target_pairs={{0,4},{2,6},{4,0},{6,2},{8,12},{10,14},{12,8},{14,10},{16,20},{18,... | collective-permute-start | bytes 4718600 | tf_op jit(solution)/shard_map/ppermute | solution.py:78
  273.9 36.1 %collective-permute-start.46 = (bf16[4,96,2048]{2,1,0:T(8,128)(2,1)S(1)}, bf16[4,96,2048]{2,1,0:T(8,128)(2,1)S(1)}, u32[]{:S(2)}, u32[]{:S(2)}) collective-permute-start(bf16[4,96,2048]{2,1,0:T(8,128)(2,1)S(1)} %pad_maximum_fusion.2.refs_1_), channel_id=1, source_target_pairs={{0,2},{2,0},{4,6},{6,4},{8,10},{10,8},{12,14},{14,12},{16,18},{18,... | collective-permute-start | bytes 4718600 | tf_op jit(solution)/shard_map/ppermute | solution.py:78
  311.5 94.4 %collective-permute-start.51 = (bf16[2,4,96,2048]{3,2,1,0:T(8,128)(2,1)}, bf16[2,4,96,2048]{3,2,1,0:T(8,128)(2,1)}, u32[]{:S(2)}, u32[]{:S(2)}) collective-permute-start(bf16[2,4,96,2048]{3,2,1,0:T(8,128)(2,1)} %copy-done.81), channel_id=1, source_target_pairs={{0,8},{2,10},{4,12},{6,14},{8,0},{10,2},{12,4},{14,6},{16,24},{18,... | collective-permute-start | bytes 9437192 | tf_op jit(solution)/shard_map/ppermute | solution.py:78
  356.6 77.3 %collective-permute-start.57 = (bf16[4,2,96,2048]{3,2,1,0:T(8,128)(2,1)}, bf16[4,2,96,2048]{3,2,1,0:T(8,128)(2,1)}, u32[]{:S(2)}, u32[]{:S(2)}) collective-permute-start(bf16[4,2,96,2048]{3,2,1,0:T(8,128)(2,1)} %get-tuple-element.215), channel_id=1, source_target_pairs={{0,2},{2,0},{4,6},{6,4},{8,10},{10,8},{12,14},{14,12},{16,18},{18,... | collective-permute-start | bytes 9437192 | tf_op jit(solution)/shard_map/ppermute | solution.py:78
  369.5 68.1 %collective-permute-start.50 = (bf16[4,2,96,2048]{3,2,1,0:T(8,128)(2,1)}, bf16[4,2,96,2048]{3,2,1,0:T(8,128)(2,1)S(1)}, u32[]{:S(2)}, u32[]{:S(2)}) collective-permute-start(bf16[4,2,96,2048]{3,2,1,0:T(8,128)(2,1)} %get-tuple-element.218), channel_id=1, source_target_pairs={{0,4},{2,6},{4,0},{6,2},{8,12},{10,14},{12,8},{14,10},{16,20},{18,... | collective-permute-start | bytes 9437192 | tf_op jit(solution)/shard_map/ppermute | solution.py:78
  387.9 21.9 %collective-permute-start.52 = (bf16[512,768]{1,0:T(8,128)(2,1)S(1)}, bf16[512,768]{1,0:T(8,128)(2,1)S(1)}, u32[]{:S(2)}, u32[]{:S(2)}) collective-permute-start(bf16[512,768]{1,0:T(8,128)(2,1)S(1)} %get-tuple-element.224), channel_id=1, source_target_pairs={{0,1},{1,0},{2,3},{3,2},{4,5},{5,4},{6,7},{7,6},{8,9},{9,8},{10,11... | collective-permute-start | bytes 2359304 | tf_op jit(solution)/shard_map/ppermute | solution.py:51
  387.9 21.8 %collective-permute-start.53 = (bf16[512,768]{1,0:T(8,128)(2,1)S(1)}, bf16[512,768]{1,0:T(8,128)(2,1)S(1)}, u32[]{:S(2)}, u32[]{:S(2)}) collective-permute-start(bf16[512,768]{1,0:T(8,128)(2,1)S(1)} %get-tuple-element.225), channel_id=1, source_target_pairs={{0,1},{1,0},{2,3},{3,2},{4,5},{5,4},{6,7},{7,6},{8,9},{9,8},{10,11... | collective-permute-start | bytes 2359304 | tf_op jit(solution)/shard_map/ppermute | solution.py:51
  416.6 84.5 %collective-permute-start.60 = (bf16[1,384,2048]{2,1,0:T(8,128)(2,1)S(1)}, bf16[1,384,2048]{2,1,0:T(8,128)(2,1)}, u32[]{:S(2)}, u32[]{:S(2)}) collective-permute-start(bf16[1,384,2048]{2,1,0:T(8,128)(2,1)S(1)} %get-tuple-element.222), channel_id=1, source_target_pairs={{0,16},{2,18},{4,20},{6,22},{8,24},{10,26},{12,28},{14,30},{16,0},... | collective-permute-start | bytes 4718600 | tf_op jit(solution)/shard_map/ppermute | solution.py:78
  444.2 59.4 %collective-permute-start.58 = (bf16[4,96,2048]{2,1,0:T(8,128)(2,1)S(1)}, bf16[4,96,2048]{2,1,0:T(8,128)(2,1)}, u32[]{:S(2)}, u32[]{:S(2)}) collective-permute-start(bf16[4,96,2048]{2,1,0:T(8,128)(2,1)S(1)} %get-tuple-element.240), channel_id=1, source_target_pairs={{0,4},{2,6},{4,0},{6,2},{8,12},{10,14},{12,8},{14,10},{16,20},{18,... | collective-permute-start | bytes 4718600 | tf_op jit(solution)/shard_map/ppermute | solution.py:78
  451.0 52.7 %collective-permute-start.56 = (bf16[4,96,2048]{2,1,0:T(8,128)(2,1)S(1)}, bf16[4,96,2048]{2,1,0:T(8,128)(2,1)}, u32[]{:S(2)}, u32[]{:S(2)}) collective-permute-start(bf16[4,96,2048]{2,1,0:T(8,128)(2,1)S(1)} %get-tuple-element.234), channel_id=1, source_target_pairs={{0,2},{2,0},{4,6},{6,4},{8,10},{10,8},{12,14},{14,12},{16,18},{18,... | collective-permute-start | bytes 4718600 | tf_op jit(solution)/shard_map/ppermute | solution.py:78
  465.0 63.7 %collective-permute-start.62 = (bf16[2,2,96,1536]{3,2,1,0:T(8,128)(2,1)}, bf16[2,2,96,1536]{3,2,1,0:T(8,128)(2,1)}, u32[]{:S(2)}, u32[]{:S(2)}) collective-permute-start(bf16[2,2,96,1536]{3,2,1,0:T(8,128)(2,1)} %get-tuple-element.243), channel_id=1, source_target_pairs={{0,2},{2,0},{4,6},{6,4},{8,10},{10,8},{12,14},{14,12},{16,18},{18,... | collective-permute-start | bytes 3538952 | tf_op jit(solution)/shard_map/ppermute | solution.py:78
  465.6 68.8 %collective-permute-start.61 = (bf16[2,2,96,1536]{3,2,1,0:T(8,128)(2,1)}, bf16[2,2,96,1536]{3,2,1,0:T(8,128)(2,1)S(1)}, u32[]{:S(2)}, u32[]{:S(2)}) collective-permute-start(bf16[2,2,96,1536]{3,2,1,0:T(8,128)(2,1)} %get-tuple-element.242), channel_id=1, source_target_pairs={{0,4},{2,6},{4,0},{6,2},{8,12},{10,14},{12,8},{14,10},{16,20},{18,... | collective-permute-start | bytes 3538952 | tf_op jit(solution)/shard_map/ppermute | solution.py:78
  522.9 37.2 %collective-permute-start.64 = (bf16[2,2,96,1536]{3,2,1,0:T(8,128)(2,1)}, bf16[2,2,96,1536]{3,2,1,0:T(8,128)(2,1)}, u32[]{:S(2)}, u32[]{:S(2)}) collective-permute-start(bf16[2,2,96,1536]{3,2,1,0:T(8,128)(2,1)} %get-tuple-element.259), channel_id=1, source_target_pairs={{0,2},{2,0},{4,6},{6,4},{8,10},{10,8},{12,14},{14,12},{16,18},{18,... | collective-permute-start | bytes 3538952 | tf_op jit(solution)/shard_map/ppermute | solution.py:78
  524.3 35.8 %collective-permute-start.63 = (bf16[2,2,96,1536]{3,2,1,0:T(8,128)(2,1)}, bf16[2,2,96,1536]{3,2,1,0:T(8,128)(2,1)}, u32[]{:S(2)}, u32[]{:S(2)}) collective-permute-start(bf16[2,2,96,1536]{3,2,1,0:T(8,128)(2,1)} %copy-done.83), channel_id=1, source_target_pairs={{0,4},{2,6},{4,0},{6,2},{8,12},{10,14},{12,8},{14,10},{16,20},{18,... | collective-permute-start | bytes 3538952 | tf_op jit(solution)/shard_map/ppermute | solution.py:78
  526.0 44.0 %collective-permute-start.59 = (bf16[2,96,4096]{2,1,0:T(8,128)(2,1)}, bf16[2,96,4096]{2,1,0:T(8,128)(2,1)}, u32[]{:S(2)}, u32[]{:S(2)}) collective-permute-start(bf16[2,96,4096]{2,1,0:T(8,128)(2,1)} %copy-done.82), channel_id=1, source_target_pairs={{0,8},{2,10},{4,12},{6,14},{8,0},{10,2},{12,4},{14,6},{16,24},{18,... | collective-permute-start | bytes 4718600 | tf_op jit(solution)/shard_map/ppermute | solution.py:78
  532.5 34.3 %collective-permute-start.69 = (bf16[2,96,1536]{2,1,0:T(8,128)(2,1)}, bf16[2,96,1536]{2,1,0:T(8,128)(2,1)}, u32[]{:S(2)}, u32[]{:S(2)}) collective-permute-start(bf16[2,96,1536]{2,1,0:T(8,128)(2,1)} %get-tuple-element.265), channel_id=1, source_target_pairs={{0,4},{2,6},{4,0},{6,2},{8,12},{10,14},{12,8},{14,10},{16,20},{18,... | collective-permute-start | bytes 1769480 | tf_op jit(solution)/shard_map/ppermute | solution.py:78
  536.8 31.5 %collective-permute-start.68 = (bf16[2,96,1536]{2,1,0:T(8,128)(2,1)}, bf16[2,96,1536]{2,1,0:T(8,128)(2,1)}, u32[]{:S(2)}, u32[]{:S(2)}) collective-permute-start(bf16[2,96,1536]{2,1,0:T(8,128)(2,1)} %get-tuple-element.262), channel_id=1, source_target_pairs={{0,2},{2,0},{4,6},{6,4},{8,10},{10,8},{12,14},{14,12},{16,18},{18,... | collective-permute-start | bytes 1769480 | tf_op jit(solution)/shard_map/ppermute | solution.py:78
  566.8 24.3 %collective-permute-start.73 = (bf16[2,2,96,896]{3,2,1,0:T(8,128)(2,1)S(1)}, bf16[2,2,96,896]{3,2,1,0:T(8,128)(2,1)}, u32[]{:S(2)}, u32[]{:S(2)}) collective-permute-start(bf16[2,2,96,896]{3,2,1,0:T(8,128)(2,1)S(1)} %copy-done.87), channel_id=1, source_target_pairs={{0,2},{2,0},{4,6},{6,4},{8,10},{10,8},{12,14},{14,12},{16,18},{18,... | collective-permute-start | bytes 2064392 | tf_op jit(solution)/shard_map/ppermute | solution.py:78
  568.3 35.4 %collective-permute-start.67 = (bf16[2,2,96,896]{3,2,1,0:T(8,128)(2,1)S(1)}, bf16[2,2,96,896]{3,2,1,0:T(8,128)(2,1)}, u32[]{:S(2)}, u32[]{:S(2)}) collective-permute-start(bf16[2,2,96,896]{3,2,1,0:T(8,128)(2,1)S(1)} %get-tuple-element.288), channel_id=1, source_target_pairs={{0,4},{2,6},{4,0},{6,2},{8,12},{10,14},{12,8},{14,10},{16,20},{18,... | collective-permute-start | bytes 2064392 | tf_op jit(solution)/shard_map/ppermute | solution.py:78
  570.1 40.4 %collective-permute-start.66 = (bf16[2,96,1536]{2,1,0:T(8,128)(2,1)S(1)}, bf16[2,96,1536]{2,1,0:T(8,128)(2,1)}, u32[]{:S(2)}, u32[]{:S(2)}) collective-permute-start(bf16[2,96,1536]{2,1,0:T(8,128)(2,1)S(1)} %get-tuple-element.283), channel_id=1, source_target_pairs={{0,4},{2,6},{4,0},{6,2},{8,12},{10,14},{12,8},{14,10},{16,20},{18,... | collective-permute-start | bytes 1769480 | tf_op jit(solution)/shard_map/ppermute | solution.py:78
  573.0 56.3 %collective-permute-start.80 = (bf16[1,96,4096]{2,1,0:T(8,128)(2,1)}, bf16[1,96,4096]{2,1,0:T(8,128)(2,1)}, u32[]{:S(2)}, u32[]{:S(2)}) collective-permute-start(bf16[1,96,4096]{2,1,0:T(8,128)(2,1)} %get-tuple-element.277), channel_id=1, source_target_pairs={{0,16},{2,18},{4,20},{6,22},{8,24},{10,26},{12,28},{14,30},{16,0},... | collective-permute-start | bytes 2359304 | tf_op jit(solution)/shard_map/ppermute | solution.py:78
  573.0 48.6 %collective-permute-start.65 = (bf16[2,96,1536]{2,1,0:T(8,128)(2,1)}, bf16[2,96,1536]{2,1,0:T(8,128)(2,1)S(1)}, u32[]{:S(2)}, u32[]{:S(2)}) collective-permute-start(bf16[2,96,1536]{2,1,0:T(8,128)(2,1)} %get-tuple-element.280), channel_id=1, source_target_pairs={{0,2},{2,0},{4,6},{6,4},{8,10},{10,8},{12,14},{14,12},{16,18},{18,... | collective-permute-start | bytes 1769480 | tf_op jit(solution)/shard_map/ppermute | solution.py:78
  591.1 34.9 %collective-permute-start.78 = (bf16[2,96,1536]{2,1,0:T(8,128)(2,1)}, bf16[2,96,1536]{2,1,0:T(8,128)(2,1)S(1)}, u32[]{:S(2)}, u32[]{:S(2)}) collective-permute-start(bf16[2,96,1536]{2,1,0:T(8,128)(2,1)} %get-tuple-element.294), channel_id=1, source_target_pairs={{0,8},{2,10},{4,12},{6,14},{8,0},{10,2},{12,4},{14,6},{16,24},{18,... | collective-permute-start | bytes 1769480 | tf_op jit(solution)/shard_map/ppermute | solution.py:78
  621.6 33.6 %collective-permute-start.82 = (bf16[1,192,2048]{2,1,0:T(8,128)(2,1)S(1)}, bf16[1,192,2048]{2,1,0:T(8,128)(2,1)S(1)}, u32[]{:S(2)}, u32[]{:S(2)}) collective-permute-start(bf16[1,192,2048]{2,1,0:T(8,128)(2,1)S(1)} %copy-done.85), channel_id=1, source_target_pairs={{0,4},{2,6},{4,0},{6,2},{8,12},{10,14},{12,8},{14,10},{16,20},{18,... | collective-permute-start | bytes 2359304 | tf_op jit(solution)/shard_map/ppermute | solution.py:78
  622.3 46.8 %collective-permute-start.76 = (bf16[512,1536]{1,0:T(8,128)(2,1)S(1)}, bf16[512,1536]{1,0:T(8,128)(2,1)S(1)}, u32[]{:S(2)}, u32[]{:S(2)}) collective-permute-start(bf16[512,1536]{1,0:T(8,128)(2,1)S(1)} %shard_map.293), channel_id=1, source_target_pairs={{0,1},{1,0},{2,3},{3,2},{4,5},{5,4},{6,7},{7,6},{8,9},{9,8},{10,11... | collective-permute-start | bytes 4718600 | tf_op jit(solution)/shard_map/ppermute | solution.py:51
  625.3 29.6 %collective-permute-start.75 = (bf16[2,96,2432]{2,1,0:T(8,128)(2,1)}, bf16[2,96,2432]{2,1,0:T(8,128)(2,1)S(1)}, u32[]{:S(2)}, u32[]{:S(2)}) collective-permute-start(bf16[2,96,2432]{2,1,0:T(8,128)(2,1)} %get-tuple-element.307), channel_id=1, source_target_pairs={{0,8},{2,10},{4,12},{6,14},{8,0},{10,2},{12,4},{14,6},{16,24},{18,... | collective-permute-start | bytes 2801672 | tf_op jit(solution)/shard_map/ppermute | solution.py:78
  626.2 30.2 %collective-permute-start.79 = (bf16[1,96,1536]{2,1,0:T(8,128)(2,1)S(1)}, bf16[1,96,1536]{2,1,0:T(8,128)(2,1)S(1)}, u32[]{:S(2)}, u32[]{:S(2)}) collective-permute-start(bf16[1,96,1536]{2,1,0:T(8,128)(2,1)S(1)} %get-tuple-element.314), channel_id=1, source_target_pairs={{0,16},{2,18},{4,20},{6,22},{8,24},{10,26},{12,28},{14,30},{16,0},... | collective-permute-start | bytes 884744 | tf_op jit(solution)/shard_map/ppermute | solution.py:78
  657.4 23.0 %collective-permute-start.77 = (bf16[1,96,2432]{2,1,0:T(8,128)(2,1)S(1)}, bf16[1,96,2432]{2,1,0:T(8,128)(2,1)S(1)}, u32[]{:S(2)}, u32[]{:S(2)}) collective-permute-start(bf16[1,96,2432]{2,1,0:T(8,128)(2,1)S(1)} %get-tuple-element.308), channel_id=1, source_target_pairs={{0,16},{2,18},{4,20},{6,22},{8,24},{10,26},{12,28},{14,30},{16,0},... | collective-permute-start | bytes 1400840 | tf_op jit(solution)/shard_map/ppermute | solution.py:78
  (150 other events, 2237.9 us)
